TPU v7x, 32 devices: a whole 2x2x4 slice. The times are simulated.
32 devices in a mesh: fsdp: 4 (over y, x), ctx: 4 (over z), tp: 2 (over core).
Axes of the slice: x: 2, y: 2, z: 4, core: 2. Of those that a mesh axis runs over, the one named last changes fastest.
Arguments:
- hidden_in: bfloat16 [8, 1024, 1024], P('fsdp', ('ctx', 'tp')), may hold values from -6 to 6
- seq_lengths: int32 [8], P('fsdp'), may hold values from 512 to 1024, as said below
- attn_gain: float32 [1024], replicated, may hold values from 0.1 to 1.9
- query_gain: float32 [64], replicated, may hold values from 0.1 to 1.9
- key_gain: float32 [64], replicated, may hold values from 0.1 to 1.9
- query_weight: bfloat16 [1024, 1024], P(('fsdp', 'ctx'), 'tp'), may hold values from -0.1875 to 0.1875
- key_projection: bfloat16 [1024, 512], P(('fsdp', 'ctx'), 'tp'), may hold values from -0.1875 to 0.1875
- value_projection: bfloat16 [1024, 512], P(('fsdp', 'ctx'), 'tp'), may hold values from -0.1875 to 0.1875
- out_weight: bfloat16 [1024, 1024], P('tp', ('fsdp', 'ctx')), may hold values from -1 to 1
- ffn_gain: float32 [1024], replicated, may hold values from 0.1 to 1.9
- gate_weight: bfloat16 [1024, 4608], P(('fsdp', 'ctx'), 'tp'), may hold values from -0.1875 to 0.1875
- up_weight: bfloat16 [1024, 4608], P(('fsdp', 'ctx'), 'tp'), may hold values from -0.1875 to 0.1875
- down_weight: bfloat16 [4608, 1024], P('tp', ('fsdp', 'ctx')), may hold values from -0.09375 to 0.09375
- cotangent: bfloat16 [8, 1024, 1024], P('fsdp', ('ctx', 'tp')), may hold values from -6 to 6
Outputs:
- block_out: bfloat16 [8, 1024, 1024], P('fsdp', ('ctx', 'tp'))
- input_grad: bfloat16 [8, 1024, 1024], P('fsdp', ('ctx', 'tp'))
- attn_gain_grad: float32 [1024], replicated
- query_gain_grad: float32 [64], replicated
- key_gain_grad: float32 [64], replicated
- query_weight_grad: float32 [1024, 1024], P(('fsdp', 'ctx'), 'tp')
- key_weight_grad: float32 [1024, 512], P(('fsdp', 'ctx'), 'tp')
- value_weight_grad: float32 [1024, 512], P(('fsdp', 'ctx'), 'tp')
- out_weight_grad: float32 [1024, 1024], P('tp', ('fsdp', 'ctx'))
- ffn_gain_grad: float32 [1024], replicated
- gate_weight_grad: float32 [1024, 4608], P(('fsdp', 'ctx'), 'tp')
- up_weight_grad: float32 [1024, 4608], P(('fsdp', 'ctx'), 'tp')
- down_weight_grad: float32 [4608, 1024], P('tp', ('fsdp', 'ctx'))
Inputs may be any that keep to these rules, and one draw needn't show every extreme that they name: `seq_lengths`: among the 2 slots of each index of fsdp (aligned blocks of 2 slots) at least one has length 1024.
All inputs are finite; a program needn't handle non-finite values.
Results may differ from a plain program's by a relative error of at most 0.017.
Values may be sent and summed in bfloat16 or wider, within the bound.
No kernel may reach another device: no remote copies, remote signals or barrier semaphores. Data moves between devices by JAX's collectives and lax.ppermute only.
A program may use at most 88 MiB of HBM per device.

v0:
```python
import jax
import jax.numpy as jnp
from jax import lax
from jax.sharding import PartitionSpec as P

QUERY_HEADS = 16
KEY_VALUE_HEADS = 8
HEAD_SIZE = 64


EPS = 1e-05
THETA = 1000000.0


def rms_scale(values, gain):
    return values * lax.rsqrt(jnp.mean(values * values, axis=-1, keepdims=True) + EPS) * gain


def rotate(values, places):
    half = HEAD_SIZE // 2
    freqs = THETA ** (-(jnp.arange(half).astype(jnp.float32) * 2.0 / HEAD_SIZE))
    angles = places.astype(jnp.float32)[:, None] * freqs[None, :]
    cosine = jnp.cos(angles)[:, None, :]
    sine = jnp.sin(angles)[:, None, :]
    first = values[..., :half]
    second = values[..., half:]
    return jnp.concatenate(
        [first * cosine - second * sine, second * cosine + first * sine], axis=-1
    )


def gather_weights(
    query_weight, key_projection, value_projection, gate_weight, up_weight, out_weight, down_weight
):
    return (
        lax.all_gather(query_weight, ("fsdp", "ctx"), axis=0, tiled=True),
        lax.all_gather(key_projection, ("fsdp", "ctx"), axis=0, tiled=True),
        lax.all_gather(value_projection, ("fsdp", "ctx"), axis=0, tiled=True),
        lax.all_gather(gate_weight, ("fsdp", "ctx"), axis=0, tiled=True),
        lax.all_gather(up_weight, ("fsdp", "ctx"), axis=0, tiled=True),
        lax.all_gather(out_weight, ("fsdp", "ctx"), axis=1, tiled=True),
        lax.all_gather(down_weight, ("fsdp", "ctx"), axis=1, tiled=True),
    )


def reduce_grads(grads):
    return (
        lax.psum_scatter(grads[0], ("fsdp", "ctx"), scatter_dimension=0, tiled=True),
        lax.psum_scatter(grads[1], ("fsdp", "ctx"), scatter_dimension=0, tiled=True),
        lax.psum_scatter(grads[2], ("fsdp", "ctx"), scatter_dimension=0, tiled=True),
        lax.psum_scatter(grads[3], ("fsdp", "ctx"), scatter_dimension=0, tiled=True),
        lax.psum_scatter(grads[4], ("fsdp", "ctx"), scatter_dimension=0, tiled=True),
        lax.psum_scatter(grads[5], ("fsdp", "ctx"), scatter_dimension=1, tiled=True),
        lax.psum_scatter(grads[6], ("fsdp", "ctx"), scatter_dimension=1, tiled=True),
    )


def add_into(totals, index, value_rows):
    return totals[index] + value_rows


def split_heads(query_rows, keys, values):
    rows = query_rows.shape[0]
    kv_heads = keys.shape[1] // HEAD_SIZE
    head_group = QUERY_HEADS // KEY_VALUE_HEADS
    per_head = (
        query_rows.reshape(rows, kv_heads, head_group, HEAD_SIZE)
        .transpose(1, 0, 2, 3)
        .reshape(kv_heads, rows * head_group, HEAD_SIZE)
    )
    key_heads = keys.reshape(keys.shape[0], kv_heads, HEAD_SIZE).transpose(1, 0, 2)
    value_heads = values.reshape(values.shape[0], kv_heads, HEAD_SIZE).transpose(1, 0, 2)
    return (per_head, key_heads, value_heads)


def merge_heads(per_head, rows):
    kv_heads = per_head.shape[0]
    head_group = QUERY_HEADS // KEY_VALUE_HEADS
    return (
        per_head.reshape(kv_heads, rows, head_group, HEAD_SIZE)
        .transpose(1, 0, 2, 3)
        .reshape(rows, kv_heads * head_group * HEAD_SIZE)
    )


def allowed_table(query_positions, key_count, length):
    row_positions = jnp.repeat(query_positions, QUERY_HEADS // KEY_VALUE_HEADS)
    key_places = jnp.arange(key_count)
    return (key_places[None, :] <= row_positions[:, None]) & (key_places[None, :] < length)


def attend_forward(query_rows, keys, values, query_positions, length):
    rows = query_rows.shape[0]
    scale_factor = HEAD_SIZE ** (-0.5)
    per_head, key_heads, value_heads = split_heads(query_rows, keys, values)
    allowed = allowed_table(query_positions, keys.shape[0], length)

    def one_head(operands):
        query_head, key_head, value_head = operands
        scores = (
            jnp.einsum("qd,kd->qk", query_head, key_head, preferred_element_type=jnp.float32)
            * scale_factor
        )
        scores = jnp.where(allowed, scores, -1e30)
        top = jnp.max(scores, axis=-1, keepdims=True)
        exp_scores = jnp.exp(scores - top)
        total = jnp.sum(exp_scores, axis=-1, keepdims=True)
        probs = exp_scores / total
        mixed = jnp.einsum(
            "qk,kd->qd", probs.astype(jnp.bfloat16), value_head, preferred_element_type=jnp.float32
        )
        return (mixed.astype(jnp.bfloat16), (top + jnp.log(total))[:, 0])

    mixed, log_total = lax.map(one_head, (per_head, key_heads, value_heads))
    return (merge_heads(mixed, rows), log_total)


def attend_backward(query_rows, keys, values, log_total, grad_attn, query_positions, length):
    rows = query_rows.shape[0]
    scale_factor = HEAD_SIZE ** (-0.5)
    per_head, key_heads, value_heads = split_heads(query_rows, keys, values)
    grad_heads = split_heads(grad_attn, keys, values)[0]
    allowed = allowed_table(query_positions, keys.shape[0], length)

    def one_head(operands):
        query_head, key_head, value_head, lse_head, grad_head = operands
        scores = (
            jnp.einsum("qd,kd->qk", query_head, key_head, preferred_element_type=jnp.float32)
            * scale_factor
        )
        scores = jnp.where(allowed, scores, -1e30)
        probs = jnp.exp(scores - lse_head[:, None])
        grad_probs = jnp.einsum(
            "qd,kd->qk", grad_head, value_head, preferred_element_type=jnp.float32
        )
        inner = jnp.sum(probs * grad_probs, axis=-1, keepdims=True)
        grad_scores = (probs * (grad_probs - inner)).astype(jnp.bfloat16)
        grad_query = scale_factor * jnp.einsum(
            "qk,kd->qd", grad_scores, key_head, preferred_element_type=jnp.float32
        )
        grad_key = scale_factor * jnp.einsum(
            "qk,qd->kd", grad_scores, query_head, preferred_element_type=jnp.float32
        )
        grad_value = jnp.einsum(
            "qk,qd->kd", probs.astype(jnp.bfloat16), grad_head, preferred_element_type=jnp.float32
        )
        return (grad_query, grad_key, grad_value)

    grad_query, grad_key, grad_value = lax.map(
        one_head, (per_head, key_heads, value_heads, log_total, grad_heads)
    )
    key_rows = keys.shape[0]
    grad_key = grad_key.transpose(1, 0, 2).reshape(key_rows, keys.shape[1])
    grad_value = grad_value.transpose(1, 0, 2).reshape(key_rows, values.shape[1])
    return (merge_heads(grad_query, rows), grad_key, grad_value)


def micro_step(weights, gains, hidden, length, grad_in, row_positions, block_places, totals):
    query_w, key_matrix, value_matrix, gate_w, up_w, out_w, down_w = weights
    attn_g, query_g, key_g, ffn_g = gains
    hidden_wide = hidden.astype(jnp.float32)
    norm_one, norm_one_pull = jax.vjp(rms_scale, hidden_wide, attn_g)
    normalized_input = lax.all_gather(norm_one.astype(jnp.bfloat16), "tp", axis=0, tiled=True)
    rows = normalized_input.shape[0]
    query_raw = jnp.dot(normalized_input, query_w, preferred_element_type=jnp.float32)
    key_unrotated = jnp.dot(normalized_input, key_matrix, preferred_element_type=jnp.float32)
    value_raw = jnp.dot(normalized_input, value_matrix, preferred_element_type=jnp.float32)

    def prepare(raw, gain):
        return rotate(rms_scale(raw.reshape(rows, -1, HEAD_SIZE), gain), block_places)

    query_prep, query_pull = jax.vjp(prepare, query_raw, query_g)
    key_prep, key_pull = jax.vjp(prepare, key_unrotated, key_g)
    query_rows = query_prep.reshape(rows, -1).astype(jnp.bfloat16)
    key = key_prep.reshape(rows, -1).astype(jnp.bfloat16)
    value_rows = value_raw.astype(jnp.bfloat16)
    keys_all, values_all = (
        lax.all_gather(key, "ctx", axis=0, tiled=True),
        lax.all_gather(value_rows, "ctx", axis=0, tiled=True),
    )
    attn, log_total = attend_forward(query_rows, keys_all, values_all, block_places, length)
    branch = lax.psum_scatter(
        jnp.dot(attn, out_w, preferred_element_type=jnp.float32),
        "tp",
        scatter_dimension=0,
        tiled=True,
    )
    middle = hidden_wide + branch
    norm_two, norm_two_pull = jax.vjp(rms_scale, middle, ffn_g)
    normed_two = lax.all_gather(norm_two.astype(jnp.bfloat16), "tp", axis=0, tiled=True)
    gate = jnp.dot(normed_two, gate_w, preferred_element_type=jnp.float32)
    upper = jnp.dot(normed_two, up_w, preferred_element_type=jnp.float32)
    act_wide, act_pull = jax.vjp(lambda left, right: jax.nn.silu(left) * right, gate, upper)
    act = act_wide.astype(jnp.bfloat16)
    ffn_part = lax.psum_scatter(
        jnp.dot(act, down_w, preferred_element_type=jnp.float32).astype(jnp.bfloat16),
        "tp",
        scatter_dimension=0,
        tiled=True,
    ).astype(jnp.float32)
    valid = (row_positions < length)[:, None]
    result = jnp.where(valid, middle + ffn_part, 0.0).astype(jnp.bfloat16)
    grad_rows = jnp.where(valid, grad_in, jnp.zeros_like(grad_in))
    grad_full = lax.all_gather(grad_rows, "tp", axis=0, tiled=True)
    grad_act = jnp.einsum("td,fd->tf", grad_full, down_w, preferred_element_type=jnp.float32)
    down_grad = add_into(
        totals, 6, jnp.einsum("tf,td->fd", act, grad_full, preferred_element_type=jnp.float32)
    )
    grad_gate, grad_up = act_pull(grad_act)
    grad_gate = grad_gate.astype(jnp.bfloat16)
    grad_up = grad_up.astype(jnp.bfloat16)
    grad_normed_two = jnp.einsum(
        "tf,df->td", grad_gate, gate_w, preferred_element_type=jnp.float32
    ) + jnp.einsum("tf,df->td", grad_up, up_w, preferred_element_type=jnp.float32)
    gate_grad = add_into(
        totals,
        3,
        jnp.einsum("td,tf->df", normed_two, grad_gate, preferred_element_type=jnp.float32),
    )
    up_grad = add_into(
        totals, 4, jnp.einsum("td,tf->df", normed_two, grad_up, preferred_element_type=jnp.float32)
    )
    grad_norm_two = lax.psum_scatter(grad_normed_two, "tp", scatter_dimension=0, tiled=True)
    grad_middle_part, ffn_gain_grad = norm_two_pull(grad_norm_two)
    grad_middle = grad_rows.astype(jnp.float32) + grad_middle_part
    grad_branch = lax.all_gather(grad_middle.astype(jnp.bfloat16), "tp", axis=0, tiled=True)
    out_grad = add_into(
        totals, 5, jnp.einsum("th,td->hd", attn, grad_branch, preferred_element_type=jnp.float32)
    )
    grad_attn = jnp.einsum(
        "td,hd->th", grad_branch, out_w, preferred_element_type=jnp.float32
    ).astype(jnp.bfloat16)
    grad_query_rot, grad_keys_all, grad_values_all = attend_backward(
        query_rows, keys_all, values_all, log_total, grad_attn, block_places, length
    )
    grad_key_rot, grad_value = (
        lax.psum_scatter(
            grad_keys_all.astype(jnp.bfloat16), "ctx", scatter_dimension=0, tiled=True
        ).astype(jnp.float32),
        lax.psum_scatter(
            grad_values_all.astype(jnp.bfloat16), "ctx", scatter_dimension=0, tiled=True
        ).astype(jnp.float32),
    )
    grad_query_raw, query_gain_grad = query_pull(grad_query_rot.reshape(rows, -1, HEAD_SIZE))
    grad_key_raw, key_gain_grad = key_pull(grad_key_rot.reshape(rows, -1, HEAD_SIZE))
    grad_query = grad_query_raw.astype(jnp.bfloat16)
    grad_key = grad_key_raw.astype(jnp.bfloat16)
    grad_value = grad_value.astype(jnp.bfloat16)
    grad_normed = jnp.einsum("th,dh->td", grad_query, query_w, preferred_element_type=jnp.float32)
    grad_normed = grad_normed + jnp.einsum(
        "th,dh->td", grad_key, key_matrix, preferred_element_type=jnp.float32
    )
    grad_normed = grad_normed + jnp.einsum(
        "th,dh->td", grad_value, value_matrix, preferred_element_type=jnp.float32
    )
    query_grad = add_into(
        totals,
        0,
        jnp.einsum("td,th->dh", normalized_input, grad_query, preferred_element_type=jnp.float32),
    )
    key_grad = add_into(
        totals,
        1,
        jnp.einsum("td,th->dh", normalized_input, grad_key, preferred_element_type=jnp.float32),
    )
    value_grad = add_into(
        totals,
        2,
        jnp.einsum("td,th->dh", normalized_input, grad_value, preferred_element_type=jnp.float32),
    )
    grad_norm_one = lax.psum_scatter(
        grad_normed.astype(jnp.bfloat16), "tp", scatter_dimension=0, tiled=True
    ).astype(jnp.float32)
    grad_hidden_part, attn_gain_grad = norm_one_pull(grad_norm_one)
    grad_hidden = (grad_middle + grad_hidden_part).astype(jnp.bfloat16)
    weight_grads = (query_grad, key_grad, value_grad, gate_grad, up_grad, out_grad, down_grad)
    gain_grads = (attn_gain_grad, query_gain_grad, key_gain_grad, ffn_gain_grad)
    return (result, grad_hidden, weight_grads, gain_grads)


def body(
    hidden_in,
    seq_lengths,
    attn_gain,
    query_gain,
    key_gain,
    query_weight,
    key_projection,
    value_projection,
    out_weight,
    ffn_gain,
    gate_weight,
    up_weight,
    down_weight,
    cotangent,
):
    shard_rows = hidden_in.shape[1]
    block_rows = shard_rows * lax.axis_size("tp")
    ctx_index = lax.axis_index("ctx")
    tp_index = lax.axis_index("tp")
    block_places = ctx_index * block_rows + jnp.arange(block_rows)
    row_positions = ctx_index * block_rows + tp_index * shard_rows + jnp.arange(shard_rows)
    gains = (attn_gain, query_gain, key_gain, ffn_gain)
    gain_zero = tuple((jnp.zeros(item.shape, jnp.float32) for item in gains))
    inputs = (hidden_in, seq_lengths, cotangent)

    def add_up(left, right):
        return jax.tree.map(lambda first, second: first + second, left, right)

    held = gather_weights(
        query_weight,
        key_projection,
        value_projection,
        gate_weight,
        up_weight,
        out_weight,
        down_weight,
    )
    full_zero = tuple((jnp.zeros(item.shape, jnp.float32) for item in held))

    def step_held(carry, item):
        result, grad_hidden, weight_grads, gain_grads = micro_step(
            held, gains, item[0], item[1], item[2], row_positions, block_places, carry[0]
        )
        return ((weight_grads, add_up(carry[1], gain_grads)), (result, grad_hidden))

    (full_grads, gain_total), (results, grad_hiddens) = lax.scan(
        step_held, (full_zero, gain_zero), inputs
    )
    shards = reduce_grads(full_grads)
    gain_sums = lax.psum(
        (gain_total[0], gain_total[1], gain_total[2], gain_total[3]), ("fsdp", "ctx", "tp")
    )
    return (
        results,
        grad_hiddens,
        gain_sums[0],
        gain_sums[1],
        gain_sums[2],
        shards[0],
        shards[1],
        shards[2],
        shards[5],
        gain_sums[3],
        shards[3],
        shards[4],
        shards[6],
    )


def solution(mesh):
    in_specs = (
        P("fsdp", ("ctx", "tp"), None),
        P("fsdp"),
        P(),
        P(),
        P(),
        P(("fsdp", "ctx"), "tp"),
        P(("fsdp", "ctx"), "tp"),
        P(("fsdp", "ctx"), "tp"),
        P("tp", ("fsdp", "ctx")),
        P(),
        P(("fsdp", "ctx"), "tp"),
        P(("fsdp", "ctx"), "tp"),
        P("tp", ("fsdp", "ctx")),
        P("fsdp", ("ctx", "tp"), None),
    )
    out_specs = (
        P("fsdp", ("ctx", "tp"), None),
        P("fsdp", ("ctx", "tp"), None),
        P(),
        P(),
        P(),
        P(("fsdp", "ctx"), "tp"),
        P(("fsdp", "ctx"), "tp"),
        P(("fsdp", "ctx"), "tp"),
        P("tp", ("fsdp", "ctx")),
        P(),
        P(("fsdp", "ctx"), "tp"),
        P(("fsdp", "ctx"), "tp"),
        P("tp", ("fsdp", "ctx")),
    )
    return jax.shard_map(body, mesh=mesh, in_specs=in_specs, out_specs=out_specs, check_vma=False)
```

profile of v0, /device:TPU:0, one launch (start us, length us, event | category | flops | bytes accessed | tf_op | source)
XLA Modules:
  0.0 1672.6 jit_solution(6908266006350671478)
XLA Ops:
  10.7 51.0 %all_gather.58 = bf16[1024,256]{1,0:T(8,128)(2,1)} all-gather(bf16[64,256]{1,0:T(8,128)(2,1)} %param.26), channel_id=1, replica_groups=mesh['fsdp'=4,'ctx'=4,'tp'=2] {'fsdp','ctx'}, dimensions={0}, use_global_device_ids=true | all-gather | bytes 557056 | tf_op jit(solution)/shard_map/all_gather | solution.py:37
  61.7 45.4 %all_gather.59 = bf16[1024,256]{1,0:T(8,128)(2,1)} all-gather(bf16[64,256]{1,0:T(8,128)(2,1)} %param.27), channel_id=1, replica_groups=mesh['fsdp'=4,'ctx'=4,'tp'=2] {'fsdp','ctx'}, dimensions={0}, use_global_device_ids=true | all-gather | bytes 557056 | tf_op jit(solution)/shard_map/all_gather | solution.py:38
  107.1 2.3 copy.84
  109.4 45.0 %all-gather.8.cloned.1.call-done = bf16[2304,1024]{0,1:T(8,128)(2,1)} async-done(((bf16[2304,64]{0,1:T(8,128)(2,1)}), bf16[2304,1024]{0,1:T(8,128)(2,1)}) %all-gather.8.cloned.1.call-update) | async-done | bytes 4718608 | tf_op jit(solution)/shard_map/all_gather | solution.py:42
  154.4 6.6 copy.83
  161.0 50.1 %all-gather.6.cloned.1.call-done = bf16[1024,512]{1,0:T(8,128)(2,1)} async-done(((bf16[64,512]{1,0:T(8,128)(2,1)}), bf16[1024,512]{1,0:T(8,128)(2,1)}) %all-gather.6.cloned.1.call-update) | async-done | bytes 1048592 | tf_op jit(solution)/shard_map/all_gather | solution.py:36
  211.2 81.9 %all-gather.14.cloned.1.call-done = bf16[1024,2304]{1,0:T(8,128)(2,1)} async-done(((bf16[64,2304]{1,0:T(8,128)(2,1)}), bf16[1024,2304]{1,0:T(8,128)(2,1)}) %all-gather.14.cloned.1.call-update) | async-done | bytes 4718608 | tf_op jit(solution)/shard_map/all_gather | solution.py:39
  293.1 81.7 %all-gather.12.cloned.1.call-done = bf16[1024,2304]{1,0:T(8,128)(2,1)} async-done(((bf16[64,2304]{1,0:T(8,128)(2,1)}), bf16[1024,2304]{1,0:T(8,128)(2,1)}) %all-gather.12.cloned.1.call-update) | async-done | bytes 4718608 | tf_op jit(solution)/shard_map/all_gather | solution.py:40
  374.8 437.0 %while.102 = (s32[]{:T(128)}, f32[1024,512]{1,0:T(8,128)}, f32[1024,256]{1,0:T(8,128)}, f32[1024,256]{1,0:T(8,128)}, f32[1024,2304]{1,0:T(8,128)}, /*index=5*/f3...) while((s32[]{:T(128)}, f32[1024,512]{1,0:T(8,128)}, ...), condition=%wide.region_26.27_spmd.clone.clone.clone, body=%wide.region_0.26_spmd.clone.clone.clone.sunk | while | flops 13810335744 | bytes 352562688 | solution.py:327
  377.4 2.2 all_gather.88
  384.0 15.9 all_gather.89
  399.8 15.6 all_gather.90
  421.5 19.3 %while.103 = (s32[]{:T(128)}, bf16[4,512,64]{1,2,0:T(8,128)(2,1)}, f32[4,512]{1,0:T(4,128)}, bf16[4,512,64]{2,1,0:T(8,128)(2,1)S(1)}, bf16[4,1024,64]{2,1,0:T(8,...) while((s32[]{:T(128)}, bf16[4,512,64]{1,2,0:T(8,128)(2,1)}, ...), condition=%wide.region_7.7_spmd.clone, body=%wide.region_4.6_spmd.clone.sunk | while | flops 139492864 | bytes 7038065 | solution.py:114
  440.8 2.1 copy.102
  444.8 2.8 fusion.249
  449.5 2.2 all_gather.92
  451.6 5.4 fusion.252
  458.4 2.3 all_gather.91
  460.7 3.9 fusion.251
  468.1 2.4 convolution_add_fusion.9
  470.6 6.4 select_add_fusion.16
  477.0 5.0 select_add_fusion.18
  485.9 2.2 all_gather.93
  491.6 27.6 %while.104 = (s32[]{:T(128)}, f32[4,512,64]{1,2,0:T(8,128)}, bf16[4,1024,64]{1,2,0:T(8,128)(2,1)}, bf16[4,1024,64]{1,2,0:T(8,128)(2,1)}, bf16[4,512,64]{2,1,0:T(...) while((s32[]{:T(128)}, f32[4,512,64]{1,2,0:T(8,128)}, ...), condition=%wide.region_14.14_spmd.clone, body=%wide.region_12.13_spmd.clone.sunk | while | flops 341409280 | bytes 29247784 | solution.py:149
  526.2 13.8 reduce-scatter.32.cloned.1.call-done
  542.7 2.5 convolution_add_fusion.12
  545.2 17.7 %reduce-scatter.34.cloned.1.call-done = bf16[256,256]{0,1:T(8,128)(2,1)} async-done(((bf16[1024,256]{0,1:T(8,128)(2,1)}), bf16[256,256]{0,1:T(8,128)(2,1)}) %reduce-scatter.34.cloned.1.call-update) | async-done | bytes 131088 | tf_op jit(solution)/shard_map/while/body/eval_jaxpr/reduce_scatter | solution.py:240
  562.9 2.6 fusion.258
  565.6 4.5 convolution_convert_fusion.9
  570.1 6.4 select_add_fusion.15
  584.7 2.3 fusion.261
  589.6 2.2 all_gather.88
  596.2 15.6 all_gather.89
  611.8 16.0 all_gather.90
  633.8 19.3 %while.103 = (s32[]{:T(128)}, bf16[4,512,64]{1,2,0:T(8,128)(2,1)}, f32[4,512]{1,0:T(4,128)}, bf16[4,512,64]{2,1,0:T(8,128)(2,1)S(1)}, bf16[4,1024,64]{2,1,0:T(8,...) while((s32[]{:T(128)}, bf16[4,512,64]{1,2,0:T(8,128)(2,1)}, ...), condition=%wide.region_7.7_spmd.clone, body=%wide.region_4.6_spmd.clone.sunk | while | flops 139492864 | bytes 7038065 | solution.py:114
  653.2 2.1 copy.102
  657.2 2.8 fusion.249
  661.8 2.2 all_gather.92
  664.0 5.3 fusion.252
  670.7 2.3 all_gather.91
  673.0 3.9 fusion.251
  677.0 1.9 multiply_convert_fusion.8
  680.4 2.4 convolution_add_fusion.9
  682.9 9.2 select_add_fusion.16
  692.1 8.7 select_add_fusion.18
  704.8 2.2 all_gather.93
  710.4 27.6 %while.104 = (s32[]{:T(128)}, f32[4,512,64]{1,2,0:T(8,128)}, bf16[4,1024,64]{1,2,0:T(8,128)(2,1)}, bf16[4,1024,64]{1,2,0:T(8,128)(2,1)}, bf16[4,512,64]{2,1,0:T(...) while((s32[]{:T(128)}, f32[4,512,64]{1,2,0:T(8,128)}, ...), condition=%wide.region_14.14_spmd.clone, body=%wide.region_12.13_spmd.clone.sunk | while | flops 341409280 | bytes 29247784 | solution.py:149
  745.0 15.9 reduce-scatter.32.cloned.1.call-done
  763.7 2.5 convolution_add_fusion.12
  766.2 17.6 %reduce-scatter.34.cloned.1.call-done = bf16[256,256]{0,1:T(8,128)(2,1)} async-done(((bf16[1024,256]{0,1:T(8,128)(2,1)}), bf16[256,256]{0,1:T(8,128)(2,1)}) %reduce-scatter.34.cloned.1.call-update) | async-done | bytes 131088 | tf_op jit(solution)/shard_map/while/body/eval_jaxpr/reduce_scatter | solution.py:240
  783.7 2.6 fusion.258
  786.4 4.5 convolution_convert_fusion.9
  790.9 9.3 select_add_fusion.15
  800.3 3.5 select_add_fusion.14
  809.5 2.3 fusion.261
  817.2 9.6 copy.86
  827.6 39.3 %all-reduce.4 = (f32[1024]{0:T(1024)}, f32[64]{0:T(128)}, f32[64]{0:T(128)}, f32[1024]{0:T(1024)}) all-reduce(f32[1024]{0:T(1024)S(1)} %copy-done.53, f32[64]{0:T(128)S(1)} %copy-done.71, f32[64]{0:T(128)S(1)} %copy-done.68, f32[1024]{0:T(1024)S(1)} %copy-done.50), channel_id=1, replica_groups=mesh['fsdp'=4,'ctx'=4,'tp'=2] {'fsdp','ctx','tp'}, use_global_device_ids=true, to_apply=%region_27.28 | all-reduce | flops 2176 | bytes 17408 | tf_op jit(solution)/shard_map/psum | solution.py:331
  866.9 26.1 %reduce-scatter.16.cloned.1.call-done = f32[64,256]{1,0:T(8,128)} async-done(((f32[1024,256]{1,0:T(8,128)}), f32[64,256]{1,0:T(8,128)}) %reduce-scatter.16.cloned.1.call-update) | async-done | bytes 65552 | tf_op jit(solution)/shard_map/reduce_scatter | solution.py:49
  892.9 78.0 %reduce-scatter.18.cloned.1.call-done = f32[64,256]{1,0:T(8,128)} async-done(((f32[1024,256]{1,0:T(8,128)}), f32[64,256]{1,0:T(8,128)}) %reduce-scatter.18.cloned.1.call-update) | async-done | bytes 65552 | tf_op jit(solution)/shard_map/reduce_scatter | solution.py:50
  970.9 84.1 %reduce-scatter.14.cloned.1.call-done = f32[64,512]{1,0:T(8,128)} async-done(((f32[1024,512]{1,0:T(8,128)}), f32[64,512]{1,0:T(8,128)}) %reduce-scatter.14.cloned.1.call-update) | async-done | bytes 131088 | tf_op jit(solution)/shard_map/reduce_scatter | solution.py:48
  1054.9 83.9 %reduce-scatter.20.cloned.1.call-done = f32[512,64]{0,1:T(8,128)} async-done(((f32[512,1024]{0,1:T(8,128)}), f32[512,64]{0,1:T(8,128)}) %reduce-scatter.20.cloned.1.call-update) | async-done | bytes 131088 | tf_op jit(solution)/shard_map/reduce_scatter | solution.py:53
  1138.8 173.8 %reduce-scatter.22.cloned.1.call-done = f32[64,2304]{1,0:T(8,128)} async-done(((f32[1024,2304]{1,0:T(8,128)}), f32[64,2304]{1,0:T(8,128)}) %reduce-scatter.22.cloned.1.call-update) | async-done | bytes 589840 | tf_op jit(solution)/shard_map/reduce_scatter | solution.py:51
  1312.6 177.2 %reduce-scatter.24.cloned.1.call-done = f32[64,2304]{1,0:T(8,128)} async-done(((f32[1024,2304]{1,0:T(8,128)}), f32[64,2304]{1,0:T(8,128)}) %reduce-scatter.24.cloned.1.call-update) | async-done | bytes 589840 | tf_op jit(solution)/shard_map/reduce_scatter | solution.py:52
  1489.8 176.0 %reduce-scatter.26.cloned.1.call-done = f32[2304,64]{0,1:T(8,128)} async-done(((f32[2304,1024]{0,1:T(8,128)}), f32[2304,64]{0,1:T(8,128)}) %reduce-scatter.26.cloned.1.call-update) | async-done | bytes 589840 | tf_op jit(solution)/shard_map/reduce_scatter | solution.py:54
  (683 shorter events, 190.1 us)
Async XLA Ops:
  7.2 99.9 %all-gather.10.cloned.1.call-start = ((), (), s32[]{:S(2)}) async-start(), calls=%async_computation.15 | async-start | bytes 1114112 | tf_op jit(solution)/shard_map/all_gather | solution.py:41
  7.9 146.5 %all-gather.8.cloned.1.call-start = ((), (), s32[]{:S(2)}) async-start(), calls=%async_computation.14 | async-start | bytes 5013504 | tf_op jit(solution)/shard_map/all_gather | solution.py:42
  8.7 202.5 %all-gather.6.cloned.1.call-start = ((), (), s32[]{:S(2)}) async-start(), calls=%async_computation.13 | async-start | bytes 1114112 | tf_op jit(solution)/shard_map/all_gather | solution.py:36
  9.4 283.7 %all-gather.14.cloned.1.call-start = ((), (), s32[]{:S(2)}) async-start(), calls=%async_computation.17 | async-start | bytes 5013504 | tf_op jit(solution)/shard_map/all_gather | solution.py:39
  10.0 364.8 %all-gather.12.cloned.1.call-start = ((), (), s32[]{:S(2)}) async-start(), calls=%async_computation.16 | async-start | bytes 5013504 | tf_op jit(solution)/shard_map/all_gather | solution.py:40
  109.4 265.4 %copy-start.10 = (bf16[2,128,1024]{2,1,0:T(8,128)(2,1)S(1)}, bf16[2,128,1024]{2,1,0:T(8,128)(2,1)}, u32[]{:S(2)}) copy-start(bf16[2,128,1024]{2,1,0:T(8,128)(2,1)} %param.20) | copy-start | bytes 1572868
  109.4 265.4 %copy-start.37 = (f32[1024]{0:T(1024)S(1)}, f32[1024]{0:T(1024)}, u32[]{:S(2)}) copy-start(f32[1024]{0:T(1024)} %param.29) | copy-start | bytes 12292
  109.4 265.4 %copy-start.41 = (f32[1024]{0:T(1024)S(1)}, f32[1024]{0:T(1024)}, u32[]{:S(2)}) copy-start(f32[1024]{0:T(1024)} %param.22) | copy-start | bytes 12292
  109.4 265.4 %copy-start.54 = (f32[64]{0:T(128)S(1)}, f32[64]{0:T(128)}, u32[]{:S(2)}) copy-start(f32[64]{0:T(128)} %param.23) | copy-start | bytes 772
  374.8 82.2 %reduce-scatter.28.cloned.1.call-start = ((), (), s32[]{:S(2)}) async-start(), calls=%async_computation.25 | async-start | bytes 1572864 | tf_op jit(solution)/shard_map/while/body/eval_jaxpr/reduce_scatter | solution.py:182
  383.1 36.3 %copy-start.28 = (f32[256,32]{0,1:T(8,128)}, f32[256,32]{0,1:T(8,128)S(1)}, u32[]{:S(2)}) copy-start(f32[256,32]{0,1:T(8,128)S(1)} %get-tuple-element.1403) | copy-start | bytes 98308 | tf_op jit(solution)/shard_map/while
  383.1 36.3 %copy-start.30 = (f32[256,32]{0,1:T(8,128)}, f32[256,32]{0,1:T(8,128)S(1)}, u32[]{:S(2)}) copy-start(f32[256,32]{0,1:T(8,128)S(1)} %get-tuple-element.1402) | copy-start | bytes 98308 | tf_op jit(solution)/shard_map/while
  440.8 6.8 copy-start
  440.8 6.8 copy-start.15
  440.8 6.8 copy-start.61
  440.8 6.8 copy-start.75
  447.7 34.3 %reduce-scatter.30.cloned.1.call-start = ((), (), s32[]{:S(2)}) async-start(), calls=%async_computation.26 | async-start | bytes 1572864 | tf_op jit(solution)/shard_map/while/body/eval_jaxpr/reduce_scatter | solution.py:223
  448.4 8.7 copy-start.59
  458.2 6.3 copy-start.74
  458.3 6.3 copy-start.46
  458.3 6.3 slice-start.2
  460.7 5.9 slice-start
  466.6 10.4 copy-start.6
  470.5 69.4 %reduce-scatter.32.cloned.1.call-start = ((), (), s32[]{:S(2)}) async-start(), calls=%async_computation.27 | async-start | bytes 655360 | tf_op jit(solution)/shard_map/while/body/eval_jaxpr/reduce_scatter | solution.py:237
  470.6 6.4 copy-start.21
  482.0 6.9 copy-start.2
  519.3 43.7 %reduce-scatter.34.cloned.1.call-start = ((), (), s32[]{:S(2)}) async-start(), calls=%async_computation.28 | async-start | bytes 655360 | tf_op jit(solution)/shard_map/while/body/eval_jaxpr/reduce_scatter | solution.py:240
  524.6 16.4 copy-start.40
  524.6 17.3 %copy-start.44 = (f32[256,4]{0,1:T(4,128)S(1)}, f32[256,4]{0,1:T(4,128)}, u32[]{:S(2)}) copy-start(f32[256,4]{0,1:T(4,128)} %copy-done.43) | copy-start | bytes 12292 | tf_op jit(solution)/shard_map/while
  526.1 57.0 %reduce-scatter.36.cloned.1.call-start = ((), (), s32[]{:S(2)}) async-start(), calls=%async_computation.29 | async-start | bytes 786432 | tf_op jit(solution)/shard_map/while/body/eval_jaxpr/reduce_scatter | solution.py:271
  542.7 22.9 %copy-start.7 = (bf16[256,2304]{1,0:T(8,128)(2,1)S(1)}, bf16[256,2304]{1,0:T(8,128)(2,1)}, u32[]{:S(2)}) copy-start(bf16[256,2304]{1,0:T(8,128)(2,1)} %copy-done.6) | copy-start | bytes 3538948 | tf_op jit(solution)/shard_map/while
  565.5 19.1 %reduce-scatter.38.cloned.1.call-start = ((), (), s32[]{:S(2)}) async-start(), calls=%async_computation.30 | async-start | bytes 786432 | tf_op jit(solution)/shard_map/while/body/eval_jaxpr/reduce_scatter | solution.py:195
  570.1 6.5 copy-start.19
  587.0 82.3 %reduce-scatter.28.cloned.1.call-start = ((), (), s32[]{:S(2)}) async-start(), calls=%async_computation.25 | async-start | bytes 1572864 | tf_op jit(solution)/shard_map/while/body/eval_jaxpr/reduce_scatter | solution.py:182
  595.3 36.4 %copy-start.28 = (f32[256,32]{0,1:T(8,128)}, f32[256,32]{0,1:T(8,128)S(1)}, u32[]{:S(2)}) copy-start(f32[256,32]{0,1:T(8,128)S(1)} %get-tuple-element.1403) | copy-start | bytes 98308 | tf_op jit(solution)/shard_map/while
  595.3 36.4 %copy-start.30 = (f32[256,32]{0,1:T(8,128)}, f32[256,32]{0,1:T(8,128)S(1)}, u32[]{:S(2)}) copy-start(f32[256,32]{0,1:T(8,128)S(1)} %get-tuple-element.1402) | copy-start | bytes 98308 | tf_op jit(solution)/shard_map/while
  653.2 6.8 copy-start
  653.2 6.8 copy-start.15
  653.2 6.8 copy-start.61
  653.2 6.8 copy-start.75
  660.0 40.8 %reduce-scatter.30.cloned.1.call-start = ((), (), s32[]{:S(2)}) async-start(), calls=%async_computation.26 | async-start | bytes 1572864 | tf_op jit(solution)/shard_map/while/body/eval_jaxpr/reduce_scatter | solution.py:223
  660.8 8.6 copy-start.59
  670.5 6.4 copy-start.74
  670.6 6.3 copy-start.46
  670.6 6.3 slice-start.2
  673.0 5.9 slice-start
  678.9 13.2 copy-start.6
  682.8 78.1 %reduce-scatter.32.cloned.1.call-start = ((), (), s32[]{:S(2)}) async-start(), calls=%async_computation.27 | async-start | bytes 655360 | tf_op jit(solution)/shard_map/while/body/eval_jaxpr/reduce_scatter | solution.py:237
  682.9 9.2 copy-start.21
  700.8 6.9 copy-start.2
  738.1 45.7 %reduce-scatter.34.cloned.1.call-start = ((), (), s32[]{:S(2)}) async-start(), calls=%async_computation.28 | async-start | bytes 655360 | tf_op jit(solution)/shard_map/while/body/eval_jaxpr/reduce_scatter | solution.py:240
  743.4 18.6 %copy-start.40 = (f32[256,4]{0,1:T(4,128)S(1)}, f32[256,4]{0,1:T(4,128)}, u32[]{:S(2)}) copy-start(f32[256,4]{0,1:T(4,128)} %copy-done.39) | copy-start | bytes 12292 | tf_op jit(solution)/shard_map/while
  743.5 19.4 %copy-start.44 = (f32[256,4]{0,1:T(4,128)S(1)}, f32[256,4]{0,1:T(4,128)}, u32[]{:S(2)}) copy-start(f32[256,4]{0,1:T(4,128)} %copy-done.43) | copy-start | bytes 12292 | tf_op jit(solution)/shard_map/while
  745.0 63.0 %reduce-scatter.36.cloned.1.call-start = ((), (), s32[]{:S(2)}) async-start(), calls=%async_computation.29 | async-start | bytes 786432 | tf_op jit(solution)/shard_map/while/body/eval_jaxpr/reduce_scatter | solution.py:271
  763.7 22.7 %copy-start.7 = (bf16[256,2304]{1,0:T(8,128)(2,1)S(1)}, bf16[256,2304]{1,0:T(8,128)(2,1)}, u32[]{:S(2)}) copy-start(bf16[256,2304]{1,0:T(8,128)(2,1)} %copy-done.6) | copy-start | bytes 3538948 | tf_op jit(solution)/shard_map/while
  786.3 23.1 %reduce-scatter.38.cloned.1.call-start = ((), (), s32[]{:S(2)}) async-start(), calls=%async_computation.30 | async-start | bytes 786432 | tf_op jit(solution)/shard_map/while/body/eval_jaxpr/reduce_scatter | solution.py:195
  790.9 9.3 copy-start.19
  811.8 81.1 %reduce-scatter.16.cloned.1.call-start = ((), (), s32[]{:S(2)}) async-start(), calls=%async_computation.19 | async-start | bytes 1114112 | tf_op jit(solution)/shard_map/reduce_scatter | solution.py:49
  812.4 158.5 %reduce-scatter.18.cloned.1.call-start = ((), (), s32[]{:S(2)}) async-start(), calls=%async_computation.20 | async-start | bytes 1114112 | tf_op jit(solution)/shard_map/reduce_scatter | solution.py:50
  813.2 241.8 %reduce-scatter.14.cloned.1.call-start = ((), (), s32[]{:S(2)}) async-start(), calls=%async_computation.18 | async-start | bytes 2228224 | tf_op jit(solution)/shard_map/reduce_scatter | solution.py:48
  813.8 325.0 %reduce-scatter.20.cloned.1.call-start = ((), (), s32[]{:S(2)}) async-start(), calls=%async_computation.21 | async-start | bytes 2228224 | tf_op jit(solution)/shard_map/reduce_scatter | solution.py:53
  815.7 496.9 %reduce-scatter.22.cloned.1.call-start = ((), (), s32[]{:S(2)}) async-start(), calls=%async_computation.22 | async-start | bytes 10027008 | tf_op jit(solution)/shard_map/reduce_scatter | solution.py:51
  816.4 673.3 %reduce-scatter.24.cloned.1.call-start = ((), (), s32[]{:S(2)}) async-start(), calls=%async_computation.23 | async-start | bytes 10027008 | tf_op jit(solution)/shard_map/reduce_scatter | solution.py:52
  817.2 848.6 %reduce-scatter.26.cloned.1.call-start = ((), (), s32[]{:S(2)}) async-start(), calls=%async_computation.24 | async-start | bytes 10027008 | tf_op jit(solution)/shard_map/reduce_scatter | solution.py:54
  (151 other events, 356.7 us)
Sparse Core Ops, SparseCore 0:
  10.8 60.1 all-gather.9
  73.8 80.6 all-gather.7
  157.2 53.9 all-gather.5
  213.8 79.2 all-gather.13
  295.7 79.0 all-gather.11
  447.8 6.9 reduce-scatter.27
  470.6 7.4 reduce-scatter.29
  519.4 20.5 reduce-scatter.31
  542.9 19.9 reduce-scatter.33
  565.7 6.2 reduce-scatter.35
  576.6 7.2 reduce-scatter.37
  660.1 9.0 reduce-scatter.27
  682.9 9.5 reduce-scatter.29
  738.2 22.6 reduce-scatter.31
  763.7 19.9 reduce-scatter.33
  786.5 6.1 reduce-scatter.35
  800.4 6.3 reduce-scatter.37
  815.2 77.6 reduce-scatter.15
  895.8 75.0 reduce-scatter.17
  973.6 81.3 reduce-scatter.13
  1057.8 80.9 reduce-scatter.19
  1145.1 167.5 reduce-scatter.21
  1319.8 169.9 reduce-scatter.23
  1495.9 169.8 reduce-scatter.25
where the time goes:
time: 1680 us; the launch traced here: 1670 us
  waiting for transfers between devices  1130 us (67%)
  blocking collectives  216 us (13%)
  matrix products  181 us (11%)
  local copies, waits for them, and re-layouts  83.8 us (5%)
  other arithmetic  44 us (3%)
    reduce_scatter x1, waiting for transfers between devices, reduce_grads(): lax.psum_scatter(grads[4], ('fsdp', 'ctx'), scatter_dimension=0, tiled=True)  177 us
    reduce_scatter x1, waiting for transfers between devices, reduce_grads(): lax.psum_scatter(grads[6], ('fsdp', 'ctx'), scatter_dimension=1, tiled=True)  176 us
    reduce_scatter x1, waiting for transfers between devices, reduce_grads(): lax.psum_scatter(grads[3], ('fsdp', 'ctx'), scatter_dimension=0, tiled=True)  174 us
    reduce_scatter x1, waiting for transfers between devices, reduce_grads(): lax.psum_scatter(grads[0], ('fsdp', 'ctx'), scatter_dimension=0, tiled=True)  84.1 us
    reduce_scatter x1, waiting for transfers between devices, reduce_grads(): lax.psum_scatter(grads[5], ('fsdp', 'ctx'), scatter_dimension=1, tiled=True)  83.9 us
    all_gather x1, waiting for transfers between devices, gather_weights(): lax.all_gather(gate_weight, ('fsdp', 'ctx'), axis=0, tiled=True)  81.9 us
    all_gather x1, waiting for transfers between devices, gather_weights(): lax.all_gather(up_weight, ('fsdp', 'ctx'), axis=0, tiled=True)  81.7 us
    reduce_scatter x1, waiting for transfers between devices, reduce_grads(): lax.psum_scatter(grads[2], ('fsdp', 'ctx'), scatter_dimension=0, tiled=True)  78 us
  transfers between devices with their start and end apart: 24, of which 15 were waited for; matrix products, arithmetic and copies ran while one was open for 7% of the time, Pallas kernels for 0%

commit v1 on v0

v1 whole, which is shorter than its diff:
```python
import functools

import jax
import jax.numpy as jnp
import numpy as np
from jax import lax
from jax.experimental import pallas as pl
from jax.experimental.pallas import tpu as pltpu
from jax.sharding import PartitionSpec as P

HEAD = 64
TILE = 128
EPS = 1e-05
THETA = 1000000.0
SCALE = HEAD**-0.5
EXP2_SCALE = SCALE * float(np.log2(np.e))
FAR = -1e30
BF = jnp.bfloat16
F32 = jnp.float32
VMEM_LIMIT = 56 * 1024 * 1024


def dot(left, right, dims):
    return lax.dot_general(left, right, (dims, ((), ())), preferred_element_type=F32)


NN = ((1,), (0,))
NT = ((1,), (1,))
TN = ((0,), (0,))


def swap_cores(value):
    return lax.ppermute(value, "tp", [(0, 1), (1, 0)])


def fsdp_xor(value, mask):
    size = lax.axis_size("fsdp")
    return lax.ppermute(value, "fsdp", [(i, i ^ mask) for i in range(size)])


def ctx_up(value, step=1):
    size = lax.axis_size("ctx")
    return lax.ppermute(value, "ctx", [(i, i + step) for i in range(size - step)])


def ctx_down(value, step=1):
    size = lax.axis_size("ctx")
    return lax.ppermute(value, "ctx", [(i + step, i) for i in range(size - step)])


def ctx_shift(value, step):
    size = lax.axis_size("ctx")
    return lax.ppermute(value, "ctx", [(i, (i + step) % size) for i in range(size)])


def sum_everywhere(value):
    for axis in ("tp", "fsdp", "ctx"):
        size = lax.axis_size(axis)
        step = 1
        while step < size:
            value = value + lax.ppermute(value, axis, [(i, i ^ step) for i in range(size)])
            step *= 2
    return value


def lane_ids(rows):
    return lax.broadcasted_iota(jnp.int32, (rows, TILE), 1)


def half_swap(x):
    low = lane_ids(x.shape[0]) % HEAD < HEAD // 2
    return jnp.where(low, pltpu.roll(x, TILE - HEAD // 2, 1), pltpu.roll(x, HEAD // 2, 1))


def head_mean(x):
    first = lane_ids(x.shape[0]) < HEAD
    left = jnp.sum(jnp.where(first, x, 0.0), axis=1, keepdims=True)
    right = jnp.sum(jnp.where(first, 0.0, x), axis=1, keepdims=True)
    return jnp.where(first, left, right) * (1.0 / HEAD)


def prepare(x, gain, cosine, sine):
    scaled = x * lax.rsqrt(head_mean(x * x) + EPS) * gain
    return scaled * cosine + half_swap(scaled) * sine


def prepare_back(x, gain, cosine, sine, grad):
    grad = grad * cosine - half_swap(grad) * sine
    inverse = lax.rsqrt(head_mean(x * x) + EPS)
    normal = x * inverse
    gain_grad = jnp.sum(grad * normal, axis=0, keepdims=True)
    grad = grad * gain
    return inverse * (grad - normal * head_mean(grad * normal)), gain_grad


def key_bias(scal_ref, slot, keys, block_rows):
    c = scal_ref[0]
    core = scal_ref[1]
    length = scal_ref[2 + slot]
    half = block_rows // 2

    def places(index):
        block = index // block_rows
        side = (index // half) % 2
        return (c - block) * block_rows + (side + core - 2 * side * core) * half + index % half

    key_at = places(lax.broadcasted_iota(jnp.int32, (keys, block_rows), 0))
    query_at = places(lax.broadcasted_iota(jnp.int32, (keys, block_rows), 1))
    seen = (key_at >= 0) & (key_at <= query_at) & (key_at < length)
    return jnp.where(seen, 0.0, FAR)


def twins(x):
    first = lane_ids(x.shape[0]) < HEAD
    turned = pltpu.roll(x, HEAD, 1)
    return jnp.where(first, x, turned).astype(BF), jnp.where(first, turned, x).astype(BF)


def attend_kernel(scal_ref, q_ref, k_ref, v_ref, cos_ref, sin_ref, qg_ref, kg_ref, o_ref, l_ref, qh_ref, kh_ref, bias_ref):
    rows = q_ref.shape[1]
    keys = k_ref.shape[1]

    @pl.when(pl.program_id(1) == 0)
    def _():
        bias_ref[...] = key_bias(scal_ref, pl.program_id(0), keys, rows)

    key = prepare(k_ref[0], kg_ref[...], cos_ref[...], sin_ref[...]).astype(BF)
    kh_ref[0] = key
    key_twins = twins(key.astype(F32))
    value = v_ref[0].astype(F32)
    value_twins = twins(value)
    first = lane_ids(rows) < HEAD
    for pair in range(2):
        lanes = slice(pair * TILE, (pair + 1) * TILE)
        query = prepare(q_ref[0, :, lanes], qg_ref[...], cos_ref[:rows], sin_ref[:rows]).astype(BF)
        qh_ref[0, :, lanes] = query
        turned_value = value_twins[pair].astype(F32).T.astype(BF)
        mixed = []
        for head in range(2):
            mine = first if head == 0 else jnp.logical_not(first)
            scores = dot(key_twins[pair], jnp.where(mine, query, jnp.zeros_like(query)), NT)
            weights = jnp.exp2(scores * EXP2_SCALE + bias_ref[...])
            inverse = 1.0 / jnp.sum(weights, axis=0, keepdims=True)
            l_ref[0, 0, pl.ds(2 * pair + head, 1), :] = inverse
            mixed.append(dot(turned_value, weights.astype(BF), NN) * inverse)
        row_first = lax.broadcasted_iota(jnp.int32, (TILE, rows), 0) < HEAD
        o_ref[0, :, lanes] = jnp.where(row_first, mixed[0], mixed[1]).T.astype(BF)


def attend_back_kernel(
    scal_ref, q_ref, k_ref, v_ref, cos_ref, sin_ref, qg_ref, kg_ref, qh_ref, kh_ref, o_ref, l_ref, d_ref,
    dq_ref, dk_ref, dv_ref, gq_ref, gk_ref, bias_ref
):
    rows = q_ref.shape[1]
    keys = k_ref.shape[1]

    @pl.when(pl.program_id(1) == 0)
    def _():
        bias_ref[...] = key_bias(scal_ref, pl.program_id(0), keys, rows)

    key_twins = twins(kh_ref[0].astype(F32))
    value_twins = twins(v_ref[0].astype(F32))
    first = lane_ids(rows) < HEAD
    key_first = lane_ids(keys) < HEAD
    row_first = lax.broadcasted_iota(jnp.int32, (TILE, rows), 0) < HEAD
    key_grads = []
    value_grads = []
    query_gain = jnp.zeros((1, TILE), F32)
    for pair in range(2):
        lanes = slice(pair * TILE, (pair + 1) * TILE)
        query = qh_ref[0, :, lanes]
        grad = d_ref[0, :, lanes]
        product = (grad.astype(F32) * o_ref[0, :, lanes].astype(F32)).T
        key_grad = jnp.zeros((keys, TILE), F32)
        value_grad = jnp.zeros((keys, TILE), F32)
        query_grads = []
        for head in range(2):
            mine = first if head == 0 else jnp.logical_not(first)
            own_query = jnp.where(mine, query, jnp.zeros_like(query))
            own_grad = jnp.where(mine, grad, jnp.zeros_like(grad))
            inner = jnp.sum(product[head * HEAD : (head + 1) * HEAD], axis=0, keepdims=True)
            inverse = l_ref[0, 0, pl.ds(2 * pair + head, 1), :]
            scores = dot(key_twins[pair], own_query, NT)
            probs = jnp.exp2(scores * EXP2_SCALE + bias_ref[...]) * inverse
            grad_probs = dot(value_twins[pair], own_grad, NT)
            grad_scores = (probs * (grad_probs - inner)).astype(BF)
            query_grads.append(dot(grad_scores, key_twins[pair], TN))
            key_grad = key_grad + dot(grad_scores, own_query, NN)
            value_grad = value_grad + dot(probs.astype(BF), own_grad, NN)
        query_rot = jnp.where(first, query_grads[0], query_grads[1]) * SCALE
        raw, gain_part = prepare_back(q_ref[0, :, lanes], qg_ref[...], cos_ref[:rows], sin_ref[:rows], query_rot)
        dq_ref[0, :, lanes] = raw.astype(BF)
        query_gain = query_gain + gain_part
        key_grads.append(key_grad + pltpu.roll(key_grad, HEAD, 1))
        value_grads.append(value_grad + pltpu.roll(value_grad, HEAD, 1))
    dv_ref[0] = jnp.where(key_first, value_grads[0], value_grads[1]).astype(BF)
    key_rot = jnp.where(key_first, key_grads[0], key_grads[1]) * SCALE
    raw, key_gain = prepare_back(k_ref[0], kg_ref[...], cos_ref[...], sin_ref[...], key_rot)
    dk_ref[0] = raw.astype(BF)

    @pl.when((pl.program_id(0) == 0) & (pl.program_id(1) == 0))
    def _():
        gq_ref[...] = jnp.zeros_like(gq_ref)
        gk_ref[...] = jnp.zeros_like(gk_ref)

    gq_ref[...] += query_gain
    gk_ref[...] += key_gain


def attention_specs(slots, rows, keys):
    smem = pl.BlockSpec(memory_space=pltpu.SMEM)
    query = pl.BlockSpec((1, rows, 2 * TILE), lambda s, p: (s, 0, p))
    key = pl.BlockSpec((1, keys, TILE), lambda s, p: (s, 0, p))
    table = pl.BlockSpec((keys, TILE), lambda s, p: (0, 0))
    gain = pl.BlockSpec((1, TILE), lambda s, p: (0, 0))
    stat = pl.BlockSpec((1, 1, 8, rows), lambda s, p: (s, p, 0, 0))
    return smem, query, key, table, gain, stat


def attend(scal, q_raw, k_raw, value, cosine, sine, query_gain, key_gain):
    slots, rows, width = q_raw.shape
    keys, kv_width = k_raw.shape[1:]
    smem, query, key, table, gain, stat = attention_specs(slots, rows, keys)
    pairs = kv_width // TILE
    return pl.pallas_call(
        attend_kernel,
        grid=(slots, pairs),
        in_specs=[smem, query, key, key, table, table, gain, gain],
        out_specs=[query, stat, query, key],
        out_shape=[
            jax.ShapeDtypeStruct((slots, rows, width), BF),
            jax.ShapeDtypeStruct((slots, pairs, 8, rows), F32),
            jax.ShapeDtypeStruct((slots, rows, width), BF),
            jax.ShapeDtypeStruct((slots, keys, kv_width), BF),
        ],
        scratch_shapes=[pltpu.VMEM((keys, rows), F32)],
        compiler_params=pltpu.CompilerParams(vmem_limit_bytes=VMEM_LIMIT),
        cost_estimate=pl.CostEstimate(
            flops=8 * slots * rows * keys * width, bytes_accessed=8 << 20, transcendentals=slots * rows * keys * width // HEAD
        ),
        name="attend",
    )(scal, q_raw, k_raw, value, cosine, sine, query_gain, key_gain)


def attend_back(scal, q_raw, k_raw, value, cosine, sine, query_gain, key_gain, q_hat, k_hat, out, stats, grad):
    slots, rows, width = q_raw.shape
    keys, kv_width = k_raw.shape[1:]
    smem, query, key, table, gain, stat = attention_specs(slots, rows, keys)
    pairs = kv_width // TILE
    return pl.pallas_call(
        attend_back_kernel,
        grid=(slots, pairs),
        in_specs=[smem, query, key, key, table, table, gain, gain, query, key, query, stat, query],
        out_specs=[query, key, key, gain, gain],
        out_shape=[
            jax.ShapeDtypeStruct((slots, rows, width), BF),
            jax.ShapeDtypeStruct((slots, keys, kv_width), BF),
            jax.ShapeDtypeStruct((slots, keys, kv_width), BF),
            jax.ShapeDtypeStruct((1, TILE), F32),
            jax.ShapeDtypeStruct((1, TILE), F32),
        ],
        scratch_shapes=[pltpu.VMEM((keys, rows), F32)],
        compiler_params=pltpu.CompilerParams(vmem_limit_bytes=VMEM_LIMIT),
        cost_estimate=pl.CostEstimate(
            flops=20 * slots * rows * keys * width, bytes_accessed=12 << 20, transcendentals=slots * rows * keys * width // HEAD
        ),
        name="attend_back",
    )(scal, q_raw, k_raw, value, cosine, sine, query_gain, key_gain, q_hat, k_hat, out, stats, grad)


def ffn_kernel(x_ref, g_ref, w_ref, y_ref, dx_ref, grad_ref, sum_ref):
    units = w_ref.shape[1] // 3
    step = pl.program_id(0)
    x = x_ref[...]
    g = g_ref[...]
    raised = dot(x, w_ref[:, : 2 * units], NN)
    gate = raised[:, :units]
    upper = raised[:, units:]
    sig = 1.0 / (1.0 + jnp.exp(-gate))
    silu = gate * sig
    act = (silu * upper).astype(BF)
    y_ref[...] = dot(act, w_ref[:, 2 * units :], NT).astype(BF)
    d_act = dot(g, w_ref[:, 2 * units :], NN)
    d_gate = (d_act * upper * (sig + silu * (1.0 - sig))).astype(BF)
    d_up = (d_act * silu).astype(BF)
    both = jnp.concatenate([d_gate, d_up], axis=1)
    dx_ref[...] = dot(both, w_ref[:, : 2 * units], NT).astype(BF)
    left = dot(x, both, TN)
    right = dot(g, act, TN)

    @pl.when(step == 0)
    def _():
        sum_ref[:, : 2 * units] = left
        sum_ref[:, 2 * units :] = right

    @pl.when(step > 0)
    def _():
        sum_ref[:, : 2 * units] += left
        sum_ref[:, 2 * units :] += right

    @pl.when(step == pl.num_programs(0) - 1)
    def _():
        grad_ref[...] = sum_ref[...].astype(BF)


def feed_forward(x, g, w, rows):
    tokens, width = x.shape
    units3 = w.shape[1]
    block = pl.BlockSpec((rows, width), lambda i: (i, 0))
    whole = pl.BlockSpec((width, units3), lambda i: (0, 0))
    return pl.pallas_call(
        ffn_kernel,
        grid=(tokens // rows,),
        in_specs=[block, block, whole],
        out_specs=[block, block, whole],
        out_shape=[
            jax.ShapeDtypeStruct((tokens, width), BF),
            jax.ShapeDtypeStruct((tokens, width), BF),
            jax.ShapeDtypeStruct((width, units3), BF),
        ],
        scratch_shapes=[pltpu.VMEM((width, units3), F32)],
        compiler_params=pltpu.CompilerParams(vmem_limit_bytes=VMEM_LIMIT),
        cost_estimate=pl.CostEstimate(
            flops=6 * tokens * width * units3, bytes_accessed=24 << 20, transcendentals=tokens * units3 // 3
        ),
        name="feed_forward",
    )(x, g, w)


def inverse_rms(values):
    return lax.rsqrt(jnp.mean(values * values, axis=-1, keepdims=True) + EPS)


def norm_back(values, gain, grad):
    inverse = inverse_rms(values)
    normal = values * inverse
    scaled = grad * gain
    return inverse * (scaled - normal * jnp.mean(scaled * normal, axis=-1, keepdims=True))


def body(
    hidden_in,
    seq_lengths,
    attn_gain,
    query_gain,
    key_gain,
    query_weight,
    key_projection,
    value_projection,
    out_weight,
    ffn_gain,
    gate_weight,
    up_weight,
    down_weight,
    cotangent,
):
    slots, shard_rows, width = hidden_in.shape
    n_fsdp = lax.axis_size("fsdp")
    n_ctx = lax.axis_size("ctx")
    f = lax.axis_index("fsdp")
    c = lax.axis_index("ctx")
    core = lax.axis_index("tp")
    rows = 2 * shard_rows
    keys = n_ctx * rows
    q_cols = query_weight.shape[1]
    k_cols = key_projection.shape[1]
    shard = query_weight.shape[0]
    ff_half = gate_weight.shape[1]
    units = ff_half // n_fsdp
    padded = -(-units // TILE) * TILE

    at = jnp.arange(keys)
    places = (c - at // rows) * rows + ((at // shard_rows) % 2 ^ core) * shard_rows + at % shard_rows
    lanes = jnp.arange(TILE)
    freqs = THETA ** (-((lanes % (HEAD // 2)).astype(F32) * 2.0 / HEAD))
    angles = places.astype(F32)[:, None] * freqs[None, :]
    cosine = jnp.cos(angles)
    sine = jnp.sin(angles) * jnp.where(lanes % HEAD < HEAD // 2, -1.0, 1.0)[None, :]
    scal = jnp.concatenate([jnp.stack([c, core]).astype(jnp.int32), seq_lengths])
    own_places = places[:shard_rows]
    valid = own_places[None, :, None] < seq_lengths[:, None, None]

    hidden = hidden_in.astype(F32)
    inverse_one = inverse_rms(hidden)
    normed = (hidden * inverse_one * attn_gain).astype(BF)

    packed = jnp.concatenate([query_weight, key_projection, value_projection, out_weight.T], axis=1)
    stack = jnp.zeros((n_ctx,) + packed.shape, BF)
    stack = lax.dynamic_update_index_in_dim(stack, packed, c, 0)
    for k in range(1, n_ctx):
        stack = lax.dynamic_update_index_in_dim(stack, ctx_shift(packed, k), (c - k) % n_ctx, 0)
    stack = stack.reshape(n_ctx * shard, -1)
    full = jnp.zeros((n_fsdp,) + stack.shape, BF)
    full = lax.dynamic_update_index_in_dim(full, stack, f, 0)
    for m in range(1, n_fsdp):
        full = lax.dynamic_update_index_in_dim(full, fsdp_xor(stack, m), f ^ m, 0)
    attn_w = full.reshape(width, -1)
    query_w = attn_w[:, :q_cols]
    kv_w = attn_w[:, q_cols : q_cols + 2 * k_cols]
    out_w = attn_w[:, q_cols + 2 * k_cols :]

    def quarters(array):
        array = array.reshape(shard, n_fsdp, units)
        return jnp.pad(array, ((0, 0), (0, 0), (0, padded - units)))

    ffn_packed = jnp.concatenate(
        [quarters(gate_weight), quarters(up_weight), quarters(down_weight.T)], axis=2
    ).transpose(1, 0, 2)
    ffn_rows = jnp.zeros_like(ffn_packed)
    ffn_rows = lax.dynamic_update_index_in_dim(
        ffn_rows, lax.dynamic_index_in_dim(ffn_packed, f, 0, keepdims=False), f, 0
    )
    for m in range(1, n_fsdp):
        piece = fsdp_xor(lax.dynamic_index_in_dim(ffn_packed, f ^ m, 0, keepdims=False), m)
        ffn_rows = lax.dynamic_update_index_in_dim(ffn_rows, piece, f ^ m, 0)
    ffn_w = lax.all_gather(ffn_rows, "ctx", axis=1, tiled=True).reshape(width, 3 * padded)

    blocks = []
    for r in range(n_ctx):
        piece = ctx_up(normed, r) if r else normed
        blocks.append(jnp.concatenate([piece, swap_cores(piece)], axis=1))
    x_all = jnp.concatenate(blocks, axis=1)
    x_own = blocks[0]

    q_raw = jnp.einsum("std,dh->sth", x_own, query_w, preferred_element_type=F32)
    k_raw = jnp.einsum("std,dh->sth", x_all, kv_w[:, :k_cols], preferred_element_type=F32)
    value = jnp.einsum("std,dh->sth", x_all, kv_w[:, k_cols:], preferred_element_type=F32).astype(BF)
    query_gain2 = jnp.tile(query_gain, 2)[None, :]
    key_gain2 = jnp.tile(key_gain, 2)[None, :]
    attn, stats, q_hat, k_hat = attend(scal, q_raw, k_raw, value, cosine, sine, query_gain2, key_gain2)

    branch = jnp.einsum("sth,dh->std", attn, out_w, preferred_element_type=F32)
    middle = hidden + (branch[:, :shard_rows] + swap_cores(branch[:, shard_rows:]))
    normed_two = (middle * inverse_rms(middle) * ffn_gain).astype(BF)
    grad_rows = jnp.where(valid, cotangent, jnp.zeros_like(cotangent))

    def gather_tokens(value):
        pieces = jnp.stack([value] + [fsdp_xor(value, m) for m in range(1, n_fsdp)])
        return jnp.concatenate([pieces, swap_cores(pieces)]).reshape(-1, width)

    def scatter_tokens(value):
        value = value.reshape(2, n_fsdp, slots, shard_rows, width)
        mine = value[0].astype(F32) + swap_cores(value[1]).astype(F32)
        total = mine[0]
        for m in range(1, n_fsdp):
            total = total + fsdp_xor(mine[m].astype(BF), m).astype(F32)
        return total

    y_part, dx_part, ffn_grads = feed_forward(gather_tokens(normed_two), gather_tokens(grad_rows), ffn_w, 2 * slots * shard_rows)
    result = jnp.where(valid, middle + scatter_tokens(y_part), 0.0).astype(BF)
    d_normed_two = scatter_tokens(dx_part)
    d_middle = grad_rows.astype(F32) + norm_back(middle, ffn_gain, d_normed_two)

    reduced = lax.psum_scatter(
        ffn_grads.reshape(n_fsdp, n_ctx * shard, 3 * padded), "ctx", scatter_dimension=1, tiled=True
    )
    ffn_out = jnp.zeros((n_fsdp,) + reduced.shape[1:], BF)
    ffn_out = lax.dynamic_update_index_in_dim(
        ffn_out, lax.dynamic_index_in_dim(reduced, f, 0, keepdims=False), f, 0
    )
    for m in range(1, n_fsdp):
        piece = fsdp_xor(lax.dynamic_index_in_dim(reduced, f ^ m, 0, keepdims=False), m)
        ffn_out = lax.dynamic_update_index_in_dim(ffn_out, piece, f ^ m, 0)
    ffn_out = ffn_out.reshape(n_fsdp, shard, 3, padded)[..., :units].astype(F32)
    ffn_out = ffn_out.transpose(2, 1, 0, 3).reshape(3, shard, ff_half)
    gate_grad, up_grad = ffn_out[0], ffn_out[1]
    down_grad = ffn_out[2].T

    d_branch = d_middle.astype(BF)
    d_branch = jnp.concatenate([d_branch, swap_cores(d_branch)], axis=1)
    d_attn = jnp.einsum("std,dh->sth", d_branch, out_w, preferred_element_type=F32).astype(BF)
    out_w_grad = jnp.einsum("std,sth->dh", d_branch, attn, preferred_element_type=F32)
    d_q, d_k, d_v, gq, gk = attend_back(
        scal, q_raw, k_raw, value, cosine, sine, query_gain2, key_gain2, q_hat, k_hat, attn, stats, d_attn
    )
    d_kv = jnp.concatenate([d_k, d_v], axis=2)
    d_own = jnp.einsum("sth,dh->std", d_q, query_w, preferred_element_type=F32)
    d_all = jnp.einsum("sth,dh->std", d_kv, kv_w, preferred_element_type=F32)
    d_all = d_all.at[:, :rows].add(d_own).reshape(slots, n_ctx, 2, shard_rows, width)
    mine = d_all[:, :, 0] + swap_cores(d_all[:, :, 1].astype(BF)).astype(F32)
    total = mine[:, n_ctx - 1]
    for r in range(n_ctx - 2, -1, -1):
        total = mine[:, r] + ctx_down(total.astype(BF)).astype(F32)
    input_grad = (d_middle + norm_back(hidden, attn_gain, total)).astype(BF)

    q_grad = jnp.einsum("std,sth->dh", x_own, d_q, preferred_element_type=F32)
    kv_grad = jnp.einsum("std,sth->dh", x_all, d_kv, preferred_element_type=F32)
    attn_grads = jnp.concatenate([q_grad, kv_grad, out_w_grad], axis=1)
    sends = attn_grads.astype(BF).reshape(n_fsdp, n_ctx * shard, -1)
    total = lax.dynamic_index_in_dim(sends, f, 0, keepdims=False).astype(F32)
    for m in range(1, n_fsdp):
        total = total + fsdp_xor(lax.dynamic_index_in_dim(sends, f ^ m, 0, keepdims=False), m).astype(F32)
    sends = total.reshape(n_ctx, shard, -1)
    total = lax.dynamic_index_in_dim(sends, c, 0, keepdims=False)
    sends = sends.astype(BF)
    for k in range(1, n_ctx):
        total = total + ctx_shift(lax.dynamic_index_in_dim(sends, (c + k) % n_ctx, 0, keepdims=False), k).astype(F32)
    query_weight_grad = total[:, :q_cols]
    key_weight_grad = total[:, q_cols : q_cols + k_cols]
    value_weight_grad = total[:, q_cols + k_cols : q_cols + 2 * k_cols]
    out_weight_grad = total[:, q_cols + 2 * k_cols :].T

    attn_gain_part = jnp.sum(attn_w[:, : q_cols + 2 * k_cols].astype(F32) * attn_grads[:, : q_cols + 2 * k_cols], axis=1) / attn_gain
    ffn_gain_part = (
        jnp.sum(ffn_w[:, : 2 * padded].astype(F32) * ffn_grads[:, : 2 * padded].astype(F32), axis=1) / ffn_gain
    )
    small = jnp.concatenate(
        [attn_gain_part, ffn_gain_part, gq[0, :HEAD] + gq[0, HEAD:], gk[0, :HEAD] + gk[0, HEAD:]]
    )
    small = sum_everywhere(small)
    return (
        result,
        input_grad,
        small[:width],
        small[2 * width : 2 * width + HEAD],
        small[2 * width + HEAD :],
        query_weight_grad,
        key_weight_grad,
        value_weight_grad,
        out_weight_grad,
        small[width : 2 * width],
        gate_grad,
        up_grad,
        down_grad,
    )


def solution(mesh):
    in_specs = (
        P("fsdp", ("ctx", "tp"), None),
        P("fsdp"),
        P(),
        P(),
        P(),
        P(("fsdp", "ctx"), "tp"),
        P(("fsdp", "ctx"), "tp"),
        P(("fsdp", "ctx"), "tp"),
        P("tp", ("fsdp", "ctx")),
        P(),
        P(("fsdp", "ctx"), "tp"),
        P(("fsdp", "ctx"), "tp"),
        P("tp", ("fsdp", "ctx")),
        P("fsdp", ("ctx", "tp"), None),
    )
    out_specs = (
        P("fsdp", ("ctx", "tp"), None),
        P("fsdp", ("ctx", "tp"), None),
        P(),
        P(),
        P(),
        P(("fsdp", "ctx"), "tp"),
        P(("fsdp", "ctx"), "tp"),
        P(("fsdp", "ctx"), "tp"),
        P("tp", ("fsdp", "ctx")),
        P(),
        P(("fsdp", "ctx"), "tp"),
        P(("fsdp", "ctx"), "tp"),
        P("tp", ("fsdp", "ctx")),
    )
    return jax.shard_map(body, mesh=mesh, in_specs=in_specs, out_specs=out_specs, check_vma=False)
```

time: 1680 us -> 445 us (0.26)
  waiting for transfers between devices: 1130 us -> 159 us
  blocking collectives: 216 us -> 0 us
  matrix products: 181 us -> 27 us
  Pallas kernels: 0 us -> 81.4 us
  starting transfers between devices: 1 us -> 58.6 us
  local copies, waits for them, and re-layouts: 83.8 us -> 64.2 us
    reduce_scatter x19 -> x1, waiting for transfers between devices: 864 us -> 0.01 us  [body(): lax.psum_scatter(ffn_grads.reshape(n_fsdp, n_ctx * shard, 3 * padded), 'c...]
    all_gather x5 -> x1, waiting for transfers between devices: 259 us -> 0.01 us  [body(): lax.all_gather(ffn_rows, 'ctx', axis=1, tiled=True)]
    all_gather x14 -> x0, blocking collectives: 177 us -> none  [the longest x1 51 us: gather_weights(): lax.all_gather(key_projection, ('fsdp', 'ctx'), axis=0, tiled=True)]
    ppermute x0 -> x52, waiting for transfers between devices: none -> 159 us  [the longest x24 123 us: fsdp_xor(): return lax.ppermute(value, 'fsdp', [(i, i ^ mask) for i in range(size)])]
    dot_general x98 -> x10, matrix products: 181 us -> 27 us  [the longest x1 4.9 us: body(): q_grad = jnp.einsum('std,sth->dh', x_own, d_q, preferred_element_type=F32)]
    pallas_call x0 -> x3, Pallas kernels: none -> 81.4 us  [the longest x1 36.7 us: feed_forward(): pl.pallas_call(ffn_kernel, grid=(tokens // rows,), in_specs=[block, block...]
    ppermute x0 -> x52, starting transfers between devices: none -> 58.3 us  [the longest x24 31.3 us: fsdp_xor(): return lax.ppermute(value, 'fsdp', [(i, i ^ mask) for i in range(size)])]
    while x374 -> x0, local copies, waits for them, and re-layouts: 42.1 us -> none
  transfers between devices with their start and end apart: 24 -> 54, of which waited for: 15 -> 23; matrix products, arithmetic and copies ran while one was open for 7% -> 23% of each run, Pallas kernels for 0% -> 10%
where the time goes in v1:
time: 445 us; the launch traced here: 438 us
  waiting for transfers between devices  159 us (36%)
  Pallas kernels  81.4 us (18%)
  local copies, waits for them, and re-layouts  64.2 us (14%)
  starting transfers between devices  58.6 us (13%)
  other arithmetic  32.8 us (7%)
  matrix products  27 us (6%)
  between operations  15.1 us (3%)
    ppermute x24, waiting for transfers between devices, fsdp_xor(): return lax.ppermute(value, 'fsdp', [(i, i ^ mask) for i in range(size)])  123 us
    pallas_call x1, Pallas kernels, feed_forward(): pl.pallas_call(ffn_kernel, grid=(tokens // rows,), in_specs=[block, block...  36.7 us
    ppermute x24, starting transfers between devices, fsdp_xor(): return lax.ppermute(value, 'fsdp', [(i, i ^ mask) for i in range(size)])  31.3 us
    pallas_call x1, Pallas kernels, attend_back(): pl.pallas_call(attend_back_kernel, grid=(slots, pairs), in_specs=[smem, q...  25.4 us
    pallas_call x1, Pallas kernels, attend(): pl.pallas_call(attend_kernel, grid=(slots, pairs), in_specs=[smem, query,...  19.4 us
    ppermute x3, waiting for transfers between devices, ctx_down(): lax.ppermute(value, 'ctx', [(i + step, i) for i in range(size - step)])  17.7 us
    unnamed x82, local copies, waits for them, and re-layouts  14.4 us
    ppermute x6, starting transfers between devices, ctx_shift(): lax.ppermute(value, 'ctx', [(i, (i + step) % size) for i in range(size)])  11.5 us
  transfers between devices with their start and end apart: 54, of which 23 were waited for; matrix products, arithmetic and copies ran while one was open for 23% of the time, Pallas kernels for 10%

profile of v1, /device:TPU:0, one launch (start us, length us, event | category | flops | bytes accessed | tf_op | source)
XLA Modules:
  0.0 438.3 jit_solution(10046433743795027700)
XLA Ops:
  8.2 3.1 collective-permute-start.1
  11.3 2.6 collective-permute-start.2
  16.5 2.2 constant_dynamic-update-slice_fusion.7
  18.7 3.4 collective-permute-start.7
  27.3 2.0 constant_dynamic-slice_fusion
  32.6 3.0 fusion.41
  38.0 2.4 collective-permute-start.9
  43.3 1.5 collective-permute-start.23
  46.9 2.1 collective-permute-done.22
  49.1 2.5 collective-permute-start.24
  53.5 5.3 %collective-permute-done.24 = bf16[64,1920]{1,0:T(8,128)(2,1)S(1)} collective-permute-done((bf16[64,1920]{1,0:T(8,128)(2,1)S(1)}, bf16[64,1920]{1,0:T(8,128)(2,1)S(1)}, u32[]{:S(2)}, u32[]{:S(2)}) %collective-permute-start.24) | collective-permute-done | bytes 245792 | tf_op jit(solution)/shard_map/ppermute | solution.py:38
  58.9 2.1 collective-permute-start.11
  61.0 1.5 collective-permute-start.5
  63.5 1.9 constant_dynamic-update-slice_fusion.6
  66.8 1.9 constant_dynamic-update-slice_fusion.5
  69.3 6.6 %collective-permute-done.4 = bf16[256,1536]{1,0:T(8,128)(2,1)} collective-permute-done((bf16[256,1536]{1,0:T(8,128)(2,1)}, bf16[256,1536]{1,0:T(8,128)(2,1)}, u32[]{:S(2)}, u32[]{:S(2)}) %collective-permute-start.4) | collective-permute-done | bytes 786464 | tf_op jit(solution)/shard_map/ppermute | solution.py:38
  77.1 16.7 %collective-permute-done.5 = bf16[256,1536]{1,0:T(8,128)(2,1)} collective-permute-done((bf16[256,1536]{1,0:T(8,128)(2,1)}, bf16[256,1536]{1,0:T(8,128)(2,1)}, u32[]{:S(2)}, u32[]{:S(2)}) %collective-permute-start.5) | collective-permute-done | bytes 786464 | tf_op jit(solution)/shard_map/ppermute | solution.py:38
  95.1 3.9 fusion.39.q_ref
  101.3 2.4 convolution_convert_fusion.v_ref
  103.7 2.6 fusion.43.k_ref
  106.3 19.4 %attend.1 = (bf16[2,256,512]{2,1,0:T(8,128)(2,1)}, f32[2,2,8,256]{3,2,1,0:T(8,128)}, bf16[2,256,512]{2,1,0:T(8,128)(2,1)}, bf16[2,1024,256]{2,1,0:T(8,128)(2,1)}) custom-call(s32[4]{0:T(128)} %pad_add_fusion.scal_ref, f32[2,256,512]{2,1,0:T(8,128)} %fusion.39.q_ref, f32[2,1024,256]{2,1,0:T(8,128)} %fusion.43.k_ref, ...), custom_call_target="tpu_custom_call" | custom-call | flops 2147483648 | bytes 8388608 | tf_op jit(solution)/shard_map/attend/pallas_call | solution.py:225
  125.8 1.8 fusion.40
  128.0 1.6 collective-permute-start.18
  129.6 1.5 collective-permute-start.19
  131.6 11.2 %collective-permute-done.18 = bf16[2,128,1024]{2,1,0:T(8,128)(2,1)S(1)} collective-permute-done((bf16[2,128,1024]{2,1,0:T(8,128)(2,1)S(1)}, bf16[2,128,1024]{2,1,0:T(8,128)(2,1)S(1)}, u32[]{:S(2)}, u32[]{:S(2)}) %collective-permute-start.18) | collective-permute-done | bytes 524320 | tf_op jit(solution)/shard_map/ppermute | solution.py:38
  142.8 12.1 %collective-permute-done.19 = bf16[2,128,1024]{2,1,0:T(8,128)(2,1)S(1)} collective-permute-done((bf16[2,128,1024]{2,1,0:T(8,128)(2,1)S(1)}, bf16[2,128,1024]{2,1,0:T(8,128)(2,1)S(1)}, u32[]{:S(2)}, u32[]{:S(2)}) %collective-permute-start.19) | collective-permute-done | bytes 524320 | tf_op jit(solution)/shard_map/ppermute | solution.py:38
  160.1 11.2 %collective-permute-done.14 = bf16[2,128,1024]{2,1,0:T(8,128)(2,1)S(1)} collective-permute-done((bf16[2,128,1024]{2,1,0:T(8,128)(2,1)S(1)}, bf16[2,128,1024]{2,1,0:T(8,128)(2,1)S(1)}, u32[]{:S(2)}, u32[]{:S(2)}) %collective-permute-start.14) | collective-permute-done | bytes 524320 | tf_op jit(solution)/shard_map/ppermute | solution.py:38
  171.3 10.1 %collective-permute-done.15 = bf16[2,128,1024]{2,1,0:T(8,128)(2,1)S(1)} collective-permute-done((bf16[2,128,1024]{2,1,0:T(8,128)(2,1)S(1)}, bf16[2,128,1024]{2,1,0:T(8,128)(2,1)S(1)}, u32[]{:S(2)}, u32[]{:S(2)}) %collective-permute-start.15) | collective-permute-done | bytes 524320 | tf_op jit(solution)/shard_map/ppermute | solution.py:38
  181.4 1.6 collective-permute-done.16
  189.0 36.7 %feed_forward.1 = (bf16[2048,1024]{1,0:T(8,128)(2,1)}, bf16[2048,1024]{1,0:T(8,128)(2,1)}, bf16[1024,1920]{1,0:T(8,128)(2,1)}) custom-call(bf16[2048,1024]{1,0:T(8,128)(2,1)} %bitcast.21.x_ref, bf16[2048,1024]{1,0:T(8,128)(2,1)} %bitcast.248, bf16[1024,1920]{1,0:T(8,128)(2,1)} %bitcast.240), custom_call_target="tpu_custom_call" | custom-call | flops 24159191040 | bytes 25165824 | tf_op jit(solution)/shard_map/feed_forward/pallas_call | solution.py:311
  225.7 2.7 fusion.74
  228.6 4.0 collective-permute-done.29
  232.6 3.2 convert_add_fusion
  237.8 1.5 collective-permute-start.31
  240.5 11.5 %collective-permute-done.30 = bf16[2,128,1024]{2,1,0:T(8,128)(2,1)S(1)} collective-permute-done((bf16[2,128,1024]{2,1,0:T(8,128)(2,1)}, bf16[2,128,1024]{2,1,0:T(8,128)(2,1)S(1)}, u32[]{:S(2)}, u32[]{:S(2)}) %collective-permute-start.30) | collective-permute-done | bytes 524320 | tf_op jit(solution)/shard_map/ppermute | solution.py:38
  252.0 10.9 %collective-permute-done.31 = bf16[2,128,1024]{2,1,0:T(8,128)(2,1)S(1)} collective-permute-done((bf16[2,128,1024]{2,1,0:T(8,128)(2,1)}, bf16[2,128,1024]{2,1,0:T(8,128)(2,1)S(1)}, u32[]{:S(2)}, u32[]{:S(2)}) %collective-permute-start.31) | collective-permute-done | bytes 524320 | tf_op jit(solution)/shard_map/ppermute | solution.py:38
  263.7 2.3 multiply_reduce_fusion.1
  268.8 5.0 %fusion.75 = (bf16[1024,1024]{1,0:T(8,128)(2,1)}, bf16[1024,1024]{1,0:T(8,128)(2,1)}) fusion(bf16[2048,1024]{1,0:T(8,128)(2,1)} %get-tuple-element.38), kind=kLoop, calls=%fused_computation.201 | loop fusion | bytes 8388608 | tf_op jit(solution)/shard_map/slice | solution.py:443
  273.8 2.7 convolution_convert_fusion.1.d_ref
  276.5 25.4 %attend_back.1 = (bf16[2,256,512]{2,1,0:T(8,128)(2,1)}, bf16[2,1024,256]{2,1,0:T(8,128)(2,1)}, bf16[2,1024,256]{2,1,0:T(8,128)(2,1)}, f32[1,128]{1,0:T(1,128)}, f32[1,128]{1,0:T(1,128)}) custom-call(s32[4]{0:T(128)} %pad_add_fusion.scal_ref, f32[2,256,512]{2,1,0:T(8,128)} %fusion.39.q_ref, f32[2,1024,256]{2,1,0:T(8,128)} %fusion.43.k_ref, ...), custom_call_target="tpu_custom_call" | custom-call | flops 5368709120 | bytes 12582912 | tf_op jit(solution)/shard_map/attend_back/pallas_call | solution.py:250
  304.5 2.4 fusion.26
  307.7 1.9 fusion.2
  310.1 4.9 %fusion.81 = (bf16[1024,512]{1,0:T(8,128)(2,1)}, f32[1024,512]{1,0:T(8,128)S(1)}) fusion(bf16[2,256,512]{2,1,0:T(8,128)(2,1)S(1)} %copy-done.13, bf16[2,128,1024]{2,1,0:T(8,128)(2,1)} %collective-permute-done, bf16[2,128,1024]{2,1,0:T(8,128)(2,1)} %get-tuple-element.58), kind=kOutput, calls=%fused_computation.207 | convolution fusion | flops 539492352 | bytes 4718592 | tf_op jit(solution)/shard_map/std,sth->dh/dot_general | solution.py:486
  315.0 3.3 fusion.80
  319.3 5.3 %fusion.70 = (bf16[4,2,128,1024]{3,2,1,0:T(8,128)(2,1)S(1)}, f32[4,2,128,1024]{3,2,1,0:T(8,128)}) fusion(bf16[4,2,128,1024]{3,2,1,0:T(8,128)(2,1)} %collective-permute-done.25, bf16[4,2,128,1024]{3,2,1,0:T(8,128)(2,1)} %bitcast.225), kind=kLoop, calls=%fused_computation.198 | loop fusion | flops 4194304 | bytes 10485760 | tf_op jit(solution)/shard_map/convert.17
  325.2 2.1 bitcast_convert_fusion
  328.4 1.5 collective-permute-start.40
  330.2 1.9 collective-permute-done.40
  335.8 1.8 collective-permute-done.41
  337.7 2.7 fusion
  345.6 7.5 %collective-permute-done.35 = bf16[2,128,1024]{2,1,0:T(8,128)(2,1)S(1)} collective-permute-done((bf16[2,128,1024]{2,1,0:T(8,128)(2,1)S(1)}, bf16[2,128,1024]{2,1,0:T(8,128)(2,1)S(1)}, u32[]{:S(2)}, u32[]{:S(2)}) %collective-permute-start.35) | collective-permute-done | bytes 524320 | tf_op jit(solution)/shard_map/ppermute | solution.py:48
  353.1 1.7 collective-permute-start.27
  356.3 11.1 %collective-permute-done.44 = bf16[256,1536]{1,0:T(8,128)(2,1)S(1)} collective-permute-done((bf16[256,1536]{1,0:T(8,128)(2,1)S(1)}, bf16[256,1536]{1,0:T(8,128)(2,1)S(1)}, u32[]{:S(2)}, u32[]{:S(2)}) %collective-permute-start.44) | collective-permute-done | bytes 786464 | tf_op jit(solution)/shard_map/ppermute | solution.py:38
  367.4 3.3 collective-permute-done.45
  371.2 2.1 collective-permute-start.46
  373.3 2.4 collective-permute-start.48
  375.9 4.4 %collective-permute-done.46 = bf16[64,1536]{1,0:T(8,128)(2,1)S(1)} collective-permute-done((bf16[64,1536]{1,0:T(8,128)(2,1)S(1)}, bf16[64,1536]{1,0:T(8,128)(2,1)S(1)}, u32[]{:S(2)}, u32[]{:S(2)}) %collective-permute-start.46) | collective-permute-done | bytes 196640 | tf_op jit(solution)/shard_map/ppermute | solution.py:53
  381.4 4.3 collective-permute-done.47
  388.7 10.2 %collective-permute-done.37 = bf16[2,128,1024]{2,1,0:T(8,128)(2,1)S(1)} collective-permute-done((bf16[2,128,1024]{2,1,0:T(8,128)(2,1)S(1)}, bf16[2,128,1024]{2,1,0:T(8,128)(2,1)S(1)}, u32[]{:S(2)}, u32[]{:S(2)}) %collective-permute-start.37) | collective-permute-done | bytes 524320 | tf_op jit(solution)/shard_map/ppermute | solution.py:48
  400.8 2.1 dynamic-slice_bitcast_fusion.3
  402.9 2.5 collective-permute-start.49
  405.3 3.8 fusion.18
  411.3 9.2 %collective-permute-done.50 = bf16[64,1920]{1,0:T(8,128)(2,1)S(1)} collective-permute-done((bf16[64,1920]{1,0:T(8,128)(2,1)S(1)}, bf16[64,1920]{1,0:T(8,128)(2,1)S(1)}, u32[]{:S(2)}, u32[]{:S(2)}) %collective-permute-start.50) | collective-permute-done | bytes 245792 | tf_op jit(solution)/shard_map/ppermute | solution.py:38
  421.9 2.7 reshape.283
  (240 shorter events, 81.8 us)
Async XLA Ops:
  7.2 18.7 %copy-start.19 = (bf16[64,2304]{1,0:T(8,128)(2,1)S(1)}, bf16[64,2304]{1,0:T(8,128)(2,1)}, u32[]{:S(2)}) copy-start(bf16[64,2304]{1,0:T(8,128)(2,1)} %param.27) | copy-start | bytes 884740
  7.2 19.1 %copy-start.20 = (bf16[2304,64]{0,1:T(8,128)(2,1)S(1)}, bf16[2304,64]{0,1:T(8,128)(2,1)}, u32[]{:S(2)}) copy-start(bf16[2304,64]{0,1:T(8,128)(2,1)} %param.28) | copy-start | bytes 884740
  7.2 181.8 %all-gather.2.cloned.1.call-start = ((), (), s32[]{:S(2)}) async-start(), calls=%async_computation.1 | async-start | bytes 4915200 | tf_op jit(solution)/shard_map/all_gather | solution.py:416
  8.2 29.8 %collective-permute-start.1 = (bf16[64,1536]{1,0:T(8,128)(2,1)S(1)}, bf16[64,1536]{1,0:T(8,128)(2,1)S(1)}, u32[]{:S(2)}, u32[]{:S(2)}) collective-permute-start(bf16[64,1536]{1,0:T(8,128)(2,1)S(1)} %pad_maximum_fusion.9), channel_id=1, source_target_pairs={{0,2},{2,4},{4,6},{6,0},{1,3},{3,5},{5,7},{7,1},{8,10},{10,12},{12... | collective-permute-start | bytes 589832 | tf_op jit(solution)/shard_map/ppermute | solution.py:53
  11.3 29.8 %collective-permute-start.2 = (bf16[64,1536]{1,0:T(8,128)(2,1)S(1)}, bf16[64,1536]{1,0:T(8,128)(2,1)S(1)}, u32[]{:S(2)}, u32[]{:S(2)}) collective-permute-start(bf16[64,1536]{1,0:T(8,128)(2,1)S(1)} %pad_maximum_fusion.9), channel_id=1, source_target_pairs={{0,4},{2,6},{4,0},{6,2},{1,5},{3,7},{5,1},{7,3},{8,12},{10,14},{12... | collective-permute-start | bytes 589832 | tf_op jit(solution)/shard_map/ppermute | solution.py:53
  13.9 29.4 %collective-permute-start.3 = (bf16[64,1536]{1,0:T(8,128)(2,1)S(1)}, bf16[64,1536]{1,0:T(8,128)(2,1)S(1)}, u32[]{:S(2)}, u32[]{:S(2)}) collective-permute-start(bf16[64,1536]{1,0:T(8,128)(2,1)S(1)} %pad_maximum_fusion.9), channel_id=1, source_target_pairs={{0,6},{2,0},{4,2},{6,4},{1,7},{3,1},{5,3},{7,5},{8,14},{10,8},{12,... | collective-permute-start | bytes 589832 | tf_op jit(solution)/shard_map/ppermute | solution.py:53
  18.7 42.3 %collective-permute-start = (bf16[2,128,1024]{2,1,0:T(8,128)(2,1)}, bf16[2,128,1024]{2,1,0:T(8,128)(2,1)}, u32[]{:S(2)}, u32[]{:S(2)}) collective-permute-start(bf16[2,128,1024]{2,1,0:T(8,128)(2,1)} %get-tuple-element.58), channel_id=1, source_target_pairs={{0,1},{1,0},{2,3},{3,2},{4,5},{5,4},{6,7},{7,6},{8,9},{9,8},{10,11... | collective-permute-start | bytes 1572872 | tf_op jit(solution)/shard_map/ppermute | solution.py:33
  18.7 46.8 %collective-permute-start.7 = (bf16[2,128,1024]{2,1,0:T(8,128)(2,1)}, bf16[2,128,1024]{2,1,0:T(8,128)(2,1)}, u32[]{:S(2)}, u32[]{:S(2)}) collective-permute-start(bf16[2,128,1024]{2,1,0:T(8,128)(2,1)} %get-tuple-element.58), channel_id=1, source_target_pairs={{0,2},{2,4},{4,6},{1,3},{3,5},{5,7},{8,10},{10,12},{12,14},{9,11},... | collective-permute-start | bytes 1572872 | tf_op jit(solution)/shard_map/ppermute | solution.py:43
  29.3 8.0 %copy-start.21 = (bf16[512,64]{0,1:T(8,128)(2,1)S(1)}, bf16[512,64]{0,1:T(8,128)(2,1)}, u32[]{:S(2)}) copy-start(bf16[512,64]{0,1:T(8,128)(2,1)} %param.24) | copy-start | bytes 196612
  29.3 8.0 %copy-start.22 = (bf16[64,512]{1,0:T(8,128)(2,1)S(1)}, bf16[64,512]{1,0:T(8,128)(2,1)}, u32[]{:S(2)}) copy-start(bf16[64,512]{1,0:T(8,128)(2,1)} %param.21) | copy-start | bytes 196612
  29.3 7.9 %copy-start.23 = (bf16[64,256]{1,0:T(8,128)(2,1)S(1)}, bf16[64,256]{1,0:T(8,128)(2,1)}, u32[]{:S(2)}) copy-start(bf16[64,256]{1,0:T(8,128)(2,1)} %param.23) | copy-start | bytes 98308
  38.0 30.8 %collective-permute-start.9 = (bf16[2,128,1024]{2,1,0:T(8,128)(2,1)}, bf16[2,128,1024]{2,1,0:T(8,128)(2,1)}, u32[]{:S(2)}, u32[]{:S(2)}) collective-permute-start(bf16[2,128,1024]{2,1,0:T(8,128)(2,1)} %get-tuple-element.58), channel_id=1, source_target_pairs={{0,4},{2,6},{1,5},{3,7},{8,12},{10,14},{9,13},{11,15},{16,20},{18,... | collective-permute-start | bytes 1572872 | tf_op jit(solution)/shard_map/ppermute | solution.py:43
  41.1 8.0 %collective-permute-start.22 = (bf16[64,1920]{1,0:T(8,128)(2,1)}, bf16[64,1920]{1,0:T(8,128)(2,1)S(1)}, u32[]{:S(2)}, u32[]{:S(2)}) collective-permute-start(bf16[64,1920]{1,0:T(8,128)(2,1)} %bitcast.210), channel_id=1, source_target_pairs={{0,8},{8,0},{16,24},{24,16},{1,9},{9,1},{17,25},{25,17},{2,10},{10... | collective-permute-start | bytes 737288 | tf_op jit(solution)/shard_map/ppermute | solution.py:38
  43.3 9.0 %collective-permute-start.23 = (bf16[64,1920]{1,0:T(8,128)(2,1)}, bf16[64,1920]{1,0:T(8,128)(2,1)S(1)}, u32[]{:S(2)}, u32[]{:S(2)}) collective-permute-start(bf16[64,1920]{1,0:T(8,128)(2,1)} %bitcast.209), channel_id=1, source_target_pairs={{0,16},{8,24},{16,0},{24,8},{1,17},{9,25},{17,1},{25,9},{2,18},{10... | collective-permute-start | bytes 737288 | tf_op jit(solution)/shard_map/ppermute | solution.py:38
  49.1 9.8 %collective-permute-start.24 = (bf16[64,1920]{1,0:T(8,128)(2,1)S(1)}, bf16[64,1920]{1,0:T(8,128)(2,1)S(1)}, u32[]{:S(2)}, u32[]{:S(2)}) collective-permute-start(bf16[64,1920]{1,0:T(8,128)(2,1)S(1)} %bitcast.247), channel_id=1, source_target_pairs={{0,24},{8,16},{16,8},{24,0},{1,25},{9,17},{17,9},{25,1},{2,26},{10... | collective-permute-start | bytes 737288 | tf_op jit(solution)/shard_map/ppermute | solution.py:38
  52.3 23.6 %collective-permute-start.4 = (bf16[256,1536]{1,0:T(8,128)(2,1)}, bf16[256,1536]{1,0:T(8,128)(2,1)}, u32[]{:S(2)}, u32[]{:S(2)}) collective-permute-start(bf16[256,1536]{1,0:T(8,128)(2,1)} %bitcast.8), channel_id=1, source_target_pairs={{0,8},{8,0},{16,24},{24,16},{1,9},{9,1},{17,25},{25,17},{2,10},{10... | collective-permute-start | bytes 2359304 | tf_op jit(solution)/shard_map/ppermute | solution.py:38
  58.9 9.9 %collective-permute-start.11 = (bf16[2,128,1024]{2,1,0:T(8,128)(2,1)}, bf16[2,128,1024]{2,1,0:T(8,128)(2,1)}, u32[]{:S(2)}, u32[]{:S(2)}) collective-permute-start(bf16[2,128,1024]{2,1,0:T(8,128)(2,1)} %get-tuple-element.58), channel_id=1, source_target_pairs={{0,6},{1,7},{8,14},{9,15},{16,22},{17,23},{24,30},{25,31}} | collective-permute-start | bytes 1572872 | tf_op jit(solution)/shard_map/ppermute | solution.py:43
  61.0 32.9 %collective-permute-start.5 = (bf16[256,1536]{1,0:T(8,128)(2,1)}, bf16[256,1536]{1,0:T(8,128)(2,1)}, u32[]{:S(2)}, u32[]{:S(2)}) collective-permute-start(bf16[256,1536]{1,0:T(8,128)(2,1)} %bitcast.8), channel_id=1, source_target_pairs={{0,16},{8,24},{16,0},{24,8},{1,17},{9,25},{17,1},{25,9},{2,18},{10... | collective-permute-start | bytes 2359304 | tf_op jit(solution)/shard_map/ppermute | solution.py:38
  63.3 336.4 %reduce-scatter.2.cloned.1.call-start = ((), (), s32[]{:S(2)}) async-start(), calls=%async_computation.2 | async-start | bytes 4915200 | tf_op jit(solution)/shard_map/reduce_scatter | solution.py:454
  65.4 29.6 %collective-permute-start.6 = (bf16[256,1536]{1,0:T(8,128)(2,1)}, bf16[256,1536]{1,0:T(8,128)(2,1)S(1)}, u32[]{:S(2)}, u32[]{:S(2)}) collective-permute-start(bf16[256,1536]{1,0:T(8,128)(2,1)} %bitcast.8), channel_id=1, source_target_pairs={{0,24},{8,16},{16,8},{24,0},{1,25},{9,17},{17,9},{25,1},{2,26},{10... | collective-permute-start | bytes 2359304 | tf_op jit(solution)/shard_map/ppermute | solution.py:38
  68.7 30.3 %collective-permute-start.8 = (bf16[2,128,1024]{2,1,0:T(8,128)(2,1)}, bf16[2,128,1024]{2,1,0:T(8,128)(2,1)S(1)}, u32[]{:S(2)}, u32[]{:S(2)}) collective-permute-start(bf16[2,128,1024]{2,1,0:T(8,128)(2,1)} %collective-permute-done.7), channel_id=1, source_target_pairs={{0,1},{1,0},{2,3},{3,2},{4,5},{5,4},{6,7},{7,6},{8,9},{9,8},{10,11... | collective-permute-start | bytes 1572872 | tf_op jit(solution)/shard_map/ppermute | solution.py:33
  68.8 31.4 %collective-permute-start.10 = (bf16[2,128,1024]{2,1,0:T(8,128)(2,1)}, bf16[2,128,1024]{2,1,0:T(8,128)(2,1)S(1)}, u32[]{:S(2)}, u32[]{:S(2)}) collective-permute-start(bf16[2,128,1024]{2,1,0:T(8,128)(2,1)} %collective-permute-done.9), channel_id=1, source_target_pairs={{0,1},{1,0},{2,3},{3,2},{4,5},{5,4},{6,7},{7,6},{8,9},{9,8},{10,11... | collective-permute-start | bytes 1572872 | tf_op jit(solution)/shard_map/ppermute | solution.py:33
  75.9 25.4 %collective-permute-start.12 = (bf16[2,128,1024]{2,1,0:T(8,128)(2,1)}, bf16[2,128,1024]{2,1,0:T(8,128)(2,1)S(1)}, u32[]{:S(2)}, u32[]{:S(2)}) collective-permute-start(bf16[2,128,1024]{2,1,0:T(8,128)(2,1)} %collective-permute-done.11), channel_id=1, source_target_pairs={{0,1},{1,0},{2,3},{3,2},{4,5},{5,4},{6,7},{7,6},{8,9},{9,8},{10,11... | collective-permute-start | bytes 1572872 | tf_op jit(solution)/shard_map/ppermute | solution.py:33
  95.1 30.6 %copy-start.1 = (bf16[4,256,1536]{2,1,0:T(8,128)(2,1)}, bf16[4,256,1536]{2,1,0:T(8,128)(2,1)S(1)}, u32[]{:S(2)}) copy-start(bf16[4,256,1536]{2,1,0:T(8,128)(2,1)S(1)} %bitcast_dynamic-update-slice_fusion) | copy-start | bytes 9437188
  127.7 27.6 %copy-start.3 = (bf16[2,128,1024]{2,1,0:T(8,128)(2,1)S(1)}, bf16[2,128,1024]{2,1,0:T(8,128)(2,1)}, u32[]{:S(2)}) copy-start(bf16[2,128,1024]{2,1,0:T(8,128)(2,1)} %param.16) | copy-start | bytes 1572868
  127.7 27.6 %collective-permute-start.13 = (f32[2,128,1024]{2,1,0:T(8,128)S(1)}, f32[2,128,1024]{2,1,0:T(8,128)S(1)}, u32[]{:S(2)}, u32[]{:S(2)}) collective-permute-start(f32[2,128,1024]{2,1,0:T(8,128)S(1)} %slice.229), channel_id=1, source_target_pairs={{0,1},{1,0},{2,3},{3,2},{4,5},{5,4},{6,7},{7,6},{8,9},{9,8},{10,11... | collective-permute-start | bytes 3145736 | tf_op jit(solution)/shard_map/ppermute | solution.py:33
  128.0 14.8 %collective-permute-start.18 = (bf16[2,128,1024]{2,1,0:T(8,128)(2,1)S(1)}, bf16[2,128,1024]{2,1,0:T(8,128)(2,1)S(1)}, u32[]{:S(2)}, u32[]{:S(2)}) collective-permute-start(bf16[2,128,1024]{2,1,0:T(8,128)(2,1)S(1)} %get-tuple-element.52), channel_id=1, source_target_pairs={{0,8},{8,0},{16,24},{24,16},{1,9},{9,1},{17,25},{25,17},{2,10},{10... | collective-permute-start | bytes 1572872 | tf_op jit(solution)/shard_map/ppermute | solution.py:38
  129.6 25.3 %collective-permute-start.19 = (bf16[2,128,1024]{2,1,0:T(8,128)(2,1)S(1)}, bf16[2,128,1024]{2,1,0:T(8,128)(2,1)S(1)}, u32[]{:S(2)}, u32[]{:S(2)}) collective-permute-start(bf16[2,128,1024]{2,1,0:T(8,128)(2,1)S(1)} %get-tuple-element.52), channel_id=1, source_target_pairs={{0,16},{8,24},{16,0},{24,8},{1,17},{9,25},{17,1},{25,9},{2,18},{10... | collective-permute-start | bytes 1572872 | tf_op jit(solution)/shard_map/ppermute | solution.py:38
  131.2 23.7 %collective-permute-start.20 = (bf16[2,128,1024]{2,1,0:T(8,128)(2,1)S(1)}, bf16[2,128,1024]{2,1,0:T(8,128)(2,1)S(1)}, u32[]{:S(2)}, u32[]{:S(2)}) collective-permute-start(bf16[2,128,1024]{2,1,0:T(8,128)(2,1)S(1)} %get-tuple-element.52), channel_id=1, source_target_pairs={{0,24},{8,16},{16,8},{24,0},{1,25},{9,17},{17,9},{25,1},{2,26},{10... | collective-permute-start | bytes 1572872 | tf_op jit(solution)/shard_map/ppermute | solution.py:38
  155.2 28.4 %collective-permute-start.21 = (bf16[4,2,128,1024]{3,2,1,0:T(8,128)(2,1)S(1)}, bf16[4,2,128,1024]{3,2,1,0:T(8,128)(2,1)S(1)}, u32[]{:S(2)}, u32[]{:S(2)}) collective-permute-start(bf16[4,2,128,1024]{3,2,1,0:T(8,128)(2,1)S(1)} %pad_maximum_fusion.2), channel_id=1, source_target_pairs={{0,1},{1,0},{2,3},{3,2},{4,5},{5,4},{6,7},{7,6},{8,9},{9,8},{10,11... | collective-permute-start | bytes 6291464 | tf_op jit(solution)/shard_map/ppermute | solution.py:33
  156.6 14.7 %collective-permute-start.14 = (bf16[2,128,1024]{2,1,0:T(8,128)(2,1)S(1)}, bf16[2,128,1024]{2,1,0:T(8,128)(2,1)S(1)}, u32[]{:S(2)}, u32[]{:S(2)}) collective-permute-start(bf16[2,128,1024]{2,1,0:T(8,128)(2,1)S(1)} %get-tuple-element.54), channel_id=1, source_target_pairs={{0,8},{8,0},{16,24},{24,16},{1,9},{9,1},{17,25},{25,17},{2,10},{10... | collective-permute-start | bytes 1572872 | tf_op jit(solution)/shard_map/ppermute | solution.py:38
  157.8 23.6 %collective-permute-start.15 = (bf16[2,128,1024]{2,1,0:T(8,128)(2,1)S(1)}, bf16[2,128,1024]{2,1,0:T(8,128)(2,1)S(1)}, u32[]{:S(2)}, u32[]{:S(2)}) collective-permute-start(bf16[2,128,1024]{2,1,0:T(8,128)(2,1)S(1)} %get-tuple-element.54), channel_id=1, source_target_pairs={{0,16},{8,24},{16,0},{24,8},{1,17},{9,25},{17,1},{25,9},{2,18},{10... | collective-permute-start | bytes 1572872 | tf_op jit(solution)/shard_map/ppermute | solution.py:38
  158.6 24.4 %collective-permute-start.16 = (bf16[2,128,1024]{2,1,0:T(8,128)(2,1)S(1)}, bf16[2,128,1024]{2,1,0:T(8,128)(2,1)S(1)}, u32[]{:S(2)}, u32[]{:S(2)}) collective-permute-start(bf16[2,128,1024]{2,1,0:T(8,128)(2,1)S(1)} %get-tuple-element.54), channel_id=1, source_target_pairs={{0,24},{8,16},{16,8},{24,0},{1,25},{9,17},{17,9},{25,1},{2,26},{10... | collective-permute-start | bytes 1572872 | tf_op jit(solution)/shard_map/ppermute | solution.py:38
  183.3 4.2 collective-permute-start.17
  228.4 4.2 collective-permute-start.29
  237.0 15.0 %collective-permute-start.30 = (bf16[2,128,1024]{2,1,0:T(8,128)(2,1)}, bf16[2,128,1024]{2,1,0:T(8,128)(2,1)S(1)}, u32[]{:S(2)}, u32[]{:S(2)}) collective-permute-start(bf16[2,128,1024]{2,1,0:T(8,128)(2,1)} %get-tuple-element.73), channel_id=1, source_target_pairs={{0,8},{8,0},{16,24},{24,16},{1,9},{9,1},{17,25},{25,17},{2,10},{10... | collective-permute-start | bytes 1572872 | tf_op jit(solution)/shard_map/ppermute | solution.py:38
  237.8 25.1 %collective-permute-start.31 = (bf16[2,128,1024]{2,1,0:T(8,128)(2,1)}, bf16[2,128,1024]{2,1,0:T(8,128)(2,1)S(1)}, u32[]{:S(2)}, u32[]{:S(2)}) collective-permute-start(bf16[2,128,1024]{2,1,0:T(8,128)(2,1)} %get-tuple-element.75), channel_id=1, source_target_pairs={{0,16},{8,24},{16,0},{24,8},{1,17},{9,25},{17,1},{25,9},{2,18},{10... | collective-permute-start | bytes 1572872 | tf_op jit(solution)/shard_map/ppermute | solution.py:38
  239.3 23.6 %collective-permute-start.32 = (bf16[2,128,1024]{2,1,0:T(8,128)(2,1)}, bf16[2,128,1024]{2,1,0:T(8,128)(2,1)}, u32[]{:S(2)}, u32[]{:S(2)}) collective-permute-start(bf16[2,128,1024]{2,1,0:T(8,128)(2,1)} %get-tuple-element.74), channel_id=1, source_target_pairs={{0,24},{8,16},{16,8},{24,0},{1,25},{9,17},{17,9},{25,1},{2,26},{10... | collective-permute-start | bytes 1572872 | tf_op jit(solution)/shard_map/ppermute | solution.py:38
  252.0 10.9 %copy-start.16 = (bf16[2,128,1024]{2,1,0:T(8,128)(2,1)}, bf16[2,128,1024]{2,1,0:T(8,128)(2,1)S(1)}, u32[]{:S(2)}) copy-start(bf16[2,128,1024]{2,1,0:T(8,128)(2,1)S(1)} %collective-permute-done.30) | copy-start | bytes 1572868
  267.1 6.7 %collective-permute-start.33 = (bf16[2,128,1024]{2,1,0:T(8,128)(2,1)}, bf16[2,128,1024]{2,1,0:T(8,128)(2,1)}, u32[]{:S(2)}, u32[]{:S(2)}) collective-permute-start(bf16[2,128,1024]{2,1,0:T(8,128)(2,1)} %fusion.46), channel_id=1, source_target_pairs={{0,1},{1,0},{2,3},{3,2},{4,5},{5,4},{6,7},{7,6},{8,9},{9,8},{10,11... | collective-permute-start | bytes 1572872 | tf_op jit(solution)/shard_map/ppermute | solution.py:33
  273.7 45.5 %collective-permute-start.25 = (bf16[4,2,128,1024]{3,2,1,0:T(8,128)(2,1)}, bf16[4,2,128,1024]{3,2,1,0:T(8,128)(2,1)}, u32[]{:S(2)}, u32[]{:S(2)}) collective-permute-start(bf16[4,2,128,1024]{3,2,1,0:T(8,128)(2,1)} %bitcast.33), channel_id=1, source_target_pairs={{0,1},{1,0},{2,3},{3,2},{4,5},{5,4},{6,7},{7,6},{8,9},{9,8},{10,11... | collective-permute-start | bytes 6291464 | tf_op jit(solution)/shard_map/ppermute | solution.py:33
  309.6 28.1 %collective-permute-start.34 = (bf16[2,4,128,1024]{3,2,0,1:T(8,128)(2,1)}, bf16[2,4,128,1024]{3,2,0,1:T(8,128)(2,1)}, u32[]{:S(2)}, u32[]{:S(2)}) collective-permute-start(bf16[2,4,128,1024]{3,2,0,1:T(8,128)(2,1)} %fusion.2), channel_id=1, source_target_pairs={{0,1},{1,0},{2,3},{3,2},{4,5},{5,4},{6,7},{7,6},{8,9},{9,8},{10,11... | collective-permute-start | bytes 6291464 | tf_op jit(solution)/shard_map/ppermute | solution.py:33
  319.2 5.4 %collective-permute-start.38 = (f32[2176]{0:T(1024)S(1)}, f32[2176]{0:T(1024)S(1)}, u32[]{:S(2)}, u32[]{:S(2)}) collective-permute-start(f32[2176]{0:T(1024)S(1)} %concatenate.59), channel_id=1, source_target_pairs={{0,1},{1,0},{2,3},{3,2},{4,5},{5,4},{6,7},{7,6},{8,9},{9,8},{10,11... | collective-permute-start | bytes 26120 | tf_op jit(solution)/shard_map/ppermute | solution.py:61
  324.6 3.8 collective-permute-start.39
  325.2 12.5 %slice-start = ((s8[8388608]{0:T(1024)(128)(4,1)}), s8[4194304]{0:T(1024)(128)(4,1)S(1)}, s32[]{:S(2)}) async-start(s8[8388608]{0:T(1024)(128)(4,1)} %bitcast.222), calls=%async_computation.3 | async-start | bytes 8388608
  328.4 3.7 collective-permute-start.40
  332.1 5.6 %collective-permute-start.41 = (f32[2176]{0:T(1024)S(1)}, f32[2176]{0:T(1024)S(1)}, u32[]{:S(2)}, u32[]{:S(2)}) collective-permute-start(f32[2176]{0:T(1024)S(1)} %add.324), channel_id=1, source_target_pairs={{0,2},{2,0},{4,6},{6,4},{1,3},{3,1},{5,7},{7,5},{8,10},{10,8},{12,... | collective-permute-start | bytes 26120 | tf_op jit(solution)/shard_map/ppermute | solution.py:61
  332.3 22.7 %collective-permute-start.43 = (bf16[256,1536]{1,0:T(8,128)(2,1)S(1)}, bf16[256,1536]{1,0:T(8,128)(2,1)S(1)}, u32[]{:S(2)}, u32[]{:S(2)}) collective-permute-start(bf16[256,1536]{1,0:T(8,128)(2,1)S(1)} %get-tuple-element.67), channel_id=1, source_target_pairs={{0,8},{8,0},{16,24},{24,16},{1,9},{9,1},{17,25},{25,17},{2,10},{10... | collective-permute-start | bytes 2359304 | tf_op jit(solution)/shard_map/ppermute | solution.py:38
  332.9 34.5 %collective-permute-start.44 = (bf16[256,1536]{1,0:T(8,128)(2,1)S(1)}, bf16[256,1536]{1,0:T(8,128)(2,1)S(1)}, u32[]{:S(2)}, u32[]{:S(2)}) collective-permute-start(bf16[256,1536]{1,0:T(8,128)(2,1)S(1)} %get-tuple-element.69), channel_id=1, source_target_pairs={{0,16},{8,24},{16,0},{24,8},{1,17},{9,25},{17,1},{25,9},{2,18},{10... | collective-permute-start | bytes 2359304 | tf_op jit(solution)/shard_map/ppermute | solution.py:38
  334.4 36.3 %collective-permute-start.45 = (bf16[256,1536]{1,0:T(8,128)(2,1)S(1)}, bf16[256,1536]{1,0:T(8,128)(2,1)S(1)}, u32[]{:S(2)}, u32[]{:S(2)}) collective-permute-start(bf16[256,1536]{1,0:T(8,128)(2,1)S(1)} %get-tuple-element.68), channel_id=1, source_target_pairs={{0,24},{8,16},{16,8},{24,0},{1,25},{9,17},{17,9},{25,1},{2,26},{10... | collective-permute-start | bytes 2359304 | tf_op jit(solution)/shard_map/ppermute | solution.py:38
  337.7 5.3 %collective-permute-start.42 = (f32[2176]{0:T(1024)S(1)}, f32[2176]{0:T(1024)S(1)}, u32[]{:S(2)}, u32[]{:S(2)}) collective-permute-start(f32[2176]{0:T(1024)S(1)} %add.325), channel_id=1, source_target_pairs={{0,4},{2,6},{4,0},{6,2},{1,5},{3,7},{5,1},{7,3},{8,12},{10,14},{12... | collective-permute-start | bytes 26120 | tf_op jit(solution)/shard_map/ppermute | solution.py:61
  340.4 58.5 %copy-start = (f32[2,4,128,1024]{3,2,0,1:T(8,128)}, f32[2,4,128,1024]{3,2,0,1:T(8,128)S(1)}, u32[]{:S(2)}) copy-start(f32[2,4,128,1024]{3,2,0,1:T(8,128)S(1)} %fusion) | copy-start | bytes 12582916
  340.5 12.6 %collective-permute-start.35 = (bf16[2,128,1024]{2,1,0:T(8,128)(2,1)S(1)}, bf16[2,128,1024]{2,1,0:T(8,128)(2,1)S(1)}, u32[]{:S(2)}, u32[]{:S(2)}) collective-permute-start(bf16[2,128,1024]{2,1,0:T(8,128)(2,1)S(1)} %fusion.42), channel_id=1, source_target_pairs={{2,0},{4,2},{6,4},{3,1},{5,3},{7,5},{10,8},{12,10},{14,12},{11,9},... | collective-permute-start | bytes 1572872 | tf_op jit(solution)/shard_map/ppermute | solution.py:48
  343.0 62.3 %collective-permute-start.26 = (bf16[2,128,1024]{2,1,0:T(8,128)(2,1)}, bf16[2,128,1024]{2,1,0:T(8,128)(2,1)}, u32[]{:S(2)}, u32[]{:S(2)}) collective-permute-start(bf16[2,128,1024]{2,1,0:T(8,128)(2,1)} %get-tuple-element.76), channel_id=1, source_target_pairs={{0,8},{8,0},{16,24},{24,16},{1,9},{9,1},{17,25},{25,17},{2,10},{10... | collective-permute-start | bytes 1572872 | tf_op jit(solution)/shard_map/ppermute | solution.py:38
  353.1 52.2 %collective-permute-start.27 = (bf16[2,128,1024]{2,1,0:T(8,128)(2,1)}, bf16[2,128,1024]{2,1,0:T(8,128)(2,1)}, u32[]{:S(2)}, u32[]{:S(2)}) collective-permute-start(bf16[2,128,1024]{2,1,0:T(8,128)(2,1)} %get-tuple-element.78), channel_id=1, source_target_pairs={{0,16},{8,24},{16,0},{24,8},{1,17},{9,25},{17,1},{25,9},{2,18},{10... | collective-permute-start | bytes 1572872 | tf_op jit(solution)/shard_map/ppermute | solution.py:38
  355.0 18.3 %collective-permute-start.36 = (bf16[2,128,1024]{2,1,0:T(8,128)(2,1)S(1)}, bf16[2,128,1024]{2,1,0:T(8,128)(2,1)S(1)}, u32[]{:S(2)}, u32[]{:S(2)}) collective-permute-start(bf16[2,128,1024]{2,1,0:T(8,128)(2,1)S(1)} %fusion.21), channel_id=1, source_target_pairs={{2,0},{4,2},{6,4},{3,1},{5,3},{7,5},{10,8},{12,10},{14,12},{11,9},... | collective-permute-start | bytes 1572872 | tf_op jit(solution)/shard_map/ppermute | solution.py:48
  371.2 9.1 %collective-permute-start.46 = (bf16[64,1536]{1,0:T(8,128)(2,1)S(1)}, bf16[64,1536]{1,0:T(8,128)(2,1)S(1)}, u32[]{:S(2)}, u32[]{:S(2)}) collective-permute-start(bf16[64,1536]{1,0:T(8,128)(2,1)S(1)} %get-tuple-element.89), channel_id=1, source_target_pairs={{0,2},{2,4},{4,6},{6,0},{1,3},{3,5},{5,7},{7,1},{8,10},{10,12},{12... | collective-permute-start | bytes 589832 | tf_op jit(solution)/shard_map/ppermute | solution.py:53
  373.3 12.5 %collective-permute-start.47 = (bf16[64,1536]{1,0:T(8,128)(2,1)S(1)}, bf16[64,1536]{1,0:T(8,128)(2,1)S(1)}, u32[]{:S(2)}, u32[]{:S(2)}) collective-permute-start(bf16[64,1536]{1,0:T(8,128)(2,1)S(1)} %get-tuple-element.91), channel_id=1, source_target_pairs={{0,4},{2,6},{4,0},{6,2},{1,5},{3,7},{5,1},{7,3},{8,12},{10,14},{12... | collective-permute-start | bytes 589832 | tf_op jit(solution)/shard_map/ppermute | solution.py:53
  373.3 14.0 %collective-permute-start.48 = (bf16[64,1536]{1,0:T(8,128)(2,1)S(1)}, bf16[64,1536]{1,0:T(8,128)(2,1)S(1)}, u32[]{:S(2)}, u32[]{:S(2)}) collective-permute-start(bf16[64,1536]{1,0:T(8,128)(2,1)S(1)} %get-tuple-element.90), channel_id=1, source_target_pairs={{0,6},{2,0},{4,2},{6,4},{1,7},{3,1},{5,3},{7,5},{8,14},{10,8},{12,... | collective-permute-start | bytes 589832 | tf_op jit(solution)/shard_map/ppermute | solution.py:53
  380.3 25.1 %collective-permute-start.28 = (bf16[2,128,1024]{2,1,0:T(8,128)(2,1)}, bf16[2,128,1024]{2,1,0:T(8,128)(2,1)}, u32[]{:S(2)}, u32[]{:S(2)}) collective-permute-start(bf16[2,128,1024]{2,1,0:T(8,128)(2,1)} %get-tuple-element.77), channel_id=1, source_target_pairs={{0,24},{8,16},{16,8},{24,0},{1,25},{9,17},{17,9},{25,1},{2,26},{10... | collective-permute-start | bytes 1572872 | tf_op jit(solution)/shard_map/ppermute | solution.py:38
  385.7 13.2 %collective-permute-start.37 = (bf16[2,128,1024]{2,1,0:T(8,128)(2,1)S(1)}, bf16[2,128,1024]{2,1,0:T(8,128)(2,1)S(1)}, u32[]{:S(2)}, u32[]{:S(2)}) collective-permute-start(bf16[2,128,1024]{2,1,0:T(8,128)(2,1)S(1)} %fusion.23), channel_id=1, source_target_pairs={{2,0},{4,2},{6,4},{3,1},{5,3},{7,5},{10,8},{12,10},{14,12},{11,9},... | collective-permute-start | bytes 1572872 | tf_op jit(solution)/shard_map/ppermute | solution.py:48
  402.9 7.7 %collective-permute-start.49 = (bf16[64,1920]{1,0:T(8,128)(2,1)S(1)}, bf16[64,1920]{1,0:T(8,128)(2,1)S(1)}, u32[]{:S(2)}, u32[]{:S(2)}) collective-permute-start(bf16[64,1920]{1,0:T(8,128)(2,1)S(1)} %get-tuple-element.83), channel_id=1, source_target_pairs={{0,8},{8,0},{16,24},{24,16},{1,9},{9,1},{17,25},{25,17},{2,10},{10... | collective-permute-start | bytes 737288 | tf_op jit(solution)/shard_map/ppermute | solution.py:38
  409.1 11.4 %collective-permute-start.50 = (bf16[64,1920]{1,0:T(8,128)(2,1)S(1)}, bf16[64,1920]{1,0:T(8,128)(2,1)S(1)}, u32[]{:S(2)}, u32[]{:S(2)}) collective-permute-start(bf16[64,1920]{1,0:T(8,128)(2,1)S(1)} %get-tuple-element.82), channel_id=1, source_target_pairs={{0,16},{8,24},{16,0},{24,8},{1,17},{9,25},{17,1},{25,9},{2,18},{10... | collective-permute-start | bytes 737288 | tf_op jit(solution)/shard_map/ppermute | solution.py:38
  409.6 11.6 %collective-permute-start.51 = (bf16[64,1920]{1,0:T(8,128)(2,1)S(1)}, bf16[64,1920]{1,0:T(8,128)(2,1)S(1)}, u32[]{:S(2)}, u32[]{:S(2)}) collective-permute-start(bf16[64,1920]{1,0:T(8,128)(2,1)S(1)} %get-tuple-element.81), channel_id=1, source_target_pairs={{0,24},{8,16},{16,8},{24,0},{1,25},{9,17},{17,9},{25,1},{2,26},{10... | collective-permute-start | bytes 737288 | tf_op jit(solution)/shard_map/ppermute | solution.py:38
  (23 other events, 88.8 us)
Sparse Core Ops, SparseCore 0:
  63.4 73.6 all-gather.1
  268.9 70.0 reduce-scatter.1

commit v2 on v1

--- a/solution.py
+++ b/solution.py
@@ -53,14 +53,25 @@
     return lax.ppermute(value, "ctx", [(i, (i + step) % size) for i in range(size)])
 
 
-def sum_everywhere(value):
-    for axis in ("tp", "fsdp", "ctx"):
-        size = lax.axis_size(axis)
-        step = 1
-        while step < size:
-            value = value + lax.ppermute(value, axis, [(i, i ^ step) for i in range(size)])
-            step *= 2
-    return value
+def tree_sum(values):
+    while len(values) > 1:
+        half = len(values) // 2
+        values = [values[i] + values[i + half] for i in range(half)]
+    return values[0]
+
+
+def two_parts(rows):
+    first = rows.astype(BF)
+    left = (rows - first.astype(F32)).astype(BF)
+    return jnp.pad(jnp.concatenate([first, left]), ((0, 16 - 2 * rows.shape[0]), (0, 0)))
+
+
+def one_part(rows):
+    return rows[:2].astype(F32) + rows[2:4].astype(F32)
+
+
+def tie(*values):
+    return lax.optimization_barrier(values)
 
 
 def lane_ids(rows):
@@ -96,7 +107,7 @@
 def key_bias(scal_ref, slot, keys, block_rows):
     c = scal_ref[0]
     core = scal_ref[1]
-    length = scal_ref[2 + slot]
+    length = scal_ref[3 + slot]
     half = block_rows // 2
 
     def places(index):
@@ -116,23 +127,46 @@
     return jnp.where(first, x, turned).astype(BF), jnp.where(first, turned, x).astype(BF)
 
 
-def attend_kernel(scal_ref, q_ref, k_ref, v_ref, cos_ref, sin_ref, qg_ref, kg_ref, o_ref, l_ref, qh_ref, kh_ref, bias_ref):
-    rows = q_ref.shape[1]
-    keys = k_ref.shape[1]
+def attend_kernel(n_pieces, n_parts, scal_ref, *refs):
+    pieces = refs[:n_pieces]
+    (
+        tq_ref, tk_ref, tv_ref, bq_ref, bk_ref, bv_ref, cos_ref, sin_ref, qg_ref, kg_ref,
+        o_ref, l_ref, qr_ref, kr_ref, v_ref, qh_ref, kh_ref, x_ref, bias_ref, wq_ref, wkv_ref,
+    ) = refs[n_pieces:]
+    rows = qr_ref.shape[1]
+    keys = kr_ref.shape[1]
+    half = rows // 2
 
     @pl.when(pl.program_id(1) == 0)
     def _():
         bias_ref[...] = key_bias(scal_ref, pl.program_id(0), keys, rows)
-
-    key = prepare(k_ref[0], kg_ref[...], cos_ref[...], sin_ref[...]).astype(BF)
+        for i, piece in enumerate(pieces):
+            x_ref[0, i * half : (i + 1) * half] = piece[0]
+
+    depth = tq_ref.shape[1]
+    bits = [1 << i for i in range(8) if 1 << i < n_parts]
+    for side, (query_w, key_w, value_w) in enumerate(((tq_ref, tk_ref, tv_ref), (bq_ref, bk_ref, bv_ref))):
+        order = bits[::-1] if side else bits
+        for i in range(n_parts):
+            mask = sum(bit for j, bit in enumerate(order) if i >> j & 1)
+            at = pl.ds(pl.multiple_of(((scal_ref[2] ^ mask) * 2 + side) * depth, depth), depth)
+            wq_ref[at, :] = query_w[i]
+            wkv_ref[at, :TILE] = key_w[i]
+            wkv_ref[at, TILE:] = value_w[i]
+    key_value = dot(x_ref[0], wkv_ref[...], NN)
+    query_raw = dot(x_ref[0, :rows], wq_ref[...], NN)
+    kr_ref[0] = key_value[:, :TILE]
+    v_ref[0] = key_value[:, TILE:].astype(BF)
+    qr_ref[0] = query_raw
+
+    key = prepare(kr_ref[0], kg_ref[...], cos_ref[...], sin_ref[...]).astype(BF)
     kh_ref[0] = key
     key_twins = twins(key.astype(F32))
-    value = v_ref[0].astype(F32)
-    value_twins = twins(value)
+    value_twins = twins(v_ref[0].astype(F32))
     first = lane_ids(rows) < HEAD
     for pair in range(2):
         lanes = slice(pair * TILE, (pair + 1) * TILE)
-        query = prepare(q_ref[0, :, lanes], qg_ref[...], cos_ref[:rows], sin_ref[:rows]).astype(BF)
+        query = prepare(qr_ref[0, :, lanes], qg_ref[...], cos_ref[:rows], sin_ref[:rows]).astype(BF)
         qh_ref[0, :, lanes] = query
         turned_value = value_twins[pair].astype(F32).T.astype(BF)
         mixed = []
@@ -217,29 +251,42 @@
     return smem, query, key, table, gain, stat
 
 
-def attend(scal, q_raw, k_raw, value, cosine, sine, query_gain, key_gain):
-    slots, rows, width = q_raw.shape
-    keys, kv_width = k_raw.shape[1:]
+def attend(scal, pieces, weights, widths, cosine, sine, query_gain, key_gain):
+    width, kv_width = widths
+    slots, half, model = pieces[0].shape
+    rows = 2 * half
+    keys = len(pieces) * half
     smem, query, key, table, gain, stat = attention_specs(slots, rows, keys)
     pairs = kv_width // TILE
+    piece = pl.BlockSpec((1, half, model), lambda s, p: (s, 0, 0))
+    parts, depth = weights[0].shape[:2]
+    w_query = pl.BlockSpec((parts, depth, 2 * TILE), lambda s, p: (0, 0, p))
+    w_key = pl.BlockSpec((parts, depth, TILE), lambda s, p: (0, 0, width // TILE + p))
+    w_value = pl.BlockSpec((parts, depth, TILE), lambda s, p: (0, 0, (width + kv_width) // TILE + p))
     return pl.pallas_call(
-        attend_kernel,
+        functools.partial(attend_kernel, len(pieces), parts),
         grid=(slots, pairs),
-        in_specs=[smem, query, key, key, table, table, gain, gain],
-        out_specs=[query, stat, query, key],
+        in_specs=[smem] + [piece] * len(pieces) + [w_query, w_key, w_value] * 2 + [table, table, gain, gain],
+        out_specs=[query, stat, query, key, key, query, key, pl.BlockSpec((1, keys, model), lambda s, p: (s, 0, 0))],
         out_shape=[
             jax.ShapeDtypeStruct((slots, rows, width), BF),
             jax.ShapeDtypeStruct((slots, pairs, 8, rows), F32),
+            jax.ShapeDtypeStruct((slots, rows, width), F32),
+            jax.ShapeDtypeStruct((slots, keys, kv_width), F32),
+            jax.ShapeDtypeStruct((slots, keys, kv_width), BF),
             jax.ShapeDtypeStruct((slots, rows, width), BF),
             jax.ShapeDtypeStruct((slots, keys, kv_width), BF),
+            jax.ShapeDtypeStruct((slots, keys, model), BF),
         ],
-        scratch_shapes=[pltpu.VMEM((keys, rows), F32)],
+        scratch_shapes=[
+            pltpu.VMEM((keys, rows), F32),
+            pltpu.VMEM((model, 2 * TILE), BF),
+            pltpu.VMEM((model, 2 * TILE), BF),
+        ],
         compiler_params=pltpu.CompilerParams(vmem_limit_bytes=VMEM_LIMIT),
-        cost_estimate=pl.CostEstimate(
-            flops=8 * slots * rows * keys * width, bytes_accessed=8 << 20, transcendentals=slots * rows * keys * width // HEAD
-        ),
+        cost_estimate=pl.CostEstimate(flops=1 << 20, bytes_accessed=1 << 20, transcendentals=0),
         name="attend",
-    )(scal, q_raw, k_raw, value, cosine, sine, query_gain, key_gain)
+    )(scal, *pieces, *[item for item in weights for _ in range(3)], cosine, sine, query_gain, key_gain)
 
 
 def attend_back(scal, q_raw, k_raw, value, cosine, sine, query_gain, key_gain, q_hat, k_hat, out, stats, grad):
@@ -268,23 +315,146 @@
     )(scal, q_raw, k_raw, value, cosine, sine, query_gain, key_gain, q_hat, k_hat, out, stats, grad)
 
 
-def ffn_kernel(x_ref, g_ref, w_ref, y_ref, dx_ref, grad_ref, sum_ref):
+def weight_kernel(at_ref, x_ref, dq_ref, dk_ref, dv_ref, b_ref, o_ref, more_ref, *out_refs):
+    slots, rows, q_cols = dq_ref.shape
+    k_cols = dk_ref.shape[2]
+    total = jnp.zeros((x_ref.shape[2], q_cols), F32)
+    key_total = jnp.zeros((x_ref.shape[2], k_cols), F32)
+    value_total = jnp.zeros((x_ref.shape[2], k_cols), F32)
+    out_total = jnp.zeros((x_ref.shape[2], q_cols), F32)
+    for s in range(slots):
+        out_total = out_total + dot(b_ref[s], o_ref[s], TN)
+        x = x_ref[s]
+        total = total + dot(x[:rows], dq_ref[s], TN)
+        key_total = key_total + dot(x, dk_ref[s], TN)
+        value_total = value_total + dot(x, dv_ref[s], TN)
+    depth = x_ref.shape[2]
+    for m, ref in enumerate(out_refs):
+
+        @pl.when(pl.program_id(0) == m)
+        def _(ref=ref):
+            ref[:depth, :q_cols] = total.astype(BF)
+            ref[:depth, q_cols : q_cols + k_cols] = key_total.astype(BF)
+            ref[:depth, q_cols + k_cols : q_cols + 2 * k_cols] = value_total.astype(BF)
+            ref[:depth, q_cols + 2 * k_cols :] = out_total.astype(BF)
+            ref[depth:] = more_ref[...]
+
+
+def weight_grads(at, x, d_q, d_k, d_v, d_branch, attn, more, parts):
+    slots, keys, width = x.shape
+    cols = 2 * d_q.shape[2] + 2 * d_k.shape[2]
+    depth = width // parts + more.shape[0]
+    spec = pltpu.PrefetchScalarGridSpec(
+        num_scalar_prefetch=1,
+        grid=(parts,),
+        in_specs=[
+            pl.BlockSpec((slots, keys, width // parts), lambda m, at: (0, 0, at[0] ^ m)),
+            pl.BlockSpec(d_q.shape, lambda m, at: (0, 0, 0)),
+            pl.BlockSpec(d_k.shape, lambda m, at: (0, 0, 0)),
+            pl.BlockSpec(d_v.shape, lambda m, at: (0, 0, 0)),
+            pl.BlockSpec(d_branch.shape[:2] + (width // parts,), lambda m, at: (0, 0, at[0] ^ m)),
+            pl.BlockSpec(attn.shape, lambda m, at: (0, 0, 0)),
+            pl.BlockSpec(more.shape, lambda m, at: (0, 0)),
+        ],
+        out_specs=[pl.BlockSpec((depth, cols), lambda m, at: (0, 0))] * parts,
+    )
+    return pl.pallas_call(
+        weight_kernel,
+        grid_spec=spec,
+        out_shape=[jax.ShapeDtypeStruct((depth, cols), BF)] * parts,
+        compiler_params=pltpu.CompilerParams(vmem_limit_bytes=VMEM_LIMIT),
+        cost_estimate=pl.CostEstimate(flops=4 << 30, bytes_accessed=8 << 20, transcendentals=0),
+        name="weight_grads",
+    )(at, x, d_q, d_k, d_v, d_branch, attn, more)
+
+
+def input_kernel(dq_ref, dk_ref, dv_ref, x_ref, w_ref, mine_ref, other_ref, gain_ref):
+    slots, rows, q_cols = dq_ref.shape
+    k_cols = dk_ref.shape[2]
+    half = rows // 2
+    gain = jnp.zeros((1, x_ref.shape[2]), F32)
+    for s in range(slots):
+        d_x = dot(dk_ref[s], w_ref[:, q_cols : q_cols + k_cols], NT)
+        d_x = d_x + dot(dv_ref[s], w_ref[:, q_cols + k_cols : q_cols + 2 * k_cols], NT)
+        gain = gain + jnp.sum(d_x * x_ref[s].astype(F32), axis=0, keepdims=True)
+        mine_ref[0, s] = d_x[:half]
+        other_ref[0, s] = d_x[half:].astype(BF)
+
+    @pl.when(pl.program_id(0) == 0)
+    def _():
+        more = jnp.zeros_like(gain)
+        for s in range(slots):
+            d_x = dot(dq_ref[s], w_ref[:, :q_cols], NT)
+            more = more + jnp.sum(d_x * x_ref[s].astype(F32), axis=0, keepdims=True)
+            mine_ref[0, s] += d_x[:half]
+            other_ref[0, s] = (other_ref[0, s].astype(F32) + d_x[half:]).astype(BF)
+        gain_ref[...] = gain + more
+
+    @pl.when(pl.program_id(0) > 0)
+    def _():
+        gain_ref[...] += gain
+
+
+def input_grads(d_q, d_k, d_v, x, w):
+    slots, rows, q_cols = d_q.shape
+    keys, k_cols = d_k.shape[1:]
+    width = w.shape[0]
+    blocks = keys // rows
+    part = pl.BlockSpec((slots, rows, k_cols), lambda r: (0, r, 0))
+    out = pl.BlockSpec((1, slots, rows // 2, width), lambda r: (r, 0, 0, 0))
+    return pl.pallas_call(
+        input_kernel,
+        grid=(blocks,),
+        in_specs=[
+            pl.BlockSpec(d_q.shape, lambda r: (0, 0, 0)),
+            part,
+            part,
+            pl.BlockSpec((slots, rows, width), lambda r: (0, r, 0)),
+            pl.BlockSpec(w.shape, lambda r: (0, 0)),
+        ],
+        out_specs=[out, out, pl.BlockSpec((1, width), lambda r: (0, 0))],
+        out_shape=[
+            jax.ShapeDtypeStruct((blocks, slots, rows // 2, width), F32),
+            jax.ShapeDtypeStruct((blocks, slots, rows // 2, width), BF),
+            jax.ShapeDtypeStruct((1, width), F32),
+        ],
+        compiler_params=pltpu.CompilerParams(vmem_limit_bytes=VMEM_LIMIT),
+        cost_estimate=pl.CostEstimate(flops=3 << 30, bytes_accessed=12 << 20, transcendentals=0),
+        name="input_grads",
+    )(d_q, d_k, d_v, x, w)
+
+
+def ffn_kernel(xo_ref, xm_ref, go_ref, gm_ref, w_ref, yo_ref, ym_ref, do_ref, dm_ref, grad_ref, gain_ref, sum_ref):
     units = w_ref.shape[1] // 3
     step = pl.program_id(0)
-    x = x_ref[...]
-    g = g_ref[...]
+    early = step < pl.num_programs(0) // 2
+    x = jnp.where(early, xo_ref[...], xm_ref[...])
+    g = jnp.where(early, go_ref[...], gm_ref[...])
     raised = dot(x, w_ref[:, : 2 * units], NN)
     gate = raised[:, :units]
     upper = raised[:, units:]
     sig = 1.0 / (1.0 + jnp.exp(-gate))
     silu = gate * sig
     act = (silu * upper).astype(BF)
-    y_ref[...] = dot(act, w_ref[:, 2 * units :], NT).astype(BF)
+    y = dot(act, w_ref[:, 2 * units :], NT).astype(BF)
     d_act = dot(g, w_ref[:, 2 * units :], NN)
     d_gate = (d_act * upper * (sig + silu * (1.0 - sig))).astype(BF)
     d_up = (d_act * silu).astype(BF)
     both = jnp.concatenate([d_gate, d_up], axis=1)
-    dx_ref[...] = dot(both, w_ref[:, : 2 * units], NT).astype(BF)
+    d_x = dot(both, w_ref[:, : 2 * units], NT)
+    gain_row = jnp.sum(d_x * x.astype(F32), axis=0, keepdims=True)
+    dx = d_x.astype(BF)
+
+    @pl.when(early)
+    def _():
+        yo_ref[...] = y
+        do_ref[...] = dx
+
+    @pl.when(jnp.logical_not(early))
+    def _():
+        ym_ref[...] = y
+        dm_ref[...] = dx
+
     left = dot(x, both, TN)
     right = dot(g, act, TN)
 
@@ -292,39 +462,106 @@
     def _():
         sum_ref[:, : 2 * units] = left
         sum_ref[:, 2 * units :] = right
+        gain_ref[...] = gain_row
 
     @pl.when(step > 0)
     def _():
         sum_ref[:, : 2 * units] += left
         sum_ref[:, 2 * units :] += right
+        gain_ref[...] += gain_row
 
     @pl.when(step == pl.num_programs(0) - 1)
     def _():
         grad_ref[...] = sum_ref[...].astype(BF)
 
 
-def feed_forward(x, g, w, rows):
-    tokens, width = x.shape
+def feed_forward(x_mine, x_other, g_mine, g_other, w, rows):
+    tokens, width = x_mine.shape
     units3 = w.shape[1]
-    block = pl.BlockSpec((rows, width), lambda i: (i, 0))
+    steps = tokens // rows
+    other = pl.BlockSpec((rows, width), lambda i: (jnp.minimum(i, steps - 1), 0))
+    mine = pl.BlockSpec((rows, width), lambda i: (jnp.maximum(i - steps, 0), 0))
     whole = pl.BlockSpec((width, units3), lambda i: (0, 0))
-    return pl.pallas_call(
+    part = jax.ShapeDtypeStruct((tokens, width), BF)
+    y_other, y_mine, dx_other, dx_mine, grads, gain_row = pl.pallas_call(
         ffn_kernel,
-        grid=(tokens // rows,),
-        in_specs=[block, block, whole],
-        out_specs=[block, block, whole],
+        grid=(2 * steps,),
+        in_specs=[other, mine, other, mine, whole],
+        out_specs=[other, mine, other, mine, whole, pl.BlockSpec((1, width), lambda i: (0, 0))],
         out_shape=[
-            jax.ShapeDtypeStruct((tokens, width), BF),
-            jax.ShapeDtypeStruct((tokens, width), BF),
-            jax.ShapeDtypeStruct((width, units3), BF),
+            part, part, part, part,
+            jax.ShapeDtypeStruct((width, units3), BF), jax.ShapeDtypeStruct((1, width), F32),
         ],
         scratch_shapes=[pltpu.VMEM((width, units3), F32)],
         compiler_params=pltpu.CompilerParams(vmem_limit_bytes=VMEM_LIMIT),
         cost_estimate=pl.CostEstimate(
-            flops=6 * tokens * width * units3, bytes_accessed=24 << 20, transcendentals=tokens * units3 // 3
+            flops=12 * tokens * width * units3, bytes_accessed=24 << 20, transcendentals=2 * tokens * units3 // 3
         ),
         name="feed_forward",
-    )(x, g, w)
+    )(x_other, x_mine, g_other, g_mine, w)
+    return y_mine, y_other, dx_mine, dx_other, grads, gain_row[0]
+
+
+def same_kernel(in_ref, out_ref):
+    pass
+
+
+def same(value, flops):
+    return pl.pallas_call(
+        same_kernel,
+        in_specs=[pl.BlockSpec(memory_space=pl.ANY)],
+        out_specs=pl.BlockSpec(memory_space=pl.ANY),
+        out_shape=jax.ShapeDtypeStruct(value.shape, value.dtype),
+        input_output_aliases={0: 0},
+        cost_estimate=pl.CostEstimate(flops=flops, bytes_accessed=0, transcendentals=0),
+        name="same",
+    )(value)
+
+
+def pack_kernel(gate_ref, up_ref, down_ref, out_ref):
+    parts, shard, units3 = out_ref.shape
+    units = units3 // 3
+    have = gate_ref.shape[1]
+    for t in range(parts):
+        for j, ref in enumerate((gate_ref, up_ref, down_ref)):
+            first = min(t * units, have)
+            count = min((t + 1) * units, have) - first
+            if count:
+                out_ref[t, :, j * units : j * units + count] = ref[:, first : first + count]
+            if count < units:
+                out_ref[t, :, j * units + count : (j + 1) * units] = jnp.zeros((shard, units - count), BF)
+
+
+def pack(gate, up, down, parts, units):
+    shard = gate.shape[0]
+    return pl.pallas_call(
+        pack_kernel,
+        out_shape=jax.ShapeDtypeStruct((parts, shard, 3 * units), BF),
+        compiler_params=pltpu.CompilerParams(vmem_limit_bytes=VMEM_LIMIT),
+        name="pack",
+    )(gate, up, down)
+
+
+def finish_kernel(parts_ref, gate_ref, up_ref, down_ref):
+    parts, shard, units3 = parts_ref.shape
+    units = units3 // 3
+    have = gate_ref.shape[1]
+    for t in range(parts):
+        for j, ref in enumerate((gate_ref, up_ref, down_ref)):
+            first = min(t * units, have)
+            count = min((t + 1) * units, have) - first
+            if count:
+                ref[:, first : first + count] = parts_ref[t, :, j * units : j * units + count].astype(F32)
+
+
+def finish(parts, columns):
+    whole = jax.ShapeDtypeStruct((parts.shape[1], columns), F32)
+    return pl.pallas_call(
+        finish_kernel,
+        out_shape=[whole, whole, whole],
+        compiler_params=pltpu.CompilerParams(vmem_limit_bytes=VMEM_LIMIT),
+        name="finish",
+    )(parts)
 
 
 def inverse_rms(values):
@@ -376,7 +613,7 @@
     angles = places.astype(F32)[:, None] * freqs[None, :]
     cosine = jnp.cos(angles)
     sine = jnp.sin(angles) * jnp.where(lanes % HEAD < HEAD // 2, -1.0, 1.0)[None, :]
-    scal = jnp.concatenate([jnp.stack([c, core]).astype(jnp.int32), seq_lengths])
+    scal = jnp.concatenate([jnp.stack([c, core, f]).astype(jnp.int32), seq_lengths])
     own_places = places[:shard_rows]
     valid = own_places[None, :, None] < seq_lengths[:, None, None]
 
@@ -384,141 +621,185 @@
     inverse_one = inverse_rms(hidden)
     normed = (hidden * inverse_one * attn_gain).astype(BF)
 
+    def ctx_stack(pieces):
+        stack = jnp.zeros((n_ctx,) + pieces[0].shape, pieces[0].dtype)
+        for k, piece in enumerate(pieces):
+            stack = lax.dynamic_update_index_in_dim(stack, piece, (c - k) % n_ctx, 0)
+        return stack
+
+    def fsdp_stack(pieces):
+        stack = jnp.zeros((n_fsdp,) + pieces[0].shape, pieces[0].dtype)
+        for m, piece in enumerate(pieces):
+            stack = lax.dynamic_update_index_in_dim(stack, piece, f ^ m, 0)
+        return stack
+
+    def spread_halves(value):
+        masks = [1 << i for i in range(8) if 1 << i < n_fsdp]
+        halves = []
+        for half, order in zip(jnp.split(value, 2), (masks, masks[::-1])):
+            half = half[None]
+            for mask in order:
+                half = jnp.concatenate([half, fsdp_xor(half, mask)])
+            halves.append(half)
+        return halves
+
+    def in_order(half, order):
+        got = jnp.zeros_like(half)
+        for i in range(n_fsdp):
+            mask = sum(bit for j, bit in enumerate(order) if i >> j & 1)
+            got = lax.dynamic_update_index_in_dim(got, half[i], f ^ mask, 0)
+        return got
+
+    def over_ctx(value):
+        return [value] + [ctx_shift(value, k) for k in range(1, n_ctx)]
+
+    def over_fsdp(value):
+        return [value] + [fsdp_xor(value, m) for m in range(1, n_fsdp)]
+
+    def part(array, index):
+        return lax.dynamic_index_in_dim(array, index, 0, keepdims=False)
+
+    def trade_parts(parts):
+        return [part(parts, f)] + [fsdp_xor(part(parts, f ^ m), m) for m in range(1, n_fsdp)]
+
+    ffn_packed = pack(gate_weight, up_weight, down_weight.T, n_fsdp, padded)
     packed = jnp.concatenate([query_weight, key_projection, value_projection, out_weight.T], axis=1)
-    stack = jnp.zeros((n_ctx,) + packed.shape, BF)
-    stack = lax.dynamic_update_index_in_dim(stack, packed, c, 0)
-    for k in range(1, n_ctx):
-        stack = lax.dynamic_update_index_in_dim(stack, ctx_shift(packed, k), (c - k) % n_ctx, 0)
-    stack = stack.reshape(n_ctx * shard, -1)
-    full = jnp.zeros((n_fsdp,) + stack.shape, BF)
-    full = lax.dynamic_update_index_in_dim(full, stack, f, 0)
-    for m in range(1, n_fsdp):
-        full = lax.dynamic_update_index_in_dim(full, fsdp_xor(stack, m), f ^ m, 0)
-    attn_w = full.reshape(width, -1)
-    query_w = attn_w[:, :q_cols]
-    kv_w = attn_w[:, q_cols : q_cols + 2 * k_cols]
-    out_w = attn_w[:, q_cols + 2 * k_cols :]
-
-    def quarters(array):
-        array = array.reshape(shard, n_fsdp, units)
-        return jnp.pad(array, ((0, 0), (0, 0), (0, padded - units)))
-
-    ffn_packed = jnp.concatenate(
-        [quarters(gate_weight), quarters(up_weight), quarters(down_weight.T)], axis=2
-    ).transpose(1, 0, 2)
-    ffn_rows = jnp.zeros_like(ffn_packed)
-    ffn_rows = lax.dynamic_update_index_in_dim(
-        ffn_rows, lax.dynamic_index_in_dim(ffn_packed, f, 0, keepdims=False), f, 0
-    )
-    for m in range(1, n_fsdp):
-        piece = fsdp_xor(lax.dynamic_index_in_dim(ffn_packed, f ^ m, 0, keepdims=False), m)
-        ffn_rows = lax.dynamic_update_index_in_dim(ffn_rows, piece, f ^ m, 0)
+    grad_rows = jnp.where(valid, cotangent, jnp.zeros_like(cotangent))
+    x_pieces = [normed, ctx_up(normed)]
+    ffn_rows = lax.all_to_all(ffn_packed, "fsdp", 0, 0, tiled=True)
+    held = tie(*x_pieces, *over_ctx(packed))
+    x_pieces = list(held[:2])
+    stack = ctx_stack(held[2:]).reshape(n_ctx * shard, -1)
+
+    top, bottom = spread_halves(stack)
+    others = [swap_cores(piece) for piece in x_pieces]
+    while len(x_pieces) < n_ctx:
+        x_pieces.append(ctx_up(x_pieces[-1]))
+        if len(x_pieces) == n_ctx:
+            ffn_rows, x_pieces[-1] = tie(ffn_rows, x_pieces[-1])
+        others.append(swap_cores(x_pieces[-1]))
     ffn_w = lax.all_gather(ffn_rows, "ctx", axis=1, tiled=True).reshape(width, 3 * padded)
-
-    blocks = []
-    for r in range(n_ctx):
-        piece = ctx_up(normed, r) if r else normed
-        blocks.append(jnp.concatenate([piece, swap_cores(piece)], axis=1))
-    x_all = jnp.concatenate(blocks, axis=1)
-    x_own = blocks[0]
-
-    q_raw = jnp.einsum("std,dh->sth", x_own, query_w, preferred_element_type=F32)
-    k_raw = jnp.einsum("std,dh->sth", x_all, kv_w[:, :k_cols], preferred_element_type=F32)
-    value = jnp.einsum("std,dh->sth", x_all, kv_w[:, k_cols:], preferred_element_type=F32).astype(BF)
+    ffn_w = same(ffn_w, 20 << 30)
+    held = tie(*x_pieces, *others, grad_rows, top, bottom)
+    x_pieces = held[:n_ctx]
+    others = held[n_ctx : 2 * n_ctx]
+    grad_rows, top, bottom = held[2 * n_ctx :]
+
     query_gain2 = jnp.tile(query_gain, 2)[None, :]
     key_gain2 = jnp.tile(key_gain, 2)[None, :]
-    attn, stats, q_hat, k_hat = attend(scal, q_raw, k_raw, value, cosine, sine, query_gain2, key_gain2)
+    attn, stats, q_raw, k_raw, value, q_hat, k_hat, x_all = attend(
+        scal, [piece for pair in zip(x_pieces, others) for piece in pair], (top, bottom), (q_cols, k_cols), cosine, sine,
+        query_gain2, key_gain2,
+    )
+    held = tie(attn, *over_fsdp(grad_rows))
+    attn = held[0]
+    g_mine = jnp.stack(held[1:])
+    g_other = swap_cores(g_mine)
+    bits = [mask for mask in (1 << i for i in range(8)) if mask < n_fsdp]
+    attn_w = jnp.stack([in_order(top, bits), in_order(bottom, bits[::-1])], axis=1).reshape(width, -1)
+    out_w = attn_w[:, q_cols + 2 * k_cols :]
 
     branch = jnp.einsum("sth,dh->std", attn, out_w, preferred_element_type=F32)
     middle = hidden + (branch[:, :shard_rows] + swap_cores(branch[:, shard_rows:]))
     normed_two = (middle * inverse_rms(middle) * ffn_gain).astype(BF)
-    grad_rows = jnp.where(valid, cotangent, jnp.zeros_like(cotangent))
-
-    def gather_tokens(value):
-        pieces = jnp.stack([value] + [fsdp_xor(value, m) for m in range(1, n_fsdp)])
-        return jnp.concatenate([pieces, swap_cores(pieces)]).reshape(-1, width)
-
-    def scatter_tokens(value):
-        value = value.reshape(2, n_fsdp, slots, shard_rows, width)
-        mine = value[0].astype(F32) + swap_cores(value[1]).astype(F32)
-        total = mine[0]
-        for m in range(1, n_fsdp):
-            total = total + fsdp_xor(mine[m].astype(BF), m).astype(F32)
-        return total
-
-    y_part, dx_part, ffn_grads = feed_forward(gather_tokens(normed_two), gather_tokens(grad_rows), ffn_w, 2 * slots * shard_rows)
-    result = jnp.where(valid, middle + scatter_tokens(y_part), 0.0).astype(BF)
-    d_normed_two = scatter_tokens(dx_part)
-    d_middle = grad_rows.astype(F32) + norm_back(middle, ffn_gain, d_normed_two)
-
-    reduced = lax.psum_scatter(
+    x_mine = jnp.stack(over_fsdp(normed_two))
+    x_other = swap_cores(x_mine)
+
+    def flat(value):
+        return value.reshape(-1, width)
+
+    place = jnp.stack([f]).astype(jnp.int32)
+    y_mine, y_other, dx_mine, dx_other, ffn_grads, ffn_gain_row = feed_forward(
+        flat(x_mine), flat(x_other), flat(g_mine), flat(g_other), ffn_w, 2 * slots * shard_rows
+    )
+
+    ffn_reduced = lax.psum_scatter(
         ffn_grads.reshape(n_fsdp, n_ctx * shard, 3 * padded), "ctx", scatter_dimension=1, tiled=True
     )
-    ffn_out = jnp.zeros((n_fsdp,) + reduced.shape[1:], BF)
-    ffn_out = lax.dynamic_update_index_in_dim(
-        ffn_out, lax.dynamic_index_in_dim(reduced, f, 0, keepdims=False), f, 0
-    )
-    for m in range(1, n_fsdp):
-        piece = fsdp_xor(lax.dynamic_index_in_dim(reduced, f ^ m, 0, keepdims=False), m)
-        ffn_out = lax.dynamic_update_index_in_dim(ffn_out, piece, f ^ m, 0)
-    ffn_out = ffn_out.reshape(n_fsdp, shard, 3, padded)[..., :units].astype(F32)
-    ffn_out = ffn_out.transpose(2, 1, 0, 3).reshape(3, shard, ff_half)
-    gate_grad, up_grad = ffn_out[0], ffn_out[1]
-    down_grad = ffn_out[2].T
-
+
+    def core_sums(mine, other):
+        mine = mine.reshape(n_fsdp, slots, shard_rows, width)
+        other = swap_cores(other.reshape(n_fsdp, slots, shard_rows, width))
+        return [mine[m].astype(F32) + other[m].astype(F32) for m in range(n_fsdp)]
+
+    def traded(sums):
+        return [sums[0]] + [fsdp_xor(sums[m].astype(BF), m) for m in range(1, n_fsdp)]
+
+    held = tie(*traded(core_sums(dx_mine, dx_other)), *core_sums(y_mine, y_other))
+    d_normed_two = sum(item.astype(F32) for item in held[:n_fsdp])
+    y_sums = held[n_fsdp:]
+    d_middle = grad_rows.astype(F32) + norm_back(middle, ffn_gain, d_normed_two)
     d_branch = d_middle.astype(BF)
     d_branch = jnp.concatenate([d_branch, swap_cores(d_branch)], axis=1)
     d_attn = jnp.einsum("std,dh->sth", d_branch, out_w, preferred_element_type=F32).astype(BF)
-    out_w_grad = jnp.einsum("std,sth->dh", d_branch, attn, preferred_element_type=F32)
+    held = tie(d_attn, *y_sums)
+    d_attn = held[0]
+    y_sums = held[1:]
+
     d_q, d_k, d_v, gq, gk = attend_back(
         scal, q_raw, k_raw, value, cosine, sine, query_gain2, key_gain2, q_hat, k_hat, attn, stats, d_attn
     )
-    d_kv = jnp.concatenate([d_k, d_v], axis=2)
-    d_own = jnp.einsum("sth,dh->std", d_q, query_w, preferred_element_type=F32)
-    d_all = jnp.einsum("sth,dh->std", d_kv, kv_w, preferred_element_type=F32)
-    d_all = d_all.at[:, :rows].add(d_own).reshape(slots, n_ctx, 2, shard_rows, width)
-    mine = d_all[:, :, 0] + swap_cores(d_all[:, :, 1].astype(BF)).astype(F32)
-    total = mine[:, n_ctx - 1]
+    y_got = traded(y_sums)
+
+    held = tie(d_q, d_k, d_v, *y_got)
+    d_q, d_k, d_v = held[:3]
+    result = jnp.where(valid, middle + sum(item.astype(F32) for item in held[3:]), 0.0).astype(BF)
+
+    mine, other, attn_gain_row = input_grads(d_q, d_k, d_v, x_all, attn_w)
+    mine, other, d_q, d_k, d_v, ffn_reduced = tie(mine, other, d_q, d_k, d_v, ffn_reduced)
+    other = swap_cores(other)
+    gains = jnp.stack([attn_gain_row[0] / attn_gain, ffn_gain_row / ffn_gain])
+    heads = jnp.stack([jnp.pad(jnp.concatenate([item[0, :HEAD] + item[0, HEAD:]]), (0, HEAD)) for item in (gq, gk)])
+    small = jnp.concatenate([gains, heads], axis=1)
+    small = jnp.pad(small, ((0, 0), (0, 2 * q_cols + 2 * k_cols - small.shape[1])))
+    grads = weight_grads(place, x_all, d_q, d_k, d_v, d_branch, attn, two_parts(small), n_fsdp)
+
+    total = mine[n_ctx - 1] + other[n_ctx - 1].astype(F32)
     for r in range(n_ctx - 2, -1, -1):
-        total = mine[:, r] + ctx_down(total.astype(BF)).astype(F32)
+        total = ctx_down(total.astype(BF)).astype(F32)
+        if r == n_ctx - 2:
+            held = tie(total, ffn_reduced, *grads)
+            total, ffn_reduced = held[:2]
+            grads = held[2:]
+        total = mine[r] + other[r].astype(F32) + total
+    attn_pieces = [grads[0]] + [fsdp_xor(grads[m], m) for m in range(1, n_fsdp)]
+    ffn_parts = lax.all_to_all(ffn_reduced, "fsdp", 0, 0, tiled=True)
+    depth = n_ctx * shard
+    attn_part = sum(piece[:depth].astype(F32) for piece in attn_pieces)
+    small = tree_sum([one_part(piece[depth:]) for piece in attn_pieces])
+    total, attn_part, ffn_parts, small = tie(total, attn_part, ffn_parts, small)
+
+    sends = attn_part.reshape(n_ctx, shard, -1)
+    more = two_parts(small)
+    got = [part(sends, c)]
+    small = [one_part(more)]
+    for k in range(1, n_ctx):
+        piece = ctx_shift(jnp.concatenate([part(sends, (c + k) % n_ctx).astype(BF), more]), k)
+        got.append(piece[:shard].astype(F32))
+        small.append(one_part(piece[shard:]))
+    gate_grad, up_grad, down_grad = finish(ffn_parts, ff_half)
+    down_grad = down_grad.T
+    attn_grads = sum(got)
+    small = tree_sum(small)
+    small = small + swap_cores(small)
     input_grad = (d_middle + norm_back(hidden, attn_gain, total)).astype(BF)
-
-    q_grad = jnp.einsum("std,sth->dh", x_own, d_q, preferred_element_type=F32)
-    kv_grad = jnp.einsum("std,sth->dh", x_all, d_kv, preferred_element_type=F32)
-    attn_grads = jnp.concatenate([q_grad, kv_grad, out_w_grad], axis=1)
-    sends = attn_grads.astype(BF).reshape(n_fsdp, n_ctx * shard, -1)
-    total = lax.dynamic_index_in_dim(sends, f, 0, keepdims=False).astype(F32)
-    for m in range(1, n_fsdp):
-        total = total + fsdp_xor(lax.dynamic_index_in_dim(sends, f ^ m, 0, keepdims=False), m).astype(F32)
-    sends = total.reshape(n_ctx, shard, -1)
-    total = lax.dynamic_index_in_dim(sends, c, 0, keepdims=False)
-    sends = sends.astype(BF)
-    for k in range(1, n_ctx):
-        total = total + ctx_shift(lax.dynamic_index_in_dim(sends, (c + k) % n_ctx, 0, keepdims=False), k).astype(F32)
-    query_weight_grad = total[:, :q_cols]
-    key_weight_grad = total[:, q_cols : q_cols + k_cols]
-    value_weight_grad = total[:, q_cols + k_cols : q_cols + 2 * k_cols]
-    out_weight_grad = total[:, q_cols + 2 * k_cols :].T
-
-    attn_gain_part = jnp.sum(attn_w[:, : q_cols + 2 * k_cols].astype(F32) * attn_grads[:, : q_cols + 2 * k_cols], axis=1) / attn_gain
-    ffn_gain_part = (
-        jnp.sum(ffn_w[:, : 2 * padded].astype(F32) * ffn_grads[:, : 2 * padded].astype(F32), axis=1) / ffn_gain
-    )
-    small = jnp.concatenate(
-        [attn_gain_part, ffn_gain_part, gq[0, :HEAD] + gq[0, HEAD:], gk[0, :HEAD] + gk[0, HEAD:]]
-    )
-    small = sum_everywhere(small)
+    qkv_total = attn_grads[:, : q_cols + 2 * k_cols]
+    query_weight_grad = qkv_total[:, :q_cols]
+    key_weight_grad = qkv_total[:, q_cols : q_cols + k_cols]
+    value_weight_grad = qkv_total[:, q_cols + k_cols :]
+    out_weight_grad = attn_grads[:, q_cols + 2 * k_cols :].T
+
     return (
         result,
         input_grad,
-        small[:width],
-        small[2 * width : 2 * width + HEAD],
-        small[2 * width + HEAD :],
+        small[0, :width],
+        small[0, width : width + HEAD],
+        small[1, width : width + HEAD],
         query_weight_grad,
         key_weight_grad,
         value_weight_grad,
         out_weight_grad,
-        small[width : 2 * width],
+        small[1, :width],
         gate_grad,
         up_grad,
         down_grad,

time: 445 us -> 374 us (0.84)
  local copies, waits for them, and re-layouts: 64.2 us -> 10 us
  waiting for transfers between devices: 159 us -> 125 us
  Pallas kernels: 81.4 us -> 112 us
  matrix products: 27 us -> 3.47 us
  starting transfers between devices: 58.6 us -> 65.2 us
  other arithmetic: 32.8 us -> 39.2 us
    ppermute x24 -> x19, waiting for transfers between devices: 123 us -> 64.3 us  [fsdp_xor(): return lax.ppermute(value, 'fsdp', [(i, i ^ mask) for i in range(size)])]
    pallas_call x2 -> x7, Pallas kernels: 56 us -> 86.1 us  [the longest x1 39.2 us: feed_forward(): pl.pallas_call(ffn_kernel, grid=(2 * steps,), in_specs=[other, mine, othe...]
    dot_general x8 -> x0, matrix products: 22.4 us -> none  [the longest x1 4.9 us: body(): q_grad = jnp.einsum('std,sth->dh', x_own, d_q, preferred_element_type=F32)]
    all_gather x1, waiting for transfers between devices: 0.01 us -> 13.5 us  [body(): lax.all_gather(ffn_rows, 'ctx', axis=1, tiled=True)]
    unnamed x82 -> x50, local copies, waits for them, and re-layouts: 14.4 us -> 2.22 us
    ppermute x3, starting transfers between devices: 7.84 us -> 19.3 us  [ctx_up(): lax.ppermute(value, 'ctx', [(i, i + step) for i in range(size - step)])]
    dynamic_update_slice x14 -> x12, local copies, waits for them, and re-layouts: 10.8 us -> 0.35 us  [the longest x8 0.27 us: in_order(): got = lax.dynamic_update_index_in_dim(got, half[i], f ^ mask, 0)]
    ppermute x24 -> x19, starting transfers between devices: 31.3 us -> 22.2 us  [fsdp_xor(): return lax.ppermute(value, 'fsdp', [(i, i ^ mask) for i in range(size)])]
  transfers between devices with their start and end apart: 54 -> 47, of which waited for: 23 -> 20; matrix products, arithmetic and copies ran while one was open for 23% -> 11% of each run, Pallas kernels for 10% -> 20%
where the time goes in v2:
time: 374 us; the launch traced here: 370 us
  waiting for transfers between devices  125 us (33%)
  Pallas kernels  112 us (30%)
  starting transfers between devices  65.2 us (17%)
  other arithmetic  39.2 us (10%)
  between operations  14.9 us (4%)
  local copies, waits for them, and re-layouts  10 us (3%)
    ppermute x19, waiting for transfers between devices, fsdp_xor(): return lax.ppermute(value, 'fsdp', [(i, i ^ mask) for i in range(size)])  64.3 us
    pallas_call x1, Pallas kernels, feed_forward(): pl.pallas_call(ffn_kernel, grid=(2 * steps,), in_specs=[other, mine, othe...  39.2 us
    pallas_call x1, Pallas kernels, attend_back(): pl.pallas_call(attend_back_kernel, grid=(slots, pairs), in_specs=[smem, q...  25.5 us
    pallas_call x1, Pallas kernels, attend(): pl.pallas_call(functools.partial(attend_kernel, len(pieces), parts), grid...  24.1 us
    ppermute x19, starting transfers between devices, fsdp_xor(): return lax.ppermute(value, 'fsdp', [(i, i ^ mask) for i in range(size)])  22.2 us
    ppermute x3, starting transfers between devices, ctx_up(): lax.ppermute(value, 'ctx', [(i, i + step) for i in range(size - step)])  19.3 us
    ppermute x6, waiting for transfers between devices, ctx_shift(): lax.ppermute(value, 'ctx', [(i, (i + step) % size) for i in range(size)])  16.4 us
    ppermute x3, waiting for transfers between devices, ctx_down(): lax.ppermute(value, 'ctx', [(i + step, i) for i in range(size - step)])  13.9 us
  transfers between devices with their start and end apart: 47, of which 20 were waited for; matrix products, arithmetic and copies ran while one was open for 11% of the time, Pallas kernels for 20%

profile of v2, /device:TPU:0, one launch (start us, length us, event | category | flops | bytes accessed | tf_op | source)
XLA Modules:
  0.0 369.7 jit_solution(682423767638546092)
XLA Ops:
  7.2 1.2 fusion.9
  8.4 1.2 fusion.3.refs_0_
  9.7 5.7 %collective-permute-start = (bf16[2,128,1024]{2,1,0:T(8,128)(2,1)S(1)}, bf16[2,128,1024]{2,1,0:T(8,128)(2,1)}, u32[]{:S(2)}, u32[]{:S(2)}) collective-permute-start(bf16[2,128,1024]{2,1,0:T(8,128)(2,1)S(1)} %fusion.3.refs_0_), channel_id=1, source_target_pairs={{0,2},{2,4},{4,6},{1,3},{3,5},{5,7},{8,10},{10,12},{12,14},{9,11},... | collective-permute-start | bytes 1572872 | tf_op jit(solution)/shard_map/ppermute | solution.py:43
  18.3 2.8 collective-permute-start.3
  21.1 2.2 pack.1
  23.3 3.7 %all-to-all-start = ((bf16[4,64,1920]{2,1,0:T(8,128)(2,1)}), bf16[4,64,1920]{2,1,0:T(8,128)(2,1)S(1)}, u32[]{:S(2)}, u32[]{:S(2)}) async-start(bf16[4,64,1920]{2,1,0:T(8,128)(2,1)} %pack.1), calls=%async_computation | async-start | bytes 1966080 | tf_op jit(solution)/shard_map/all_to_all | solution.py:669
  27.0 4.1 %collective-permute-done.1 = bf16[64,1536]{1,0:T(8,128)(2,1)S(1)} collective-permute-done((bf16[64,1536]{1,0:T(8,128)(2,1)S(1)}, bf16[64,1536]{1,0:T(8,128)(2,1)S(1)}, u32[]{:S(2)}, u32[]{:S(2)}) %collective-permute-start.1) | collective-permute-done | bytes 196640 | tf_op jit(solution)/shard_map/ppermute | solution.py:53
  31.1 4.3 %collective-permute-done.2 = bf16[64,1536]{1,0:T(8,128)(2,1)S(1)} collective-permute-done((bf16[64,1536]{1,0:T(8,128)(2,1)S(1)}, bf16[64,1536]{1,0:T(8,128)(2,1)S(1)}, u32[]{:S(2)}, u32[]{:S(2)}) %collective-permute-start.2) | collective-permute-done | bytes 196640 | tf_op jit(solution)/shard_map/ppermute | solution.py:53
  35.4 3.1 collective-permute-done.3
  38.7 1.6 collective-permute-start.12
  40.3 1.6 collective-permute-start.10
  42.0 8.4 %collective-permute-start.4 = (bf16[2,128,1024]{2,1,0:T(8,128)(2,1)}, bf16[2,128,1024]{2,1,0:T(8,128)(2,1)}, u32[]{:S(2)}, u32[]{:S(2)}) collective-permute-start(bf16[2,128,1024]{2,1,0:T(8,128)(2,1)} %collective-permute-done.refs_2_), channel_id=1, source_target_pairs={{0,2},{2,4},{4,6},{1,3},{3,5},{5,7},{8,10},{10,12},{12,14},{9,11},... | collective-permute-start | bytes 1572872 | tf_op jit(solution)/shard_map/ppermute | solution.py:43
  53.8 5.9 %collective-permute-done.4.refs_4_ = bf16[2,128,1024]{2,1,0:T(8,128)(2,1)} collective-permute-done((bf16[2,128,1024]{2,1,0:T(8,128)(2,1)}, bf16[2,128,1024]{2,1,0:T(8,128)(2,1)}, u32[]{:S(2)}, u32[]{:S(2)}) %collective-permute-start.4) | collective-permute-done | bytes 524320 | tf_op jit(solution)/shard_map/ppermute | solution.py:43
  59.6 5.2 %collective-permute-start.5 = (bf16[2,128,1024]{2,1,0:T(8,128)(2,1)}, bf16[2,128,1024]{2,1,0:T(8,128)(2,1)}, u32[]{:S(2)}, u32[]{:S(2)}) collective-permute-start(bf16[2,128,1024]{2,1,0:T(8,128)(2,1)} %collective-permute-done.4.refs_4_), channel_id=1, source_target_pairs={{0,2},{2,4},{4,6},{1,3},{3,5},{5,7},{8,10},{10,12},{12,14},{9,11},... | collective-permute-start | bytes 1572872 | tf_op jit(solution)/shard_map/ppermute | solution.py:43
  66.6 1.1 broadcast_select_fusion
  67.8 3.1 fusion.16
  71.4 1.8 collective-permute-done.5.refs_6_
  74.8 1.3 pad_maximum_fusion.4.refs_11_.refs_12_.refs_13_
  76.2 1.8 pad_maximum_fusion.3.refs_8_.refs_9_.refs_10_
  79.2 2.4 collective-permute-start.16
  82.2 24.1 %attend.1 = (bf16[2,256,512]{2,1,0:T(8,128)(2,1)}, f32[2,2,8,256]{3,2,1,0:T(8,128)}, f32[2,256,512]{2,1,0:T(8,128)}, f32[2,1024,256]{2,1,0:T(8,128)}, bf16[2,102...) custom-call(s32[5]{0:T(128)} %pad_add_fusion.scal_ref, ...), custom_call_target="tpu_custom_call" | custom-call | flops 1048576 | bytes 1048576 | tf_op jit(solution)/shard_map/attend/pallas_call | solution.py:266
  108.3 2.6 collective-permute-done.17
  112.3 2.7 collective-permute-start.20
  115.0 1.6 pad_maximum_fusion.2
  116.8 9.5 %collective-permute-done.18 = bf16[2,128,1024]{2,1,0:T(8,128)(2,1)S(1)} collective-permute-done((bf16[2,128,1024]{2,1,0:T(8,128)(2,1)S(1)}, bf16[2,128,1024]{2,1,0:T(8,128)(2,1)S(1)}, u32[]{:S(2)}, u32[]{:S(2)}) %collective-permute-start.18) | collective-permute-done | bytes 524320 | tf_op jit(solution)/shard_map/ppermute | solution.py:38
  126.3 10.7 %collective-permute-done.19 = bf16[2,128,1024]{2,1,0:T(8,128)(2,1)S(1)} collective-permute-done((bf16[2,128,1024]{2,1,0:T(8,128)(2,1)S(1)}, bf16[2,128,1024]{2,1,0:T(8,128)(2,1)S(1)}, u32[]{:S(2)}, u32[]{:S(2)}) %collective-permute-start.19) | collective-permute-done | bytes 524320 | tf_op jit(solution)/shard_map/ppermute | solution.py:38
  137.0 1.6 pad_maximum_fusion.1
  138.5 13.5 %all-gather.2.cloned.1.call-done = bf16[4,256,1920]{2,1,0:T(8,128)(2,1)} async-done(((bf16[4,64,1920]{2,1,0:T(8,128)(2,1)}), bf16[4,256,1920]{2,1,0:T(8,128)(2,1)}) %all-gather.2.cloned.1.call-update) | async-done | bytes 3932176 | tf_op jit(solution)/shard_map/all_gather | solution.py:681
  152.0 39.2 %feed_forward.1 = (bf16[1024,1024]{1,0:T(8,128)(2,1)}, bf16[1024,1024]{1,0:T(8,128)(2,1)}, bf16[1024,1024]{1,0:T(8,128)(2,1)}, bf16[1024,1024]{1,0:T(8,128)(2,1)...) custom-call(bf16[1024,1024]{1,0:T(8,128)(2,1)} %bitcast.25.xo_ref, bf16[1024,1024]{1,0:T(8,128)(2,1)} %bitcast.26.xm_ref, ...), custom_call_target="tpu_custom_call" | custom-call | flops 24159191040 | bytes 25165824 | tf_op jit(solution)/shard_map/feed_forward/pallas_call | solution.py:486
  191.9 1.8 fusion.53
  194.3 1.5 collective-permute-done.23
  196.7 1.5 collective-permute-start.24
  198.3 1.5 collective-permute-start.25
  200.3 1.2 convert_add_fusion.5
  202.2 9.4 %collective-permute-done.24 = bf16[2,128,1024]{2,1,0:T(8,128)(2,1)S(1)} collective-permute-done((bf16[2,128,1024]{2,1,0:T(8,128)(2,1)S(1)}, bf16[2,128,1024]{2,1,0:T(8,128)(2,1)S(1)}, u32[]{:S(2)}, u32[]{:S(2)}) %collective-permute-start.24) | collective-permute-done | bytes 524320 | tf_op jit(solution)/shard_map/ppermute | solution.py:38
  211.6 11.6 %collective-permute-done.25 = bf16[2,128,1024]{2,1,0:T(8,128)(2,1)S(1)} collective-permute-done((bf16[2,128,1024]{2,1,0:T(8,128)(2,1)S(1)}, bf16[2,128,1024]{2,1,0:T(8,128)(2,1)S(1)}, u32[]{:S(2)}, u32[]{:S(2)}) %collective-permute-start.25) | collective-permute-done | bytes 524320 | tf_op jit(solution)/shard_map/ppermute | solution.py:38
  224.0 1.9 collective-permute-done.28
  225.9 2.7 convolution_convert_fusion.d_ref
  228.7 1.2 collective-permute-start.29
  230.7 1.5 collective-permute-start.31
  232.2 25.5 %attend_back.1 = (bf16[2,256,512]{2,1,0:T(8,128)(2,1)}, bf16[2,1024,256]{2,1,0:T(8,128)(2,1)}, bf16[2,1024,256]{2,1,0:T(8,128)(2,1)}, f32[1,128]{1,0:T(1,128)}, f32[1,128]{1,0:T(1,128)}) custom-call(s32[5]{0:T(128)} %pad_add_fusion.scal_ref, f32[2,256,512]{2,1,0:T(8,128)} %get-tuple-element.122.q_ref, f32[2,1024,256]{2,1,0:T(8,128)} %get-tuple-element.123.k_ref, ...), custom_call_target="tpu_custom_call" | custom-call | flops 5368709120 | bytes 12582912 | tf_op jit(solution)/shard_map/attend_back/pallas_call | solution.py:297
  257.7 9.4 %input_grads.1 = (f32[4,2,128,1024]{3,2,1,0:T(8,128)}, bf16[4,2,128,1024]{3,2,1,0:T(8,128)(2,1)}, f32[1,1024]{1,0:T(1,128)}) custom-call(bf16[2,256,512]{2,1,0:T(8,128)(2,1)} %get-tuple-element.167.dq_ref, bf16[2,1024,256]{2,1,0:T(8,128)(2,1)} %get-tuple-element.168.dk_ref, bf16[2,1024,256]{2,1,0:T(8,128)(2,1)} %get-tuple-element.169.dv_ref, ...), custom_call_target="tpu_custom_call" | custom-call | flops 3221225472 | bytes 12582912 | tf_op jit(solution)/shard_map/input_grads/pallas_call | solution.py:405
  268.6 3.0 collective-permute-done.32
  271.6 2.1 fusion.17
  273.8 1.3 collective-permute-start.33
  275.7 8.7 %weight_grads.1 = (bf16[272,1536]{1,0:T(8,128)(2,1)}, bf16[272,1536]{1,0:T(8,128)(2,1)}, bf16[272,1536]{1,0:T(8,128)(2,1)}, bf16[272,1536]{1,0:T(8,128)(2,1)}) custom-call(s32[1]{0:T(128)} %bitcast.2.at_ref, bf16[2,1024,1024]{2,1,0:T(8,128)(2,1)} %get-tuple-element.160.x_ref, bf16[2,256,512]{2,1,0:T(8,128)(2,1)} %get-tuple-element.167.dq_ref, ...), custom_call_target="tpu_custom_call" | custom-call | flops 4294967296 | bytes 8388608 | tf_op jit(solution)/shard_map/weight_grads/pallas_call | solution.py:361
  284.4 5.2 %collective-permute-done.33 = bf16[2,128,1024]{2,1,0:T(8,128)(2,1)S(1)} collective-permute-done((bf16[2,128,1024]{2,1,0:T(8,128)(2,1)S(1)}, bf16[2,128,1024]{2,1,0:T(8,128)(2,1)S(1)}, u32[]{:S(2)}, u32[]{:S(2)}) %collective-permute-start.33) | collective-permute-done | bytes 524320 | tf_op jit(solution)/shard_map/ppermute | solution.py:48
  289.7 1.2 collective-permute-start.36
  291.8 1.4 collective-permute-start.38
  293.3 2.3 fusion.13
  295.6 1.3 collective-permute-start.34
  296.9 4.4 %all-to-all-start.1 = ((bf16[4,64,1920]{2,1,0:T(8,128)(2,1)}), bf16[4,64,1920]{2,1,0:T(8,128)(2,1)}, u32[]{:S(2)}, u32[]{:S(2)}) async-start(bf16[4,64,1920]{2,1,0:T(8,128)(2,1)} %reduce-scatter.2.cloned.1.call-done), calls=%async_computation.2 | async-start | bytes 1966080 | tf_op jit(solution)/shard_map/all_to_all | solution.py:766
  301.3 8.7 %collective-permute-done.34 = bf16[2,128,1024]{2,1,0:T(8,128)(2,1)S(1)} collective-permute-done((bf16[2,128,1024]{2,1,0:T(8,128)(2,1)}, bf16[2,128,1024]{2,1,0:T(8,128)(2,1)S(1)}, u32[]{:S(2)}, u32[]{:S(2)}) %collective-permute-start.34) | collective-permute-done | bytes 524320 | tf_op jit(solution)/shard_map/ppermute | solution.py:48
  310.0 1.6 fusion.14
  311.6 1.3 collective-permute-start.35
  312.9 23.1 %collective-permute-done.37 = bf16[272,1536]{1,0:T(8,128)(2,1)} collective-permute-done((bf16[272,1536]{1,0:T(8,128)(2,1)}, bf16[272,1536]{1,0:T(8,128)(2,1)}, u32[]{:S(2)}, u32[]{:S(2)}) %collective-permute-start.37) | collective-permute-done | bytes 835616 | tf_op jit(solution)/shard_map/ppermute | solution.py:38
  336.0 3.1 convert_add_fusion
  340.0 1.6 bitcast_add_fusion.2
  341.6 1.3 fusion.20
  343.0 1.1 collective-permute-start.39
  344.1 3.8 %collective-permute-start.41 = (bf16[80,1536]{1,0:T(8,128)(2,1)S(1)}, bf16[80,1536]{1,0:T(8,128)(2,1)S(1)}, u32[]{:S(2)}, u32[]{:S(2)}) collective-permute-start(bf16[80,1536]{1,0:T(8,128)(2,1)S(1)} %get-tuple-element.225), channel_id=1, source_target_pairs={{0,6},{2,0},{4,2},{6,4},{1,7},{3,1},{5,3},{7,5},{8,14},{10,8},{12,... | collective-permute-start | bytes 737288 | tf_op jit(solution)/shard_map/ppermute | solution.py:53
  347.9 2.4 finish.1
  350.7 3.0 fusion.8
  353.7 4.5 %collective-permute-done.39 = bf16[80,1536]{1,0:T(8,128)(2,1)S(1)} collective-permute-done((bf16[80,1536]{1,0:T(8,128)(2,1)S(1)}, bf16[80,1536]{1,0:T(8,128)(2,1)S(1)}, u32[]{:S(2)}, u32[]{:S(2)}) %collective-permute-start.39) | collective-permute-done | bytes 245792 | tf_op jit(solution)/shard_map/ppermute | solution.py:53
  (173 shorter events, 29.5 us)
Async XLA Ops:
  9.7 61.2 %copy-start.8 = (bf16[2,128,1024]{2,1,0:T(8,128)(2,1)}, bf16[2,128,1024]{2,1,0:T(8,128)(2,1)S(1)}, u32[]{:S(2)}) copy-start(bf16[2,128,1024]{2,1,0:T(8,128)(2,1)S(1)} %fusion.3.refs_0_) | copy-start | bytes 1572868
  9.7 28.8 %collective-permute-start = (bf16[2,128,1024]{2,1,0:T(8,128)(2,1)S(1)}, bf16[2,128,1024]{2,1,0:T(8,128)(2,1)}, u32[]{:S(2)}, u32[]{:S(2)}) collective-permute-start(bf16[2,128,1024]{2,1,0:T(8,128)(2,1)S(1)} %fusion.3.refs_0_), channel_id=1, source_target_pairs={{0,2},{2,4},{4,6},{1,3},{3,5},{5,7},{8,10},{10,12},{12,14},{9,11},... | collective-permute-start | bytes 1572872 | tf_op jit(solution)/shard_map/ppermute | solution.py:43
  16.3 14.8 %collective-permute-start.1 = (bf16[64,1536]{1,0:T(8,128)(2,1)S(1)}, bf16[64,1536]{1,0:T(8,128)(2,1)S(1)}, u32[]{:S(2)}, u32[]{:S(2)}) collective-permute-start(bf16[64,1536]{1,0:T(8,128)(2,1)S(1)} %pad_maximum_fusion.11), channel_id=1, source_target_pairs={{0,2},{2,4},{4,6},{6,0},{1,3},{3,5},{5,7},{7,1},{8,10},{10,12},{12... | collective-permute-start | bytes 589832 | tf_op jit(solution)/shard_map/ppermute | solution.py:53
  17.2 18.2 %collective-permute-start.2 = (bf16[64,1536]{1,0:T(8,128)(2,1)S(1)}, bf16[64,1536]{1,0:T(8,128)(2,1)S(1)}, u32[]{:S(2)}, u32[]{:S(2)}) collective-permute-start(bf16[64,1536]{1,0:T(8,128)(2,1)S(1)} %pad_maximum_fusion.11), channel_id=1, source_target_pairs={{0,4},{2,6},{4,0},{6,2},{1,5},{3,7},{5,1},{7,3},{8,12},{10,14},{12... | collective-permute-start | bytes 589832 | tf_op jit(solution)/shard_map/ppermute | solution.py:53
  18.3 20.2 %collective-permute-start.3 = (bf16[64,1536]{1,0:T(8,128)(2,1)S(1)}, bf16[64,1536]{1,0:T(8,128)(2,1)S(1)}, u32[]{:S(2)}, u32[]{:S(2)}) collective-permute-start(bf16[64,1536]{1,0:T(8,128)(2,1)S(1)} %pad_maximum_fusion.11), channel_id=1, source_target_pairs={{0,6},{2,0},{4,2},{6,4},{1,7},{3,1},{5,3},{7,5},{8,14},{10,8},{12,... | collective-permute-start | bytes 589832 | tf_op jit(solution)/shard_map/ppermute | solution.py:53
  23.3 49.9 %all-to-all-start = ((bf16[4,64,1920]{2,1,0:T(8,128)(2,1)}), bf16[4,64,1920]{2,1,0:T(8,128)(2,1)S(1)}, u32[]{:S(2)}, u32[]{:S(2)}) async-start(bf16[4,64,1920]{2,1,0:T(8,128)(2,1)} %pack.1), calls=%async_computation | async-start | bytes 1966080 | tf_op jit(solution)/shard_map/all_to_all | solution.py:669
  27.0 14.9 %copy-start.20 = (s32[2]{0:T(128)S(1)}, s32[2]{0:T(128)}, u32[]{:S(2)}) copy-start(s32[2]{0:T(128)} %param.15) | copy-start | bytes 28
  27.0 125.0 %all-gather.2.cloned.1.call-start = ((), (), s32[]{:S(2)}) async-start(), calls=%async_computation.3 | async-start | bytes 4915200 | tf_op jit(solution)/shard_map/all_gather | solution.py:681
  38.6 26.8 %copy-start.21 = (f32[64]{0:T(128)S(1)}, f32[64]{0:T(128)}, u32[]{:S(2)}) copy-start(f32[64]{0:T(128)} %param.17) | copy-start | bytes 772
  38.6 27.4 %copy-start.22 = (f32[64]{0:T(128)S(1)}, f32[64]{0:T(128)}, u32[]{:S(2)}) copy-start(f32[64]{0:T(128)} %param.18) | copy-start | bytes 772
  38.7 11.7 %collective-permute-start.12 = (bf16[1,128,1536]{2,1,0:T(8,128)(2,1)S(1)}, bf16[1,128,1536]{2,1,0:T(8,128)(2,1)S(1)}, u32[]{:S(2)}, u32[]{:S(2)}) collective-permute-start(bf16[1,128,1536]{2,1,0:T(8,128)(2,1)S(1)} %bitcast.166), channel_id=1, source_target_pairs={{0,16},{8,24},{16,0},{24,8},{1,17},{9,25},{17,1},{25,9},{2,18},{10... | collective-permute-start | bytes 1179656 | tf_op jit(solution)/shard_map/ppermute | solution.py:38
  40.3 11.6 %collective-permute-start.10 = (bf16[1,128,1536]{2,1,0:T(8,128)(2,1)S(1)}, bf16[1,128,1536]{2,1,0:T(8,128)(2,1)S(1)}, u32[]{:S(2)}, u32[]{:S(2)}) collective-permute-start(bf16[1,128,1536]{2,1,0:T(8,128)(2,1)S(1)} %bitcast.163), channel_id=1, source_target_pairs={{0,8},{8,0},{16,24},{24,16},{1,9},{9,1},{17,25},{25,17},{2,10},{10... | collective-permute-start | bytes 1179656 | tf_op jit(solution)/shard_map/ppermute | solution.py:38
  42.0 17.7 %collective-permute-start.4 = (bf16[2,128,1024]{2,1,0:T(8,128)(2,1)}, bf16[2,128,1024]{2,1,0:T(8,128)(2,1)}, u32[]{:S(2)}, u32[]{:S(2)}) collective-permute-start(bf16[2,128,1024]{2,1,0:T(8,128)(2,1)} %collective-permute-done.refs_2_), channel_id=1, source_target_pairs={{0,2},{2,4},{4,6},{1,3},{3,5},{5,7},{8,10},{10,12},{12,14},{9,11},... | collective-permute-start | bytes 1572872 | tf_op jit(solution)/shard_map/ppermute | solution.py:43
  51.4 22.9 %collective-permute-start.13 = (bf16[2,128,1536]{2,1,0:T(8,128)(2,1)}, bf16[2,128,1536]{2,1,0:T(8,128)(2,1)}, u32[]{:S(2)}, u32[]{:S(2)}) collective-permute-start(bf16[2,128,1536]{2,1,0:T(8,128)(2,1)} %pad_maximum_fusion.7), channel_id=1, source_target_pairs={{0,8},{8,0},{16,24},{24,16},{1,9},{9,1},{17,25},{25,17},{2,10},{10... | collective-permute-start | bytes 2359304 | tf_op jit(solution)/shard_map/ppermute | solution.py:38
  51.9 14.7 %copy-start.11 = (bf16[1,128,1536]{2,1,0:T(8,128)(2,1)}, bf16[1,128,1536]{2,1,0:T(8,128)(2,1)S(1)}, u32[]{:S(2)}) copy-start(bf16[1,128,1536]{2,1,0:T(8,128)(2,1)S(1)} %collective-permute-done.10) | copy-start | bytes 1179652
  52.9 23.2 %collective-permute-start.11 = (bf16[2,128,1536]{2,1,0:T(8,128)(2,1)}, bf16[2,128,1536]{2,1,0:T(8,128)(2,1)}, u32[]{:S(2)}, u32[]{:S(2)}) collective-permute-start(bf16[2,128,1536]{2,1,0:T(8,128)(2,1)} %pad_maximum_fusion.6), channel_id=1, source_target_pairs={{0,16},{8,24},{16,0},{24,8},{1,17},{9,25},{17,1},{25,9},{2,18},{10... | collective-permute-start | bytes 2359304 | tf_op jit(solution)/shard_map/ppermute | solution.py:38
  59.6 13.5 %collective-permute-start.5 = (bf16[2,128,1024]{2,1,0:T(8,128)(2,1)}, bf16[2,128,1024]{2,1,0:T(8,128)(2,1)}, u32[]{:S(2)}, u32[]{:S(2)}) collective-permute-start(bf16[2,128,1024]{2,1,0:T(8,128)(2,1)} %collective-permute-done.4.refs_4_), channel_id=1, source_target_pairs={{0,2},{2,4},{4,6},{1,3},{3,5},{5,7},{8,10},{10,12},{12,14},{9,11},... | collective-permute-start | bytes 1572872 | tf_op jit(solution)/shard_map/ppermute | solution.py:43
  70.9 7.2 %collective-permute-start.7 = (bf16[2,128,1024]{2,1,0:T(8,128)(2,1)}, bf16[2,128,1024]{2,1,0:T(8,128)(2,1)}, u32[]{:S(2)}, u32[]{:S(2)}) collective-permute-start(bf16[2,128,1024]{2,1,0:T(8,128)(2,1)} %collective-permute-done.refs_2_), channel_id=1, source_target_pairs={{0,1},{1,0},{2,3},{3,2},{4,5},{5,4},{6,7},{7,6},{8,9},{9,8},{10,11... | collective-permute-start | bytes 1572872 | tf_op jit(solution)/shard_map/ppermute | solution.py:33
  70.9 7.2 %collective-permute-start.6 = (bf16[2,128,1024]{2,1,0:T(8,128)(2,1)S(1)}, bf16[2,128,1024]{2,1,0:T(8,128)(2,1)}, u32[]{:S(2)}, u32[]{:S(2)}) collective-permute-start(bf16[2,128,1024]{2,1,0:T(8,128)(2,1)S(1)} %fusion.3.refs_0_), channel_id=1, source_target_pairs={{0,1},{1,0},{2,3},{3,2},{4,5},{5,4},{6,7},{7,6},{8,9},{9,8},{10,11... | collective-permute-start | bytes 1572872 | tf_op jit(solution)/shard_map/ppermute | solution.py:33
  73.2 4.9 %collective-permute-start.8 = (bf16[2,128,1024]{2,1,0:T(8,128)(2,1)}, bf16[2,128,1024]{2,1,0:T(8,128)(2,1)}, u32[]{:S(2)}, u32[]{:S(2)}) collective-permute-start(bf16[2,128,1024]{2,1,0:T(8,128)(2,1)} %collective-permute-done.4.refs_4_), channel_id=1, source_target_pairs={{0,1},{1,0},{2,3},{3,2},{4,5},{5,4},{6,7},{7,6},{8,9},{9,8},{10,11... | collective-permute-start | bytes 1572872 | tf_op jit(solution)/shard_map/ppermute | solution.py:33
  74.2 193.0 %reduce-scatter.2.cloned.1.call-start = ((), (), s32[]{:S(2)}) async-start(), calls=%async_computation.4 | async-start | bytes 4915200 | tf_op jit(solution)/shard_map/reduce_scatter | solution.py:716
  74.3 3.8 %collective-permute-start.9 = (bf16[2,128,1024]{2,1,0:T(8,128)(2,1)}, bf16[2,128,1024]{2,1,0:T(8,128)(2,1)S(1)}, u32[]{:S(2)}, u32[]{:S(2)}) collective-permute-start(bf16[2,128,1024]{2,1,0:T(8,128)(2,1)} %collective-permute-done.5.refs_6_), channel_id=1, source_target_pairs={{0,1},{1,0},{2,3},{3,2},{4,5},{5,4},{6,7},{7,6},{8,9},{9,8},{10,11... | collective-permute-start | bytes 1572872 | tf_op jit(solution)/shard_map/ppermute | solution.py:33
  76.1 6.1 %copy-start = (bf16[4,128,1536]{2,1,0:T(8,128)(2,1)}, bf16[4,128,1536]{2,1,0:T(8,128)(2,1)S(1)}, u32[]{:S(2)}) copy-start(bf16[4,128,1536]{2,1,0:T(8,128)(2,1)S(1)} %pad_maximum_fusion.4.refs_11_.refs_12_.refs_13_) | copy-start | bytes 4718596
  78.0 4.1 %copy-start.1 = (bf16[4,128,1536]{2,1,0:T(8,128)(2,1)}, bf16[4,128,1536]{2,1,0:T(8,128)(2,1)S(1)}, u32[]{:S(2)}) copy-start(bf16[4,128,1536]{2,1,0:T(8,128)(2,1)S(1)} %pad_maximum_fusion.3.refs_8_.refs_9_.refs_10_) | copy-start | bytes 4718596
  78.1 3.9 %copy-start.15 = (bf16[2,128,1024]{2,1,0:T(8,128)(2,1)}, bf16[2,128,1024]{2,1,0:T(8,128)(2,1)S(1)}, u32[]{:S(2)}) copy-start(bf16[2,128,1024]{2,1,0:T(8,128)(2,1)S(1)} %collective-permute-done.9.refs_7_) | copy-start | bytes 1572868
  78.1 28.6 %collective-permute-start.14 = (bf16[2,128,1024]{2,1,0:T(8,128)(2,1)S(1)}, bf16[2,128,1024]{2,1,0:T(8,128)(2,1)S(1)}, u32[]{:S(2)}, u32[]{:S(2)}) collective-permute-start(bf16[2,128,1024]{2,1,0:T(8,128)(2,1)S(1)} %broadcast_select_fusion), channel_id=1, source_target_pairs={{0,8},{8,0},{16,24},{24,16},{1,9},{9,1},{17,25},{25,17},{2,10},{10... | collective-permute-start | bytes 1572872 | tf_op jit(solution)/shard_map/ppermute | solution.py:38
  78.7 28.0 %collective-permute-start.15 = (bf16[2,128,1024]{2,1,0:T(8,128)(2,1)S(1)}, bf16[2,128,1024]{2,1,0:T(8,128)(2,1)S(1)}, u32[]{:S(2)}, u32[]{:S(2)}) collective-permute-start(bf16[2,128,1024]{2,1,0:T(8,128)(2,1)S(1)} %broadcast_select_fusion), channel_id=1, source_target_pairs={{0,16},{8,24},{16,0},{24,8},{1,17},{9,25},{17,1},{25,9},{2,18},{10... | collective-permute-start | bytes 1572872 | tf_op jit(solution)/shard_map/ppermute | solution.py:38
  79.2 27.5 %collective-permute-start.16 = (bf16[2,128,1024]{2,1,0:T(8,128)(2,1)S(1)}, bf16[2,128,1024]{2,1,0:T(8,128)(2,1)S(1)}, u32[]{:S(2)}, u32[]{:S(2)}) collective-permute-start(bf16[2,128,1024]{2,1,0:T(8,128)(2,1)S(1)} %broadcast_select_fusion), channel_id=1, source_target_pairs={{0,24},{8,16},{16,8},{24,0},{1,25},{9,17},{17,9},{25,1},{2,26},{10... | collective-permute-start | bytes 1572872 | tf_op jit(solution)/shard_map/ppermute | solution.py:38
  107.4 3.6 copy-start.2
  108.3 2.7 collective-permute-start.17
  111.4 14.8 %collective-permute-start.18 = (bf16[2,128,1024]{2,1,0:T(8,128)(2,1)S(1)}, bf16[2,128,1024]{2,1,0:T(8,128)(2,1)S(1)}, u32[]{:S(2)}, u32[]{:S(2)}) collective-permute-start(bf16[2,128,1024]{2,1,0:T(8,128)(2,1)S(1)} %multiply_convert_fusion), channel_id=1, source_target_pairs={{0,8},{8,0},{16,24},{24,16},{1,9},{9,1},{17,25},{25,17},{2,10},{10... | collective-permute-start | bytes 1572872 | tf_op jit(solution)/shard_map/ppermute | solution.py:38
  112.0 24.9 %collective-permute-start.19 = (bf16[2,128,1024]{2,1,0:T(8,128)(2,1)S(1)}, bf16[2,128,1024]{2,1,0:T(8,128)(2,1)S(1)}, u32[]{:S(2)}, u32[]{:S(2)}) collective-permute-start(bf16[2,128,1024]{2,1,0:T(8,128)(2,1)S(1)} %multiply_convert_fusion), channel_id=1, source_target_pairs={{0,16},{8,24},{16,0},{24,8},{1,17},{9,25},{17,1},{25,9},{2,18},{10... | collective-permute-start | bytes 1572872 | tf_op jit(solution)/shard_map/ppermute | solution.py:38
  112.3 24.7 %collective-permute-start.20 = (bf16[2,128,1024]{2,1,0:T(8,128)(2,1)S(1)}, bf16[2,128,1024]{2,1,0:T(8,128)(2,1)S(1)}, u32[]{:S(2)}, u32[]{:S(2)}) collective-permute-start(bf16[2,128,1024]{2,1,0:T(8,128)(2,1)S(1)} %multiply_convert_fusion), channel_id=1, source_target_pairs={{0,24},{8,16},{16,8},{24,0},{1,25},{9,17},{17,9},{25,1},{2,26},{10... | collective-permute-start | bytes 1572872 | tf_op jit(solution)/shard_map/ppermute | solution.py:38
  116.6 35.4 %collective-permute-start.22 = (bf16[4,2,128,1024]{3,2,1,0:T(8,128)(2,1)}, bf16[4,2,128,1024]{3,2,1,0:T(8,128)(2,1)}, u32[]{:S(2)}, u32[]{:S(2)}) collective-permute-start(bf16[4,2,128,1024]{3,2,1,0:T(8,128)(2,1)} %pad_maximum_fusion.2), channel_id=1, source_target_pairs={{0,1},{1,0},{2,3},{3,2},{4,5},{5,4},{6,7},{7,6},{8,9},{9,8},{10,11... | collective-permute-start | bytes 6291464 | tf_op jit(solution)/shard_map/ppermute | solution.py:33
  138.5 13.5 %collective-permute-start.21 = (bf16[4,2,128,1024]{3,2,1,0:T(8,128)(2,1)}, bf16[4,2,128,1024]{3,2,1,0:T(8,128)(2,1)}, u32[]{:S(2)}, u32[]{:S(2)}) collective-permute-start(bf16[4,2,128,1024]{3,2,1,0:T(8,128)(2,1)} %pad_maximum_fusion.1), channel_id=1, source_target_pairs={{0,1},{1,0},{2,3},{3,2},{4,5},{5,4},{6,7},{7,6},{8,9},{9,8},{10,11... | collective-permute-start | bytes 6291464 | tf_op jit(solution)/shard_map/ppermute | solution.py:33
  191.3 4.4 %collective-permute-start.23 = (bf16[4,2,128,1024]{3,2,1,0:T(8,128)(2,1)}, bf16[4,2,128,1024]{3,2,1,0:T(8,128)(2,1)S(1)}, u32[]{:S(2)}, u32[]{:S(2)}) collective-permute-start(bf16[4,2,128,1024]{3,2,1,0:T(8,128)(2,1)} %bitcast.193), channel_id=1, source_target_pairs={{0,1},{1,0},{2,3},{3,2},{4,5},{5,4},{6,7},{7,6},{8,9},{9,8},{10,11... | collective-permute-start | bytes 6291464 | tf_op jit(solution)/shard_map/ppermute | solution.py:33
  191.4 8.9 %collective-permute-start.27 = (bf16[4,2,128,1024]{3,2,1,0:T(8,128)(2,1)}, bf16[4,2,128,1024]{3,2,1,0:T(8,128)(2,1)S(1)}, u32[]{:S(2)}, u32[]{:S(2)}) collective-permute-start(bf16[4,2,128,1024]{3,2,1,0:T(8,128)(2,1)} %bitcast.192), channel_id=1, source_target_pairs={{0,1},{1,0},{2,3},{3,2},{4,5},{5,4},{6,7},{7,6},{8,9},{9,8},{10,11... | collective-permute-start | bytes 6291464 | tf_op jit(solution)/shard_map/ppermute | solution.py:33
  196.7 14.8 %collective-permute-start.24 = (bf16[2,128,1024]{2,1,0:T(8,128)(2,1)S(1)}, bf16[2,128,1024]{2,1,0:T(8,128)(2,1)S(1)}, u32[]{:S(2)}, u32[]{:S(2)}) collective-permute-start(bf16[2,128,1024]{2,1,0:T(8,128)(2,1)S(1)} %get-tuple-element.206), channel_id=1, source_target_pairs={{0,8},{8,0},{16,24},{24,16},{1,9},{9,1},{17,25},{25,17},{2,10},{10... | collective-permute-start | bytes 1572872 | tf_op jit(solution)/shard_map/ppermute | solution.py:38
  198.3 24.9 %collective-permute-start.25 = (bf16[2,128,1024]{2,1,0:T(8,128)(2,1)S(1)}, bf16[2,128,1024]{2,1,0:T(8,128)(2,1)S(1)}, u32[]{:S(2)}, u32[]{:S(2)}) collective-permute-start(bf16[2,128,1024]{2,1,0:T(8,128)(2,1)S(1)} %get-tuple-element.205), channel_id=1, source_target_pairs={{0,16},{8,24},{16,0},{24,8},{1,17},{9,25},{17,1},{25,9},{2,18},{10... | collective-permute-start | bytes 1572872 | tf_op jit(solution)/shard_map/ppermute | solution.py:38
  199.7 23.4 %collective-permute-start.26 = (bf16[2,128,1024]{2,1,0:T(8,128)(2,1)S(1)}, bf16[2,128,1024]{2,1,0:T(8,128)(2,1)S(1)}, u32[]{:S(2)}, u32[]{:S(2)}) collective-permute-start(bf16[2,128,1024]{2,1,0:T(8,128)(2,1)S(1)} %get-tuple-element.204), channel_id=1, source_target_pairs={{0,24},{8,16},{16,8},{24,0},{1,25},{9,17},{17,9},{25,1},{2,26},{10... | collective-permute-start | bytes 1572872 | tf_op jit(solution)/shard_map/ppermute | solution.py:38
  223.6 5.0 %copy-start.3 = (f32[2,128,1024]{2,1,0:T(8,128)}, f32[2,128,1024]{2,1,0:T(8,128)S(1)}, u32[]{:S(2)}) copy-start(f32[2,128,1024]{2,1,0:T(8,128)S(1)} %get-tuple-element.194) | copy-start | bytes 3145732
  224.0 2.0 collective-permute-start.28
  228.7 29.0 %collective-permute-start.29 = (bf16[2,128,1024]{2,1,0:T(8,128)(2,1)S(1)}, bf16[2,128,1024]{2,1,0:T(8,128)(2,1)}, u32[]{:S(2)}, u32[]{:S(2)}) collective-permute-start(bf16[2,128,1024]{2,1,0:T(8,128)(2,1)S(1)} %get-tuple-element.150), channel_id=1, source_target_pairs={{0,8},{8,0},{16,24},{24,16},{1,9},{9,1},{17,25},{25,17},{2,10},{10... | collective-permute-start | bytes 1572872 | tf_op jit(solution)/shard_map/ppermute | solution.py:38
  229.9 27.8 %collective-permute-start.30 = (bf16[2,128,1024]{2,1,0:T(8,128)(2,1)S(1)}, bf16[2,128,1024]{2,1,0:T(8,128)(2,1)}, u32[]{:S(2)}, u32[]{:S(2)}) collective-permute-start(bf16[2,128,1024]{2,1,0:T(8,128)(2,1)S(1)} %get-tuple-element.151), channel_id=1, source_target_pairs={{0,16},{8,24},{16,0},{24,8},{1,17},{9,25},{17,1},{25,9},{2,18},{10... | collective-permute-start | bytes 1572872 | tf_op jit(solution)/shard_map/ppermute | solution.py:38
  230.7 27.0 %collective-permute-start.31 = (bf16[2,128,1024]{2,1,0:T(8,128)(2,1)S(1)}, bf16[2,128,1024]{2,1,0:T(8,128)(2,1)}, u32[]{:S(2)}, u32[]{:S(2)}) collective-permute-start(bf16[2,128,1024]{2,1,0:T(8,128)(2,1)S(1)} %get-tuple-element.152), channel_id=1, source_target_pairs={{0,24},{8,16},{16,8},{24,0},{1,25},{9,17},{17,9},{25,1},{2,26},{10... | collective-permute-start | bytes 1572872 | tf_op jit(solution)/shard_map/ppermute | solution.py:38
  257.7 9.6 %copy-start.18 = (f32[1,1024]{1,0:T(1,128)S(1)}, f32[1,1024]{1,0:T(1,128)}, u32[]{:S(2)}) copy-start(f32[1,1024]{1,0:T(1,128)} %get-tuple-element.171) | copy-start | bytes 12292
  257.7 9.6 %copy-start.24 = (f32[1,128]{1,0:T(1,128)S(1)}, f32[1,128]{1,0:T(1,128)}, u32[]{:S(2)}) copy-start(f32[1,128]{1,0:T(1,128)} %get-tuple-element.173) | copy-start | bytes 1540
  257.7 9.7 %copy-start.23 = (f32[1,128]{1,0:T(1,128)S(1)}, f32[1,128]{1,0:T(1,128)}, u32[]{:S(2)}) copy-start(f32[1,128]{1,0:T(1,128)} %get-tuple-element.172) | copy-start | bytes 1540
  267.2 4.4 %collective-permute-start.32 = (bf16[4,2,128,1024]{3,2,1,0:T(8,128)(2,1)}, bf16[4,2,128,1024]{3,2,1,0:T(8,128)(2,1)S(1)}, u32[]{:S(2)}, u32[]{:S(2)}) collective-permute-start(bf16[4,2,128,1024]{3,2,1,0:T(8,128)(2,1)} %get-tuple-element.165), channel_id=1, source_target_pairs={{0,1},{1,0},{2,3},{3,2},{4,5},{5,4},{6,7},{7,6},{8,9},{9,8},{10,11... | collective-permute-start | bytes 6291464 | tf_op jit(solution)/shard_map/ppermute | solution.py:33
  271.6 21.7 %copy-start.10 = (bf16[4,2,128,1024]{3,2,1,0:T(8,128)(2,1)}, bf16[4,2,128,1024]{3,2,1,0:T(8,128)(2,1)S(1)}, u32[]{:S(2)}) copy-start(bf16[4,2,128,1024]{3,2,1,0:T(8,128)(2,1)S(1)} %collective-permute-done.32) | copy-start | bytes 6291460
  273.8 15.9 %collective-permute-start.33 = (bf16[2,128,1024]{2,1,0:T(8,128)(2,1)S(1)}, bf16[2,128,1024]{2,1,0:T(8,128)(2,1)S(1)}, u32[]{:S(2)}, u32[]{:S(2)}) collective-permute-start(bf16[2,128,1024]{2,1,0:T(8,128)(2,1)S(1)} %fusion.17), channel_id=1, source_target_pairs={{2,0},{4,2},{6,4},{3,1},{5,3},{7,5},{10,8},{12,10},{14,12},{11,9},... | collective-permute-start | bytes 1572872 | tf_op jit(solution)/shard_map/ppermute | solution.py:48
  289.7 23.1 %collective-permute-start.36 = (bf16[272,1536]{1,0:T(8,128)(2,1)}, bf16[272,1536]{1,0:T(8,128)(2,1)}, u32[]{:S(2)}, u32[]{:S(2)}) collective-permute-start(bf16[272,1536]{1,0:T(8,128)(2,1)} %get-tuple-element.180), channel_id=1, source_target_pairs={{0,8},{8,0},{16,24},{24,16},{1,9},{9,1},{17,25},{25,17},{2,10},{10... | collective-permute-start | bytes 2506760 | tf_op jit(solution)/shard_map/ppermute | solution.py:38
  290.9 45.0 %collective-permute-start.37 = (bf16[272,1536]{1,0:T(8,128)(2,1)}, bf16[272,1536]{1,0:T(8,128)(2,1)}, u32[]{:S(2)}, u32[]{:S(2)}) collective-permute-start(bf16[272,1536]{1,0:T(8,128)(2,1)} %get-tuple-element.181), channel_id=1, source_target_pairs={{0,16},{8,24},{16,0},{24,8},{1,17},{9,25},{17,1},{25,9},{2,18},{10... | collective-permute-start | bytes 2506760 | tf_op jit(solution)/shard_map/ppermute | solution.py:38
  291.8 44.1 %collective-permute-start.38 = (bf16[272,1536]{1,0:T(8,128)(2,1)}, bf16[272,1536]{1,0:T(8,128)(2,1)}, u32[]{:S(2)}, u32[]{:S(2)}) collective-permute-start(bf16[272,1536]{1,0:T(8,128)(2,1)} %get-tuple-element.182), channel_id=1, source_target_pairs={{0,24},{8,16},{16,8},{24,0},{1,25},{9,17},{17,9},{25,1},{2,26},{10... | collective-permute-start | bytes 2506760 | tf_op jit(solution)/shard_map/ppermute | solution.py:38
  295.6 14.4 %collective-permute-start.34 = (bf16[2,128,1024]{2,1,0:T(8,128)(2,1)}, bf16[2,128,1024]{2,1,0:T(8,128)(2,1)S(1)}, u32[]{:S(2)}, u32[]{:S(2)}) collective-permute-start(bf16[2,128,1024]{2,1,0:T(8,128)(2,1)} %fusion.13), channel_id=1, source_target_pairs={{2,0},{4,2},{6,4},{3,1},{5,3},{7,5},{10,8},{12,10},{14,12},{11,9},... | collective-permute-start | bytes 1572872 | tf_op jit(solution)/shard_map/ppermute | solution.py:48
  296.9 39.1 %copy-start.13 = (bf16[272,1536]{1,0:T(8,128)(2,1)S(1)}, bf16[272,1536]{1,0:T(8,128)(2,1)}, u32[]{:S(2)}) copy-start(bf16[272,1536]{1,0:T(8,128)(2,1)} %get-tuple-element.179) | copy-start | bytes 2506756
  296.9 44.6 %all-to-all-start.1 = ((bf16[4,64,1920]{2,1,0:T(8,128)(2,1)}), bf16[4,64,1920]{2,1,0:T(8,128)(2,1)}, u32[]{:S(2)}, u32[]{:S(2)}) async-start(bf16[4,64,1920]{2,1,0:T(8,128)(2,1)} %reduce-scatter.2.cloned.1.call-done), calls=%async_computation.2 | async-start | bytes 1966080 | tf_op jit(solution)/shard_map/all_to_all | solution.py:766
  311.6 28.4 %collective-permute-start.35 = (bf16[2,128,1024]{2,1,0:T(8,128)(2,1)S(1)}, bf16[2,128,1024]{2,1,0:T(8,128)(2,1)S(1)}, u32[]{:S(2)}, u32[]{:S(2)}) collective-permute-start(bf16[2,128,1024]{2,1,0:T(8,128)(2,1)S(1)} %fusion.14), channel_id=1, source_target_pairs={{2,0},{4,2},{6,4},{3,1},{5,3},{7,5},{10,8},{12,10},{14,12},{11,9},... | collective-permute-start | bytes 1572872 | tf_op jit(solution)/shard_map/ppermute | solution.py:48
  342.9 7.8 %copy-start.4 = (f32[2,128,1024]{2,1,0:T(8,128)S(1)}, f32[2,128,1024]{2,1,0:T(8,128)}, u32[]{:S(2)}) copy-start(f32[2,128,1024]{2,1,0:T(8,128)} %copy-done.3) | copy-start | bytes 3145732
  342.9 7.8 %copy-start.6 = (f32[2,128,1024]{2,1,0:T(8,128)S(1)}, f32[2,128,1024]{2,1,0:T(8,128)}, u32[]{:S(2)}) copy-start(f32[2,128,1024]{2,1,0:T(8,128)} %convert_add_fusion.5) | copy-start | bytes 3145732
  343.0 15.2 %collective-permute-start.39 = (bf16[80,1536]{1,0:T(8,128)(2,1)S(1)}, bf16[80,1536]{1,0:T(8,128)(2,1)S(1)}, u32[]{:S(2)}, u32[]{:S(2)}) collective-permute-start(bf16[80,1536]{1,0:T(8,128)(2,1)S(1)} %get-tuple-element.223), channel_id=1, source_target_pairs={{0,4},{2,6},{4,0},{6,2},{1,5},{3,7},{5,1},{7,3},{8,12},{10,14},{12... | collective-permute-start | bytes 737288 | tf_op jit(solution)/shard_map/ppermute | solution.py:53
  344.1 14.1 %collective-permute-start.40 = (bf16[80,1536]{1,0:T(8,128)(2,1)S(1)}, bf16[80,1536]{1,0:T(8,128)(2,1)S(1)}, u32[]{:S(2)}, u32[]{:S(2)}) collective-permute-start(bf16[80,1536]{1,0:T(8,128)(2,1)S(1)} %get-tuple-element.224), channel_id=1, source_target_pairs={{0,2},{2,4},{4,6},{6,0},{1,3},{3,5},{5,7},{7,1},{8,10},{10,12},{12... | collective-permute-start | bytes 737288 | tf_op jit(solution)/shard_map/ppermute | solution.py:53
  344.1 14.5 %collective-permute-start.41 = (bf16[80,1536]{1,0:T(8,128)(2,1)S(1)}, bf16[80,1536]{1,0:T(8,128)(2,1)S(1)}, u32[]{:S(2)}, u32[]{:S(2)}) collective-permute-start(bf16[80,1536]{1,0:T(8,128)(2,1)S(1)} %get-tuple-element.225), channel_id=1, source_target_pairs={{0,6},{2,0},{4,2},{6,4},{1,7},{3,1},{5,3},{7,5},{8,14},{10,8},{12,... | collective-permute-start | bytes 737288 | tf_op jit(solution)/shard_map/ppermute | solution.py:53
  360.5 1.2 collective-permute-start.42
  (8 other events, 13.7 us)
Sparse Core Ops, SparseCore 0:
  74.3 77.6 all-gather.1
  191.4 71.2 reduce-scatter.1

commit v3 on v2

--- a/solution.py
+++ b/solution.py
@@ -18,6 +18,8 @@
 BF = jnp.bfloat16
 F32 = jnp.float32
 VMEM_LIMIT = 56 * 1024 * 1024
+LATE = 12 << 30
+LATER = 5 << 30
 
 
 def dot(left, right, dims):
@@ -309,122 +311,236 @@
         scratch_shapes=[pltpu.VMEM((keys, rows), F32)],
         compiler_params=pltpu.CompilerParams(vmem_limit_bytes=VMEM_LIMIT),
         cost_estimate=pl.CostEstimate(
-            flops=20 * slots * rows * keys * width, bytes_accessed=12 << 20, transcendentals=slots * rows * keys * width // HEAD
+            flops=24 << 30, bytes_accessed=12 << 20, transcendentals=0
         ),
         name="attend_back",
     )(scal, q_raw, k_raw, value, cosine, sine, query_gain, key_gain, q_hat, k_hat, out, stats, grad)
 
 
-def weight_kernel(at_ref, x_ref, dq_ref, dk_ref, dv_ref, b_ref, o_ref, more_ref, *out_refs):
+def bits_of(size):
+    return [1 << i for i in range(8) if 1 << i < size]
+
+
+def weight_kernel(parts, at_ref, x_ref, dq_ref, dk_ref, dv_ref, b_ref, o_ref, w_ref, gain_ref, more_ref, *refs):
+    top_send, top_keep, low_send, low_keep, sum_ref = refs
     slots, rows, q_cols = dq_ref.shape
     k_cols = dk_ref.shape[2]
-    total = jnp.zeros((x_ref.shape[2], q_cols), F32)
-    key_total = jnp.zeros((x_ref.shape[2], k_cols), F32)
-    value_total = jnp.zeros((x_ref.shape[2], k_cols), F32)
-    out_total = jnp.zeros((x_ref.shape[2], q_cols), F32)
+    depth = x_ref.shape[2]
+    half = depth // 2
+    m = pl.program_id(0)
+    query = jnp.zeros((depth, q_cols), F32)
+    key = jnp.zeros((depth, k_cols), F32)
+    value = jnp.zeros((depth, k_cols), F32)
+    out = jnp.zeros((depth, q_cols), F32)
     for s in range(slots):
-        out_total = out_total + dot(b_ref[s], o_ref[s], TN)
         x = x_ref[s]
-        total = total + dot(x[:rows], dq_ref[s], TN)
-        key_total = key_total + dot(x, dk_ref[s], TN)
-        value_total = value_total + dot(x, dv_ref[s], TN)
-    depth = x_ref.shape[2]
-    for m, ref in enumerate(out_refs):
-
-        @pl.when(pl.program_id(0) == m)
-        def _(ref=ref):
-            ref[:depth, :q_cols] = total.astype(BF)
-            ref[:depth, q_cols : q_cols + k_cols] = key_total.astype(BF)
-            ref[:depth, q_cols + k_cols : q_cols + 2 * k_cols] = value_total.astype(BF)
-            ref[:depth, q_cols + 2 * k_cols :] = out_total.astype(BF)
-            ref[depth:] = more_ref[...]
-
-
-def weight_grads(at, x, d_q, d_k, d_v, d_branch, attn, more, parts):
+        query = query + dot(x[:rows], dq_ref[s], TN)
+        key = key + dot(x, dk_ref[s], TN)
+        value = value + dot(x, dv_ref[s], TN)
+        out = out + dot(b_ref[s], o_ref[s], TN)
+    total = jnp.concatenate([query, key, value, out], axis=1)
+    product = total[:, : q_cols + 2 * k_cols] * w_ref[:, : q_cols + 2 * k_cols].astype(F32)
+    ones = jnp.ones((8, q_cols + 2 * k_cols), BF)
+    high = product.astype(BF)
+    low = (product - high.astype(F32)).astype(BF)
+    place = pl.ds(pl.multiple_of((at_ref[0] ^ m) * depth, TILE), depth)
+    sum_ref[:, place] = dot(ones, high, NT) + dot(ones, low, NT)
+    total = total.astype(BF)
+    bits = bits_of(parts)
+    for bit, rows_of, send, keep in (
+        (bits[0], total[:half], top_send, top_keep),
+        (bits[-1], total[half:], low_send, low_keep),
+    ):
+        chosen = [i for i in range(parts) if i & bit]
+        for i in range(parts):
+            ref = send if i & bit else keep
+            rank = chosen.index(i | bit)
+
+            @pl.when(m == i)
+            def _(ref=ref, rank=rank, rows_of=rows_of):
+                ref[rank * half : (rank + 1) * half] = rows_of
+
+    @pl.when(m == parts - 1)
+    def _():
+        width = sum_ref.shape[1]
+        row = sum_ref[:1] / gain_ref[...]
+        first = row.astype(BF).astype(F32)
+        left = row - first
+        ids = lax.broadcasted_iota(jnp.int32, (16, width), 0)
+        more = more_ref[...].astype(F32)
+        here = jnp.where(ids == 0, first, jnp.where(ids == 2, left, more[:, :width]))
+        top_send[parts // 2 * half :, :width] = here.astype(BF)
+        top_send[parts // 2 * half :, width:] = more_ref[:, width:]
+
+
+def weight_grads(at, x, d_q, d_k, d_v, d_branch, attn, w, gain, more, parts):
     slots, keys, width = x.shape
     cols = 2 * d_q.shape[2] + 2 * d_k.shape[2]
-    depth = width // parts + more.shape[0]
+    depth = width // parts
+    shapes = [(width // 4 + more.shape[0], cols), (width // 4, cols), (width // 4, cols), (width // 4, cols)]
     spec = pltpu.PrefetchScalarGridSpec(
         num_scalar_prefetch=1,
         grid=(parts,),
         in_specs=[
-            pl.BlockSpec((slots, keys, width // parts), lambda m, at: (0, 0, at[0] ^ m)),
+            pl.BlockSpec((slots, keys, depth), lambda m, at: (0, 0, at[0] ^ m)),
             pl.BlockSpec(d_q.shape, lambda m, at: (0, 0, 0)),
             pl.BlockSpec(d_k.shape, lambda m, at: (0, 0, 0)),
             pl.BlockSpec(d_v.shape, lambda m, at: (0, 0, 0)),
-            pl.BlockSpec(d_branch.shape[:2] + (width // parts,), lambda m, at: (0, 0, at[0] ^ m)),
+            pl.BlockSpec(d_branch.shape[:2] + (depth,), lambda m, at: (0, 0, at[0] ^ m)),
             pl.BlockSpec(attn.shape, lambda m, at: (0, 0, 0)),
+            pl.BlockSpec((depth, cols), lambda m, at: (at[0] ^ m, 0)),
+            pl.BlockSpec(gain.shape, lambda m, at: (0, 0)),
             pl.BlockSpec(more.shape, lambda m, at: (0, 0)),
         ],
-        out_specs=[pl.BlockSpec((depth, cols), lambda m, at: (0, 0))] * parts,
+        out_specs=[pl.BlockSpec(shape, lambda m, at: (0, 0)) for shape in shapes],
+        scratch_shapes=[pltpu.VMEM((8, width), F32)],
     )
     return pl.pallas_call(
-        weight_kernel,
+        functools.partial(weight_kernel, parts),
         grid_spec=spec,
-        out_shape=[jax.ShapeDtypeStruct((depth, cols), BF)] * parts,
+        out_shape=[jax.ShapeDtypeStruct(shape, BF) for shape in shapes],
         compiler_params=pltpu.CompilerParams(vmem_limit_bytes=VMEM_LIMIT),
-        cost_estimate=pl.CostEstimate(flops=4 << 30, bytes_accessed=8 << 20, transcendentals=0),
+        cost_estimate=pl.CostEstimate(flops=10 << 30, bytes_accessed=8 << 20, transcendentals=0),
         name="weight_grads",
-    )(at, x, d_q, d_k, d_v, d_branch, attn, more)
-
-
-def input_kernel(dq_ref, dk_ref, dv_ref, x_ref, w_ref, mine_ref, other_ref, gain_ref):
+    )(at, x, d_q, d_k, d_v, d_branch, attn, w, gain, more)
+
+
+def input_kernel(with_own, dq_ref, dk_ref, dv_ref, w_ref, mine_ref, other_ref):
     slots, rows, q_cols = dq_ref.shape
     k_cols = dk_ref.shape[2]
     half = rows // 2
-    gain = jnp.zeros((1, x_ref.shape[2]), F32)
     for s in range(slots):
         d_x = dot(dk_ref[s], w_ref[:, q_cols : q_cols + k_cols], NT)
         d_x = d_x + dot(dv_ref[s], w_ref[:, q_cols + k_cols : q_cols + 2 * k_cols], NT)
-        gain = gain + jnp.sum(d_x * x_ref[s].astype(F32), axis=0, keepdims=True)
         mine_ref[0, s] = d_x[:half]
         other_ref[0, s] = d_x[half:].astype(BF)
 
-    @pl.when(pl.program_id(0) == 0)
-    def _():
-        more = jnp.zeros_like(gain)
+    @pl.when(with_own & (pl.program_id(0) == 0))
+    def _():
         for s in range(slots):
             d_x = dot(dq_ref[s], w_ref[:, :q_cols], NT)
-            more = more + jnp.sum(d_x * x_ref[s].astype(F32), axis=0, keepdims=True)
             mine_ref[0, s] += d_x[:half]
             other_ref[0, s] = (other_ref[0, s].astype(F32) + d_x[half:]).astype(BF)
-        gain_ref[...] = gain + more
-
-    @pl.when(pl.program_id(0) > 0)
-    def _():
-        gain_ref[...] += gain
-
-
-def input_grads(d_q, d_k, d_v, x, w):
+
+
+def input_grads(d_q, d_k, d_v, w, first, blocks):
     slots, rows, q_cols = d_q.shape
-    keys, k_cols = d_k.shape[1:]
+    k_cols = d_k.shape[2]
     width = w.shape[0]
-    blocks = keys // rows
-    part = pl.BlockSpec((slots, rows, k_cols), lambda r: (0, r, 0))
+    part = pl.BlockSpec((slots, rows, k_cols), lambda r: (0, r + first, 0))
     out = pl.BlockSpec((1, slots, rows // 2, width), lambda r: (r, 0, 0, 0))
     return pl.pallas_call(
-        input_kernel,
+        functools.partial(input_kernel, first == 0),
         grid=(blocks,),
         in_specs=[
             pl.BlockSpec(d_q.shape, lambda r: (0, 0, 0)),
             part,
             part,
-            pl.BlockSpec((slots, rows, width), lambda r: (0, r, 0)),
             pl.BlockSpec(w.shape, lambda r: (0, 0)),
         ],
-        out_specs=[out, out, pl.BlockSpec((1, width), lambda r: (0, 0))],
+        out_specs=[out, out],
         out_shape=[
             jax.ShapeDtypeStruct((blocks, slots, rows // 2, width), F32),
             jax.ShapeDtypeStruct((blocks, slots, rows // 2, width), BF),
-            jax.ShapeDtypeStruct((1, width), F32),
         ],
         compiler_params=pltpu.CompilerParams(vmem_limit_bytes=VMEM_LIMIT),
-        cost_estimate=pl.CostEstimate(flops=3 << 30, bytes_accessed=12 << 20, transcendentals=0),
+        cost_estimate=pl.CostEstimate(flops=6 << 30, bytes_accessed=1 << 20, transcendentals=0),
         name="input_grads",
-    )(d_q, d_k, d_v, x, w)
-
-
-def ffn_kernel(xo_ref, xm_ref, go_ref, gm_ref, w_ref, yo_ref, ym_ref, do_ref, dm_ref, grad_ref, gain_ref, sum_ref):
+    )(d_q, d_k, d_v, w)
+
+
+def in_parts(rows):
+    first = rows.astype(BF).astype(F32)
+    return jnp.concatenate([first, rows - first, jnp.zeros((12, rows.shape[1]), F32)]).astype(BF)
+
+
+def down_kernel(*refs):
+    mine_ref, other_ref, *came, out_ref = refs
+    total = mine_ref[0] + other_ref[0].astype(F32)
+    if came:
+        total = total + came[0][...].astype(F32)
+    out_ref[...] = total.astype(BF)
+
+
+def down_add(mine, other, block, *came):
+    shape = mine.shape[1:]
+    one = pl.BlockSpec((1, 1) + shape[1:], lambda s: (block, s, 0, 0))
+    here = pl.BlockSpec((1,) + shape[1:], lambda s: (s, 0, 0))
+    return pl.pallas_call(
+        down_kernel,
+        grid=(shape[0],),
+        in_specs=[one, one] + [here] * len(came),
+        out_specs=here,
+        out_shape=jax.ShapeDtypeStruct(shape, BF),
+        cost_estimate=pl.CostEstimate(flops=LATER, bytes_accessed=0, transcendentals=0),
+        name="down_add",
+    )(mine, other, *came)
+
+
+def half_kernel(half, sends, keeps, extra, keep_ref, came_ref, *refs):
+    own_ref = refs[0] if extra else None
+    send_ref, left_ref = refs[-2:]
+    for ranks, ref in ((sends, send_ref), (keeps, left_ref)):
+        for place, i in enumerate(ranks):
+            rows = slice(i * half, (i + 1) * half)
+            total = keep_ref[rows].astype(F32) + came_ref[rows].astype(F32)
+            ref[place * half : (place + 1) * half] = total.astype(BF)
+    if extra:
+        ours, theirs = own_ref[...].astype(F32), came_ref[-16:].astype(F32)
+        send_ref[len(sends) * half :] = in_parts((ours[:2] + ours[2:4]) + (theirs[:2] + theirs[2:4]))
+
+
+def half_sum(keep, came, own, half, sends, keeps):
+    cols = keep.shape[1]
+    riding = 0 if own is None else 16
+    return pl.pallas_call(
+        functools.partial(half_kernel, half, sends, keeps, own is not None),
+        out_shape=[
+            jax.ShapeDtypeStruct((len(sends) * half + riding, cols), BF),
+            jax.ShapeDtypeStruct((len(keeps) * half, cols), BF),
+        ],
+        compiler_params=pltpu.CompilerParams(vmem_limit_bytes=VMEM_LIMIT),
+        cost_estimate=pl.CostEstimate(flops=LATE, bytes_accessed=0, transcendentals=0),
+        name="half_sum",
+    )(keep, came, *(() if own is None else (own,)))
+
+
+def ctx_kernel(parts, at_ref, top_ref, top_came, low_ref, low_came, own_ref, mine_ref, small_ref, *refs):
+    *sends, sum_ref = refs
+    half = top_ref.shape[0]
+    shard = mine_ref.shape[0]
+    sum_ref[:half] = top_ref[...].astype(F32) + top_came[:half].astype(F32)
+    sum_ref[half:] = low_ref[...].astype(F32) + low_came[...].astype(F32)
+    ours, theirs = own_ref[...].astype(F32), top_came[half:].astype(F32)
+    small = in_parts((ours[:2] + ours[2:4]) + (theirs[:2] + theirs[2:4]))
+    small_ref[...] = small
+
+    def rows(k):
+        return sum_ref[pl.ds(pl.multiple_of(((at_ref[1] + k) % parts) * shard, 8), shard)]
+
+    mine_ref[...] = rows(0)
+    for k, ref in enumerate(sends, 1):
+        ref[:shard] = rows(k).astype(BF)
+        ref[shard:] = small
+
+
+def to_ctx(at, top, top_came, low, low_came, own, parts):
+    half, cols = top.shape
+    shard = 2 * half // parts
+    vmem = pl.BlockSpec(memory_space=pltpu.VMEM)
+    message = jax.ShapeDtypeStruct((shard + 16, cols), BF)
+    return pl.pallas_call(
+        functools.partial(ctx_kernel, parts),
+        in_specs=[pl.BlockSpec(memory_space=pltpu.SMEM)] + [vmem] * 5,
+        out_shape=[jax.ShapeDtypeStruct((shard, cols), F32), jax.ShapeDtypeStruct((16, cols), BF)] + [message] * (parts - 1),
+        scratch_shapes=[pltpu.VMEM((2 * half, cols), F32)],
+        compiler_params=pltpu.CompilerParams(vmem_limit_bytes=VMEM_LIMIT),
+        cost_estimate=pl.CostEstimate(flops=LATE, bytes_accessed=0, transcendentals=0),
+        name="to_ctx",
+    )(at, top, top_came, low, low_came, own)
+
+
+def ffn_kernel(xo_ref, xm_ref, go_ref, gm_ref, w_ref, yo_ref, ym_ref, do_ref, dm_ref, inner_ref, gain_ref):
     units = w_ref.shape[1] // 3
     step = pl.program_id(0)
     early = step < pl.num_programs(0) // 2
@@ -440,8 +556,10 @@
     d_act = dot(g, w_ref[:, 2 * units :], NN)
     d_gate = (d_act * upper * (sig + silu * (1.0 - sig))).astype(BF)
     d_up = (d_act * silu).astype(BF)
-    both = jnp.concatenate([d_gate, d_up], axis=1)
-    d_x = dot(both, w_ref[:, : 2 * units], NT)
+    inner_ref[:, :units] = d_gate
+    inner_ref[:, units : 2 * units] = d_up
+    inner_ref[:, 2 * units :] = act
+    d_x = dot(inner_ref[:, : 2 * units], w_ref[:, : 2 * units], NT)
     gain_row = jnp.sum(d_x * x.astype(F32), axis=0, keepdims=True)
     dx = d_x.astype(BF)
 
@@ -455,51 +573,87 @@
         ym_ref[...] = y
         dm_ref[...] = dx
 
-    left = dot(x, both, TN)
-    right = dot(g, act, TN)
+    @pl.when(step == 0)
+    def _():
+        gain_ref[...] = gain_row
+
+    @pl.when(step > 0)
+    def _():
+        gain_ref[...] += gain_row
+
+
+def ffn_weight_kernel(xo_ref, xm_ref, go_ref, gm_ref, inner_ref, grad_ref, sum_ref):
+    units = inner_ref.shape[1] // 3
+    step = pl.program_id(0)
+    early = step < pl.num_programs(0) // 2
+    x = jnp.where(early, xo_ref[...], xm_ref[...])
+    g = jnp.where(early, go_ref[...], gm_ref[...])
+    left = dot(x, inner_ref[:, : 2 * units], TN)
+    right = dot(g, inner_ref[:, 2 * units :], TN)
 
     @pl.when(step == 0)
     def _():
         sum_ref[:, : 2 * units] = left
         sum_ref[:, 2 * units :] = right
-        gain_ref[...] = gain_row
-
-    @pl.when(step > 0)
+
+    @pl.when((step > 0) & (step < pl.num_programs(0) - 1))
     def _():
         sum_ref[:, : 2 * units] += left
         sum_ref[:, 2 * units :] += right
-        gain_ref[...] += gain_row
 
     @pl.when(step == pl.num_programs(0) - 1)
     def _():
-        grad_ref[...] = sum_ref[...].astype(BF)
-
-
-def feed_forward(x_mine, x_other, g_mine, g_other, w, rows):
-    tokens, width = x_mine.shape
-    units3 = w.shape[1]
+        grad_ref[:, : 2 * units] = (sum_ref[:, : 2 * units] + left).astype(BF)
+        grad_ref[:, 2 * units :] = (sum_ref[:, 2 * units :] + right).astype(BF)
+
+
+def ffn_specs(tokens, width, units3, rows):
     steps = tokens // rows
     other = pl.BlockSpec((rows, width), lambda i: (jnp.minimum(i, steps - 1), 0))
     mine = pl.BlockSpec((rows, width), lambda i: (jnp.maximum(i - steps, 0), 0))
     whole = pl.BlockSpec((width, units3), lambda i: (0, 0))
+    inner = pl.BlockSpec((rows, units3), lambda i: (i, 0))
+    return 2 * steps, other, mine, whole, inner
+
+
+def feed_forward(x_mine, x_other, g_mine, g_other, w, rows):
+    tokens, width = x_mine.shape
+    units3 = w.shape[1]
+    grid, other, mine, whole, inner = ffn_specs(tokens, width, units3, rows)
     part = jax.ShapeDtypeStruct((tokens, width), BF)
-    y_other, y_mine, dx_other, dx_mine, grads, gain_row = pl.pallas_call(
+    y_other, y_mine, dx_other, dx_mine, inside, gain_row = pl.pallas_call(
         ffn_kernel,
-        grid=(2 * steps,),
+        grid=(grid,),
         in_specs=[other, mine, other, mine, whole],
-        out_specs=[other, mine, other, mine, whole, pl.BlockSpec((1, width), lambda i: (0, 0))],
+        out_specs=[other, mine, other, mine, inner, pl.BlockSpec((1, width), lambda i: (0, 0))],
         out_shape=[
             part, part, part, part,
-            jax.ShapeDtypeStruct((width, units3), BF), jax.ShapeDtypeStruct((1, width), F32),
+            jax.ShapeDtypeStruct((2 * tokens, units3), BF), jax.ShapeDtypeStruct((1, width), F32),
         ],
-        scratch_shapes=[pltpu.VMEM((width, units3), F32)],
         compiler_params=pltpu.CompilerParams(vmem_limit_bytes=VMEM_LIMIT),
         cost_estimate=pl.CostEstimate(
-            flops=12 * tokens * width * units3, bytes_accessed=24 << 20, transcendentals=2 * tokens * units3 // 3
+            flops=8 * tokens * width * units3, bytes_accessed=24 << 20, transcendentals=2 * tokens * units3 // 3
         ),
         name="feed_forward",
     )(x_other, x_mine, g_other, g_mine, w)
-    return y_mine, y_other, dx_mine, dx_other, grads, gain_row[0]
+    return y_mine, y_other, dx_mine, dx_other, inside, gain_row[0]
+
+
+def ffn_weight_grads(x_mine, x_other, g_mine, g_other, inside, rows):
+    tokens, width = x_mine.shape
+    units3 = inside.shape[1]
+    grid, other, mine, whole, inner = ffn_specs(tokens, width, units3, rows)
+    return pl.pallas_call(
+        ffn_weight_kernel,
+        grid=(grid,),
+        in_specs=[other, mine, other, mine, inner],
+        out_specs=whole,
+        out_shape=jax.ShapeDtypeStruct((width, units3), BF),
+        scratch_shapes=[pltpu.VMEM((width, units3), F32)],
+        compiler_params=pltpu.CompilerParams(vmem_limit_bytes=VMEM_LIMIT),
+        cost_estimate=pl.CostEstimate(flops=16 << 30, bytes_accessed=24 << 20, transcendentals=0),
+        name="ffn_weight_grads",
+    )(x_other, x_mine, g_other, g_mine, inside)
 
 
 def same_kernel(in_ref, out_ref):
@@ -675,7 +829,7 @@
     others = [swap_cores(piece) for piece in x_pieces]
     while len(x_pieces) < n_ctx:
         x_pieces.append(ctx_up(x_pieces[-1]))
-        if len(x_pieces) == n_ctx:
+        if len(x_pieces) == 3:
             ffn_rows, x_pieces[-1] = tie(ffn_rows, x_pieces[-1])
         others.append(swap_cores(x_pieces[-1]))
     ffn_w = lax.all_gather(ffn_rows, "ctx", axis=1, tiled=True).reshape(width, 3 * padded)
@@ -709,12 +863,8 @@
         return value.reshape(-1, width)
 
     place = jnp.stack([f]).astype(jnp.int32)
-    y_mine, y_other, dx_mine, dx_other, ffn_grads, ffn_gain_row = feed_forward(
+    y_mine, y_other, dx_mine, dx_other, inside, ffn_gain_row = feed_forward(
         flat(x_mine), flat(x_other), flat(g_mine), flat(g_other), ffn_w, 2 * slots * shard_rows
-    )
-
-    ffn_reduced = lax.psum_scatter(
-        ffn_grads.reshape(n_fsdp, n_ctx * shard, 3 * padded), "ctx", scatter_dimension=1, tiled=True
     )
 
     def core_sums(mine, other):
@@ -723,11 +873,20 @@
         return [mine[m].astype(F32) + other[m].astype(F32) for m in range(n_fsdp)]
 
     def traded(sums):
-        return [sums[0]] + [fsdp_xor(sums[m].astype(BF), m) for m in range(1, n_fsdp)]
-
-    held = tie(*traded(core_sums(dx_mine, dx_other)), *core_sums(y_mine, y_other))
-    d_normed_two = sum(item.astype(F32) for item in held[:n_fsdp])
-    y_sums = held[n_fsdp:]
+        return [sums[0]] + [fsdp_xor(sums[m], m) for m in range(1, n_fsdp)]
+
+    dx_sums = core_sums(dx_mine, dx_other)
+    inside, *dx_sums = tie(inside, dx_sums[0], *[item.astype(BF) for item in dx_sums[1:]])
+    y_sums = core_sums(y_mine, y_other)
+    inside, *y_sums = tie(inside, y_sums[0], *[item.astype(BF) for item in y_sums[1:]])
+    ffn_grads = ffn_weight_grads(
+        flat(x_mine), flat(x_other), flat(g_mine), flat(g_other), inside, 2 * slots * shard_rows
+    )
+    ffn_grads, *held = tie(ffn_grads, *traded(dx_sums))
+    ffn_reduced = lax.psum_scatter(
+        ffn_grads.reshape(n_fsdp, n_ctx * shard, 3 * padded), "ctx", scatter_dimension=1, tiled=True
+    )
+    d_normed_two = sum(item.astype(F32) for item in held)
     d_middle = grad_rows.astype(F32) + norm_back(middle, ffn_gain, d_normed_two)
     d_branch = d_middle.astype(BF)
     d_branch = jnp.concatenate([d_branch, swap_cores(d_branch)], axis=1)
@@ -741,42 +900,65 @@
     )
     y_got = traded(y_sums)
 
-    held = tie(d_q, d_k, d_v, *y_got)
-    d_q, d_k, d_v = held[:3]
-    result = jnp.where(valid, middle + sum(item.astype(F32) for item in held[3:]), 0.0).astype(BF)
-
-    mine, other, attn_gain_row = input_grads(d_q, d_k, d_v, x_all, attn_w)
-    mine, other, d_q, d_k, d_v, ffn_reduced = tie(mine, other, d_q, d_k, d_v, ffn_reduced)
+    held = tie(d_q, d_k, d_v, gq, gk, d_branch, ffn_gain_row, *y_got)
+    d_q, d_k, d_v, gq, gk, d_branch, ffn_gain_row = held[:7]
+    result = jnp.where(valid, middle + sum(item.astype(F32) for item in held[7:]), 0.0).astype(BF)
+
+    heads = jnp.stack([jnp.pad(item[0, :HEAD] + item[0, HEAD:], (0, HEAD)) for item in (gq, gk)])
+    small = jnp.stack([jnp.zeros_like(ffn_gain), ffn_gain_row / ffn_gain])
+    small = jnp.concatenate([small, heads], axis=1)
+    small = jnp.pad(small, ((0, 0), (0, 2 * q_cols + 2 * k_cols - small.shape[1])))
+    top_send, top, low_send, low = weight_grads(
+        place, x_all, d_q, d_k, d_v, d_branch, attn, attn_w, attn_gain[None, :], two_parts(small), n_fsdp
+    )
+    top_send, top, low_send, low, d_q, d_k, d_v = tie(top_send, top, low_send, low, d_q, d_k, d_v)
+
+    half = n_ctx * shard // 2
+    bits = bits_of(n_fsdp)
+    own = top_send[n_fsdp // 2 * half :]
+    came = [fsdp_xor(top_send, bits[0]), fsdp_xor(low_send, bits[-1])]
+    mine, other = input_grads(d_q, d_k, d_v, attn_w, 0, n_ctx)
+    mine, other, *came = tie(mine, other, *came)
     other = swap_cores(other)
-    gains = jnp.stack([attn_gain_row[0] / attn_gain, ffn_gain_row / ffn_gain])
-    heads = jnp.stack([jnp.pad(jnp.concatenate([item[0, :HEAD] + item[0, HEAD:]]), (0, HEAD)) for item in (gq, gk)])
-    small = jnp.concatenate([gains, heads], axis=1)
-    small = jnp.pad(small, ((0, 0), (0, 2 * q_cols + 2 * k_cols - small.shape[1])))
-    grads = weight_grads(place, x_all, d_q, d_k, d_v, d_branch, attn, two_parts(small), n_fsdp)
-
-    total = mine[n_ctx - 1] + other[n_ctx - 1].astype(F32)
-    for r in range(n_ctx - 2, -1, -1):
-        total = ctx_down(total.astype(BF)).astype(F32)
-        if r == n_ctx - 2:
-            held = tie(total, ffn_reduced, *grads)
-            total, ffn_reduced = held[:2]
-            grads = held[2:]
-        total = mine[r] + other[r].astype(F32) + total
-    attn_pieces = [grads[0]] + [fsdp_xor(grads[m], m) for m in range(1, n_fsdp)]
+    block = n_ctx - 1
+    total = None
+    for step in range(1, len(bits)):
+        count = n_fsdp >> step
+        sent = []
+        kept = []
+        for side, keep in enumerate((top, low)):
+            order = bits if side == 0 else bits[::-1]
+            masks = sorted(sum(bit for j, bit in enumerate(order[step:]) if i >> j & 1) for i in range(count))
+            sends = [i for i, mask in enumerate(masks) if mask & order[step]]
+            keeps = [i for i, mask in enumerate(masks) if not mask & order[step]]
+            send, keep = half_sum(keep, came[side], own if side == 0 else None, half, sends, keeps)
+            sent.append(send)
+            kept.append(keep)
+        if step == 1:
+            other, mine, *held = tie(other, mine, *sent, *kept)
+            sent, kept = held[:2], held[2:]
+        top, low = kept
+        own = sent[0][count // 2 * half :]
+        came = [fsdp_xor(sent[0], bits[step]), fsdp_xor(sent[1], bits[-1 - step])]
+        if block > 0:
+            total = ctx_down(down_add(mine, other, block, *(() if total is None else (total,))))
+            block -= 1
+            total, *came = tie(total, *came)
+    ctx_place = jnp.stack([f, c]).astype(jnp.int32)
+    mine_rows, small, *messages = to_ctx(ctx_place, top, came[0], low, came[1], own, n_ctx)
+    got = [ctx_shift(message, k) for k, message in enumerate(messages, 1)]
     ffn_parts = lax.all_to_all(ffn_reduced, "fsdp", 0, 0, tiled=True)
-    depth = n_ctx * shard
-    attn_part = sum(piece[:depth].astype(F32) for piece in attn_pieces)
-    small = tree_sum([one_part(piece[depth:]) for piece in attn_pieces])
-    total, attn_part, ffn_parts, small = tie(total, attn_part, ffn_parts, small)
-
-    sends = attn_part.reshape(n_ctx, shard, -1)
-    more = two_parts(small)
-    got = [part(sends, c)]
-    small = [one_part(more)]
-    for k in range(1, n_ctx):
-        piece = ctx_shift(jnp.concatenate([part(sends, (c + k) % n_ctx).astype(BF), more]), k)
-        got.append(piece[:shard].astype(F32))
-        small.append(one_part(piece[shard:]))
+    if block > 0:
+        total = ctx_down(down_add(mine, other, block, total))
+        block -= 1
+        total, ffn_parts, *got = tie(total, ffn_parts, *got)
+    while block > 0:
+        total = ctx_down(down_add(mine, other, block, total))
+        block -= 1
+    total = mine[0] + other[0].astype(F32) + total.astype(F32)
+
+    small = [one_part(small)] + [one_part(piece[shard:]) for piece in got]
+    got = [mine_rows] + [piece[:shard].astype(F32) for piece in got]
     gate_grad, up_grad, down_grad = finish(ffn_parts, ff_half)
     down_grad = down_grad.T
     attn_grads = sum(got)

time: 374 us -> 372 us (level)
  Pallas kernels: 112 us -> 130 us
  waiting for transfers between devices: 125 us -> 108 us
  other arithmetic: 39.2 us -> 32.1 us
    ppermute x19 -> x20, waiting for transfers between devices: 64.3 us -> 42 us  [fsdp_xor(): return lax.ppermute(value, 'fsdp', [(i, i ^ mask) for i in range(size)])]
    pallas_call x3 -> x10, Pallas kernels: 57.4 us -> 76.1 us  [the longest x1 26.1 us: feed_forward(): pl.pallas_call(ffn_kernel, grid=(grid,), in_specs=[other, mine, other, mi...]
    ppermute x6, waiting for transfers between devices: 16.4 us -> 31.3 us  [ctx_shift(): lax.ppermute(value, 'ctx', [(i, (i + step) % size) for i in range(size)])]
    add x4 -> x0, other arithmetic: 6.57 us -> none  [the longest x1 3.12 us: body(): attn_part = sum((piece[:depth].astype(F32) for piece in attn_pieces))]
    all_gather x1, waiting for transfers between devices: 13.5 us -> 7.28 us  [body(): lax.all_gather(ffn_rows, 'ctx', axis=1, tiled=True)]
    convert_element_type x6 -> x2, other arithmetic: 7.12 us -> 3.1 us  [body(): item.astype(BF)]
    ppermute x19 -> x20, starting transfers between devices: 22.2 us -> 23.1 us  [fsdp_xor(): return lax.ppermute(value, 'fsdp', [(i, i ^ mask) for i in range(size)])]
  transfers between devices with their start and end apart: 47 -> 48, of which waited for: 20 -> 20; matrix products, arithmetic and copies ran while one was open for 11% -> 9% of each run, Pallas kernels for 20% -> 28%
where the time goes in v3:
time: 372 us; the launch traced here: 367 us
  Pallas kernels  130 us (35%)
  waiting for transfers between devices  108 us (29%)
  starting transfers between devices  66.3 us (18%)
  other arithmetic  32.1 us (9%)
  between operations  15.3 us (4%)
  local copies, waits for them, and re-layouts  11.3 us (3%)
    ppermute x20, waiting for transfers between devices, fsdp_xor(): return lax.ppermute(value, 'fsdp', [(i, i ^ mask) for i in range(size)])  42 us
    ppermute x6, waiting for transfers between devices, ctx_shift(): lax.ppermute(value, 'ctx', [(i, (i + step) % size) for i in range(size)])  31.3 us
    pallas_call x1, Pallas kernels, feed_forward(): pl.pallas_call(ffn_kernel, grid=(grid,), in_specs=[other, mine, other, mi...  26.1 us
    pallas_call x1, Pallas kernels, attend_back(): pl.pallas_call(attend_back_kernel, grid=(slots, pairs), in_specs=[smem, q...  25.5 us
    pallas_call x1, Pallas kernels, attend(): pl.pallas_call(functools.partial(attend_kernel, len(pieces), parts), grid...  23.9 us
    ppermute x20, starting transfers between devices, fsdp_xor(): return lax.ppermute(value, 'fsdp', [(i, i ^ mask) for i in range(size)])  23.1 us
    ppermute x3, starting transfers between devices, ctx_up(): lax.ppermute(value, 'ctx', [(i, i + step) for i in range(size - step)])  19.5 us
    pallas_call x1, Pallas kernels, ffn_weight_grads(): pl.pallas_call(ffn_weight_kernel, grid=(grid,), in_specs=[other, mine, ot...  17.1 us
  transfers between devices with their start and end apart: 48, of which 20 were waited for; matrix products, arithmetic and copies ran while one was open for 9% of the time, Pallas kernels for 28%

profile of v3, /device:TPU:0, one launch (start us, length us, event | category | flops | bytes accessed | tf_op | source)
XLA Modules:
  0.0 367.2 jit_solution(7610344293040098480)
XLA Ops:
  9.7 5.7 %collective-permute-start = (bf16[2,128,1024]{2,1,0:T(8,128)(2,1)S(1)}, bf16[2,128,1024]{2,1,0:T(8,128)(2,1)}, u32[]{:S(2)}, u32[]{:S(2)}) collective-permute-start(bf16[2,128,1024]{2,1,0:T(8,128)(2,1)S(1)} %fusion.3.refs_0_), channel_id=1, source_target_pairs={{0,2},{2,4},{4,6},{1,3},{3,5},{5,7},{8,10},{10,12},{12,14},{9,11},... | collective-permute-start | bytes 1572872 | tf_op jit(solution)/shard_map/ppermute | solution.py:45
  17.0 1.6 collective-permute-start.2
  18.6 1.6 collective-permute-start.1
  20.2 2.1 pack.1
  22.4 3.7 %all-to-all-start = ((bf16[4,64,1920]{2,1,0:T(8,128)(2,1)}), bf16[4,64,1920]{2,1,0:T(8,128)(2,1)S(1)}, u32[]{:S(2)}, u32[]{:S(2)}) async-start(bf16[4,64,1920]{2,1,0:T(8,128)(2,1)} %pack.1), calls=%async_computation | async-start | bytes 1966080 | tf_op jit(solution)/shard_map/all_to_all | solution.py:823
  26.1 5.1 %collective-permute-done.3 = bf16[64,1536]{1,0:T(8,128)(2,1)S(1)} collective-permute-done((bf16[64,1536]{1,0:T(8,128)(2,1)S(1)}, bf16[64,1536]{1,0:T(8,128)(2,1)S(1)}, u32[]{:S(2)}, u32[]{:S(2)}) %collective-permute-start.3) | collective-permute-done | bytes 196640 | tf_op jit(solution)/shard_map/ppermute | solution.py:55
  31.2 4.4 %collective-permute-done.2 = bf16[64,1536]{1,0:T(8,128)(2,1)S(1)} collective-permute-done((bf16[64,1536]{1,0:T(8,128)(2,1)S(1)}, bf16[64,1536]{1,0:T(8,128)(2,1)S(1)}, u32[]{:S(2)}, u32[]{:S(2)}) %collective-permute-start.2) | collective-permute-done | bytes 196640 | tf_op jit(solution)/shard_map/ppermute | solution.py:55
  35.6 2.8 collective-permute-done.1
  38.7 1.6 collective-permute-start.10
  40.3 1.6 collective-permute-start.12
  42.0 8.5 %collective-permute-start.4 = (bf16[2,128,1024]{2,1,0:T(8,128)(2,1)}, bf16[2,128,1024]{2,1,0:T(8,128)(2,1)}, u32[]{:S(2)}, u32[]{:S(2)}) collective-permute-start(bf16[2,128,1024]{2,1,0:T(8,128)(2,1)} %collective-permute-done.refs_2_), channel_id=1, source_target_pairs={{0,2},{2,4},{4,6},{1,3},{3,5},{5,7},{8,10},{10,12},{12,14},{9,11},... | collective-permute-start | bytes 1572872 | tf_op jit(solution)/shard_map/ppermute | solution.py:45
  53.8 5.9 %collective-permute-done.4.refs_4_ = bf16[2,128,1024]{2,1,0:T(8,128)(2,1)} collective-permute-done((bf16[2,128,1024]{2,1,0:T(8,128)(2,1)}, bf16[2,128,1024]{2,1,0:T(8,128)(2,1)}, u32[]{:S(2)}, u32[]{:S(2)}) %collective-permute-start.4) | collective-permute-done | bytes 524320 | tf_op jit(solution)/shard_map/ppermute | solution.py:45
  59.7 5.2 %collective-permute-start.5 = (bf16[2,128,1024]{2,1,0:T(8,128)(2,1)}, bf16[2,128,1024]{2,1,0:T(8,128)(2,1)}, u32[]{:S(2)}, u32[]{:S(2)}) collective-permute-start(bf16[2,128,1024]{2,1,0:T(8,128)(2,1)} %collective-permute-done.4.refs_4_), channel_id=1, source_target_pairs={{0,2},{2,4},{4,6},{1,3},{3,5},{5,7},{8,10},{10,12},{12,14},{9,11},... | collective-permute-start | bytes 1572872 | tf_op jit(solution)/shard_map/ppermute | solution.py:45
  67.9 3.1 fusion.18
  71.5 1.7 collective-permute-done.5.refs_6_
  73.7 1.3 pad_maximum_fusion.3.refs_8_.refs_9_.refs_10_
  75.0 1.9 pad_maximum_fusion.4.refs_11_.refs_12_.refs_13_
  77.5 1.5 collective-permute-start.15
  79.0 1.5 collective-permute-start.14
  81.2 23.9 %attend.1 = (bf16[2,256,512]{2,1,0:T(8,128)(2,1)}, f32[2,2,8,256]{3,2,1,0:T(8,128)}, f32[2,256,512]{2,1,0:T(8,128)}, f32[2,1024,256]{2,1,0:T(8,128)}, bf16[2,102...) custom-call(s32[5]{0:T(128)} %pad_add_fusion.scal_ref, ...), custom_call_target="tpu_custom_call" | custom-call | flops 1048576 | bytes 1048576 | tf_op jit(solution)/shard_map/attend/pallas_call | solution.py:268
  107.1 2.6 collective-permute-done.17
  111.2 2.5 collective-permute-start.20
  113.7 1.6 pad_maximum_fusion.2
  115.5 8.8 %collective-permute-done.19 = bf16[2,128,1024]{2,1,0:T(8,128)(2,1)S(1)} collective-permute-done((bf16[2,128,1024]{2,1,0:T(8,128)(2,1)S(1)}, bf16[2,128,1024]{2,1,0:T(8,128)(2,1)S(1)}, u32[]{:S(2)}, u32[]{:S(2)}) %collective-permute-start.19) | collective-permute-done | bytes 524320 | tf_op jit(solution)/shard_map/ppermute | solution.py:40
  124.2 1.3 collective-permute-done.18
  125.5 11.1 %collective-permute-done.20 = bf16[2,128,1024]{2,1,0:T(8,128)(2,1)S(1)} collective-permute-done((bf16[2,128,1024]{2,1,0:T(8,128)(2,1)S(1)}, bf16[2,128,1024]{2,1,0:T(8,128)(2,1)S(1)}, u32[]{:S(2)}, u32[]{:S(2)}) %collective-permute-start.20) | collective-permute-done | bytes 524320 | tf_op jit(solution)/shard_map/ppermute | solution.py:40
  136.6 1.6 pad_maximum_fusion.1
  138.2 7.3 %all-gather.2.cloned.1.call-done = bf16[4,256,1920]{2,1,0:T(8,128)(2,1)} async-done(((bf16[4,64,1920]{2,1,0:T(8,128)(2,1)}), bf16[4,256,1920]{2,1,0:T(8,128)(2,1)}) %all-gather.2.cloned.1.call-update) | async-done | bytes 3932176 | tf_op jit(solution)/shard_map/all_gather | solution.py:835
  145.5 26.1 %feed_forward.1 = (bf16[1024,1024]{1,0:T(8,128)(2,1)}, bf16[1024,1024]{1,0:T(8,128)(2,1)}, bf16[1024,1024]{1,0:T(8,128)(2,1)}, bf16[1024,1024]{1,0:T(8,128)(2,1)...) custom-call(bf16[1024,1024]{1,0:T(8,128)(2,1)} %bitcast.25.xo_ref, bf16[1024,1024]{1,0:T(8,128)(2,1)} %bitcast.26.xm_ref, ...), custom_call_target="tpu_custom_call" | custom-call | flops 16106127360 | bytes 25165824 | tf_op jit(solution)/shard_map/feed_forward/pallas_call | solution.py:624
  172.2 1.9 fusion.44
  174.6 1.5 collective-permute-done.23
  177.0 1.5 collective-permute-start.25
  178.6 1.5 collective-permute-start.26
  180.6 2.2 fusion.10
  182.8 17.1 %ffn_weight_grads.1 = bf16[1024,1920]{1,0:T(8,128)(2,1)} custom-call(bf16[1024,1024]{1,0:T(8,128)(2,1)} %bitcast.25.xo_ref, bf16[1024,1024]{1,0:T(8,128)(2,1)} %bitcast.26.xm_ref, bf16[1024,1024]{1,0:T(8,128)(2,1)} %bitcast.31.go_ref, bf16[1024,1024]{1,0:T(8,128)(2,1)} %bitcast.32.gm_ref, bf16[2048,1920]{1,0:T(8,128)(2,1)} %get-tuple-element.167.inner_ref), custom_call_target="tpu_custom_call" | custom-call | flops 17179869184 | bytes 25165824 | tf_op jit(solution)/shard_map/ffn_weight_grads/pallas_call | solution.py:646
  199.9 3.6 collective-permute-done.26
  204.3 2.0 collective-permute-done.28
  206.3 2.9 convolution_convert_fusion.d_ref
  211.2 1.5 collective-permute-start.31
  212.7 25.5 %attend_back.1 = (bf16[2,256,512]{2,1,0:T(8,128)(2,1)}, bf16[2,1024,256]{2,1,0:T(8,128)(2,1)}, bf16[2,1024,256]{2,1,0:T(8,128)(2,1)}, f32[1,128]{1,0:T(1,128)}, f32[1,128]{1,0:T(1,128)}) custom-call(s32[5]{0:T(128)} %pad_add_fusion.scal_ref, f32[2,256,512]{2,1,0:T(8,128)} %get-tuple-element.150.q_ref, f32[2,1024,256]{2,1,0:T(8,128)} %get-tuple-element.151.k_ref, ...), custom_call_target="tpu_custom_call" | custom-call | flops 25769803776 | bytes 12582912 | tf_op jit(solution)/shard_map/attend_back/pallas_call | solution.py:299
  238.2 2.2 pad_maximum_fusion.5.b_ref
  241.5 10.7 %weight_grads.1 = (bf16[272,1536]{1,0:T(8,128)(2,1)}, bf16[256,1536]{1,0:T(8,128)(2,1)}, bf16[256,1536]{1,0:T(8,128)(2,1)}, bf16[256,1536]{1,0:T(8,128)(2,1)}) custom-call(s32[1]{0:T(128)} %bitcast.2.at_ref, bf16[2,1024,1024]{2,1,0:T(8,128)(2,1)} %get-tuple-element.195.x_ref, bf16[2,256,512]{2,1,0:T(8,128)(2,1)} %get-tuple-element.207.dq_ref, ...), custom_call_target="tpu_custom_call" | custom-call | flops 10737418240 | bytes 8388608 | tf_op jit(solution)/shard_map/weight_grads/pallas_call | solution.py:398
  254.4 1.4 slice.220.refs_0_
  255.8 8.0 %input_grads.1 = (f32[4,2,128,1024]{3,2,1,0:T(8,128)}, bf16[4,2,128,1024]{3,2,1,0:T(8,128)(2,1)}) custom-call(bf16[2,256,512]{2,1,0:T(8,128)(2,1)} %get-tuple-element.207.dq_ref, bf16[2,1024,256]{2,1,0:T(8,128)(2,1)} %get-tuple-element.208.dk_ref, bf16[2,1024,256]{2,1,0:T(8,128)(2,1)} %get-tuple-element.209.dv_ref, bf16[1024,1536]{1,0:T(8,128)(2,1)} %bitcast.142), custom_call_target="tpu_custom_call" | custom-call | flops 6442450944 | bytes 1048576 | tf_op jit(solution)/shard_map/input_grads/pallas_call | solution.py:432
  263.8 8.4 %collective-permute-done.33.came_ref = bf16[256,1536]{1,0:T(8,128)(2,1)S(1)} collective-permute-done((bf16[256,1536]{1,0:T(8,128)(2,1)}, bf16[256,1536]{1,0:T(8,128)(2,1)S(1)}, u32[]{:S(2)}, u32[]{:S(2)}) %collective-permute-start.33) | collective-permute-done | bytes 786464 | tf_op jit(solution)/shard_map/ppermute | solution.py:40
  273.1 2.3 half_sum.3
  275.4 2.5 half_sum.2
  277.9 2.2 down_add.3
  284.9 8.7 %collective-permute-done.37.low_came = bf16[128,1536]{1,0:T(8,128)(2,1)S(1)} collective-permute-done((bf16[128,1536]{1,0:T(8,128)(2,1)}, bf16[128,1536]{1,0:T(8,128)(2,1)S(1)}, u32[]{:S(2)}, u32[]{:S(2)}) %collective-permute-start.37) | collective-permute-done | bytes 393248 | tf_op jit(solution)/shard_map/ppermute | solution.py:40
  294.4 1.5 collective-permute-done.35.refs_2_
  295.8 2.3 down_add.4
  299.4 4.2 %all-to-all-start.1 = ((bf16[4,64,1920]{2,1,0:T(8,128)(2,1)}), bf16[4,64,1920]{2,1,0:T(8,128)(2,1)}, u32[]{:S(2)}, u32[]{:S(2)}) async-start(bf16[4,64,1920]{2,1,0:T(8,128)(2,1)} %reduce-scatter.2.cloned.1.call-done), calls=%async_computation.2 | async-start | bytes 1966080 | tf_op jit(solution)/shard_map/all_to_all | solution.py:950
  303.7 2.7 to_ctx.1
  306.3 2.6 collective-permute-start.39
  309.0 1.9 collective-permute-start.40
  310.8 1.6 collective-permute-start.41
  312.4 8.5 %collective-permute-done.39 = bf16[80,1536]{1,0:T(8,128)(2,1)S(1)} collective-permute-done((bf16[80,1536]{1,0:T(8,128)(2,1)}, bf16[80,1536]{1,0:T(8,128)(2,1)S(1)}, u32[]{:S(2)}, u32[]{:S(2)}) %collective-permute-start.39) | collective-permute-done | bytes 245792 | tf_op jit(solution)/shard_map/ppermute | solution.py:55
  320.9 10.4 %collective-permute-done.40 = bf16[80,1536]{1,0:T(8,128)(2,1)S(1)} collective-permute-done((bf16[80,1536]{1,0:T(8,128)(2,1)}, bf16[80,1536]{1,0:T(8,128)(2,1)S(1)}, u32[]{:S(2)}, u32[]{:S(2)}) %collective-permute-start.40) | collective-permute-done | bytes 245792 | tf_op jit(solution)/shard_map/ppermute | solution.py:55
  333.4 2.3 down_add.5
  336.6 1.4 collective-permute-start.42
  338.7 2.4 finish.1
  342.2 12.6 %collective-permute-done.42 = bf16[2,128,1024]{2,1,0:T(8,128)(2,1)S(1)} collective-permute-done((bf16[2,128,1024]{2,1,0:T(8,128)(2,1)}, bf16[2,128,1024]{2,1,0:T(8,128)(2,1)S(1)}, u32[]{:S(2)}, u32[]{:S(2)}) %collective-permute-start.42) | collective-permute-done | bytes 524320 | tf_op jit(solution)/shard_map/ppermute | solution.py:50
  354.9 1.8 fusion.4
  356.7 3.2 fusion.8
  (206 shorter events, 37.4 us)
Async XLA Ops:
  9.7 61.3 %copy-start.7 = (bf16[2,128,1024]{2,1,0:T(8,128)(2,1)}, bf16[2,128,1024]{2,1,0:T(8,128)(2,1)S(1)}, u32[]{:S(2)}) copy-start(bf16[2,128,1024]{2,1,0:T(8,128)(2,1)S(1)} %fusion.3.refs_0_) | copy-start | bytes 1572868
  9.7 28.8 %collective-permute-start = (bf16[2,128,1024]{2,1,0:T(8,128)(2,1)S(1)}, bf16[2,128,1024]{2,1,0:T(8,128)(2,1)}, u32[]{:S(2)}, u32[]{:S(2)}) collective-permute-start(bf16[2,128,1024]{2,1,0:T(8,128)(2,1)S(1)} %fusion.3.refs_0_), channel_id=1, source_target_pairs={{0,2},{2,4},{4,6},{1,3},{3,5},{5,7},{8,10},{10,12},{12,14},{9,11},... | collective-permute-start | bytes 1572872 | tf_op jit(solution)/shard_map/ppermute | solution.py:45
  16.3 14.8 %collective-permute-start.3 = (bf16[64,1536]{1,0:T(8,128)(2,1)S(1)}, bf16[64,1536]{1,0:T(8,128)(2,1)S(1)}, u32[]{:S(2)}, u32[]{:S(2)}) collective-permute-start(bf16[64,1536]{1,0:T(8,128)(2,1)S(1)} %pad_maximum_fusion.8), channel_id=1, source_target_pairs={{0,6},{2,0},{4,2},{6,4},{1,7},{3,1},{5,3},{7,5},{8,14},{10,8},{12,... | collective-permute-start | bytes 589832 | tf_op jit(solution)/shard_map/ppermute | solution.py:55
  17.0 18.6 %collective-permute-start.2 = (bf16[64,1536]{1,0:T(8,128)(2,1)S(1)}, bf16[64,1536]{1,0:T(8,128)(2,1)S(1)}, u32[]{:S(2)}, u32[]{:S(2)}) collective-permute-start(bf16[64,1536]{1,0:T(8,128)(2,1)S(1)} %pad_maximum_fusion.8), channel_id=1, source_target_pairs={{0,4},{2,6},{4,0},{6,2},{1,5},{3,7},{5,1},{7,3},{8,12},{10,14},{12... | collective-permute-start | bytes 589832 | tf_op jit(solution)/shard_map/ppermute | solution.py:55
  18.6 19.8 %collective-permute-start.1 = (bf16[64,1536]{1,0:T(8,128)(2,1)S(1)}, bf16[64,1536]{1,0:T(8,128)(2,1)S(1)}, u32[]{:S(2)}, u32[]{:S(2)}) collective-permute-start(bf16[64,1536]{1,0:T(8,128)(2,1)S(1)} %pad_maximum_fusion.8), channel_id=1, source_target_pairs={{0,2},{2,4},{4,6},{6,0},{1,3},{3,5},{5,7},{7,1},{8,10},{10,12},{12... | collective-permute-start | bytes 589832 | tf_op jit(solution)/shard_map/ppermute | solution.py:55
  22.4 31.4 %all-to-all-start = ((bf16[4,64,1920]{2,1,0:T(8,128)(2,1)}), bf16[4,64,1920]{2,1,0:T(8,128)(2,1)S(1)}, u32[]{:S(2)}, u32[]{:S(2)}) async-start(bf16[4,64,1920]{2,1,0:T(8,128)(2,1)} %pack.1), calls=%async_computation | async-start | bytes 1966080 | tf_op jit(solution)/shard_map/all_to_all | solution.py:823
  26.1 15.8 %copy-start.32 = (s32[2]{0:T(128)S(1)}, s32[2]{0:T(128)}, u32[]{:S(2)}) copy-start(s32[2]{0:T(128)} %param.15) | copy-start | bytes 28
  26.1 119.4 %all-gather.2.cloned.1.call-start = ((), (), s32[]{:S(2)}) async-start(), calls=%async_computation.3 | async-start | bytes 4915200 | tf_op jit(solution)/shard_map/all_gather | solution.py:835
  38.6 26.9 %copy-start.37 = (f32[64]{0:T(128)S(1)}, f32[64]{0:T(128)}, u32[]{:S(2)}) copy-start(f32[64]{0:T(128)} %param.17) | copy-start | bytes 772
  38.7 27.4 %copy-start.38 = (f32[64]{0:T(128)S(1)}, f32[64]{0:T(128)}, u32[]{:S(2)}) copy-start(f32[64]{0:T(128)} %param.18) | copy-start | bytes 772
  38.7 11.7 %collective-permute-start.10 = (bf16[1,128,1536]{2,1,0:T(8,128)(2,1)S(1)}, bf16[1,128,1536]{2,1,0:T(8,128)(2,1)S(1)}, u32[]{:S(2)}, u32[]{:S(2)}) collective-permute-start(bf16[1,128,1536]{2,1,0:T(8,128)(2,1)S(1)} %bitcast.147), channel_id=1, source_target_pairs={{0,8},{8,0},{16,24},{24,16},{1,9},{9,1},{17,25},{25,17},{2,10},{10... | collective-permute-start | bytes 1179656 | tf_op jit(solution)/shard_map/ppermute | solution.py:40
  40.3 11.7 %collective-permute-start.12 = (bf16[1,128,1536]{2,1,0:T(8,128)(2,1)S(1)}, bf16[1,128,1536]{2,1,0:T(8,128)(2,1)S(1)}, u32[]{:S(2)}, u32[]{:S(2)}) collective-permute-start(bf16[1,128,1536]{2,1,0:T(8,128)(2,1)S(1)} %bitcast.144), channel_id=1, source_target_pairs={{0,16},{8,24},{16,0},{24,8},{1,17},{9,25},{17,1},{25,9},{2,18},{10... | collective-permute-start | bytes 1179656 | tf_op jit(solution)/shard_map/ppermute | solution.py:40
  42.0 25.9 %copy-start.30 = (pred[2,128]{1,0:T(4,128)(4,1)}, pred[2,128]{1,0:T(4,128)(4,1)S(1)}, u32[]{:S(2)}) copy-start(pred[2,128]{1,0:T(4,128)(4,1)S(1)} %broadcast_compare_fusion) | copy-start | bytes 772
  42.0 17.7 %collective-permute-start.4 = (bf16[2,128,1024]{2,1,0:T(8,128)(2,1)}, bf16[2,128,1024]{2,1,0:T(8,128)(2,1)}, u32[]{:S(2)}, u32[]{:S(2)}) collective-permute-start(bf16[2,128,1024]{2,1,0:T(8,128)(2,1)} %collective-permute-done.refs_2_), channel_id=1, source_target_pairs={{0,2},{2,4},{4,6},{1,3},{3,5},{5,7},{8,10},{10,12},{12,14},{9,11},... | collective-permute-start | bytes 1572872 | tf_op jit(solution)/shard_map/ppermute | solution.py:45
  51.4 21.8 %collective-permute-start.11 = (bf16[2,128,1536]{2,1,0:T(8,128)(2,1)}, bf16[2,128,1536]{2,1,0:T(8,128)(2,1)}, u32[]{:S(2)}, u32[]{:S(2)}) collective-permute-start(bf16[2,128,1536]{2,1,0:T(8,128)(2,1)} %pad_maximum_fusion.6), channel_id=1, source_target_pairs={{0,16},{8,24},{16,0},{24,8},{1,17},{9,25},{17,1},{25,9},{2,18},{10... | collective-permute-start | bytes 2359304 | tf_op jit(solution)/shard_map/ppermute | solution.py:40
  51.9 14.8 %copy-start.9 = (bf16[1,128,1536]{2,1,0:T(8,128)(2,1)}, bf16[1,128,1536]{2,1,0:T(8,128)(2,1)S(1)}, u32[]{:S(2)}) copy-start(bf16[1,128,1536]{2,1,0:T(8,128)(2,1)S(1)} %collective-permute-done.12) | copy-start | bytes 1179652
  53.0 22.1 %collective-permute-start.13 = (bf16[2,128,1536]{2,1,0:T(8,128)(2,1)}, bf16[2,128,1536]{2,1,0:T(8,128)(2,1)}, u32[]{:S(2)}, u32[]{:S(2)}) collective-permute-start(bf16[2,128,1536]{2,1,0:T(8,128)(2,1)} %pad_maximum_fusion.7), channel_id=1, source_target_pairs={{0,8},{8,0},{16,24},{24,16},{1,9},{9,1},{17,25},{25,17},{2,10},{10... | collective-permute-start | bytes 2359304 | tf_op jit(solution)/shard_map/ppermute | solution.py:40
  53.8 17.7 %copy-start.6 = (bf16[4,64,1920]{2,1,0:T(8,128)(2,1)}, bf16[4,64,1920]{2,1,0:T(8,128)(2,1)S(1)}, u32[]{:S(2)}) copy-start(bf16[4,64,1920]{2,1,0:T(8,128)(2,1)S(1)} %all-to-all-done) | copy-start | bytes 2949124
  59.7 13.5 %collective-permute-start.5 = (bf16[2,128,1024]{2,1,0:T(8,128)(2,1)}, bf16[2,128,1024]{2,1,0:T(8,128)(2,1)}, u32[]{:S(2)}, u32[]{:S(2)}) collective-permute-start(bf16[2,128,1024]{2,1,0:T(8,128)(2,1)} %collective-permute-done.4.refs_4_), channel_id=1, source_target_pairs={{0,2},{2,4},{4,6},{1,3},{3,5},{5,7},{8,10},{10,12},{12,14},{9,11},... | collective-permute-start | bytes 1572872 | tf_op jit(solution)/shard_map/ppermute | solution.py:45
  70.9 6.0 %collective-permute-start.7 = (bf16[2,128,1024]{2,1,0:T(8,128)(2,1)}, bf16[2,128,1024]{2,1,0:T(8,128)(2,1)}, u32[]{:S(2)}, u32[]{:S(2)}) collective-permute-start(bf16[2,128,1024]{2,1,0:T(8,128)(2,1)} %collective-permute-done.refs_2_), channel_id=1, source_target_pairs={{0,1},{1,0},{2,3},{3,2},{4,5},{5,4},{6,7},{7,6},{8,9},{9,8},{10,11... | collective-permute-start | bytes 1572872 | tf_op jit(solution)/shard_map/ppermute | solution.py:35
  70.9 6.0 %collective-permute-start.6 = (bf16[2,128,1024]{2,1,0:T(8,128)(2,1)S(1)}, bf16[2,128,1024]{2,1,0:T(8,128)(2,1)}, u32[]{:S(2)}, u32[]{:S(2)}) collective-permute-start(bf16[2,128,1024]{2,1,0:T(8,128)(2,1)S(1)} %fusion.3.refs_0_), channel_id=1, source_target_pairs={{0,1},{1,0},{2,3},{3,2},{4,5},{5,4},{6,7},{7,6},{8,9},{9,8},{10,11... | collective-permute-start | bytes 1572872 | tf_op jit(solution)/shard_map/ppermute | solution.py:35
  71.5 227.9 %reduce-scatter.2.cloned.1.call-start = ((), (), s32[]{:S(2)}) async-start(), calls=%async_computation.4 | async-start | bytes 4915200 | tf_op jit(solution)/shard_map/reduce_scatter | solution.py:886
  73.2 3.8 %collective-permute-start.8 = (bf16[2,128,1024]{2,1,0:T(8,128)(2,1)}, bf16[2,128,1024]{2,1,0:T(8,128)(2,1)S(1)}, u32[]{:S(2)}, u32[]{:S(2)}) collective-permute-start(bf16[2,128,1024]{2,1,0:T(8,128)(2,1)} %collective-permute-done.4.refs_4_), channel_id=1, source_target_pairs={{0,1},{1,0},{2,3},{3,2},{4,5},{5,4},{6,7},{7,6},{8,9},{9,8},{10,11... | collective-permute-start | bytes 1572872 | tf_op jit(solution)/shard_map/ppermute | solution.py:35
  73.2 3.8 %collective-permute-start.9 = (bf16[2,128,1024]{2,1,0:T(8,128)(2,1)}, bf16[2,128,1024]{2,1,0:T(8,128)(2,1)S(1)}, u32[]{:S(2)}, u32[]{:S(2)}) collective-permute-start(bf16[2,128,1024]{2,1,0:T(8,128)(2,1)} %collective-permute-done.5.refs_6_), channel_id=1, source_target_pairs={{0,1},{1,0},{2,3},{3,2},{4,5},{5,4},{6,7},{7,6},{8,9},{9,8},{10,11... | collective-permute-start | bytes 1572872 | tf_op jit(solution)/shard_map/ppermute | solution.py:35
  77.0 28.4 %collective-permute-start.16 = (bf16[2,128,1024]{2,1,0:T(8,128)(2,1)S(1)}, bf16[2,128,1024]{2,1,0:T(8,128)(2,1)S(1)}, u32[]{:S(2)}, u32[]{:S(2)}) collective-permute-start(bf16[2,128,1024]{2,1,0:T(8,128)(2,1)S(1)} %broadcast_select_fusion), channel_id=1, source_target_pairs={{0,24},{8,16},{16,8},{24,0},{1,25},{9,17},{17,9},{25,1},{2,26},{10... | collective-permute-start | bytes 1572872 | tf_op jit(solution)/shard_map/ppermute | solution.py:40
  77.5 27.9 %collective-permute-start.15 = (bf16[2,128,1024]{2,1,0:T(8,128)(2,1)S(1)}, bf16[2,128,1024]{2,1,0:T(8,128)(2,1)S(1)}, u32[]{:S(2)}, u32[]{:S(2)}) collective-permute-start(bf16[2,128,1024]{2,1,0:T(8,128)(2,1)S(1)} %broadcast_select_fusion), channel_id=1, source_target_pairs={{0,16},{8,24},{16,0},{24,8},{1,17},{9,25},{17,1},{25,9},{2,18},{10... | collective-permute-start | bytes 1572872 | tf_op jit(solution)/shard_map/ppermute | solution.py:40
  79.0 26.4 %collective-permute-start.14 = (bf16[2,128,1024]{2,1,0:T(8,128)(2,1)S(1)}, bf16[2,128,1024]{2,1,0:T(8,128)(2,1)S(1)}, u32[]{:S(2)}, u32[]{:S(2)}) collective-permute-start(bf16[2,128,1024]{2,1,0:T(8,128)(2,1)S(1)} %broadcast_select_fusion), channel_id=1, source_target_pairs={{0,8},{8,0},{16,24},{24,16},{1,9},{9,1},{17,25},{25,17},{2,10},{10... | collective-permute-start | bytes 1572872 | tf_op jit(solution)/shard_map/ppermute | solution.py:40
  107.0 2.7 collective-permute-start.17
  110.2 14.0 %collective-permute-start.19 = (bf16[2,128,1024]{2,1,0:T(8,128)(2,1)S(1)}, bf16[2,128,1024]{2,1,0:T(8,128)(2,1)S(1)}, u32[]{:S(2)}, u32[]{:S(2)}) collective-permute-start(bf16[2,128,1024]{2,1,0:T(8,128)(2,1)S(1)} %multiply_convert_fusion), channel_id=1, source_target_pairs={{0,16},{8,24},{16,0},{24,8},{1,17},{9,25},{17,1},{25,9},{2,18},{10... | collective-permute-start | bytes 1572872 | tf_op jit(solution)/shard_map/ppermute | solution.py:40
  110.7 14.8 %collective-permute-start.18 = (bf16[2,128,1024]{2,1,0:T(8,128)(2,1)S(1)}, bf16[2,128,1024]{2,1,0:T(8,128)(2,1)S(1)}, u32[]{:S(2)}, u32[]{:S(2)}) collective-permute-start(bf16[2,128,1024]{2,1,0:T(8,128)(2,1)S(1)} %multiply_convert_fusion), channel_id=1, source_target_pairs={{0,8},{8,0},{16,24},{24,16},{1,9},{9,1},{17,25},{25,17},{2,10},{10... | collective-permute-start | bytes 1572872 | tf_op jit(solution)/shard_map/ppermute | solution.py:40
  111.2 25.4 %collective-permute-start.20 = (bf16[2,128,1024]{2,1,0:T(8,128)(2,1)S(1)}, bf16[2,128,1024]{2,1,0:T(8,128)(2,1)S(1)}, u32[]{:S(2)}, u32[]{:S(2)}) collective-permute-start(bf16[2,128,1024]{2,1,0:T(8,128)(2,1)S(1)} %multiply_convert_fusion), channel_id=1, source_target_pairs={{0,24},{8,16},{16,8},{24,0},{1,25},{9,17},{17,9},{25,1},{2,26},{10... | collective-permute-start | bytes 1572872 | tf_op jit(solution)/shard_map/ppermute | solution.py:40
  115.3 30.2 %collective-permute-start.22 = (bf16[4,2,128,1024]{3,2,1,0:T(8,128)(2,1)}, bf16[4,2,128,1024]{3,2,1,0:T(8,128)(2,1)}, u32[]{:S(2)}, u32[]{:S(2)}) collective-permute-start(bf16[4,2,128,1024]{3,2,1,0:T(8,128)(2,1)} %pad_maximum_fusion.2), channel_id=1, source_target_pairs={{0,1},{1,0},{2,3},{3,2},{4,5},{5,4},{6,7},{7,6},{8,9},{9,8},{10,11... | collective-permute-start | bytes 6291464 | tf_op jit(solution)/shard_map/ppermute | solution.py:35
  138.2 7.3 %collective-permute-start.21 = (bf16[4,2,128,1024]{3,2,1,0:T(8,128)(2,1)}, bf16[4,2,128,1024]{3,2,1,0:T(8,128)(2,1)}, u32[]{:S(2)}, u32[]{:S(2)}) collective-permute-start(bf16[4,2,128,1024]{3,2,1,0:T(8,128)(2,1)} %pad_maximum_fusion.1), channel_id=1, source_target_pairs={{0,1},{1,0},{2,3},{3,2},{4,5},{5,4},{6,7},{7,6},{8,9},{9,8},{10,11... | collective-permute-start | bytes 6291464 | tf_op jit(solution)/shard_map/ppermute | solution.py:35
  171.6 4.4 %collective-permute-start.23 = (bf16[4,2,128,1024]{3,2,1,0:T(8,128)(2,1)}, bf16[4,2,128,1024]{3,2,1,0:T(8,128)(2,1)S(1)}, u32[]{:S(2)}, u32[]{:S(2)}) collective-permute-start(bf16[4,2,128,1024]{3,2,1,0:T(8,128)(2,1)} %bitcast.173), channel_id=1, source_target_pairs={{0,1},{1,0},{2,3},{3,2},{4,5},{5,4},{6,7},{7,6},{8,9},{9,8},{10,11... | collective-permute-start | bytes 6291464 | tf_op jit(solution)/shard_map/ppermute | solution.py:35
  171.7 8.9 %collective-permute-start.24 = (bf16[4,2,128,1024]{3,2,1,0:T(8,128)(2,1)}, bf16[4,2,128,1024]{3,2,1,0:T(8,128)(2,1)S(1)}, u32[]{:S(2)}, u32[]{:S(2)}) collective-permute-start(bf16[4,2,128,1024]{3,2,1,0:T(8,128)(2,1)} %bitcast.172), channel_id=1, source_target_pairs={{0,1},{1,0},{2,3},{3,2},{4,5},{5,4},{6,7},{7,6},{8,9},{9,8},{10,11... | collective-permute-start | bytes 6291464 | tf_op jit(solution)/shard_map/ppermute | solution.py:35
  177.0 22.9 %collective-permute-start.25 = (bf16[2,128,1024]{2,1,0:T(8,128)(2,1)S(1)}, bf16[2,128,1024]{2,1,0:T(8,128)(2,1)S(1)}, u32[]{:S(2)}, u32[]{:S(2)}) collective-permute-start(bf16[2,128,1024]{2,1,0:T(8,128)(2,1)S(1)} %get-tuple-element.169), channel_id=1, source_target_pairs={{0,8},{8,0},{16,24},{24,16},{1,9},{9,1},{17,25},{25,17},{2,10},{10... | collective-permute-start | bytes 1572872 | tf_op jit(solution)/shard_map/ppermute | solution.py:40
  178.6 24.9 %collective-permute-start.26 = (bf16[2,128,1024]{2,1,0:T(8,128)(2,1)S(1)}, bf16[2,128,1024]{2,1,0:T(8,128)(2,1)S(1)}, u32[]{:S(2)}, u32[]{:S(2)}) collective-permute-start(bf16[2,128,1024]{2,1,0:T(8,128)(2,1)S(1)} %get-tuple-element.170), channel_id=1, source_target_pairs={{0,16},{8,24},{16,0},{24,8},{1,17},{9,25},{17,1},{25,9},{2,18},{10... | collective-permute-start | bytes 1572872 | tf_op jit(solution)/shard_map/ppermute | solution.py:40
  180.0 23.4 %collective-permute-start.27 = (bf16[2,128,1024]{2,1,0:T(8,128)(2,1)S(1)}, bf16[2,128,1024]{2,1,0:T(8,128)(2,1)S(1)}, u32[]{:S(2)}, u32[]{:S(2)}) collective-permute-start(bf16[2,128,1024]{2,1,0:T(8,128)(2,1)S(1)} %get-tuple-element.171), channel_id=1, source_target_pairs={{0,24},{8,16},{16,8},{24,0},{1,25},{9,17},{17,9},{25,1},{2,26},{10... | collective-permute-start | bytes 1572872 | tf_op jit(solution)/shard_map/ppermute | solution.py:40
  204.2 2.1 collective-permute-start.28
  209.2 31.2 %collective-permute-start.29 = (bf16[2,128,1024]{2,1,0:T(8,128)(2,1)S(1)}, bf16[2,128,1024]{2,1,0:T(8,128)(2,1)S(1)}, u32[]{:S(2)}, u32[]{:S(2)}) collective-permute-start(bf16[2,128,1024]{2,1,0:T(8,128)(2,1)S(1)} %copy-done.16), channel_id=1, source_target_pairs={{0,8},{8,0},{16,24},{24,16},{1,9},{9,1},{17,25},{25,17},{2,10},{10... | collective-permute-start | bytes 1572872 | tf_op jit(solution)/shard_map/ppermute | solution.py:40
  210.4 30.0 %collective-permute-start.30 = (bf16[2,128,1024]{2,1,0:T(8,128)(2,1)S(1)}, bf16[2,128,1024]{2,1,0:T(8,128)(2,1)S(1)}, u32[]{:S(2)}, u32[]{:S(2)}) collective-permute-start(bf16[2,128,1024]{2,1,0:T(8,128)(2,1)S(1)} %copy-done.15), channel_id=1, source_target_pairs={{0,16},{8,24},{16,0},{24,8},{1,17},{9,25},{17,1},{25,9},{2,18},{10... | collective-permute-start | bytes 1572872 | tf_op jit(solution)/shard_map/ppermute | solution.py:40
  211.2 29.2 %collective-permute-start.31 = (bf16[2,128,1024]{2,1,0:T(8,128)(2,1)S(1)}, bf16[2,128,1024]{2,1,0:T(8,128)(2,1)S(1)}, u32[]{:S(2)}, u32[]{:S(2)}) collective-permute-start(bf16[2,128,1024]{2,1,0:T(8,128)(2,1)S(1)} %copy-done.14), channel_id=1, source_target_pairs={{0,24},{8,16},{16,8},{24,0},{1,25},{9,17},{17,9},{25,1},{2,26},{10... | collective-permute-start | bytes 1572872 | tf_op jit(solution)/shard_map/ppermute | solution.py:40
  240.4 11.8 %copy-start.17 = (bf16[2,128,1024]{2,1,0:T(8,128)(2,1)}, bf16[2,128,1024]{2,1,0:T(8,128)(2,1)S(1)}, u32[]{:S(2)}) copy-start(bf16[2,128,1024]{2,1,0:T(8,128)(2,1)S(1)} %collective-permute-done.29) | copy-start | bytes 1572868
  252.2 20.1 %collective-permute-start.32 = (bf16[272,1536]{1,0:T(8,128)(2,1)}, bf16[272,1536]{1,0:T(8,128)(2,1)S(1)}, u32[]{:S(2)}, u32[]{:S(2)}) collective-permute-start(bf16[272,1536]{1,0:T(8,128)(2,1)} %get-tuple-element.212), channel_id=1, source_target_pairs={{0,8},{8,0},{16,24},{24,16},{1,9},{9,1},{17,25},{25,17},{2,10},{10... | collective-permute-start | bytes 2506760 | tf_op jit(solution)/shard_map/ppermute | solution.py:40
  253.5 18.7 %collective-permute-start.33 = (bf16[256,1536]{1,0:T(8,128)(2,1)}, bf16[256,1536]{1,0:T(8,128)(2,1)S(1)}, u32[]{:S(2)}, u32[]{:S(2)}) collective-permute-start(bf16[256,1536]{1,0:T(8,128)(2,1)} %get-tuple-element.213), channel_id=1, source_target_pairs={{0,16},{8,24},{16,0},{24,8},{1,17},{9,25},{17,1},{25,9},{2,18},{10... | collective-permute-start | bytes 2359304 | tf_op jit(solution)/shard_map/ppermute | solution.py:40
  272.3 5.6 %collective-permute-start.34 = (bf16[4,2,128,1024]{3,2,1,0:T(8,128)(2,1)}, bf16[4,2,128,1024]{3,2,1,0:T(8,128)(2,1)}, u32[]{:S(2)}, u32[]{:S(2)}) collective-permute-start(bf16[4,2,128,1024]{3,2,1,0:T(8,128)(2,1)} %get-tuple-element.214), channel_id=1, source_target_pairs={{0,1},{1,0},{2,3},{3,2},{4,5},{5,4},{6,7},{7,6},{8,9},{9,8},{10,11... | collective-permute-start | bytes 6291464 | tf_op jit(solution)/shard_map/ppermute | solution.py:35
  280.0 15.8 %collective-permute-start.35 = (bf16[2,128,1024]{2,1,0:T(8,128)(2,1)}, bf16[2,128,1024]{2,1,0:T(8,128)(2,1)}, u32[]{:S(2)}, u32[]{:S(2)}) collective-permute-start(bf16[2,128,1024]{2,1,0:T(8,128)(2,1)} %down_add.3), channel_id=1, source_target_pairs={{2,0},{4,2},{6,4},{3,1},{5,3},{7,5},{10,8},{12,10},{14,12},{11,9},... | collective-permute-start | bytes 1572872 | tf_op jit(solution)/shard_map/ppermute | solution.py:50
  281.3 12.3 %collective-permute-start.36 = (bf16[144,1536]{1,0:T(8,128)(2,1)S(1)}, bf16[144,1536]{1,0:T(8,128)(2,1)S(1)}, u32[]{:S(2)}, u32[]{:S(2)}) collective-permute-start(bf16[144,1536]{1,0:T(8,128)(2,1)S(1)} %copy-done.28), channel_id=1, source_target_pairs={{0,16},{8,24},{16,0},{24,8},{1,17},{9,25},{17,1},{25,9},{2,18},{10... | collective-permute-start | bytes 1327112 | tf_op jit(solution)/shard_map/ppermute | solution.py:40
  282.4 11.2 %collective-permute-start.37 = (bf16[128,1536]{1,0:T(8,128)(2,1)}, bf16[128,1536]{1,0:T(8,128)(2,1)S(1)}, u32[]{:S(2)}, u32[]{:S(2)}) collective-permute-start(bf16[128,1536]{1,0:T(8,128)(2,1)} %get-tuple-element.227), channel_id=1, source_target_pairs={{0,8},{8,0},{16,24},{24,16},{1,9},{9,1},{17,25},{25,17},{2,10},{10... | collective-permute-start | bytes 1179656 | tf_op jit(solution)/shard_map/ppermute | solution.py:40
  298.1 33.3 %collective-permute-start.38 = (bf16[2,128,1024]{2,1,0:T(8,128)(2,1)}, bf16[2,128,1024]{2,1,0:T(8,128)(2,1)}, u32[]{:S(2)}, u32[]{:S(2)}) collective-permute-start(bf16[2,128,1024]{2,1,0:T(8,128)(2,1)} %down_add.4), channel_id=1, source_target_pairs={{2,0},{4,2},{6,4},{3,1},{5,3},{7,5},{10,8},{12,10},{14,12},{11,9},... | collective-permute-start | bytes 1572872 | tf_op jit(solution)/shard_map/ppermute | solution.py:50
  299.4 32.0 %all-to-all-start.1 = ((bf16[4,64,1920]{2,1,0:T(8,128)(2,1)}), bf16[4,64,1920]{2,1,0:T(8,128)(2,1)}, u32[]{:S(2)}, u32[]{:S(2)}) async-start(bf16[4,64,1920]{2,1,0:T(8,128)(2,1)} %reduce-scatter.2.cloned.1.call-done), calls=%async_computation.2 | async-start | bytes 1966080 | tf_op jit(solution)/shard_map/all_to_all | solution.py:950
  306.3 14.6 %collective-permute-start.39 = (bf16[80,1536]{1,0:T(8,128)(2,1)}, bf16[80,1536]{1,0:T(8,128)(2,1)S(1)}, u32[]{:S(2)}, u32[]{:S(2)}) collective-permute-start(bf16[80,1536]{1,0:T(8,128)(2,1)} %get-tuple-element.234), channel_id=1, source_target_pairs={{0,2},{2,4},{4,6},{6,0},{1,3},{3,5},{5,7},{7,1},{8,10},{10,12},{12... | collective-permute-start | bytes 737288 | tf_op jit(solution)/shard_map/ppermute | solution.py:55
  309.0 22.4 %collective-permute-start.40 = (bf16[80,1536]{1,0:T(8,128)(2,1)}, bf16[80,1536]{1,0:T(8,128)(2,1)S(1)}, u32[]{:S(2)}, u32[]{:S(2)}) collective-permute-start(bf16[80,1536]{1,0:T(8,128)(2,1)} %get-tuple-element.235), channel_id=1, source_target_pairs={{0,4},{2,6},{4,0},{6,2},{1,5},{3,7},{5,1},{7,3},{8,12},{10,14},{12... | collective-permute-start | bytes 737288 | tf_op jit(solution)/shard_map/ppermute | solution.py:55
  310.8 20.5 %collective-permute-start.41 = (bf16[80,1536]{1,0:T(8,128)(2,1)}, bf16[80,1536]{1,0:T(8,128)(2,1)S(1)}, u32[]{:S(2)}, u32[]{:S(2)}) collective-permute-start(bf16[80,1536]{1,0:T(8,128)(2,1)} %get-tuple-element.236), channel_id=1, source_target_pairs={{0,6},{2,0},{4,2},{6,4},{1,7},{3,1},{5,3},{7,5},{8,14},{10,8},{12,... | collective-permute-start | bytes 737288 | tf_op jit(solution)/shard_map/ppermute | solution.py:55
  333.4 21.5 %copy-start.25 = (f32[1024]{0:T(1024)S(1)}, f32[1024]{0:T(1024)}, u32[]{:S(2)}) copy-start(f32[1024]{0:T(1024)} %param.16) | copy-start | bytes 12292
  333.4 21.5 %copy-start.27 = (f32[2,128]{1,0:T(2,128)S(1)}, f32[2,128]{1,0:T(2,128)}, u32[]{:S(2)}) copy-start(f32[2,128]{1,0:T(2,128)} %copy-done.26) | copy-start | bytes 3076
  335.7 19.1 %copy-start.3 = (bf16[2,128,1024]{2,1,0:T(8,128)(2,1)S(1)}, bf16[2,128,1024]{2,1,0:T(8,128)(2,1)}, u32[]{:S(2)}) copy-start(bf16[2,128,1024]{2,1,0:T(8,128)(2,1)} %param.14) | copy-start | bytes 1572868
  335.7 21.0 %copy-start.5 = (f32[2,128,1024]{2,1,0:T(8,128)S(1)}, f32[2,128,1024]{2,1,0:T(8,128)}, u32[]{:S(2)}) copy-start(f32[2,128,1024]{2,1,0:T(8,128)} %get-tuple-element.191) | copy-start | bytes 3145732
  335.7 21.0 %copy-start.18 = (bf16[2,128,1024]{2,1,0:T(8,128)(2,1)S(1)}, bf16[2,128,1024]{2,1,0:T(8,128)(2,1)}, u32[]{:S(2)}) copy-start(bf16[2,128,1024]{2,1,0:T(8,128)(2,1)} %copy-done.17) | copy-start | bytes 1572868
  335.7 21.0 %copy-start.20 = (bf16[2,128,1024]{2,1,0:T(8,128)(2,1)S(1)}, bf16[2,128,1024]{2,1,0:T(8,128)(2,1)}, u32[]{:S(2)}) copy-start(bf16[2,128,1024]{2,1,0:T(8,128)(2,1)} %copy-done.19) | copy-start | bytes 1572868
  335.8 21.0 %copy-start.22 = (bf16[2,128,1024]{2,1,0:T(8,128)(2,1)S(1)}, bf16[2,128,1024]{2,1,0:T(8,128)(2,1)}, u32[]{:S(2)}) copy-start(bf16[2,128,1024]{2,1,0:T(8,128)(2,1)} %copy-done.21) | copy-start | bytes 1572868
  335.8 21.0 %copy-start.31 = (pred[2,128]{1,0:T(4,128)(4,1)S(1)}, pred[2,128]{1,0:T(4,128)(4,1)}, u32[]{:S(2)}) copy-start(pred[2,128]{1,0:T(4,128)(4,1)} %copy-done.30) | copy-start | bytes 772
  335.8 5.3 %collective-permute-start.43 = (f32[2,1536]{1,0:T(2,128)S(1)}, f32[2,1536]{1,0:T(2,128)S(1)}, u32[]{:S(2)}, u32[]{:S(2)}) collective-permute-start(f32[2,1536]{1,0:T(2,128)S(1)} %add_add_fusion), channel_id=1, source_target_pairs={{0,1},{1,0},{2,3},{3,2},{4,5},{5,4},{6,7},{7,6},{8,9},{9,8},{10,11... | collective-permute-start | bytes 36872 | tf_op jit(solution)/shard_map/ppermute | solution.py:35
  336.6 18.3 %collective-permute-start.42 = (bf16[2,128,1024]{2,1,0:T(8,128)(2,1)}, bf16[2,128,1024]{2,1,0:T(8,128)(2,1)S(1)}, u32[]{:S(2)}, u32[]{:S(2)}) collective-permute-start(bf16[2,128,1024]{2,1,0:T(8,128)(2,1)} %down_add.5), channel_id=1, source_target_pairs={{2,0},{4,2},{6,4},{3,1},{5,3},{7,5},{10,8},{12,10},{14,12},{11,9},... | collective-permute-start | bytes 1572872 | tf_op jit(solution)/shard_map/ppermute | solution.py:50
  (25 other events, 101.5 us)
Sparse Core Ops, SparseCore 0:
  71.6 73.8 all-gather.1
  204.4 70.4 reduce-scatter.1

commit v4 on v3

--- a/solution.py
+++ b/solution.py
@@ -269,7 +269,9 @@
         functools.partial(attend_kernel, len(pieces), parts),
         grid=(slots, pairs),
         in_specs=[smem] + [piece] * len(pieces) + [w_query, w_key, w_value] * 2 + [table, table, gain, gain],
-        out_specs=[query, stat, query, key, key, query, key, pl.BlockSpec((1, keys, model), lambda s, p: (s, 0, 0))],
+        out_specs=[
+            query, stat, query, key, key, query, key, pl.BlockSpec((1, keys, model), lambda s, p: (s, 0, 0)),
+        ],
         out_shape=[
             jax.ShapeDtypeStruct((slots, rows, width), BF),
             jax.ShapeDtypeStruct((slots, pairs, 8, rows), F32),
@@ -321,7 +323,7 @@
     return [1 << i for i in range(8) if 1 << i < size]
 
 
-def weight_kernel(parts, at_ref, x_ref, dq_ref, dk_ref, dv_ref, b_ref, o_ref, w_ref, gain_ref, more_ref, *refs):
+def weight_kernel(parts, at_ref, x_ref, dq_ref, dk_ref, dv_ref, bm_ref, bo_ref, o_ref, w_ref, gain_ref, more_ref, *refs):
     top_send, top_keep, low_send, low_keep, sum_ref = refs
     slots, rows, q_cols = dq_ref.shape
     k_cols = dk_ref.shape[2]
@@ -337,7 +339,7 @@
         query = query + dot(x[:rows], dq_ref[s], TN)
         key = key + dot(x, dk_ref[s], TN)
         value = value + dot(x, dv_ref[s], TN)
-        out = out + dot(b_ref[s], o_ref[s], TN)
+        out = out + dot(jnp.concatenate([bm_ref[s], bo_ref[s]]), o_ref[s], TN)
     total = jnp.concatenate([query, key, value, out], axis=1)
     product = total[:, : q_cols + 2 * k_cols] * w_ref[:, : q_cols + 2 * k_cols].astype(F32)
     ones = jnp.ones((8, q_cols + 2 * k_cols), BF)
@@ -373,7 +375,7 @@
         top_send[parts // 2 * half :, width:] = more_ref[:, width:]
 
 
-def weight_grads(at, x, d_q, d_k, d_v, d_branch, attn, w, gain, more, parts):
+def weight_grads(at, x, d_q, d_k, d_v, d_mine, d_other, attn, w, gain, more, parts):
     slots, keys, width = x.shape
     cols = 2 * d_q.shape[2] + 2 * d_k.shape[2]
     depth = width // parts
@@ -386,7 +388,8 @@
             pl.BlockSpec(d_q.shape, lambda m, at: (0, 0, 0)),
             pl.BlockSpec(d_k.shape, lambda m, at: (0, 0, 0)),
             pl.BlockSpec(d_v.shape, lambda m, at: (0, 0, 0)),
-            pl.BlockSpec(d_branch.shape[:2] + (depth,), lambda m, at: (0, 0, at[0] ^ m)),
+            pl.BlockSpec(d_mine.shape[:2] + (depth,), lambda m, at: (0, 0, at[0] ^ m)),
+            pl.BlockSpec(d_mine.shape[:2] + (depth,), lambda m, at: (0, 0, at[0] ^ m)),
             pl.BlockSpec(attn.shape, lambda m, at: (0, 0, 0)),
             pl.BlockSpec((depth, cols), lambda m, at: (at[0] ^ m, 0)),
             pl.BlockSpec(gain.shape, lambda m, at: (0, 0)),
@@ -402,7 +405,7 @@
         compiler_params=pltpu.CompilerParams(vmem_limit_bytes=VMEM_LIMIT),
         cost_estimate=pl.CostEstimate(flops=10 << 30, bytes_accessed=8 << 20, transcendentals=0),
         name="weight_grads",
-    )(at, x, d_q, d_k, d_v, d_branch, attn, w, gain, more)
+    )(at, x, d_q, d_k, d_v, d_mine, d_other, attn, w, gain, more)
 
 
 def input_kernel(with_own, dq_ref, dk_ref, dv_ref, w_ref, mine_ref, other_ref):
@@ -888,8 +891,9 @@
     )
     d_normed_two = sum(item.astype(F32) for item in held)
     d_middle = grad_rows.astype(F32) + norm_back(middle, ffn_gain, d_normed_two)
-    d_branch = d_middle.astype(BF)
-    d_branch = jnp.concatenate([d_branch, swap_cores(d_branch)], axis=1)
+    d_mine = d_middle.astype(BF)
+    d_other = swap_cores(d_mine)
+    d_branch = jnp.concatenate([d_mine, d_other], axis=1)
     d_attn = jnp.einsum("std,dh->sth", d_branch, out_w, preferred_element_type=F32).astype(BF)
     held = tie(d_attn, *y_sums)
     d_attn = held[0]
@@ -900,16 +904,16 @@
     )
     y_got = traded(y_sums)
 
-    held = tie(d_q, d_k, d_v, gq, gk, d_branch, ffn_gain_row, *y_got)
-    d_q, d_k, d_v, gq, gk, d_branch, ffn_gain_row = held[:7]
-    result = jnp.where(valid, middle + sum(item.astype(F32) for item in held[7:]), 0.0).astype(BF)
+    held = tie(d_q, d_k, d_v, gq, gk, ffn_gain_row, *y_got)
+    d_q, d_k, d_v, gq, gk, ffn_gain_row = held[:6]
+    result = jnp.where(valid, middle + sum(item.astype(F32) for item in held[6:]), 0.0).astype(BF)
 
     heads = jnp.stack([jnp.pad(item[0, :HEAD] + item[0, HEAD:], (0, HEAD)) for item in (gq, gk)])
     small = jnp.stack([jnp.zeros_like(ffn_gain), ffn_gain_row / ffn_gain])
     small = jnp.concatenate([small, heads], axis=1)
     small = jnp.pad(small, ((0, 0), (0, 2 * q_cols + 2 * k_cols - small.shape[1])))
     top_send, top, low_send, low = weight_grads(
-        place, x_all, d_q, d_k, d_v, d_branch, attn, attn_w, attn_gain[None, :], two_parts(small), n_fsdp
+        place, x_all, d_q, d_k, d_v, d_mine, d_other, attn, attn_w, attn_gain[None, :], two_parts(small), n_fsdp
     )
     top_send, top, low_send, low, d_q, d_k, d_v = tie(top_send, top, low_send, low, d_q, d_k, d_v)
 
@@ -917,11 +921,13 @@
     bits = bits_of(n_fsdp)
     own = top_send[n_fsdp // 2 * half :]
     came = [fsdp_xor(top_send, bits[0]), fsdp_xor(low_send, bits[-1])]
-    mine, other = input_grads(d_q, d_k, d_v, attn_w, 0, n_ctx)
-    mine, other, *came = tie(mine, other, *came)
+    last_mine, last_other = input_grads(d_q, d_k, d_v, attn_w, n_ctx - 1, 1)
+    last_other = swap_cores(last_other)
+    mine, other = input_grads(d_q, d_k, d_v, attn_w, 0, n_ctx - 1)
+    mine, other, last_other, *came = tie(mine, other, last_other, *came)
     other = swap_cores(other)
-    block = n_ctx - 1
-    total = None
+    total = ctx_down(down_add(last_mine, last_other, 0))
+    block = n_ctx - 2
     for step in range(1, len(bits)):
         count = n_fsdp >> step
         sent = []
@@ -935,26 +941,22 @@
             sent.append(send)
             kept.append(keep)
         if step == 1:
-            other, mine, *held = tie(other, mine, *sent, *kept)
+            total, other, mine, ffn_reduced, *held = tie(total, other, mine, ffn_reduced, *sent, *kept)
             sent, kept = held[:2], held[2:]
         top, low = kept
         own = sent[0][count // 2 * half :]
         came = [fsdp_xor(sent[0], bits[step]), fsdp_xor(sent[1], bits[-1 - step])]
         if block > 0:
-            total = ctx_down(down_add(mine, other, block, *(() if total is None else (total,))))
+            total = ctx_down(down_add(mine, other, block, total))
             block -= 1
             total, *came = tie(total, *came)
     ctx_place = jnp.stack([f, c]).astype(jnp.int32)
     mine_rows, small, *messages = to_ctx(ctx_place, top, came[0], low, came[1], own, n_ctx)
-    got = [ctx_shift(message, k) for k, message in enumerate(messages, 1)]
-    ffn_parts = lax.all_to_all(ffn_reduced, "fsdp", 0, 0, tiled=True)
-    if block > 0:
-        total = ctx_down(down_add(mine, other, block, total))
-        block -= 1
-        total, ffn_parts, *got = tie(total, ffn_parts, *got)
     while block > 0:
         total = ctx_down(down_add(mine, other, block, total))
         block -= 1
+    got = [ctx_shift(message, k) for k, message in enumerate(messages, 1)]
+    ffn_parts = lax.all_to_all(ffn_reduced, "fsdp", 0, 0, tiled=True)
     total = mine[0] + other[0].astype(F32) + total.astype(F32)
 
     small = [one_part(small)] + [one_part(piece[shard:]) for piece in got]

time: 372 us -> 355 us (0.954)
  waiting for transfers between devices: 108 us -> 89.5 us
  Pallas kernels: 130 us -> 134 us
    ppermute x6, waiting for transfers between devices: 31.3 us -> 18.2 us  [ctx_shift(): lax.ppermute(value, 'ctx', [(i, (i + step) % size) for i in range(size)])]
    ppermute x3, waiting for transfers between devices: 14.1 us -> 8.97 us  [ctx_down(): lax.ppermute(value, 'ctx', [(i + step, i) for i in range(size - step)])]
    pallas_call x1 -> x2, Pallas kernels: 8.01 us -> 11.2 us  [input_grads(): pl.pallas_call(functools.partial(input_kernel, first == 0), grid=(blocks,...]
  transfers between devices with their start and end apart: 48 -> 49, of which waited for: 20 -> 21; matrix products, arithmetic and copies ran while one was open for 9% -> 10% of each run, Pallas kernels for 28% -> 30%
where the time goes in v4:
time: 355 us; the launch traced here: 348 us
  Pallas kernels  134 us (38%)
  waiting for transfers between devices  89.5 us (25%)
  starting transfers between devices  64.5 us (18%)
  other arithmetic  30.8 us (9%)
  between operations  15.3 us (4%)
  local copies, waits for them, and re-layouts  10.7 us (3%)
  matrix products  3.63 us (1%)
    ppermute x20, waiting for transfers between devices, fsdp_xor(): return lax.ppermute(value, 'fsdp', [(i, i ^ mask) for i in range(size)])  41.5 us
    pallas_call x1, Pallas kernels, feed_forward(): pl.pallas_call(ffn_kernel, grid=(grid,), in_specs=[other, mine, other, mi...  26.2 us
    pallas_call x1, Pallas kernels, attend_back(): pl.pallas_call(attend_back_kernel, grid=(slots, pairs), in_specs=[smem, q...  25.5 us
    pallas_call x1, Pallas kernels, attend(): pl.pallas_call(functools.partial(attend_kernel, len(pieces), parts), grid...  23.9 us
    ppermute x20, starting transfers between devices, fsdp_xor(): return lax.ppermute(value, 'fsdp', [(i, i ^ mask) for i in range(size)])  22.5 us
    ppermute x3, starting transfers between devices, ctx_up(): lax.ppermute(value, 'ctx', [(i, i + step) for i in range(size - step)])  19.5 us
    ppermute x6, waiting for transfers between devices, ctx_shift(): lax.ppermute(value, 'ctx', [(i, (i + step) % size) for i in range(size)])  18.2 us
    pallas_call x1, Pallas kernels, ffn_weight_grads(): pl.pallas_call(ffn_weight_kernel, grid=(grid,), in_specs=[other, mine, ot...  17.1 us
  transfers between devices with their start and end apart: 49, of which 21 were waited for; matrix products, arithmetic and copies ran while one was open for 10% of the time, Pallas kernels for 30%

profile of v4, /device:TPU:0, one launch (start us, length us, event | category | flops | bytes accessed | tf_op | source)
XLA Modules:
  0.0 348.1 jit_solution(11061333597450860749)
XLA Ops:
  9.8 5.7 %collective-permute-start = (bf16[2,128,1024]{2,1,0:T(8,128)(2,1)S(1)}, bf16[2,128,1024]{2,1,0:T(8,128)(2,1)}, u32[]{:S(2)}, u32[]{:S(2)}) collective-permute-start(bf16[2,128,1024]{2,1,0:T(8,128)(2,1)S(1)} %fusion.3.refs_0_), channel_id=1, source_target_pairs={{0,2},{2,4},{4,6},{1,3},{3,5},{5,7},{8,10},{10,12},{12,14},{9,11},... | collective-permute-start | bytes 1572872 | tf_op jit(solution)/shard_map/ppermute | solution.py:45
  16.2 1.6 collective-permute-start.2
  17.9 1.6 collective-permute-start.1
  19.4 2.2 pack.1
  21.6 3.7 %all-to-all-start = ((bf16[4,64,1920]{2,1,0:T(8,128)(2,1)}), bf16[4,64,1920]{2,1,0:T(8,128)(2,1)S(1)}, u32[]{:S(2)}, u32[]{:S(2)}) async-start(bf16[4,64,1920]{2,1,0:T(8,128)(2,1)} %pack.1), calls=%async_computation | async-start | bytes 1966080 | tf_op jit(solution)/shard_map/all_to_all | solution.py:826
  25.3 6.0 %collective-permute-done.3 = bf16[64,1536]{1,0:T(8,128)(2,1)S(1)} collective-permute-done((bf16[64,1536]{1,0:T(8,128)(2,1)S(1)}, bf16[64,1536]{1,0:T(8,128)(2,1)S(1)}, u32[]{:S(2)}, u32[]{:S(2)}) %collective-permute-start.3) | collective-permute-done | bytes 196640 | tf_op jit(solution)/shard_map/ppermute | solution.py:55
  31.3 4.2 %collective-permute-done.2 = bf16[64,1536]{1,0:T(8,128)(2,1)S(1)} collective-permute-done((bf16[64,1536]{1,0:T(8,128)(2,1)S(1)}, bf16[64,1536]{1,0:T(8,128)(2,1)S(1)}, u32[]{:S(2)}, u32[]{:S(2)}) %collective-permute-start.2) | collective-permute-done | bytes 196640 | tf_op jit(solution)/shard_map/ppermute | solution.py:55
  35.5 3.1 collective-permute-done.1
  38.8 1.6 collective-permute-start.10
  40.4 1.6 collective-permute-start.12
  42.0 8.5 %collective-permute-start.4 = (bf16[2,128,1024]{2,1,0:T(8,128)(2,1)}, bf16[2,128,1024]{2,1,0:T(8,128)(2,1)}, u32[]{:S(2)}, u32[]{:S(2)}) collective-permute-start(bf16[2,128,1024]{2,1,0:T(8,128)(2,1)} %collective-permute-done.refs_2_), channel_id=1, source_target_pairs={{0,2},{2,4},{4,6},{1,3},{3,5},{5,7},{8,10},{10,12},{12,14},{9,11},... | collective-permute-start | bytes 1572872 | tf_op jit(solution)/shard_map/ppermute | solution.py:45
  53.9 5.9 %collective-permute-done.4.refs_4_ = bf16[2,128,1024]{2,1,0:T(8,128)(2,1)} collective-permute-done((bf16[2,128,1024]{2,1,0:T(8,128)(2,1)}, bf16[2,128,1024]{2,1,0:T(8,128)(2,1)}, u32[]{:S(2)}, u32[]{:S(2)}) %collective-permute-start.4) | collective-permute-done | bytes 524320 | tf_op jit(solution)/shard_map/ppermute | solution.py:45
  59.8 5.2 %collective-permute-start.5 = (bf16[2,128,1024]{2,1,0:T(8,128)(2,1)}, bf16[2,128,1024]{2,1,0:T(8,128)(2,1)}, u32[]{:S(2)}, u32[]{:S(2)}) collective-permute-start(bf16[2,128,1024]{2,1,0:T(8,128)(2,1)} %collective-permute-done.4.refs_4_), channel_id=1, source_target_pairs={{0,2},{2,4},{4,6},{1,3},{3,5},{5,7},{8,10},{10,12},{12,14},{9,11},... | collective-permute-start | bytes 1572872 | tf_op jit(solution)/shard_map/ppermute | solution.py:45
  67.9 3.1 fusion.21
  71.6 1.7 collective-permute-done.5.refs_6_
  73.8 1.3 pad_maximum_fusion.3.refs_8_.refs_9_.refs_10_
  75.1 1.9 pad_maximum_fusion.4.refs_11_.refs_12_.refs_13_
  77.6 1.5 collective-permute-start.15
  79.1 1.5 collective-permute-start.14
  81.3 23.9 %attend.1 = (bf16[2,256,512]{2,1,0:T(8,128)(2,1)}, f32[2,2,8,256]{3,2,1,0:T(8,128)}, f32[2,256,512]{2,1,0:T(8,128)}, f32[2,1024,256]{2,1,0:T(8,128)}, bf16[2,102...) custom-call(s32[5]{0:T(128)} %pad_add_fusion.scal_ref, ...), custom_call_target="tpu_custom_call" | custom-call | flops 1048576 | bytes 1048576 | tf_op jit(solution)/shard_map/attend/pallas_call | solution.py:268
  107.3 2.6 collective-permute-done.17
  111.5 2.5 collective-permute-start.20
  114.0 1.6 pad_maximum_fusion.2
  115.7 8.7 %collective-permute-done.19 = bf16[2,128,1024]{2,1,0:T(8,128)(2,1)S(1)} collective-permute-done((bf16[2,128,1024]{2,1,0:T(8,128)(2,1)S(1)}, bf16[2,128,1024]{2,1,0:T(8,128)(2,1)S(1)}, u32[]{:S(2)}, u32[]{:S(2)}) %collective-permute-start.19) | collective-permute-done | bytes 524320 | tf_op jit(solution)/shard_map/ppermute | solution.py:40
  124.4 1.3 collective-permute-done.18
  125.8 11.1 %collective-permute-done.20 = bf16[2,128,1024]{2,1,0:T(8,128)(2,1)S(1)} collective-permute-done((bf16[2,128,1024]{2,1,0:T(8,128)(2,1)S(1)}, bf16[2,128,1024]{2,1,0:T(8,128)(2,1)S(1)}, u32[]{:S(2)}, u32[]{:S(2)}) %collective-permute-start.20) | collective-permute-done | bytes 524320 | tf_op jit(solution)/shard_map/ppermute | solution.py:40
  136.9 1.6 pad_maximum_fusion.1
  138.5 7.1 %all-gather.2.cloned.1.call-done = bf16[4,256,1920]{2,1,0:T(8,128)(2,1)} async-done(((bf16[4,64,1920]{2,1,0:T(8,128)(2,1)}), bf16[4,256,1920]{2,1,0:T(8,128)(2,1)}) %all-gather.2.cloned.1.call-update) | async-done | bytes 3932176 | tf_op jit(solution)/shard_map/all_gather | solution.py:838
  145.6 26.2 %feed_forward.1 = (bf16[1024,1024]{1,0:T(8,128)(2,1)}, bf16[1024,1024]{1,0:T(8,128)(2,1)}, bf16[1024,1024]{1,0:T(8,128)(2,1)}, bf16[1024,1024]{1,0:T(8,128)(2,1)...) custom-call(bf16[1024,1024]{1,0:T(8,128)(2,1)} %bitcast.25.xo_ref, bf16[1024,1024]{1,0:T(8,128)(2,1)} %bitcast.26.xm_ref, ...), custom_call_target="tpu_custom_call" | custom-call | flops 16106127360 | bytes 25165824 | tf_op jit(solution)/shard_map/feed_forward/pallas_call | solution.py:627
  172.4 1.9 fusion.48
  174.8 1.5 collective-permute-done.23
  177.2 1.5 collective-permute-start.25
  178.7 1.5 collective-permute-start.26
  180.7 2.2 fusion.13
  182.9 17.1 %ffn_weight_grads.1 = bf16[1024,1920]{1,0:T(8,128)(2,1)} custom-call(bf16[1024,1024]{1,0:T(8,128)(2,1)} %bitcast.25.xo_ref, bf16[1024,1024]{1,0:T(8,128)(2,1)} %bitcast.26.xm_ref, bf16[1024,1024]{1,0:T(8,128)(2,1)} %bitcast.31.go_ref, bf16[1024,1024]{1,0:T(8,128)(2,1)} %bitcast.32.gm_ref, bf16[2048,1920]{1,0:T(8,128)(2,1)} %get-tuple-element.166.inner_ref), custom_call_target="tpu_custom_call" | custom-call | flops 17179869184 | bytes 25165824 | tf_op jit(solution)/shard_map/ffn_weight_grads/pallas_call | solution.py:649
  200.0 3.6 %collective-permute-done.26 = bf16[2,128,1024]{2,1,0:T(8,128)(2,1)S(1)} collective-permute-done((bf16[2,128,1024]{2,1,0:T(8,128)(2,1)S(1)}, bf16[2,128,1024]{2,1,0:T(8,128)(2,1)S(1)}, u32[]{:S(2)}, u32[]{:S(2)}) %collective-permute-start.26) | collective-permute-done | bytes 524320 | tf_op jit(solution)/shard_map/ppermute | solution.py:40
  204.5 2.0 collective-permute-done.28.bo_ref
  206.5 2.9 convolution_convert_fusion.d_ref
  211.4 1.4 collective-permute-start.31
  212.9 25.5 %attend_back.1 = (bf16[2,256,512]{2,1,0:T(8,128)(2,1)}, bf16[2,1024,256]{2,1,0:T(8,128)(2,1)}, bf16[2,1024,256]{2,1,0:T(8,128)(2,1)}, f32[1,128]{1,0:T(1,128)}, f32[1,128]{1,0:T(1,128)}) custom-call(s32[5]{0:T(128)} %pad_add_fusion.scal_ref, f32[2,256,512]{2,1,0:T(8,128)} %get-tuple-element.149.q_ref, f32[2,1024,256]{2,1,0:T(8,128)} %get-tuple-element.150.k_ref, ...), custom_call_target="tpu_custom_call" | custom-call | flops 25769803776 | bytes 12582912 | tf_op jit(solution)/shard_map/attend_back/pallas_call | solution.py:301
  240.7 10.7 %weight_grads.1 = (bf16[272,1536]{1,0:T(8,128)(2,1)}, bf16[256,1536]{1,0:T(8,128)(2,1)}, bf16[256,1536]{1,0:T(8,128)(2,1)}, bf16[256,1536]{1,0:T(8,128)(2,1)}) custom-call(s32[1]{0:T(128)} %bitcast.2.at_ref, bf16[2,1024,1024]{2,1,0:T(8,128)(2,1)} %get-tuple-element.194.x_ref, bf16[2,256,512]{2,1,0:T(8,128)(2,1)} %get-tuple-element.205.dq_ref, ...), custom_call_target="tpu_custom_call" | custom-call | flops 10737418240 | bytes 8388608 | tf_op jit(solution)/shard_map/weight_grads/pallas_call | solution.py:401
  251.5 1.6 collective-permute-start.34
  253.7 4.1 %input_grads.2 = (f32[1,2,128,1024]{3,2,1,0:T(8,128)}, bf16[1,2,128,1024]{3,2,1,0:T(8,128)(2,1)}) custom-call(bf16[2,256,512]{2,1,0:T(8,128)(2,1)} %get-tuple-element.205.dq_ref, bf16[2,1024,256]{2,1,0:T(8,128)(2,1)} %get-tuple-element.206.dk_ref, bf16[2,1024,256]{2,1,0:T(8,128)(2,1)} %get-tuple-element.207.dv_ref, bf16[1024,1536]{1,0:T(8,128)(2,1)} %bitcast.142), custom_call_target="tpu_custom_call" | custom-call | flops 6442450944 | bytes 1048576 | tf_op jit(solution)/shard_map/input_grads/pallas_call | solution.py:435
  257.7 1.4 slice.220.refs_0_
  259.1 7.1 %input_grads.3 = (f32[3,2,128,1024]{3,2,1,0:T(8,128)}, bf16[3,2,128,1024]{3,2,1,0:T(8,128)(2,1)}) custom-call(bf16[2,256,512]{2,1,0:T(8,128)(2,1)} %get-tuple-element.205.dq_ref, bf16[2,1024,256]{2,1,0:T(8,128)(2,1)} %get-tuple-element.206.dk_ref, bf16[2,1024,256]{2,1,0:T(8,128)(2,1)} %get-tuple-element.207.dv_ref, bf16[1024,1536]{1,0:T(8,128)(2,1)} %bitcast.143), custom_call_target="tpu_custom_call" | custom-call | flops 6442450944 | bytes 1048576 | tf_op jit(solution)/shard_map/input_grads/pallas_call | solution.py:435
  266.2 4.3 %collective-permute-done.34.came_ref = bf16[256,1536]{1,0:T(8,128)(2,1)S(1)} collective-permute-done((bf16[256,1536]{1,0:T(8,128)(2,1)}, bf16[256,1536]{1,0:T(8,128)(2,1)S(1)}, u32[]{:S(2)}, u32[]{:S(2)}) %collective-permute-start.34) | collective-permute-done | bytes 786464 | tf_op jit(solution)/shard_map/ppermute | solution.py:40
  270.6 2.2 collective-permute-done.33.came_ref
  272.8 2.4 down_add.3
  276.6 2.3 half_sum.3
  278.9 2.5 half_sum.2
  281.4 8.1 %collective-permute-done.35.refs_2_ = bf16[2,128,1024]{2,1,0:T(8,128)(2,1)} collective-permute-done((bf16[2,128,1024]{2,1,0:T(8,128)(2,1)}, bf16[2,128,1024]{2,1,0:T(8,128)(2,1)}, u32[]{:S(2)}, u32[]{:S(2)}) %collective-permute-start.35) | collective-permute-done | bytes 524320 | tf_op jit(solution)/shard_map/ppermute | solution.py:50
  289.5 2.3 down_add.4
  296.1 4.2 %all-to-all-start.1 = ((bf16[4,64,1920]{2,1,0:T(8,128)(2,1)}), bf16[4,64,1920]{2,1,0:T(8,128)(2,1)}, u32[]{:S(2)}, u32[]{:S(2)}) async-start(bf16[4,64,1920]{2,1,0:T(8,128)(2,1)} %reduce-scatter.2.cloned.1.call-done), calls=%async_computation.2 | async-start | bytes 1966080 | tf_op jit(solution)/shard_map/all_to_all | solution.py:959
  300.4 4.1 %collective-permute-done.39.low_came = bf16[128,1536]{1,0:T(8,128)(2,1)} collective-permute-done((bf16[128,1536]{1,0:T(8,128)(2,1)}, bf16[128,1536]{1,0:T(8,128)(2,1)}, u32[]{:S(2)}, u32[]{:S(2)}) %collective-permute-start.39) | collective-permute-done | bytes 393248 | tf_op jit(solution)/shard_map/ppermute | solution.py:40
  304.4 6.0 %collective-permute-done.38.top_came = bf16[144,1536]{1,0:T(8,128)(2,1)S(1)} collective-permute-done((bf16[144,1536]{1,0:T(8,128)(2,1)S(1)}, bf16[144,1536]{1,0:T(8,128)(2,1)S(1)}, u32[]{:S(2)}, u32[]{:S(2)}) %collective-permute-start.38) | collective-permute-done | bytes 442400 | tf_op jit(solution)/shard_map/ppermute | solution.py:40
  311.2 2.6 to_ctx.1
  314.8 2.0 collective-permute-start.42
  316.8 1.8 collective-permute-start.43
  318.6 2.3 down_add.5
  320.9 1.4 collective-permute-start.40
  322.4 2.4 finish.1
  324.8 4.5 %collective-permute-done.41 = bf16[80,1536]{1,0:T(8,128)(2,1)} collective-permute-done((bf16[80,1536]{1,0:T(8,128)(2,1)}, bf16[80,1536]{1,0:T(8,128)(2,1)}, u32[]{:S(2)}, u32[]{:S(2)}) %collective-permute-start.41) | collective-permute-done | bytes 245792 | tf_op jit(solution)/shard_map/ppermute | solution.py:55
  335.4 2.0 fusion.4
  337.5 3.4 fusion.8
  (214 shorter events, 37.4 us)
Async XLA Ops:
  8.5 13.1 %copy-start.31 = (f32[2,128]{1,0:T(2,128)}, f32[2,128]{1,0:T(2,128)S(1)}, u32[]{:S(2)}) copy-start(f32[2,128]{1,0:T(2,128)S(1)} %add_rsqrt_fusion.1) | copy-start | bytes 3076
  9.8 61.3 %copy-start.7 = (bf16[2,128,1024]{2,1,0:T(8,128)(2,1)}, bf16[2,128,1024]{2,1,0:T(8,128)(2,1)S(1)}, u32[]{:S(2)}) copy-start(bf16[2,128,1024]{2,1,0:T(8,128)(2,1)S(1)} %fusion.3.refs_0_) | copy-start | bytes 1572868
  9.8 28.8 %collective-permute-start = (bf16[2,128,1024]{2,1,0:T(8,128)(2,1)S(1)}, bf16[2,128,1024]{2,1,0:T(8,128)(2,1)}, u32[]{:S(2)}, u32[]{:S(2)}) collective-permute-start(bf16[2,128,1024]{2,1,0:T(8,128)(2,1)S(1)} %fusion.3.refs_0_), channel_id=1, source_target_pairs={{0,2},{2,4},{4,6},{1,3},{3,5},{5,7},{8,10},{10,12},{12,14},{9,11},... | collective-permute-start | bytes 1572872 | tf_op jit(solution)/shard_map/ppermute | solution.py:45
  15.5 15.8 %collective-permute-start.3 = (bf16[64,1536]{1,0:T(8,128)(2,1)S(1)}, bf16[64,1536]{1,0:T(8,128)(2,1)S(1)}, u32[]{:S(2)}, u32[]{:S(2)}) collective-permute-start(bf16[64,1536]{1,0:T(8,128)(2,1)S(1)} %pad_maximum_fusion.7), channel_id=1, source_target_pairs={{0,6},{2,0},{4,2},{6,4},{1,7},{3,1},{5,3},{7,5},{8,14},{10,8},{12,... | collective-permute-start | bytes 589832 | tf_op jit(solution)/shard_map/ppermute | solution.py:55
  16.2 19.3 %collective-permute-start.2 = (bf16[64,1536]{1,0:T(8,128)(2,1)S(1)}, bf16[64,1536]{1,0:T(8,128)(2,1)S(1)}, u32[]{:S(2)}, u32[]{:S(2)}) collective-permute-start(bf16[64,1536]{1,0:T(8,128)(2,1)S(1)} %pad_maximum_fusion.7), channel_id=1, source_target_pairs={{0,4},{2,6},{4,0},{6,2},{1,5},{3,7},{5,1},{7,3},{8,12},{10,14},{12... | collective-permute-start | bytes 589832 | tf_op jit(solution)/shard_map/ppermute | solution.py:55
  17.9 20.7 %collective-permute-start.1 = (bf16[64,1536]{1,0:T(8,128)(2,1)S(1)}, bf16[64,1536]{1,0:T(8,128)(2,1)S(1)}, u32[]{:S(2)}, u32[]{:S(2)}) collective-permute-start(bf16[64,1536]{1,0:T(8,128)(2,1)S(1)} %pad_maximum_fusion.7), channel_id=1, source_target_pairs={{0,2},{2,4},{4,6},{6,0},{1,3},{3,5},{5,7},{7,1},{8,10},{10,12},{12... | collective-permute-start | bytes 589832 | tf_op jit(solution)/shard_map/ppermute | solution.py:55
  21.6 32.3 %all-to-all-start = ((bf16[4,64,1920]{2,1,0:T(8,128)(2,1)}), bf16[4,64,1920]{2,1,0:T(8,128)(2,1)S(1)}, u32[]{:S(2)}, u32[]{:S(2)}) async-start(bf16[4,64,1920]{2,1,0:T(8,128)(2,1)} %pack.1), calls=%async_computation | async-start | bytes 1966080 | tf_op jit(solution)/shard_map/all_to_all | solution.py:826
  25.3 120.3 %all-gather.2.cloned.1.call-start = ((), (), s32[]{:S(2)}) async-start(), calls=%async_computation.3 | async-start | bytes 4915200 | tf_op jit(solution)/shard_map/all_gather | solution.py:838
  38.8 11.8 %collective-permute-start.10 = (bf16[1,128,1536]{2,1,0:T(8,128)(2,1)S(1)}, bf16[1,128,1536]{2,1,0:T(8,128)(2,1)S(1)}, u32[]{:S(2)}, u32[]{:S(2)}) collective-permute-start(bf16[1,128,1536]{2,1,0:T(8,128)(2,1)S(1)} %bitcast.148), channel_id=1, source_target_pairs={{0,8},{8,0},{16,24},{24,16},{1,9},{9,1},{17,25},{25,17},{2,10},{10... | collective-permute-start | bytes 1179656 | tf_op jit(solution)/shard_map/ppermute | solution.py:40
  40.4 11.7 %collective-permute-start.12 = (bf16[1,128,1536]{2,1,0:T(8,128)(2,1)S(1)}, bf16[1,128,1536]{2,1,0:T(8,128)(2,1)S(1)}, u32[]{:S(2)}, u32[]{:S(2)}) collective-permute-start(bf16[1,128,1536]{2,1,0:T(8,128)(2,1)S(1)} %bitcast.145), channel_id=1, source_target_pairs={{0,16},{8,24},{16,0},{24,8},{1,17},{9,25},{17,1},{25,9},{2,18},{10... | collective-permute-start | bytes 1179656 | tf_op jit(solution)/shard_map/ppermute | solution.py:40
  42.0 24.8 %copy-start.35 = (pred[2,128]{1,0:T(4,128)(4,1)}, pred[2,128]{1,0:T(4,128)(4,1)S(1)}, u32[]{:S(2)}) copy-start(pred[2,128]{1,0:T(4,128)(4,1)S(1)} %broadcast_compare_fusion) | copy-start | bytes 772
  42.0 17.7 %collective-permute-start.4 = (bf16[2,128,1024]{2,1,0:T(8,128)(2,1)}, bf16[2,128,1024]{2,1,0:T(8,128)(2,1)}, u32[]{:S(2)}, u32[]{:S(2)}) collective-permute-start(bf16[2,128,1024]{2,1,0:T(8,128)(2,1)} %collective-permute-done.refs_2_), channel_id=1, source_target_pairs={{0,2},{2,4},{4,6},{1,3},{3,5},{5,7},{8,10},{10,12},{12,14},{9,11},... | collective-permute-start | bytes 1572872 | tf_op jit(solution)/shard_map/ppermute | solution.py:45
  50.6 15.0 %copy-start.42 = (f32[64]{0:T(128)S(1)}, f32[64]{0:T(128)}, u32[]{:S(2)}) copy-start(f32[64]{0:T(128)} %param.17) | copy-start | bytes 772
  50.6 15.6 %copy-start.43 = (f32[64]{0:T(128)S(1)}, f32[64]{0:T(128)}, u32[]{:S(2)}) copy-start(f32[64]{0:T(128)} %param.18) | copy-start | bytes 772
  51.5 21.8 %collective-permute-start.11 = (bf16[2,128,1536]{2,1,0:T(8,128)(2,1)}, bf16[2,128,1536]{2,1,0:T(8,128)(2,1)}, u32[]{:S(2)}, u32[]{:S(2)}) collective-permute-start(bf16[2,128,1536]{2,1,0:T(8,128)(2,1)} %pad_maximum_fusion.5), channel_id=1, source_target_pairs={{0,16},{8,24},{16,0},{24,8},{1,17},{9,25},{17,1},{25,9},{2,18},{10... | collective-permute-start | bytes 2359304 | tf_op jit(solution)/shard_map/ppermute | solution.py:40
  52.0 14.7 %copy-start.9 = (bf16[1,128,1536]{2,1,0:T(8,128)(2,1)}, bf16[1,128,1536]{2,1,0:T(8,128)(2,1)S(1)}, u32[]{:S(2)}) copy-start(bf16[1,128,1536]{2,1,0:T(8,128)(2,1)S(1)} %collective-permute-done.12) | copy-start | bytes 1179652
  53.1 22.0 %collective-permute-start.13 = (bf16[2,128,1536]{2,1,0:T(8,128)(2,1)}, bf16[2,128,1536]{2,1,0:T(8,128)(2,1)}, u32[]{:S(2)}, u32[]{:S(2)}) collective-permute-start(bf16[2,128,1536]{2,1,0:T(8,128)(2,1)} %pad_maximum_fusion.6), channel_id=1, source_target_pairs={{0,8},{8,0},{16,24},{24,16},{1,9},{9,1},{17,25},{25,17},{2,10},{10... | collective-permute-start | bytes 2359304 | tf_op jit(solution)/shard_map/ppermute | solution.py:40
  53.9 17.7 %copy-start.6 = (bf16[4,64,1920]{2,1,0:T(8,128)(2,1)}, bf16[4,64,1920]{2,1,0:T(8,128)(2,1)S(1)}, u32[]{:S(2)}) copy-start(bf16[4,64,1920]{2,1,0:T(8,128)(2,1)S(1)} %all-to-all-done) | copy-start | bytes 2949124
  59.8 13.5 %collective-permute-start.5 = (bf16[2,128,1024]{2,1,0:T(8,128)(2,1)}, bf16[2,128,1024]{2,1,0:T(8,128)(2,1)}, u32[]{:S(2)}, u32[]{:S(2)}) collective-permute-start(bf16[2,128,1024]{2,1,0:T(8,128)(2,1)} %collective-permute-done.4.refs_4_), channel_id=1, source_target_pairs={{0,2},{2,4},{4,6},{1,3},{3,5},{5,7},{8,10},{10,12},{12,14},{9,11},... | collective-permute-start | bytes 1572872 | tf_op jit(solution)/shard_map/ppermute | solution.py:45
  71.0 6.0 %collective-permute-start.7 = (bf16[2,128,1024]{2,1,0:T(8,128)(2,1)}, bf16[2,128,1024]{2,1,0:T(8,128)(2,1)}, u32[]{:S(2)}, u32[]{:S(2)}) collective-permute-start(bf16[2,128,1024]{2,1,0:T(8,128)(2,1)} %collective-permute-done.refs_2_), channel_id=1, source_target_pairs={{0,1},{1,0},{2,3},{3,2},{4,5},{5,4},{6,7},{7,6},{8,9},{9,8},{10,11... | collective-permute-start | bytes 1572872 | tf_op jit(solution)/shard_map/ppermute | solution.py:35
  71.0 6.0 %collective-permute-start.6 = (bf16[2,128,1024]{2,1,0:T(8,128)(2,1)S(1)}, bf16[2,128,1024]{2,1,0:T(8,128)(2,1)}, u32[]{:S(2)}, u32[]{:S(2)}) collective-permute-start(bf16[2,128,1024]{2,1,0:T(8,128)(2,1)S(1)} %fusion.3.refs_0_), channel_id=1, source_target_pairs={{0,1},{1,0},{2,3},{3,2},{4,5},{5,4},{6,7},{7,6},{8,9},{9,8},{10,11... | collective-permute-start | bytes 1572872 | tf_op jit(solution)/shard_map/ppermute | solution.py:35
  71.6 217.9 %reduce-scatter.2.cloned.1.call-start = ((), (), s32[]{:S(2)}) async-start(), calls=%async_computation.4 | async-start | bytes 4915200 | tf_op jit(solution)/shard_map/reduce_scatter | solution.py:889
  73.3 3.8 %collective-permute-start.8 = (bf16[2,128,1024]{2,1,0:T(8,128)(2,1)}, bf16[2,128,1024]{2,1,0:T(8,128)(2,1)S(1)}, u32[]{:S(2)}, u32[]{:S(2)}) collective-permute-start(bf16[2,128,1024]{2,1,0:T(8,128)(2,1)} %collective-permute-done.4.refs_4_), channel_id=1, source_target_pairs={{0,1},{1,0},{2,3},{3,2},{4,5},{5,4},{6,7},{7,6},{8,9},{9,8},{10,11... | collective-permute-start | bytes 1572872 | tf_op jit(solution)/shard_map/ppermute | solution.py:35
  73.3 3.8 %collective-permute-start.9 = (bf16[2,128,1024]{2,1,0:T(8,128)(2,1)}, bf16[2,128,1024]{2,1,0:T(8,128)(2,1)S(1)}, u32[]{:S(2)}, u32[]{:S(2)}) collective-permute-start(bf16[2,128,1024]{2,1,0:T(8,128)(2,1)} %collective-permute-done.5.refs_6_), channel_id=1, source_target_pairs={{0,1},{1,0},{2,3},{3,2},{4,5},{5,4},{6,7},{7,6},{8,9},{9,8},{10,11... | collective-permute-start | bytes 1572872 | tf_op jit(solution)/shard_map/ppermute | solution.py:35
  77.1 28.4 %collective-permute-start.16 = (bf16[2,128,1024]{2,1,0:T(8,128)(2,1)S(1)}, bf16[2,128,1024]{2,1,0:T(8,128)(2,1)S(1)}, u32[]{:S(2)}, u32[]{:S(2)}) collective-permute-start(bf16[2,128,1024]{2,1,0:T(8,128)(2,1)S(1)} %broadcast_select_fusion), channel_id=1, source_target_pairs={{0,24},{8,16},{16,8},{24,0},{1,25},{9,17},{17,9},{25,1},{2,26},{10... | collective-permute-start | bytes 1572872 | tf_op jit(solution)/shard_map/ppermute | solution.py:40
  77.6 27.9 %collective-permute-start.15 = (bf16[2,128,1024]{2,1,0:T(8,128)(2,1)S(1)}, bf16[2,128,1024]{2,1,0:T(8,128)(2,1)S(1)}, u32[]{:S(2)}, u32[]{:S(2)}) collective-permute-start(bf16[2,128,1024]{2,1,0:T(8,128)(2,1)S(1)} %broadcast_select_fusion), channel_id=1, source_target_pairs={{0,16},{8,24},{16,0},{24,8},{1,17},{9,25},{17,1},{25,9},{2,18},{10... | collective-permute-start | bytes 1572872 | tf_op jit(solution)/shard_map/ppermute | solution.py:40
  79.1 26.4 %collective-permute-start.14 = (bf16[2,128,1024]{2,1,0:T(8,128)(2,1)S(1)}, bf16[2,128,1024]{2,1,0:T(8,128)(2,1)S(1)}, u32[]{:S(2)}, u32[]{:S(2)}) collective-permute-start(bf16[2,128,1024]{2,1,0:T(8,128)(2,1)S(1)} %broadcast_select_fusion), channel_id=1, source_target_pairs={{0,8},{8,0},{16,24},{24,16},{1,9},{9,1},{17,25},{25,17},{2,10},{10... | collective-permute-start | bytes 1572872 | tf_op jit(solution)/shard_map/ppermute | solution.py:40
  107.2 2.7 collective-permute-start.17
  110.4 14.0 %collective-permute-start.19 = (bf16[2,128,1024]{2,1,0:T(8,128)(2,1)S(1)}, bf16[2,128,1024]{2,1,0:T(8,128)(2,1)S(1)}, u32[]{:S(2)}, u32[]{:S(2)}) collective-permute-start(bf16[2,128,1024]{2,1,0:T(8,128)(2,1)S(1)} %multiply_convert_fusion), channel_id=1, source_target_pairs={{0,16},{8,24},{16,0},{24,8},{1,17},{9,25},{17,1},{25,9},{2,18},{10... | collective-permute-start | bytes 1572872 | tf_op jit(solution)/shard_map/ppermute | solution.py:40
  110.9 14.8 %collective-permute-start.18 = (bf16[2,128,1024]{2,1,0:T(8,128)(2,1)S(1)}, bf16[2,128,1024]{2,1,0:T(8,128)(2,1)S(1)}, u32[]{:S(2)}, u32[]{:S(2)}) collective-permute-start(bf16[2,128,1024]{2,1,0:T(8,128)(2,1)S(1)} %multiply_convert_fusion), channel_id=1, source_target_pairs={{0,8},{8,0},{16,24},{24,16},{1,9},{9,1},{17,25},{25,17},{2,10},{10... | collective-permute-start | bytes 1572872 | tf_op jit(solution)/shard_map/ppermute | solution.py:40
  111.5 25.4 %collective-permute-start.20 = (bf16[2,128,1024]{2,1,0:T(8,128)(2,1)S(1)}, bf16[2,128,1024]{2,1,0:T(8,128)(2,1)S(1)}, u32[]{:S(2)}, u32[]{:S(2)}) collective-permute-start(bf16[2,128,1024]{2,1,0:T(8,128)(2,1)S(1)} %multiply_convert_fusion), channel_id=1, source_target_pairs={{0,24},{8,16},{16,8},{24,0},{1,25},{9,17},{17,9},{25,1},{2,26},{10... | collective-permute-start | bytes 1572872 | tf_op jit(solution)/shard_map/ppermute | solution.py:40
  115.5 30.0 %collective-permute-start.22 = (bf16[4,2,128,1024]{3,2,1,0:T(8,128)(2,1)}, bf16[4,2,128,1024]{3,2,1,0:T(8,128)(2,1)}, u32[]{:S(2)}, u32[]{:S(2)}) collective-permute-start(bf16[4,2,128,1024]{3,2,1,0:T(8,128)(2,1)} %pad_maximum_fusion.2), channel_id=1, source_target_pairs={{0,1},{1,0},{2,3},{3,2},{4,5},{5,4},{6,7},{7,6},{8,9},{9,8},{10,11... | collective-permute-start | bytes 6291464 | tf_op jit(solution)/shard_map/ppermute | solution.py:35
  138.5 7.1 %collective-permute-start.21 = (bf16[4,2,128,1024]{3,2,1,0:T(8,128)(2,1)}, bf16[4,2,128,1024]{3,2,1,0:T(8,128)(2,1)}, u32[]{:S(2)}, u32[]{:S(2)}) collective-permute-start(bf16[4,2,128,1024]{3,2,1,0:T(8,128)(2,1)} %pad_maximum_fusion.1), channel_id=1, source_target_pairs={{0,1},{1,0},{2,3},{3,2},{4,5},{5,4},{6,7},{7,6},{8,9},{9,8},{10,11... | collective-permute-start | bytes 6291464 | tf_op jit(solution)/shard_map/ppermute | solution.py:35
  171.8 4.4 %collective-permute-start.23 = (bf16[4,2,128,1024]{3,2,1,0:T(8,128)(2,1)}, bf16[4,2,128,1024]{3,2,1,0:T(8,128)(2,1)S(1)}, u32[]{:S(2)}, u32[]{:S(2)}) collective-permute-start(bf16[4,2,128,1024]{3,2,1,0:T(8,128)(2,1)} %bitcast.174), channel_id=1, source_target_pairs={{0,1},{1,0},{2,3},{3,2},{4,5},{5,4},{6,7},{7,6},{8,9},{9,8},{10,11... | collective-permute-start | bytes 6291464 | tf_op jit(solution)/shard_map/ppermute | solution.py:35
  171.9 8.9 %collective-permute-start.24 = (bf16[4,2,128,1024]{3,2,1,0:T(8,128)(2,1)}, bf16[4,2,128,1024]{3,2,1,0:T(8,128)(2,1)S(1)}, u32[]{:S(2)}, u32[]{:S(2)}) collective-permute-start(bf16[4,2,128,1024]{3,2,1,0:T(8,128)(2,1)} %bitcast.173), channel_id=1, source_target_pairs={{0,1},{1,0},{2,3},{3,2},{4,5},{5,4},{6,7},{7,6},{8,9},{9,8},{10,11... | collective-permute-start | bytes 6291464 | tf_op jit(solution)/shard_map/ppermute | solution.py:35
  177.2 22.9 %collective-permute-start.25 = (bf16[2,128,1024]{2,1,0:T(8,128)(2,1)S(1)}, bf16[2,128,1024]{2,1,0:T(8,128)(2,1)S(1)}, u32[]{:S(2)}, u32[]{:S(2)}) collective-permute-start(bf16[2,128,1024]{2,1,0:T(8,128)(2,1)S(1)} %get-tuple-element.168), channel_id=1, source_target_pairs={{0,8},{8,0},{16,24},{24,16},{1,9},{9,1},{17,25},{25,17},{2,10},{10... | collective-permute-start | bytes 1572872 | tf_op jit(solution)/shard_map/ppermute | solution.py:40
  178.7 24.9 %collective-permute-start.26 = (bf16[2,128,1024]{2,1,0:T(8,128)(2,1)S(1)}, bf16[2,128,1024]{2,1,0:T(8,128)(2,1)S(1)}, u32[]{:S(2)}, u32[]{:S(2)}) collective-permute-start(bf16[2,128,1024]{2,1,0:T(8,128)(2,1)S(1)} %get-tuple-element.169), channel_id=1, source_target_pairs={{0,16},{8,24},{16,0},{24,8},{1,17},{9,25},{17,1},{25,9},{2,18},{10... | collective-permute-start | bytes 1572872 | tf_op jit(solution)/shard_map/ppermute | solution.py:40
  180.2 23.4 %collective-permute-start.27 = (bf16[2,128,1024]{2,1,0:T(8,128)(2,1)S(1)}, bf16[2,128,1024]{2,1,0:T(8,128)(2,1)S(1)}, u32[]{:S(2)}, u32[]{:S(2)}) collective-permute-start(bf16[2,128,1024]{2,1,0:T(8,128)(2,1)S(1)} %get-tuple-element.170), channel_id=1, source_target_pairs={{0,24},{8,16},{16,8},{24,0},{1,25},{9,17},{17,9},{25,1},{2,26},{10... | collective-permute-start | bytes 1572872 | tf_op jit(solution)/shard_map/ppermute | solution.py:40
  204.4 2.1 collective-permute-start.28
  209.4 29.0 %collective-permute-start.29 = (bf16[2,128,1024]{2,1,0:T(8,128)(2,1)S(1)}, bf16[2,128,1024]{2,1,0:T(8,128)(2,1)S(1)}, u32[]{:S(2)}, u32[]{:S(2)}) collective-permute-start(bf16[2,128,1024]{2,1,0:T(8,128)(2,1)S(1)} %copy-done.17), channel_id=1, source_target_pairs={{0,8},{8,0},{16,24},{24,16},{1,9},{9,1},{17,25},{25,17},{2,10},{10... | collective-permute-start | bytes 1572872 | tf_op jit(solution)/shard_map/ppermute | solution.py:40
  210.6 27.8 %collective-permute-start.30 = (bf16[2,128,1024]{2,1,0:T(8,128)(2,1)S(1)}, bf16[2,128,1024]{2,1,0:T(8,128)(2,1)S(1)}, u32[]{:S(2)}, u32[]{:S(2)}) collective-permute-start(bf16[2,128,1024]{2,1,0:T(8,128)(2,1)S(1)} %copy-done.16), channel_id=1, source_target_pairs={{0,16},{8,24},{16,0},{24,8},{1,17},{9,25},{17,1},{25,9},{2,18},{10... | collective-permute-start | bytes 1572872 | tf_op jit(solution)/shard_map/ppermute | solution.py:40
  211.4 27.0 %collective-permute-start.31 = (bf16[2,128,1024]{2,1,0:T(8,128)(2,1)S(1)}, bf16[2,128,1024]{2,1,0:T(8,128)(2,1)S(1)}, u32[]{:S(2)}, u32[]{:S(2)}) collective-permute-start(bf16[2,128,1024]{2,1,0:T(8,128)(2,1)S(1)} %copy-done.15), channel_id=1, source_target_pairs={{0,24},{8,16},{16,8},{24,0},{1,25},{9,17},{17,9},{25,1},{2,26},{10... | collective-permute-start | bytes 1572872 | tf_op jit(solution)/shard_map/ppermute | solution.py:40
  212.9 25.5 %copy-start.34 = (f32[1,1024]{1,0:T(1,128)S(1)}, f32[1,1024]{1,0:T(1,128)}, u32[]{:S(2)}) copy-start(f32[1,1024]{1,0:T(1,128)} %get-tuple-element.185) | copy-start | bytes 12292
  238.3 13.1 %copy-start.18 = (bf16[2,128,1024]{2,1,0:T(8,128)(2,1)}, bf16[2,128,1024]{2,1,0:T(8,128)(2,1)S(1)}, u32[]{:S(2)}) copy-start(bf16[2,128,1024]{2,1,0:T(8,128)(2,1)S(1)} %collective-permute-done.29) | copy-start | bytes 1572868
  238.4 13.1 %copy-start.20 = (bf16[2,128,1024]{2,1,0:T(8,128)(2,1)}, bf16[2,128,1024]{2,1,0:T(8,128)(2,1)S(1)}, u32[]{:S(2)}) copy-start(bf16[2,128,1024]{2,1,0:T(8,128)(2,1)S(1)} %collective-permute-done.30) | copy-start | bytes 1572868
  238.4 13.1 %copy-start.22 = (bf16[2,128,1024]{2,1,0:T(8,128)(2,1)}, bf16[2,128,1024]{2,1,0:T(8,128)(2,1)S(1)}, u32[]{:S(2)}) copy-start(bf16[2,128,1024]{2,1,0:T(8,128)(2,1)S(1)} %collective-permute-done.31) | copy-start | bytes 1572868
  251.5 19.1 %collective-permute-start.34 = (bf16[256,1536]{1,0:T(8,128)(2,1)}, bf16[256,1536]{1,0:T(8,128)(2,1)S(1)}, u32[]{:S(2)}, u32[]{:S(2)}) collective-permute-start(bf16[256,1536]{1,0:T(8,128)(2,1)} %get-tuple-element.213), channel_id=1, source_target_pairs={{0,16},{8,24},{16,0},{24,8},{1,17},{9,25},{17,1},{25,9},{2,18},{10... | collective-permute-start | bytes 2359304 | tf_op jit(solution)/shard_map/ppermute | solution.py:40
  253.1 19.7 %collective-permute-start.33 = (bf16[272,1536]{1,0:T(8,128)(2,1)}, bf16[272,1536]{1,0:T(8,128)(2,1)S(1)}, u32[]{:S(2)}, u32[]{:S(2)}) collective-permute-start(bf16[272,1536]{1,0:T(8,128)(2,1)} %get-tuple-element.212), channel_id=1, source_target_pairs={{0,8},{8,0},{16,24},{24,16},{1,9},{9,1},{17,25},{25,17},{2,10},{10... | collective-permute-start | bytes 2506760 | tf_op jit(solution)/shard_map/ppermute | solution.py:40
  259.1 7.1 %collective-permute-start.32 = (bf16[1,2,128,1024]{3,2,1,0:T(8,128)(2,1)}, bf16[1,2,128,1024]{3,2,1,0:T(8,128)(2,1)S(1)}, u32[]{:S(2)}, u32[]{:S(2)}) collective-permute-start(bf16[1,2,128,1024]{3,2,1,0:T(8,128)(2,1)} %get-tuple-element.211), channel_id=1, source_target_pairs={{0,1},{1,0},{2,3},{3,2},{4,5},{5,4},{6,7},{7,6},{8,9},{9,8},{10,11... | collective-permute-start | bytes 1572872 | tf_op jit(solution)/shard_map/ppermute | solution.py:35
  275.2 14.2 %collective-permute-start.35 = (bf16[2,128,1024]{2,1,0:T(8,128)(2,1)}, bf16[2,128,1024]{2,1,0:T(8,128)(2,1)}, u32[]{:S(2)}, u32[]{:S(2)}) collective-permute-start(bf16[2,128,1024]{2,1,0:T(8,128)(2,1)} %down_add.3), channel_id=1, source_target_pairs={{2,0},{4,2},{6,4},{3,1},{5,3},{7,5},{10,8},{12,10},{14,12},{11,9},... | collective-permute-start | bytes 1572872 | tf_op jit(solution)/shard_map/ppermute | solution.py:50
  276.5 13.0 %collective-permute-start.36 = (bf16[3,2,128,1024]{3,2,1,0:T(8,128)(2,1)}, bf16[3,2,128,1024]{3,2,1,0:T(8,128)(2,1)}, u32[]{:S(2)}, u32[]{:S(2)}) collective-permute-start(bf16[3,2,128,1024]{3,2,1,0:T(8,128)(2,1)} %get-tuple-element.215), channel_id=1, source_target_pairs={{0,1},{1,0},{2,3},{3,2},{4,5},{5,4},{6,7},{7,6},{8,9},{9,8},{10,11... | collective-permute-start | bytes 4718600 | tf_op jit(solution)/shard_map/ppermute | solution.py:35
  291.8 18.6 %collective-permute-start.37 = (bf16[2,128,1024]{2,1,0:T(8,128)(2,1)}, bf16[2,128,1024]{2,1,0:T(8,128)(2,1)}, u32[]{:S(2)}, u32[]{:S(2)}) collective-permute-start(bf16[2,128,1024]{2,1,0:T(8,128)(2,1)} %down_add.4), channel_id=1, source_target_pairs={{2,0},{4,2},{6,4},{3,1},{5,3},{7,5},{10,8},{12,10},{14,12},{11,9},... | collective-permute-start | bytes 1572872 | tf_op jit(solution)/shard_map/ppermute | solution.py:50
  293.1 17.3 %collective-permute-start.38 = (bf16[144,1536]{1,0:T(8,128)(2,1)S(1)}, bf16[144,1536]{1,0:T(8,128)(2,1)S(1)}, u32[]{:S(2)}, u32[]{:S(2)}) collective-permute-start(bf16[144,1536]{1,0:T(8,128)(2,1)S(1)} %copy-done.33), channel_id=1, source_target_pairs={{0,16},{8,24},{16,0},{24,8},{1,17},{9,25},{17,1},{25,9},{2,18},{10... | collective-permute-start | bytes 1327112 | tf_op jit(solution)/shard_map/ppermute | solution.py:40
  293.8 10.6 %collective-permute-start.39 = (bf16[128,1536]{1,0:T(8,128)(2,1)}, bf16[128,1536]{1,0:T(8,128)(2,1)}, u32[]{:S(2)}, u32[]{:S(2)}) collective-permute-start(bf16[128,1536]{1,0:T(8,128)(2,1)} %get-tuple-element.230), channel_id=1, source_target_pairs={{0,8},{8,0},{16,24},{24,16},{1,9},{9,1},{17,25},{25,17},{2,10},{10... | collective-permute-start | bytes 1179656 | tf_op jit(solution)/shard_map/ppermute | solution.py:40
  296.1 26.3 %all-to-all-start.1 = ((bf16[4,64,1920]{2,1,0:T(8,128)(2,1)}), bf16[4,64,1920]{2,1,0:T(8,128)(2,1)}, u32[]{:S(2)}, u32[]{:S(2)}) async-start(bf16[4,64,1920]{2,1,0:T(8,128)(2,1)} %reduce-scatter.2.cloned.1.call-done), calls=%async_computation.2 | async-start | bytes 1966080 | tf_op jit(solution)/shard_map/all_to_all | solution.py:959
  313.9 15.4 %collective-permute-start.41 = (bf16[80,1536]{1,0:T(8,128)(2,1)}, bf16[80,1536]{1,0:T(8,128)(2,1)}, u32[]{:S(2)}, u32[]{:S(2)}) collective-permute-start(bf16[80,1536]{1,0:T(8,128)(2,1)} %get-tuple-element.237), channel_id=1, source_target_pairs={{0,4},{2,6},{4,0},{6,2},{1,5},{3,7},{5,1},{7,3},{8,12},{10,14},{12... | collective-permute-start | bytes 737288 | tf_op jit(solution)/shard_map/ppermute | solution.py:55
  314.8 14.5 %collective-permute-start.42 = (bf16[80,1536]{1,0:T(8,128)(2,1)}, bf16[80,1536]{1,0:T(8,128)(2,1)}, u32[]{:S(2)}, u32[]{:S(2)}) collective-permute-start(bf16[80,1536]{1,0:T(8,128)(2,1)} %get-tuple-element.238), channel_id=1, source_target_pairs={{0,2},{2,4},{4,6},{6,0},{1,3},{3,5},{5,7},{7,1},{8,10},{10,12},{12... | collective-permute-start | bytes 737288 | tf_op jit(solution)/shard_map/ppermute | solution.py:55
  316.8 14.0 %copy-start.24 = (f32[64,1536]{1,0:T(8,128)S(1)}, f32[64,1536]{1,0:T(8,128)}, u32[]{:S(2)}) copy-start(f32[64,1536]{1,0:T(8,128)} %get-tuple-element.240) | copy-start | bytes 1179652
  316.8 13.0 %collective-permute-start.43 = (bf16[80,1536]{1,0:T(8,128)(2,1)}, bf16[80,1536]{1,0:T(8,128)(2,1)}, u32[]{:S(2)}, u32[]{:S(2)}) collective-permute-start(bf16[80,1536]{1,0:T(8,128)(2,1)} %get-tuple-element.239), channel_id=1, source_target_pairs={{0,6},{2,0},{4,2},{6,4},{1,7},{3,1},{5,3},{7,5},{8,14},{10,8},{12,... | collective-permute-start | bytes 737288 | tf_op jit(solution)/shard_map/ppermute | solution.py:55
  320.9 14.5 %copy-start.3 = (bf16[2,128,1024]{2,1,0:T(8,128)(2,1)S(1)}, bf16[2,128,1024]{2,1,0:T(8,128)(2,1)}, u32[]{:S(2)}) copy-start(bf16[2,128,1024]{2,1,0:T(8,128)(2,1)} %param.14) | copy-start | bytes 1572868
  320.9 14.5 %copy-start.28 = (f32[1024]{0:T(1024)S(1)}, f32[1024]{0:T(1024)}, u32[]{:S(2)}) copy-start(f32[1024]{0:T(1024)} %param.16) | copy-start | bytes 12292
  320.9 14.5 %copy-start.32 = (f32[2,128]{1,0:T(2,128)S(1)}, f32[2,128]{1,0:T(2,128)}, u32[]{:S(2)}) copy-start(f32[2,128]{1,0:T(2,128)} %copy-done.31) | copy-start | bytes 3076
  320.9 14.5 %collective-permute-start.40 = (bf16[2,128,1024]{2,1,0:T(8,128)(2,1)}, bf16[2,128,1024]{2,1,0:T(8,128)(2,1)}, u32[]{:S(2)}, u32[]{:S(2)}) collective-permute-start(bf16[2,128,1024]{2,1,0:T(8,128)(2,1)} %down_add.5), channel_id=1, source_target_pairs={{2,0},{4,2},{6,4},{3,1},{5,3},{7,5},{10,8},{12,10},{14,12},{11,9},... | collective-permute-start | bytes 1572872 | tf_op jit(solution)/shard_map/ppermute | solution.py:50
  330.7 2.7 collective-permute-start.44
  (29 other events, 127.8 us)
Sparse Core Ops, SparseCore 0:
  71.7 73.8 all-gather.1
  204.6 70.4 reduce-scatter.1

commit v5 on v4

--- a/solution.py
+++ b/solution.py
@@ -127,6 +127,12 @@
     first = lane_ids(x.shape[0]) < HEAD
     turned = pltpu.roll(x, HEAD, 1)
     return jnp.where(first, x, turned).astype(BF), jnp.where(first, turned, x).astype(BF)
+
+
+def by_head(x):
+    first = lane_ids(x.shape[0]) < HEAD
+    none = jnp.zeros_like(x)
+    return jnp.concatenate([jnp.where(first, x, none), jnp.where(first, none, x)])
 
 
 def attend_kernel(n_pieces, n_parts, scal_ref, *refs):
@@ -170,17 +176,13 @@
         lanes = slice(pair * TILE, (pair + 1) * TILE)
         query = prepare(qr_ref[0, :, lanes], qg_ref[...], cos_ref[:rows], sin_ref[:rows]).astype(BF)
         qh_ref[0, :, lanes] = query
-        turned_value = value_twins[pair].astype(F32).T.astype(BF)
-        mixed = []
-        for head in range(2):
-            mine = first if head == 0 else jnp.logical_not(first)
-            scores = dot(key_twins[pair], jnp.where(mine, query, jnp.zeros_like(query)), NT)
-            weights = jnp.exp2(scores * EXP2_SCALE + bias_ref[...])
-            inverse = 1.0 / jnp.sum(weights, axis=0, keepdims=True)
-            l_ref[0, 0, pl.ds(2 * pair + head, 1), :] = inverse
-            mixed.append(dot(turned_value, weights.astype(BF), NN) * inverse)
-        row_first = lax.broadcasted_iota(jnp.int32, (TILE, rows), 0) < HEAD
-        o_ref[0, :, lanes] = jnp.where(row_first, mixed[0], mixed[1]).T.astype(BF)
+        scores = dot(key_twins[pair], by_head(query), NT)
+        weights = jnp.exp2(scores * EXP2_SCALE + jnp.concatenate([bias_ref[...]] * 2, axis=1))
+        inverse = 1.0 / jnp.sum(weights, axis=0, keepdims=True)
+        l_ref[0, 0, pl.ds(2 * pair, 1), :] = inverse[:, :rows]
+        l_ref[0, 0, pl.ds(2 * pair + 1, 1), :] = inverse[:, rows:]
+        mixed = dot(weights.astype(BF), value_twins[pair], TN) * jnp.broadcast_to(inverse, (TILE, 2 * rows)).T
+        o_ref[0, :, lanes] = jnp.where(first, mixed[:rows], mixed[rows:]).astype(BF)
 
 
 def attend_back_kernel(
@@ -239,8 +241,8 @@
         gq_ref[...] = jnp.zeros_like(gq_ref)
         gk_ref[...] = jnp.zeros_like(gk_ref)
 
-    gq_ref[...] += query_gain
-    gk_ref[...] += key_gain
+    gq_ref[...] += query_gain + pltpu.roll(query_gain, HEAD, 1)
+    gk_ref[...] += key_gain + pltpu.roll(key_gain, HEAD, 1)
 
 
 def attention_specs(slots, rows, keys):
@@ -324,7 +326,7 @@
 
 
 def weight_kernel(parts, at_ref, x_ref, dq_ref, dk_ref, dv_ref, bm_ref, bo_ref, o_ref, w_ref, gain_ref, more_ref, *refs):
-    top_send, top_keep, low_send, low_keep, sum_ref = refs
+    top_send, top_keep, low_send, low_keep, own_ref, sum_ref = refs
     slots, rows, q_cols = dq_ref.shape
     k_cols = dk_ref.shape[2]
     depth = x_ref.shape[2]
@@ -371,15 +373,17 @@
         ids = lax.broadcasted_iota(jnp.int32, (16, width), 0)
         more = more_ref[...].astype(F32)
         here = jnp.where(ids == 0, first, jnp.where(ids == 2, left, more[:, :width]))
-        top_send[parts // 2 * half :, :width] = here.astype(BF)
-        top_send[parts // 2 * half :, width:] = more_ref[:, width:]
+        for ref, rows_at in ((top_send, slice(parts // 2 * half, parts // 2 * half + 16)), (own_ref, slice(0, 16))):
+            ref[rows_at, :width] = here.astype(BF)
+            ref[rows_at, width:] = more_ref[:, width:]
 
 
 def weight_grads(at, x, d_q, d_k, d_v, d_mine, d_other, attn, w, gain, more, parts):
     slots, keys, width = x.shape
     cols = 2 * d_q.shape[2] + 2 * d_k.shape[2]
     depth = width // parts
-    shapes = [(width // 4 + more.shape[0], cols), (width // 4, cols), (width // 4, cols), (width // 4, cols)]
+    rows = parts // 2 * (depth // 2)
+    shapes = [(rows + more.shape[0], cols), (rows, cols), (rows, cols), (rows, cols), more.shape]
     spec = pltpu.PrefetchScalarGridSpec(
         num_scalar_prefetch=1,
         grid=(parts,),
@@ -480,6 +484,30 @@
     )(mine, other, *came)
 
 
+def last_kernel(mine_ref, other_ref, came_ref, middle_ref, hidden_ref, gain_ref, out_ref):
+    grad = (mine_ref[0, 0] + other_ref[0, 0].astype(F32) + came_ref[0].astype(F32)) * gain_ref[...]
+    values = hidden_ref[0].astype(F32)
+    inverse = lax.rsqrt(jnp.mean(values * values, axis=1, keepdims=True) + EPS)
+    normal = values * inverse
+    back = inverse * (grad - normal * jnp.mean(grad * normal, axis=1, keepdims=True))
+    out_ref[0] = (middle_ref[0] + back).astype(BF)
+
+
+def last_step(mine, other, came, d_middle, hidden, gain):
+    slots, rows, width = hidden.shape
+    block = pl.BlockSpec((1, 1, rows, width), lambda s: (0, s, 0, 0))
+    here = pl.BlockSpec((1, rows, width), lambda s: (s, 0, 0))
+    return pl.pallas_call(
+        last_kernel,
+        grid=(slots,),
+        in_specs=[block, block, here, here, here, pl.BlockSpec((1, width), lambda s: (0, 0))],
+        out_specs=here,
+        out_shape=jax.ShapeDtypeStruct((slots, rows, width), BF),
+        cost_estimate=pl.CostEstimate(flops=2 << 30, bytes_accessed=0, transcendentals=0),
+        name="last_step",
+    )(mine, other, came, d_middle, hidden, gain)
+
+
 def half_kernel(half, sends, keeps, extra, keep_ref, came_ref, *refs):
     own_ref = refs[0] if extra else None
     send_ref, left_ref = refs[-2:]
@@ -543,12 +571,8 @@
     )(at, top, top_came, low, low_came, own)
 
 
-def ffn_kernel(xo_ref, xm_ref, go_ref, gm_ref, w_ref, yo_ref, ym_ref, do_ref, dm_ref, inner_ref, gain_ref):
+def ffn_block(x, g, w_ref, inner_ref):
     units = w_ref.shape[1] // 3
-    step = pl.program_id(0)
-    early = step < pl.num_programs(0) // 2
-    x = jnp.where(early, xo_ref[...], xm_ref[...])
-    g = jnp.where(early, go_ref[...], gm_ref[...])
     raised = dot(x, w_ref[:, : 2 * units], NN)
     gate = raised[:, :units]
     upper = raised[:, units:]
@@ -557,40 +581,54 @@
     act = (silu * upper).astype(BF)
     y = dot(act, w_ref[:, 2 * units :], NT).astype(BF)
     d_act = dot(g, w_ref[:, 2 * units :], NN)
-    d_gate = (d_act * upper * (sig + silu * (1.0 - sig))).astype(BF)
-    d_up = (d_act * silu).astype(BF)
-    inner_ref[:, :units] = d_gate
-    inner_ref[:, units : 2 * units] = d_up
+    inner_ref[:, :units] = (d_act * upper * (sig + silu * (1.0 - sig))).astype(BF)
+    inner_ref[:, units : 2 * units] = (d_act * silu).astype(BF)
     inner_ref[:, 2 * units :] = act
     d_x = dot(inner_ref[:, : 2 * units], w_ref[:, : 2 * units], NT)
-    gain_row = jnp.sum(d_x * x.astype(F32), axis=0, keepdims=True)
-    dx = d_x.astype(BF)
-
-    @pl.when(early)
-    def _():
-        yo_ref[...] = y
-        do_ref[...] = dx
-
-    @pl.when(jnp.logical_not(early))
-    def _():
-        ym_ref[...] = y
-        dm_ref[...] = dx
+    return y, d_x.astype(BF), jnp.sum(d_x * x.astype(F32), axis=0, keepdims=True)
+
+
+def ffn_kernel(xm_ref, xo_ref, gm_ref, go_ref, w_ref, ym_ref, yo_ref, dm_ref, do_ref, inner_ref, gain_ref):
+    half = xm_ref.shape[0]
+    x = jnp.concatenate([xm_ref[...], xo_ref[...]])
+    g = jnp.concatenate([gm_ref[...], go_ref[...]])
+    y, d_x, gain_row = ffn_block(x, g, w_ref, inner_ref)
+    ym_ref[...] = y[:half]
+    yo_ref[...] = y[half:]
+    dm_ref[...] = d_x[:half]
+    do_ref[...] = d_x[half:]
+
+    @pl.when(pl.program_id(0) == 0)
+    def _():
+        gain_ref[...] = gain_row
+
+    @pl.when(pl.program_id(0) > 0)
+    def _():
+        gain_ref[...] += gain_row
+
+
+def ffn_rest_kernel(
+    xm_ref, xo_ref, gm_ref, go_ref, w_ref, inside_ref, ym_ref, yo_ref, dm_ref, do_ref, gain_ref, grad_ref, inner_ref, sum_ref
+):
+    units = w_ref.shape[1] // 3
+    half = xm_ref.shape[0]
+    step = pl.program_id(0)
+    x = jnp.concatenate([xm_ref[...], xo_ref[...]])
+    g = jnp.concatenate([gm_ref[...], go_ref[...]])
 
     @pl.when(step == 0)
     def _():
+        y, d_x, gain_row = ffn_block(x, g, w_ref, inner_ref)
+        ym_ref[...] = y[:half]
+        yo_ref[...] = y[half:]
+        dm_ref[...] = d_x[:half]
+        do_ref[...] = d_x[half:]
         gain_ref[...] = gain_row
 
     @pl.when(step > 0)
     def _():
-        gain_ref[...] += gain_row
-
-
-def ffn_weight_kernel(xo_ref, xm_ref, go_ref, gm_ref, inner_ref, grad_ref, sum_ref):
-    units = inner_ref.shape[1] // 3
-    step = pl.program_id(0)
-    early = step < pl.num_programs(0) // 2
-    x = jnp.where(early, xo_ref[...], xm_ref[...])
-    g = jnp.where(early, go_ref[...], gm_ref[...])
+        inner_ref[...] = inside_ref[...]
+
     left = dot(x, inner_ref[:, : 2 * units], TN)
     right = dot(g, inner_ref[:, 2 * units :], TN)
 
@@ -610,53 +648,46 @@
         grad_ref[:, 2 * units :] = (sum_ref[:, 2 * units :] + right).astype(BF)
 
 
-def ffn_specs(tokens, width, units3, rows):
-    steps = tokens // rows
-    other = pl.BlockSpec((rows, width), lambda i: (jnp.minimum(i, steps - 1), 0))
-    mine = pl.BlockSpec((rows, width), lambda i: (jnp.maximum(i - steps, 0), 0))
+def feed_forward(x_mine, x_other, g_mine, g_other, w, parts):
+    tokens, width = x_mine.shape
+    rows = tokens // parts
+    units3 = w.shape[1]
+    block = pl.BlockSpec((rows, width), lambda i: (i + 1, 0))
+    out = pl.BlockSpec((rows, width), lambda i: (i, 0))
+    part = jax.ShapeDtypeStruct((tokens - rows, width), BF)
+    return pl.pallas_call(
+        ffn_kernel,
+        grid=(parts - 1,),
+        in_specs=[block] * 4 + [pl.BlockSpec((width, units3), lambda i: (0, 0))],
+        out_specs=[out] * 4 + [pl.BlockSpec((2 * rows, units3), lambda i: (i, 0)), pl.BlockSpec((1, width), lambda i: (0, 0))],
+        out_shape=[part] * 4
+        + [jax.ShapeDtypeStruct((2 * (tokens - rows), units3), BF), jax.ShapeDtypeStruct((1, width), F32)],
+        compiler_params=pltpu.CompilerParams(vmem_limit_bytes=VMEM_LIMIT),
+        cost_estimate=pl.CostEstimate(flops=8 * tokens * width * units3, bytes_accessed=24 << 20, transcendentals=0),
+        name="feed_forward",
+    )(x_mine, x_other, g_mine, g_other, w)
+
+
+def ffn_rest(x_mine, x_other, g_mine, g_other, w, inside, parts):
+    tokens, width = x_mine.shape
+    rows = tokens // parts
+    units3 = w.shape[1]
+    block = pl.BlockSpec((rows, width), lambda i: (i, 0))
     whole = pl.BlockSpec((width, units3), lambda i: (0, 0))
-    inner = pl.BlockSpec((rows, units3), lambda i: (i, 0))
-    return 2 * steps, other, mine, whole, inner
-
-
-def feed_forward(x_mine, x_other, g_mine, g_other, w, rows):
-    tokens, width = x_mine.shape
-    units3 = w.shape[1]
-    grid, other, mine, whole, inner = ffn_specs(tokens, width, units3, rows)
-    part = jax.ShapeDtypeStruct((tokens, width), BF)
-    y_other, y_mine, dx_other, dx_mine, inside, gain_row = pl.pallas_call(
-        ffn_kernel,
-        grid=(grid,),
-        in_specs=[other, mine, other, mine, whole],
-        out_specs=[other, mine, other, mine, inner, pl.BlockSpec((1, width), lambda i: (0, 0))],
-        out_shape=[
-            part, part, part, part,
-            jax.ShapeDtypeStruct((2 * tokens, units3), BF), jax.ShapeDtypeStruct((1, width), F32),
-        ],
+    own = pl.BlockSpec((rows, width), lambda i: (0, 0))
+    part = jax.ShapeDtypeStruct((rows, width), BF)
+    return pl.pallas_call(
+        ffn_rest_kernel,
+        grid=(parts,),
+        in_specs=[block] * 4 + [whole, pl.BlockSpec((2 * rows, units3), lambda i: (jnp.maximum(i - 1, 0), 0))],
+        out_specs=[own] * 4 + [pl.BlockSpec((1, width), lambda i: (0, 0)), whole],
+        out_shape=[part] * 4
+        + [jax.ShapeDtypeStruct((1, width), F32), jax.ShapeDtypeStruct((width, units3), BF)],
+        scratch_shapes=[pltpu.VMEM((2 * rows, units3), BF), pltpu.VMEM((width, units3), F32)],
         compiler_params=pltpu.CompilerParams(vmem_limit_bytes=VMEM_LIMIT),
-        cost_estimate=pl.CostEstimate(
-            flops=8 * tokens * width * units3, bytes_accessed=24 << 20, transcendentals=2 * tokens * units3 // 3
-        ),
-        name="feed_forward",
-    )(x_other, x_mine, g_other, g_mine, w)
-    return y_mine, y_other, dx_mine, dx_other, inside, gain_row[0]
-
-
-def ffn_weight_grads(x_mine, x_other, g_mine, g_other, inside, rows):
-    tokens, width = x_mine.shape
-    units3 = inside.shape[1]
-    grid, other, mine, whole, inner = ffn_specs(tokens, width, units3, rows)
-    return pl.pallas_call(
-        ffn_weight_kernel,
-        grid=(grid,),
-        in_specs=[other, mine, other, mine, inner],
-        out_specs=whole,
-        out_shape=jax.ShapeDtypeStruct((width, units3), BF),
-        scratch_shapes=[pltpu.VMEM((width, units3), F32)],
-        compiler_params=pltpu.CompilerParams(vmem_limit_bytes=VMEM_LIMIT),
-        cost_estimate=pl.CostEstimate(flops=16 << 30, bytes_accessed=24 << 20, transcendentals=0),
-        name="ffn_weight_grads",
-    )(x_other, x_mine, g_other, g_mine, inside)
+        cost_estimate=pl.CostEstimate(flops=24 << 30, bytes_accessed=24 << 20, transcendentals=0),
+        name="ffn_rest",
+    )(x_mine, x_other, g_mine, g_other, w, inside)
 
 
 def same_kernel(in_ref, out_ref):
@@ -836,7 +867,7 @@
             ffn_rows, x_pieces[-1] = tie(ffn_rows, x_pieces[-1])
         others.append(swap_cores(x_pieces[-1]))
     ffn_w = lax.all_gather(ffn_rows, "ctx", axis=1, tiled=True).reshape(width, 3 * padded)
-    ffn_w = same(ffn_w, 20 << 30)
+    ffn_w = same(ffn_w, 60 << 30)
     held = tie(*x_pieces, *others, grad_rows, top, bottom)
     x_pieces = held[:n_ctx]
     others = held[n_ctx : 2 * n_ctx]
@@ -866,30 +897,31 @@
         return value.reshape(-1, width)
 
     place = jnp.stack([f]).astype(jnp.int32)
-    y_mine, y_other, dx_mine, dx_other, inside, ffn_gain_row = feed_forward(
-        flat(x_mine), flat(x_other), flat(g_mine), flat(g_other), ffn_w, 2 * slots * shard_rows
-    )
+
+    tokens = (flat(x_mine), flat(x_other), flat(g_mine), flat(g_other))
+    y_mine, y_other, dx_mine, dx_other, inside, gain_row = feed_forward(*tokens, ffn_w, n_fsdp)
 
     def core_sums(mine, other):
-        mine = mine.reshape(n_fsdp, slots, shard_rows, width)
-        other = swap_cores(other.reshape(n_fsdp, slots, shard_rows, width))
-        return [mine[m].astype(F32) + other[m].astype(F32) for m in range(n_fsdp)]
+        mine = mine.reshape(n_fsdp - 1, slots, shard_rows, width)
+        other = swap_cores(other.reshape(n_fsdp - 1, slots, shard_rows, width))
+        return [(mine[m].astype(F32) + other[m].astype(F32)).astype(BF) for m in range(n_fsdp - 1)]
 
     def traded(sums):
-        return [sums[0]] + [fsdp_xor(sums[m], m) for m in range(1, n_fsdp)]
-
-    dx_sums = core_sums(dx_mine, dx_other)
-    inside, *dx_sums = tie(inside, dx_sums[0], *[item.astype(BF) for item in dx_sums[1:]])
-    y_sums = core_sums(y_mine, y_other)
-    inside, *y_sums = tie(inside, y_sums[0], *[item.astype(BF) for item in y_sums[1:]])
-    ffn_grads = ffn_weight_grads(
-        flat(x_mine), flat(x_other), flat(g_mine), flat(g_other), inside, 2 * slots * shard_rows
-    )
-    ffn_grads, *held = tie(ffn_grads, *traded(dx_sums))
+        return [fsdp_xor(item, m) for m, item in enumerate(sums, 1)]
+
+    def own(value):
+        return value.reshape(slots, shard_rows, width)
+
+    inside, *dx_sums = tie(inside, *core_sums(dx_mine, dx_other))
+    inside, *y_sums = tie(inside, *core_sums(y_mine, y_other))
+    y_mine, y_other, dx_mine, dx_other, own_gain_row, ffn_grads = ffn_rest(*tokens, ffn_w, inside, n_fsdp)
+    ffn_gain_row = (gain_row + own_gain_row)[0]
+    ffn_grads, dx_mine, dx_other, *held = tie(ffn_grads, dx_mine, dx_other, *traded(dx_sums))
     ffn_reduced = lax.psum_scatter(
         ffn_grads.reshape(n_fsdp, n_ctx * shard, 3 * padded), "ctx", scatter_dimension=1, tiled=True
     )
-    d_normed_two = sum(item.astype(F32) for item in held)
+    d_normed_two = own(dx_mine).astype(F32) + swap_cores(own(dx_other)).astype(F32)
+    d_normed_two = d_normed_two + sum(item.astype(F32) for item in held)
     d_middle = grad_rows.astype(F32) + norm_back(middle, ffn_gain, d_normed_two)
     d_mine = d_middle.astype(BF)
     d_other = swap_cores(d_mine)
@@ -902,29 +934,28 @@
     d_q, d_k, d_v, gq, gk = attend_back(
         scal, q_raw, k_raw, value, cosine, sine, query_gain2, key_gain2, q_hat, k_hat, attn, stats, d_attn
     )
-    y_got = traded(y_sums)
+    y_got = [own(y_mine), swap_cores(own(y_other))] + traded(y_sums)
 
     held = tie(d_q, d_k, d_v, gq, gk, ffn_gain_row, *y_got)
     d_q, d_k, d_v, gq, gk, ffn_gain_row = held[:6]
     result = jnp.where(valid, middle + sum(item.astype(F32) for item in held[6:]), 0.0).astype(BF)
 
-    heads = jnp.stack([jnp.pad(item[0, :HEAD] + item[0, HEAD:], (0, HEAD)) for item in (gq, gk)])
+    heads = jnp.concatenate([gq, gk])
     small = jnp.stack([jnp.zeros_like(ffn_gain), ffn_gain_row / ffn_gain])
     small = jnp.concatenate([small, heads], axis=1)
     small = jnp.pad(small, ((0, 0), (0, 2 * q_cols + 2 * k_cols - small.shape[1])))
-    top_send, top, low_send, low = weight_grads(
+    top_send, top, low_send, low, own = weight_grads(
         place, x_all, d_q, d_k, d_v, d_mine, d_other, attn, attn_w, attn_gain[None, :], two_parts(small), n_fsdp
     )
-    top_send, top, low_send, low, d_q, d_k, d_v = tie(top_send, top, low_send, low, d_q, d_k, d_v)
+    top_send, top, low_send, low, own, d_q, d_k, d_v = tie(top_send, top, low_send, low, own, d_q, d_k, d_v)
 
     half = n_ctx * shard // 2
     bits = bits_of(n_fsdp)
-    own = top_send[n_fsdp // 2 * half :]
     came = [fsdp_xor(top_send, bits[0]), fsdp_xor(low_send, bits[-1])]
     last_mine, last_other = input_grads(d_q, d_k, d_v, attn_w, n_ctx - 1, 1)
     last_other = swap_cores(last_other)
     mine, other = input_grads(d_q, d_k, d_v, attn_w, 0, n_ctx - 1)
-    mine, other, last_other, *came = tie(mine, other, last_other, *came)
+    mine, other, last_other, result, *came = tie(mine, other, last_other, result, *came)
     other = swap_cores(other)
     total = ctx_down(down_add(last_mine, last_other, 0))
     block = n_ctx - 2
@@ -949,7 +980,7 @@
         if block > 0:
             total = ctx_down(down_add(mine, other, block, total))
             block -= 1
-            total, *came = tie(total, *came)
+            total, ffn_reduced, *came = tie(total, ffn_reduced, *came)
     ctx_place = jnp.stack([f, c]).astype(jnp.int32)
     mine_rows, small, *messages = to_ctx(ctx_place, top, came[0], low, came[1], own, n_ctx)
     while block > 0:
@@ -957,16 +988,15 @@
         block -= 1
     got = [ctx_shift(message, k) for k, message in enumerate(messages, 1)]
     ffn_parts = lax.all_to_all(ffn_reduced, "fsdp", 0, 0, tiled=True)
-    total = mine[0] + other[0].astype(F32) + total.astype(F32)
-
+    gate_grad, up_grad, down_grad = finish(ffn_parts, ff_half)
+    total, gate_grad, up_grad, down_grad = tie(total, gate_grad, up_grad, down_grad)
     small = [one_part(small)] + [one_part(piece[shard:]) for piece in got]
     got = [mine_rows] + [piece[:shard].astype(F32) for piece in got]
-    gate_grad, up_grad, down_grad = finish(ffn_parts, ff_half)
     down_grad = down_grad.T
     attn_grads = sum(got)
     small = tree_sum(small)
     small = small + swap_cores(small)
-    input_grad = (d_middle + norm_back(hidden, attn_gain, total)).astype(BF)
+    input_grad = last_step(mine, other, total, d_middle, hidden_in, attn_gain[None, :])
     qkv_total = attn_grads[:, : q_cols + 2 * k_cols]
     query_weight_grad = qkv_total[:, :q_cols]
     key_weight_grad = qkv_total[:, q_cols : q_cols + k_cols]

time: 355 us -> 353 us (level)
  other arithmetic: 30.8 us -> 26.6 us
    ppermute x20, waiting for transfers between devices: 41.5 us -> 32.9 us  [fsdp_xor(): return lax.ppermute(value, 'fsdp', [(i, i ^ mask) for i in range(size)])]
    ppermute x3, waiting for transfers between devices: 8.97 us -> 14.4 us  [ctx_down(): lax.ppermute(value, 'ctx', [(i + step, i) for i in range(size - step)])]
    pallas_call x2 -> x3, Pallas kernels: 43.3 us -> 46.9 us  [the longest x1 24.4 us: ffn_rest(): pl.pallas_call(ffn_rest_kernel, grid=(parts,), in_specs=[block] * 4 + [wh...]
    ppermute x13 -> x15, waiting for transfers between devices: 6.11 us -> 7.59 us  [swap_cores(): return lax.ppermute(value, 'tp', [(0, 1), (1, 0)])]
  transfers between devices with their start and end apart: 49 -> 51, of which waited for: 21 -> 22; matrix products, arithmetic and copies ran while one was open for 10% -> 9% of each run, Pallas kernels for 30% -> 31%
where the time goes in v5:
time: 353 us; the launch traced here: 347 us
  Pallas kernels  136 us (39%)
  waiting for transfers between devices  88.9 us (25%)
  starting transfers between devices  65.6 us (19%)
  other arithmetic  26.6 us (8%)
  between operations  15 us (4%)
  local copies, waits for them, and re-layouts  11.2 us (3%)
  matrix products  3.79 us (1%)
    ppermute x20, waiting for transfers between devices, fsdp_xor(): return lax.ppermute(value, 'fsdp', [(i, i ^ mask) for i in range(size)])  32.9 us
    pallas_call x1, Pallas kernels, attend_back(): pl.pallas_call(attend_back_kernel, grid=(slots, pairs), in_specs=[smem, q...  25.4 us
    pallas_call x1, Pallas kernels, ffn_rest(): pl.pallas_call(ffn_rest_kernel, grid=(parts,), in_specs=[block] * 4 + [wh...  24.4 us
    ppermute x20, starting transfers between devices, fsdp_xor(): return lax.ppermute(value, 'fsdp', [(i, i ^ mask) for i in range(size)])  23.6 us
    pallas_call x1, Pallas kernels, attend(): pl.pallas_call(functools.partial(attend_kernel, len(pieces), parts), grid...  22 us
    pallas_call x1, Pallas kernels, feed_forward(): pl.pallas_call(ffn_kernel, grid=(parts - 1,), in_specs=[block] * 4 + [pl....  19.5 us
    ppermute x3, starting transfers between devices, ctx_up(): lax.ppermute(value, 'ctx', [(i, i + step) for i in range(size - step)])  19.4 us
    ppermute x6, waiting for transfers between devices, ctx_shift(): lax.ppermute(value, 'ctx', [(i, (i + step) % size) for i in range(size)])  17.5 us
  transfers between devices with their start and end apart: 51, of which 22 were waited for; matrix products, arithmetic and copies ran while one was open for 9% of the time, Pallas kernels for 31%

profile of v5, /device:TPU:0, one launch (start us, length us, event | category | flops | bytes accessed | tf_op | source)
XLA Modules:
  0.0 346.6 jit_solution(2276197104922255760)
XLA Ops:
  9.8 5.8 %collective-permute-start = (bf16[2,128,1024]{2,1,0:T(8,128)(2,1)S(1)}, bf16[2,128,1024]{2,1,0:T(8,128)(2,1)}, u32[]{:S(2)}, u32[]{:S(2)}) collective-permute-start(bf16[2,128,1024]{2,1,0:T(8,128)(2,1)S(1)} %fusion.2.refs_0_), channel_id=1, source_target_pairs={{0,2},{2,4},{4,6},{1,3},{3,5},{5,7},{8,10},{10,12},{12,14},{9,11},... | collective-permute-start | bytes 1572872 | tf_op jit(solution)/shard_map/ppermute | solution.py:45
  16.2 1.6 collective-permute-start.2
  17.9 1.6 collective-permute-start.1
  19.4 2.2 pack.1
  21.6 3.7 %all-to-all-start = ((bf16[4,64,1920]{2,1,0:T(8,128)(2,1)}), bf16[4,64,1920]{2,1,0:T(8,128)(2,1)S(1)}, u32[]{:S(2)}, u32[]{:S(2)}) async-start(bf16[4,64,1920]{2,1,0:T(8,128)(2,1)} %pack.1), calls=%async_computation | async-start | bytes 1966080 | tf_op jit(solution)/shard_map/all_to_all | solution.py:857
  25.3 5.9 %collective-permute-done.3 = bf16[64,1536]{1,0:T(8,128)(2,1)S(1)} collective-permute-done((bf16[64,1536]{1,0:T(8,128)(2,1)S(1)}, bf16[64,1536]{1,0:T(8,128)(2,1)S(1)}, u32[]{:S(2)}, u32[]{:S(2)}) %collective-permute-start.3) | collective-permute-done | bytes 196640 | tf_op jit(solution)/shard_map/ppermute | solution.py:55
  31.3 4.2 %collective-permute-done.2 = bf16[64,1536]{1,0:T(8,128)(2,1)S(1)} collective-permute-done((bf16[64,1536]{1,0:T(8,128)(2,1)S(1)}, bf16[64,1536]{1,0:T(8,128)(2,1)S(1)}, u32[]{:S(2)}, u32[]{:S(2)}) %collective-permute-start.2) | collective-permute-done | bytes 196640 | tf_op jit(solution)/shard_map/ppermute | solution.py:55
  35.5 3.1 collective-permute-done.1
  38.8 1.6 collective-permute-start.10
  40.4 1.6 collective-permute-start.12
  42.0 8.5 %collective-permute-start.4 = (bf16[2,128,1024]{2,1,0:T(8,128)(2,1)}, bf16[2,128,1024]{2,1,0:T(8,128)(2,1)}, u32[]{:S(2)}, u32[]{:S(2)}) collective-permute-start(bf16[2,128,1024]{2,1,0:T(8,128)(2,1)} %collective-permute-done.refs_2_), channel_id=1, source_target_pairs={{0,2},{2,4},{4,6},{1,3},{3,5},{5,7},{8,10},{10,12},{12,14},{9,11},... | collective-permute-start | bytes 1572872 | tf_op jit(solution)/shard_map/ppermute | solution.py:45
  53.8 5.9 %collective-permute-done.4.refs_4_ = bf16[2,128,1024]{2,1,0:T(8,128)(2,1)} collective-permute-done((bf16[2,128,1024]{2,1,0:T(8,128)(2,1)}, bf16[2,128,1024]{2,1,0:T(8,128)(2,1)}, u32[]{:S(2)}, u32[]{:S(2)}) %collective-permute-start.4) | collective-permute-done | bytes 524320 | tf_op jit(solution)/shard_map/ppermute | solution.py:45
  59.8 5.2 %collective-permute-start.5 = (bf16[2,128,1024]{2,1,0:T(8,128)(2,1)}, bf16[2,128,1024]{2,1,0:T(8,128)(2,1)}, u32[]{:S(2)}, u32[]{:S(2)}) collective-permute-start(bf16[2,128,1024]{2,1,0:T(8,128)(2,1)} %collective-permute-done.4.refs_4_), channel_id=1, source_target_pairs={{0,2},{2,4},{4,6},{1,3},{3,5},{5,7},{8,10},{10,12},{12,14},{9,11},... | collective-permute-start | bytes 1572872 | tf_op jit(solution)/shard_map/ppermute | solution.py:45
  67.9 3.1 fusion.15
  71.8 1.5 collective-permute-done.5.refs_6_
  75.1 1.9 pad_maximum_fusion.4.refs_11_.refs_12_.refs_13_
  77.6 1.5 collective-permute-start.15
  79.1 1.5 collective-permute-start.14
  81.3 22.0 %attend.1 = (bf16[2,256,512]{2,1,0:T(8,128)(2,1)}, f32[2,2,8,256]{3,2,1,0:T(8,128)}, f32[2,256,512]{2,1,0:T(8,128)}, f32[2,1024,256]{2,1,0:T(8,128)}, bf16[2,102...) custom-call(s32[5]{0:T(128)} %pad_add_fusion.scal_ref, ...), custom_call_target="tpu_custom_call" | custom-call | flops 1048576 | bytes 1048576 | tf_op jit(solution)/shard_map/attend/pallas_call | solution.py:270
  105.4 2.6 collective-permute-done.17
  109.6 2.5 collective-permute-start.20
  112.1 1.6 pad_maximum_fusion.2
  113.9 8.7 %collective-permute-done.19 = bf16[2,128,1024]{2,1,0:T(8,128)(2,1)S(1)} collective-permute-done((bf16[2,128,1024]{2,1,0:T(8,128)(2,1)S(1)}, bf16[2,128,1024]{2,1,0:T(8,128)(2,1)S(1)}, u32[]{:S(2)}, u32[]{:S(2)}) %collective-permute-start.19) | collective-permute-done | bytes 524320 | tf_op jit(solution)/shard_map/ppermute | solution.py:40
  123.9 11.1 %collective-permute-done.20 = bf16[2,128,1024]{2,1,0:T(8,128)(2,1)S(1)} collective-permute-done((bf16[2,128,1024]{2,1,0:T(8,128)(2,1)S(1)}, bf16[2,128,1024]{2,1,0:T(8,128)(2,1)S(1)}, u32[]{:S(2)}, u32[]{:S(2)}) %collective-permute-start.20) | collective-permute-done | bytes 524320 | tf_op jit(solution)/shard_map/ppermute | solution.py:40
  135.0 1.7 pad_maximum_fusion.1
  136.6 8.9 %all-gather.2.cloned.1.call-done = bf16[4,256,1920]{2,1,0:T(8,128)(2,1)} async-done(((bf16[4,64,1920]{2,1,0:T(8,128)(2,1)}), bf16[4,256,1920]{2,1,0:T(8,128)(2,1)}) %all-gather.2.cloned.1.call-update) | async-done | bytes 3932176 | tf_op jit(solution)/shard_map/all_gather | solution.py:869
  145.6 19.5 %feed_forward.1 = (bf16[768,1024]{1,0:T(8,128)(2,1)}, bf16[768,1024]{1,0:T(8,128)(2,1)}, bf16[768,1024]{1,0:T(8,128)(2,1)}, bf16[768,1024]{1,0:T(8,128)(2,1)}, b...) custom-call(bf16[1024,1024]{1,0:T(8,128)(2,1)} %bitcast.25.xm_ref, bf16[1024,1024]{1,0:T(8,128)(2,1)} %bitcast.26.xo_ref, ...), custom_call_target="tpu_custom_call" | custom-call | flops 16106127360 | bytes 25165824 | tf_op jit(solution)/shard_map/feed_forward/pallas_call | solution.py:658
  165.6 1.6 fusion.42
  168.7 1.6 fusion.11
  170.3 1.5 collective-permute-start.25
  171.8 1.5 collective-permute-start.26
  174.5 24.4 %ffn_rest.1 = (bf16[256,1024]{1,0:T(8,128)(2,1)}, bf16[256,1024]{1,0:T(8,128)(2,1)}, bf16[256,1024]{1,0:T(8,128)(2,1)}, bf16[256,1024]{1,0:T(8,128)(2,1)}, f32[1...) custom-call(bf16[1024,1024]{1,0:T(8,128)(2,1)} %bitcast.25.xm_ref, bf16[1024,1024]{1,0:T(8,128)(2,1)} %bitcast.26.xo_ref, ...), custom_call_target="tpu_custom_call" | custom-call | flops 25769803776 | bytes 25165824 | tf_op jit(solution)/shard_map/ffn_rest/pallas_call | solution.py:679
  199.0 2.1 collective-permute-done.28
  201.1 1.6 multiply_reduce_fusion
  202.8 1.7 fusion.40
  205.1 1.7 collective-permute-done.29.bo_ref
  206.8 3.0 convolution_convert_fusion.d_ref
  209.8 1.5 collective-permute-start.31
  211.3 1.5 collective-permute-start.32
  213.3 25.4 %attend_back.1 = (bf16[2,256,512]{2,1,0:T(8,128)(2,1)}, bf16[2,1024,256]{2,1,0:T(8,128)(2,1)}, bf16[2,1024,256]{2,1,0:T(8,128)(2,1)}, f32[1,128]{1,0:T(1,128)}, f32[1,128]{1,0:T(1,128)}) custom-call(s32[5]{0:T(128)} %pad_add_fusion.scal_ref, f32[2,256,512]{2,1,0:T(8,128)} %get-tuple-element.160.q_ref, f32[2,1024,256]{2,1,0:T(8,128)} %get-tuple-element.161.k_ref, ...), custom_call_target="tpu_custom_call" | custom-call | flops 25769803776 | bytes 12582912 | tf_op jit(solution)/shard_map/attend_back/pallas_call | solution.py:303
  240.2 10.7 %weight_grads.1 = (bf16[272,1536]{1,0:T(8,128)(2,1)}, bf16[256,1536]{1,0:T(8,128)(2,1)}, bf16[256,1536]{1,0:T(8,128)(2,1)}, bf16[256,1536]{1,0:T(8,128)(2,1)}, bf16[16,1536]{1,0:T(8,128)(2,1)}) custom-call(s32[1]{0:T(128)} %bitcast.at_ref, bf16[2,1024,1024]{2,1,0:T(8,128)(2,1)} %get-tuple-element.159.x_ref, bf16[2,256,512]{2,1,0:T(8,128)(2,1)} %get-tuple-element.219.dq_ref, ...), custom_call_target="tpu_custom_call" | custom-call | flops 10737418240 | bytes 8388608 | tf_op jit(solution)/shard_map/weight_grads/pallas_call | solution.py:405
  250.9 1.5 collective-permute-start.36
  252.4 1.5 collective-permute-start.35
  253.9 4.1 %input_grads.3 = (f32[1,2,128,1024]{3,2,1,0:T(8,128)}, bf16[1,2,128,1024]{3,2,1,0:T(8,128)(2,1)}) custom-call(bf16[2,256,512]{2,1,0:T(8,128)(2,1)} %get-tuple-element.219.dq_ref, bf16[2,1024,256]{2,1,0:T(8,128)(2,1)} %get-tuple-element.220.dk_ref, bf16[2,1024,256]{2,1,0:T(8,128)(2,1)} %get-tuple-element.221.dv_ref, bf16[1024,1536]{1,0:T(8,128)(2,1)} %bitcast.118), custom_call_target="tpu_custom_call" | custom-call | flops 6442450944 | bytes 1048576 | tf_op jit(solution)/shard_map/input_grads/pallas_call | solution.py:439
  258.0 1.4 select_convert_fusion
  259.4 7.2 %input_grads.2 = (f32[3,2,128,1024]{3,2,1,0:T(8,128)}, bf16[3,2,128,1024]{3,2,1,0:T(8,128)(2,1)}) custom-call(bf16[2,256,512]{2,1,0:T(8,128)(2,1)} %get-tuple-element.219.dq_ref, bf16[2,1024,256]{2,1,0:T(8,128)(2,1)} %get-tuple-element.220.dk_ref, bf16[2,1024,256]{2,1,0:T(8,128)(2,1)} %get-tuple-element.221.dv_ref, bf16[1024,1536]{1,0:T(8,128)(2,1)} %bitcast.119), custom_call_target="tpu_custom_call" | custom-call | flops 6442450944 | bytes 1048576 | tf_op jit(solution)/shard_map/input_grads/pallas_call | solution.py:439
  266.5 3.4 collective-permute-done.36.came_ref
  269.9 2.2 collective-permute-done.35.came_ref
  272.2 2.4 down_add.3
  276.0 2.4 half_sum.3
  278.3 2.5 half_sum.2
  280.8 7.9 %collective-permute-done.37.refs_2_ = bf16[2,128,1024]{2,1,0:T(8,128)(2,1)S(1)} collective-permute-done((bf16[2,128,1024]{2,1,0:T(8,128)(2,1)}, bf16[2,128,1024]{2,1,0:T(8,128)(2,1)S(1)}, u32[]{:S(2)}, u32[]{:S(2)}) %collective-permute-start.37) | collective-permute-done | bytes 524320 | tf_op jit(solution)/shard_map/ppermute | solution.py:50
  290.0 2.4 down_add.4
  294.3 1.5 collective-permute-start.41
  297.0 5.3 %collective-permute-done.41.low_came = bf16[128,1536]{1,0:T(8,128)(2,1)S(1)} collective-permute-done((bf16[128,1536]{1,0:T(8,128)(2,1)S(1)}, bf16[128,1536]{1,0:T(8,128)(2,1)S(1)}, u32[]{:S(2)}, u32[]{:S(2)}) %collective-permute-start.41) | collective-permute-done | bytes 393248 | tf_op jit(solution)/shard_map/ppermute | solution.py:40
  303.1 2.5 collective-permute-done.39.refs_2_
  305.6 2.8 to_ctx.1
  310.2 3.1 collective-permute-start.45
  313.3 2.3 down_add.5
  315.6 3.6 %all-to-all-start.1 = ((bf16[4,64,1920]{2,1,0:T(8,128)(2,1)}), bf16[4,64,1920]{2,1,0:T(8,128)(2,1)S(1)}, u32[]{:S(2)}, u32[]{:S(2)}) async-start(bf16[4,64,1920]{2,1,0:T(8,128)(2,1)} %reduce-scatter.2.cloned.1.call-done), calls=%async_computation.2 | async-start | bytes 1966080 | tf_op jit(solution)/shard_map/all_to_all | solution.py:990
  320.5 3.7 %collective-permute-done.43 = bf16[80,1536]{1,0:T(8,128)(2,1)S(1)} collective-permute-done((bf16[80,1536]{1,0:T(8,128)(2,1)}, bf16[80,1536]{1,0:T(8,128)(2,1)S(1)}, u32[]{:S(2)}, u32[]{:S(2)}) %collective-permute-start.43) | collective-permute-done | bytes 245792 | tf_op jit(solution)/shard_map/ppermute | solution.py:55
  329.4 2.4 finish.1
  331.8 4.0 %collective-permute-done.42.came_ref = bf16[2,128,1024]{2,1,0:T(8,128)(2,1)S(1)} collective-permute-done((bf16[2,128,1024]{2,1,0:T(8,128)(2,1)S(1)}, bf16[2,128,1024]{2,1,0:T(8,128)(2,1)S(1)}, u32[]{:S(2)}, u32[]{:S(2)}) %collective-permute-start.42) | collective-permute-done | bytes 524320 | tf_op jit(solution)/shard_map/ppermute | solution.py:50
  336.6 3.0 last_step.1
  (205 shorter events, 39.7 us)
Async XLA Ops:
  7.2 8.3 %copy-start.17 = (bf16[512,64]{0,1:T(8,128)(2,1)S(1)}, bf16[512,64]{0,1:T(8,128)(2,1)}, u32[]{:S(2)}) copy-start(bf16[512,64]{0,1:T(8,128)(2,1)} %param.22) | copy-start | bytes 196612
  7.2 8.3 %copy-start.19 = (bf16[64,256]{1,0:T(8,128)(2,1)S(1)}, bf16[64,256]{1,0:T(8,128)(2,1)}, u32[]{:S(2)}) copy-start(bf16[64,256]{1,0:T(8,128)(2,1)} %param.21) | copy-start | bytes 98308
  7.2 8.3 %copy-start.20 = (bf16[64,256]{1,0:T(8,128)(2,1)S(1)}, bf16[64,256]{1,0:T(8,128)(2,1)}, u32[]{:S(2)}) copy-start(bf16[64,256]{1,0:T(8,128)(2,1)} %param.20) | copy-start | bytes 98308
  7.2 8.3 %copy-start.18 = (bf16[64,512]{1,0:T(8,128)(2,1)S(1)}, bf16[64,512]{1,0:T(8,128)(2,1)}, u32[]{:S(2)}) copy-start(bf16[64,512]{1,0:T(8,128)(2,1)} %param.19) | copy-start | bytes 196612
  9.7 61.2 %copy-start.6 = (bf16[2,128,1024]{2,1,0:T(8,128)(2,1)}, bf16[2,128,1024]{2,1,0:T(8,128)(2,1)S(1)}, u32[]{:S(2)}) copy-start(bf16[2,128,1024]{2,1,0:T(8,128)(2,1)S(1)} %fusion.2.refs_0_) | copy-start | bytes 1572868
  9.8 28.8 %collective-permute-start = (bf16[2,128,1024]{2,1,0:T(8,128)(2,1)S(1)}, bf16[2,128,1024]{2,1,0:T(8,128)(2,1)}, u32[]{:S(2)}, u32[]{:S(2)}) collective-permute-start(bf16[2,128,1024]{2,1,0:T(8,128)(2,1)S(1)} %fusion.2.refs_0_), channel_id=1, source_target_pairs={{0,2},{2,4},{4,6},{1,3},{3,5},{5,7},{8,10},{10,12},{12,14},{9,11},... | collective-permute-start | bytes 1572872 | tf_op jit(solution)/shard_map/ppermute | solution.py:45
  15.6 15.7 %collective-permute-start.3 = (bf16[64,1536]{1,0:T(8,128)(2,1)S(1)}, bf16[64,1536]{1,0:T(8,128)(2,1)S(1)}, u32[]{:S(2)}, u32[]{:S(2)}) collective-permute-start(bf16[64,1536]{1,0:T(8,128)(2,1)S(1)} %pad_maximum_fusion.7), channel_id=1, source_target_pairs={{0,6},{2,0},{4,2},{6,4},{1,7},{3,1},{5,3},{7,5},{8,14},{10,8},{12,... | collective-permute-start | bytes 589832 | tf_op jit(solution)/shard_map/ppermute | solution.py:55
  16.2 19.3 %collective-permute-start.2 = (bf16[64,1536]{1,0:T(8,128)(2,1)S(1)}, bf16[64,1536]{1,0:T(8,128)(2,1)S(1)}, u32[]{:S(2)}, u32[]{:S(2)}) collective-permute-start(bf16[64,1536]{1,0:T(8,128)(2,1)S(1)} %pad_maximum_fusion.7), channel_id=1, source_target_pairs={{0,4},{2,6},{4,0},{6,2},{1,5},{3,7},{5,1},{7,3},{8,12},{10,14},{12... | collective-permute-start | bytes 589832 | tf_op jit(solution)/shard_map/ppermute | solution.py:55
  17.9 20.7 %collective-permute-start.1 = (bf16[64,1536]{1,0:T(8,128)(2,1)S(1)}, bf16[64,1536]{1,0:T(8,128)(2,1)S(1)}, u32[]{:S(2)}, u32[]{:S(2)}) collective-permute-start(bf16[64,1536]{1,0:T(8,128)(2,1)S(1)} %pad_maximum_fusion.7), channel_id=1, source_target_pairs={{0,2},{2,4},{4,6},{6,0},{1,3},{3,5},{5,7},{7,1},{8,10},{10,12},{12... | collective-permute-start | bytes 589832 | tf_op jit(solution)/shard_map/ppermute | solution.py:55
  21.6 32.2 %all-to-all-start = ((bf16[4,64,1920]{2,1,0:T(8,128)(2,1)}), bf16[4,64,1920]{2,1,0:T(8,128)(2,1)S(1)}, u32[]{:S(2)}, u32[]{:S(2)}) async-start(bf16[4,64,1920]{2,1,0:T(8,128)(2,1)} %pack.1), calls=%async_computation | async-start | bytes 1966080 | tf_op jit(solution)/shard_map/all_to_all | solution.py:857
  25.3 120.3 %all-gather.2.cloned.1.call-start = ((), (), s32[]{:S(2)}) async-start(), calls=%async_computation.3 | async-start | bytes 4915200 | tf_op jit(solution)/shard_map/all_gather | solution.py:869
  38.8 11.8 %collective-permute-start.10 = (bf16[1,128,1536]{2,1,0:T(8,128)(2,1)S(1)}, bf16[1,128,1536]{2,1,0:T(8,128)(2,1)S(1)}, u32[]{:S(2)}, u32[]{:S(2)}) collective-permute-start(bf16[1,128,1536]{2,1,0:T(8,128)(2,1)S(1)} %bitcast.125), channel_id=1, source_target_pairs={{0,8},{8,0},{16,24},{24,16},{1,9},{9,1},{17,25},{25,17},{2,10},{10... | collective-permute-start | bytes 1179656 | tf_op jit(solution)/shard_map/ppermute | solution.py:40
  40.4 11.7 %collective-permute-start.12 = (bf16[1,128,1536]{2,1,0:T(8,128)(2,1)S(1)}, bf16[1,128,1536]{2,1,0:T(8,128)(2,1)S(1)}, u32[]{:S(2)}, u32[]{:S(2)}) collective-permute-start(bf16[1,128,1536]{2,1,0:T(8,128)(2,1)S(1)} %bitcast.122), channel_id=1, source_target_pairs={{0,16},{8,24},{16,0},{24,8},{1,17},{9,25},{17,1},{25,9},{2,18},{10... | collective-permute-start | bytes 1179656 | tf_op jit(solution)/shard_map/ppermute | solution.py:40
  42.0 24.7 %copy-start.24 = (pred[2,128]{1,0:T(4,128)(4,1)}, pred[2,128]{1,0:T(4,128)(4,1)S(1)}, u32[]{:S(2)}) copy-start(pred[2,128]{1,0:T(4,128)(4,1)S(1)} %broadcast_compare_fusion) | copy-start | bytes 772
  42.0 17.7 %collective-permute-start.4 = (bf16[2,128,1024]{2,1,0:T(8,128)(2,1)}, bf16[2,128,1024]{2,1,0:T(8,128)(2,1)}, u32[]{:S(2)}, u32[]{:S(2)}) collective-permute-start(bf16[2,128,1024]{2,1,0:T(8,128)(2,1)} %collective-permute-done.refs_2_), channel_id=1, source_target_pairs={{0,2},{2,4},{4,6},{1,3},{3,5},{5,7},{8,10},{10,12},{12,14},{9,11},... | collective-permute-start | bytes 1572872 | tf_op jit(solution)/shard_map/ppermute | solution.py:45
  50.5 15.0 %copy-start.38 = (f32[64]{0:T(128)S(1)}, f32[64]{0:T(128)}, u32[]{:S(2)}) copy-start(f32[64]{0:T(128)} %param.17) | copy-start | bytes 772
  50.5 15.6 %copy-start.39 = (f32[64]{0:T(128)S(1)}, f32[64]{0:T(128)}, u32[]{:S(2)}) copy-start(f32[64]{0:T(128)} %param.18) | copy-start | bytes 772
  51.5 21.8 %collective-permute-start.11 = (bf16[2,128,1536]{2,1,0:T(8,128)(2,1)}, bf16[2,128,1536]{2,1,0:T(8,128)(2,1)}, u32[]{:S(2)}, u32[]{:S(2)}) collective-permute-start(bf16[2,128,1536]{2,1,0:T(8,128)(2,1)} %pad_maximum_fusion.5), channel_id=1, source_target_pairs={{0,16},{8,24},{16,0},{24,8},{1,17},{9,25},{17,1},{25,9},{2,18},{10... | collective-permute-start | bytes 2359304 | tf_op jit(solution)/shard_map/ppermute | solution.py:40
  52.0 14.7 %copy-start.9 = (bf16[1,128,1536]{2,1,0:T(8,128)(2,1)}, bf16[1,128,1536]{2,1,0:T(8,128)(2,1)S(1)}, u32[]{:S(2)}) copy-start(bf16[1,128,1536]{2,1,0:T(8,128)(2,1)S(1)} %collective-permute-done.12) | copy-start | bytes 1179652
  53.0 22.1 %collective-permute-start.13 = (bf16[2,128,1536]{2,1,0:T(8,128)(2,1)}, bf16[2,128,1536]{2,1,0:T(8,128)(2,1)}, u32[]{:S(2)}, u32[]{:S(2)}) collective-permute-start(bf16[2,128,1536]{2,1,0:T(8,128)(2,1)} %pad_maximum_fusion.6), channel_id=1, source_target_pairs={{0,8},{8,0},{16,24},{24,16},{1,9},{9,1},{17,25},{25,17},{2,10},{10... | collective-permute-start | bytes 2359304 | tf_op jit(solution)/shard_map/ppermute | solution.py:40
  53.8 17.6 %copy-start.4 = (bf16[4,64,1920]{2,1,0:T(8,128)(2,1)}, bf16[4,64,1920]{2,1,0:T(8,128)(2,1)S(1)}, u32[]{:S(2)}) copy-start(bf16[4,64,1920]{2,1,0:T(8,128)(2,1)S(1)} %all-to-all-done) | copy-start | bytes 2949124
  59.8 13.5 %collective-permute-start.5 = (bf16[2,128,1024]{2,1,0:T(8,128)(2,1)}, bf16[2,128,1024]{2,1,0:T(8,128)(2,1)}, u32[]{:S(2)}, u32[]{:S(2)}) collective-permute-start(bf16[2,128,1024]{2,1,0:T(8,128)(2,1)} %collective-permute-done.4.refs_4_), channel_id=1, source_target_pairs={{0,2},{2,4},{4,6},{1,3},{3,5},{5,7},{8,10},{10,12},{12,14},{9,11},... | collective-permute-start | bytes 1572872 | tf_op jit(solution)/shard_map/ppermute | solution.py:45
  71.0 6.1 %collective-permute-start.7 = (bf16[2,128,1024]{2,1,0:T(8,128)(2,1)}, bf16[2,128,1024]{2,1,0:T(8,128)(2,1)}, u32[]{:S(2)}, u32[]{:S(2)}) collective-permute-start(bf16[2,128,1024]{2,1,0:T(8,128)(2,1)} %collective-permute-done.refs_2_), channel_id=1, source_target_pairs={{0,1},{1,0},{2,3},{3,2},{4,5},{5,4},{6,7},{7,6},{8,9},{9,8},{10,11... | collective-permute-start | bytes 1572872 | tf_op jit(solution)/shard_map/ppermute | solution.py:35
  71.0 6.0 %collective-permute-start.6 = (bf16[2,128,1024]{2,1,0:T(8,128)(2,1)S(1)}, bf16[2,128,1024]{2,1,0:T(8,128)(2,1)}, u32[]{:S(2)}, u32[]{:S(2)}) collective-permute-start(bf16[2,128,1024]{2,1,0:T(8,128)(2,1)S(1)} %fusion.2.refs_0_), channel_id=1, source_target_pairs={{0,1},{1,0},{2,3},{3,2},{4,5},{5,4},{6,7},{7,6},{8,9},{9,8},{10,11... | collective-permute-start | bytes 1572872 | tf_op jit(solution)/shard_map/ppermute | solution.py:35
  71.5 217.2 %reduce-scatter.2.cloned.1.call-start = ((), (), s32[]{:S(2)}) async-start(), calls=%async_computation.4 | async-start | bytes 4915200 | tf_op jit(solution)/shard_map/reduce_scatter | solution.py:920
  73.3 3.8 %collective-permute-start.8 = (bf16[2,128,1024]{2,1,0:T(8,128)(2,1)}, bf16[2,128,1024]{2,1,0:T(8,128)(2,1)S(1)}, u32[]{:S(2)}, u32[]{:S(2)}) collective-permute-start(bf16[2,128,1024]{2,1,0:T(8,128)(2,1)} %collective-permute-done.4.refs_4_), channel_id=1, source_target_pairs={{0,1},{1,0},{2,3},{3,2},{4,5},{5,4},{6,7},{7,6},{8,9},{9,8},{10,11... | collective-permute-start | bytes 1572872 | tf_op jit(solution)/shard_map/ppermute | solution.py:35
  73.3 3.8 %collective-permute-start.9 = (bf16[2,128,1024]{2,1,0:T(8,128)(2,1)}, bf16[2,128,1024]{2,1,0:T(8,128)(2,1)S(1)}, u32[]{:S(2)}, u32[]{:S(2)}) collective-permute-start(bf16[2,128,1024]{2,1,0:T(8,128)(2,1)} %collective-permute-done.5.refs_6_), channel_id=1, source_target_pairs={{0,1},{1,0},{2,3},{3,2},{4,5},{5,4},{6,7},{7,6},{8,9},{9,8},{10,11... | collective-permute-start | bytes 1572872 | tf_op jit(solution)/shard_map/ppermute | solution.py:35
  77.1 26.5 %collective-permute-start.16 = (bf16[2,128,1024]{2,1,0:T(8,128)(2,1)S(1)}, bf16[2,128,1024]{2,1,0:T(8,128)(2,1)S(1)}, u32[]{:S(2)}, u32[]{:S(2)}) collective-permute-start(bf16[2,128,1024]{2,1,0:T(8,128)(2,1)S(1)} %broadcast_select_fusion), channel_id=1, source_target_pairs={{0,24},{8,16},{16,8},{24,0},{1,25},{9,17},{17,9},{25,1},{2,26},{10... | collective-permute-start | bytes 1572872 | tf_op jit(solution)/shard_map/ppermute | solution.py:40
  77.6 26.0 %collective-permute-start.15 = (bf16[2,128,1024]{2,1,0:T(8,128)(2,1)S(1)}, bf16[2,128,1024]{2,1,0:T(8,128)(2,1)S(1)}, u32[]{:S(2)}, u32[]{:S(2)}) collective-permute-start(bf16[2,128,1024]{2,1,0:T(8,128)(2,1)S(1)} %broadcast_select_fusion), channel_id=1, source_target_pairs={{0,16},{8,24},{16,0},{24,8},{1,17},{9,25},{17,1},{25,9},{2,18},{10... | collective-permute-start | bytes 1572872 | tf_op jit(solution)/shard_map/ppermute | solution.py:40
  79.1 24.4 %collective-permute-start.14 = (bf16[2,128,1024]{2,1,0:T(8,128)(2,1)S(1)}, bf16[2,128,1024]{2,1,0:T(8,128)(2,1)S(1)}, u32[]{:S(2)}, u32[]{:S(2)}) collective-permute-start(bf16[2,128,1024]{2,1,0:T(8,128)(2,1)S(1)} %broadcast_select_fusion), channel_id=1, source_target_pairs={{0,8},{8,0},{16,24},{24,16},{1,9},{9,1},{17,25},{25,17},{2,10},{10... | collective-permute-start | bytes 1572872 | tf_op jit(solution)/shard_map/ppermute | solution.py:40
  105.4 2.7 collective-permute-start.17
  108.5 14.0 %collective-permute-start.19 = (bf16[2,128,1024]{2,1,0:T(8,128)(2,1)S(1)}, bf16[2,128,1024]{2,1,0:T(8,128)(2,1)S(1)}, u32[]{:S(2)}, u32[]{:S(2)}) collective-permute-start(bf16[2,128,1024]{2,1,0:T(8,128)(2,1)S(1)} %multiply_convert_fusion), channel_id=1, source_target_pairs={{0,16},{8,24},{16,0},{24,8},{1,17},{9,25},{17,1},{25,9},{2,18},{10... | collective-permute-start | bytes 1572872 | tf_op jit(solution)/shard_map/ppermute | solution.py:40
  109.1 14.8 %collective-permute-start.18 = (bf16[2,128,1024]{2,1,0:T(8,128)(2,1)S(1)}, bf16[2,128,1024]{2,1,0:T(8,128)(2,1)S(1)}, u32[]{:S(2)}, u32[]{:S(2)}) collective-permute-start(bf16[2,128,1024]{2,1,0:T(8,128)(2,1)S(1)} %multiply_convert_fusion), channel_id=1, source_target_pairs={{0,8},{8,0},{16,24},{24,16},{1,9},{9,1},{17,25},{25,17},{2,10},{10... | collective-permute-start | bytes 1572872 | tf_op jit(solution)/shard_map/ppermute | solution.py:40
  109.6 25.4 %collective-permute-start.20 = (bf16[2,128,1024]{2,1,0:T(8,128)(2,1)S(1)}, bf16[2,128,1024]{2,1,0:T(8,128)(2,1)S(1)}, u32[]{:S(2)}, u32[]{:S(2)}) collective-permute-start(bf16[2,128,1024]{2,1,0:T(8,128)(2,1)S(1)} %multiply_convert_fusion), channel_id=1, source_target_pairs={{0,24},{8,16},{16,8},{24,0},{1,25},{9,17},{17,9},{25,1},{2,26},{10... | collective-permute-start | bytes 1572872 | tf_op jit(solution)/shard_map/ppermute | solution.py:40
  113.7 31.9 %collective-permute-start.22 = (bf16[4,2,128,1024]{3,2,1,0:T(8,128)(2,1)}, bf16[4,2,128,1024]{3,2,1,0:T(8,128)(2,1)}, u32[]{:S(2)}, u32[]{:S(2)}) collective-permute-start(bf16[4,2,128,1024]{3,2,1,0:T(8,128)(2,1)} %pad_maximum_fusion.2), channel_id=1, source_target_pairs={{0,1},{1,0},{2,3},{3,2},{4,5},{5,4},{6,7},{7,6},{8,9},{9,8},{10,11... | collective-permute-start | bytes 6291464 | tf_op jit(solution)/shard_map/ppermute | solution.py:35
  136.6 9.0 %collective-permute-start.21 = (bf16[4,2,128,1024]{3,2,1,0:T(8,128)(2,1)}, bf16[4,2,128,1024]{3,2,1,0:T(8,128)(2,1)}, u32[]{:S(2)}, u32[]{:S(2)}) collective-permute-start(bf16[4,2,128,1024]{3,2,1,0:T(8,128)(2,1)} %pad_maximum_fusion.1), channel_id=1, source_target_pairs={{0,1},{1,0},{2,3},{3,2},{4,5},{5,4},{6,7},{7,6},{8,9},{9,8},{10,11... | collective-permute-start | bytes 6291464 | tf_op jit(solution)/shard_map/ppermute | solution.py:35
  165.0 3.7 %collective-permute-start.23 = (bf16[3,2,128,1024]{3,2,1,0:T(8,128)(2,1)}, bf16[3,2,128,1024]{3,2,1,0:T(8,128)(2,1)S(1)}, u32[]{:S(2)}, u32[]{:S(2)}) collective-permute-start(bf16[3,2,128,1024]{3,2,1,0:T(8,128)(2,1)} %bitcast.152), channel_id=1, source_target_pairs={{0,1},{1,0},{2,3},{3,2},{4,5},{5,4},{6,7},{7,6},{8,9},{9,8},{10,11... | collective-permute-start | bytes 4718600 | tf_op jit(solution)/shard_map/ppermute | solution.py:35
  165.1 8.7 %collective-permute-start.24 = (bf16[3,2,128,1024]{3,2,1,0:T(8,128)(2,1)}, bf16[3,2,128,1024]{3,2,1,0:T(8,128)(2,1)S(1)}, u32[]{:S(2)}, u32[]{:S(2)}) collective-permute-start(bf16[3,2,128,1024]{3,2,1,0:T(8,128)(2,1)} %bitcast.151), channel_id=1, source_target_pairs={{0,1},{1,0},{2,3},{3,2},{4,5},{5,4},{6,7},{7,6},{8,9},{9,8},{10,11... | collective-permute-start | bytes 4718600 | tf_op jit(solution)/shard_map/ppermute | solution.py:35
  170.3 28.6 %collective-permute-start.25 = (bf16[2,128,1024]{2,1,0:T(8,128)(2,1)}, bf16[2,128,1024]{2,1,0:T(8,128)(2,1)S(1)}, u32[]{:S(2)}, u32[]{:S(2)}) collective-permute-start(bf16[2,128,1024]{2,1,0:T(8,128)(2,1)} %get-tuple-element.184), channel_id=1, source_target_pairs={{0,8},{8,0},{16,24},{24,16},{1,9},{9,1},{17,25},{25,17},{2,10},{10... | collective-permute-start | bytes 1572872 | tf_op jit(solution)/shard_map/ppermute | solution.py:40
  171.8 27.2 %collective-permute-start.26 = (bf16[2,128,1024]{2,1,0:T(8,128)(2,1)}, bf16[2,128,1024]{2,1,0:T(8,128)(2,1)S(1)}, u32[]{:S(2)}, u32[]{:S(2)}) collective-permute-start(bf16[2,128,1024]{2,1,0:T(8,128)(2,1)} %get-tuple-element.185), channel_id=1, source_target_pairs={{0,16},{8,24},{16,0},{24,8},{1,17},{9,25},{17,1},{25,9},{2,18},{10... | collective-permute-start | bytes 1572872 | tf_op jit(solution)/shard_map/ppermute | solution.py:40
  173.3 25.7 %collective-permute-start.27 = (bf16[2,128,1024]{2,1,0:T(8,128)(2,1)}, bf16[2,128,1024]{2,1,0:T(8,128)(2,1)S(1)}, u32[]{:S(2)}, u32[]{:S(2)}) collective-permute-start(bf16[2,128,1024]{2,1,0:T(8,128)(2,1)} %get-tuple-element.186), channel_id=1, source_target_pairs={{0,24},{8,16},{16,8},{24,0},{1,25},{9,17},{17,9},{25,1},{2,26},{10... | collective-permute-start | bytes 1572872 | tf_op jit(solution)/shard_map/ppermute | solution.py:40
  199.0 2.2 collective-permute-start.28
  204.5 2.3 collective-permute-start.29
  204.7 34.1 %collective-permute-start.30 = (bf16[2,128,1024]{2,1,0:T(8,128)(2,1)}, bf16[2,128,1024]{2,1,0:T(8,128)(2,1)S(1)}, u32[]{:S(2)}, u32[]{:S(2)}) collective-permute-start(bf16[2,128,1024]{2,1,0:T(8,128)(2,1)} %bitcast.52), channel_id=1, source_target_pairs={{0,1},{1,0},{2,3},{3,2},{4,5},{5,4},{6,7},{7,6},{8,9},{9,8},{10,11... | collective-permute-start | bytes 1572872 | tf_op jit(solution)/shard_map/ppermute | solution.py:35
  209.8 29.0 %collective-permute-start.31 = (bf16[2,128,1024]{2,1,0:T(8,128)(2,1)S(1)}, bf16[2,128,1024]{2,1,0:T(8,128)(2,1)S(1)}, u32[]{:S(2)}, u32[]{:S(2)}) collective-permute-start(bf16[2,128,1024]{2,1,0:T(8,128)(2,1)S(1)} %get-tuple-element.205), channel_id=1, source_target_pairs={{0,8},{8,0},{16,24},{24,16},{1,9},{9,1},{17,25},{25,17},{2,10},{10... | collective-permute-start | bytes 1572872 | tf_op jit(solution)/shard_map/ppermute | solution.py:40
  211.3 27.5 %collective-permute-start.32 = (bf16[2,128,1024]{2,1,0:T(8,128)(2,1)S(1)}, bf16[2,128,1024]{2,1,0:T(8,128)(2,1)S(1)}, u32[]{:S(2)}, u32[]{:S(2)}) collective-permute-start(bf16[2,128,1024]{2,1,0:T(8,128)(2,1)S(1)} %get-tuple-element.206), channel_id=1, source_target_pairs={{0,16},{8,24},{16,0},{24,8},{1,17},{9,25},{17,1},{25,9},{2,18},{10... | collective-permute-start | bytes 1572872 | tf_op jit(solution)/shard_map/ppermute | solution.py:40
  212.8 26.0 %collective-permute-start.33 = (bf16[2,128,1024]{2,1,0:T(8,128)(2,1)S(1)}, bf16[2,128,1024]{2,1,0:T(8,128)(2,1)S(1)}, u32[]{:S(2)}, u32[]{:S(2)}) collective-permute-start(bf16[2,128,1024]{2,1,0:T(8,128)(2,1)S(1)} %get-tuple-element.207), channel_id=1, source_target_pairs={{0,24},{8,16},{16,8},{24,0},{1,25},{9,17},{17,9},{25,1},{2,26},{10... | collective-permute-start | bytes 1572872 | tf_op jit(solution)/shard_map/ppermute | solution.py:40
  250.9 7.1 %copy-start.12 = (bf16[256,1024]{1,0:T(8,128)(2,1)S(1)}, bf16[256,1024]{1,0:T(8,128)(2,1)}, u32[]{:S(2)}) copy-start(bf16[256,1024]{1,0:T(8,128)(2,1)} %get-tuple-element.203) | copy-start | bytes 1572868
  250.9 7.1 %copy-start.25 = (pred[2,128]{1,0:T(4,128)(4,1)S(1)}, pred[2,128]{1,0:T(4,128)(4,1)}, u32[]{:S(2)}) copy-start(pred[2,128]{1,0:T(4,128)(4,1)} %copy-done.24) | copy-start | bytes 772
  250.9 19.0 %collective-permute-start.36 = (bf16[256,1536]{1,0:T(8,128)(2,1)}, bf16[256,1536]{1,0:T(8,128)(2,1)S(1)}, u32[]{:S(2)}, u32[]{:S(2)}) collective-permute-start(bf16[256,1536]{1,0:T(8,128)(2,1)} %get-tuple-element.231), channel_id=1, source_target_pairs={{0,16},{8,24},{16,0},{24,8},{1,17},{9,25},{17,1},{25,9},{2,18},{10... | collective-permute-start | bytes 2359304 | tf_op jit(solution)/shard_map/ppermute | solution.py:40
  252.4 19.7 %collective-permute-start.35 = (bf16[272,1536]{1,0:T(8,128)(2,1)}, bf16[272,1536]{1,0:T(8,128)(2,1)S(1)}, u32[]{:S(2)}, u32[]{:S(2)}) collective-permute-start(bf16[272,1536]{1,0:T(8,128)(2,1)} %get-tuple-element.230), channel_id=1, source_target_pairs={{0,8},{8,0},{16,24},{24,16},{1,9},{9,1},{17,25},{25,17},{2,10},{10... | collective-permute-start | bytes 2506760 | tf_op jit(solution)/shard_map/ppermute | solution.py:40
  258.0 8.5 %collective-permute-start.34 = (bf16[1,2,128,1024]{3,2,1,0:T(8,128)(2,1)}, bf16[1,2,128,1024]{3,2,1,0:T(8,128)(2,1)S(1)}, u32[]{:S(2)}, u32[]{:S(2)}) collective-permute-start(bf16[1,2,128,1024]{3,2,1,0:T(8,128)(2,1)} %get-tuple-element.224), channel_id=1, source_target_pairs={{0,1},{1,0},{2,3},{3,2},{4,5},{5,4},{6,7},{7,6},{8,9},{9,8},{10,11... | collective-permute-start | bytes 1572872 | tf_op jit(solution)/shard_map/ppermute | solution.py:35
  274.6 14.1 %collective-permute-start.37 = (bf16[2,128,1024]{2,1,0:T(8,128)(2,1)}, bf16[2,128,1024]{2,1,0:T(8,128)(2,1)S(1)}, u32[]{:S(2)}, u32[]{:S(2)}) collective-permute-start(bf16[2,128,1024]{2,1,0:T(8,128)(2,1)} %down_add.3), channel_id=1, source_target_pairs={{2,0},{4,2},{6,4},{3,1},{5,3},{7,5},{10,8},{12,10},{14,12},{11,9},... | collective-permute-start | bytes 1572872 | tf_op jit(solution)/shard_map/ppermute | solution.py:50
  275.9 12.8 %collective-permute-start.38 = (bf16[3,2,128,1024]{3,2,1,0:T(8,128)(2,1)}, bf16[3,2,128,1024]{3,2,1,0:T(8,128)(2,1)S(1)}, u32[]{:S(2)}, u32[]{:S(2)}) collective-permute-start(bf16[3,2,128,1024]{3,2,1,0:T(8,128)(2,1)} %get-tuple-element.235), channel_id=1, source_target_pairs={{0,1},{1,0},{2,3},{3,2},{4,5},{5,4},{6,7},{7,6},{8,9},{9,8},{10,11... | collective-permute-start | bytes 4718600 | tf_op jit(solution)/shard_map/ppermute | solution.py:35
  292.4 13.2 %collective-permute-start.39 = (bf16[2,128,1024]{2,1,0:T(8,128)(2,1)}, bf16[2,128,1024]{2,1,0:T(8,128)(2,1)S(1)}, u32[]{:S(2)}, u32[]{:S(2)}) collective-permute-start(bf16[2,128,1024]{2,1,0:T(8,128)(2,1)} %down_add.4), channel_id=1, source_target_pairs={{2,0},{4,2},{6,4},{3,1},{5,3},{7,5},{10,8},{12,10},{14,12},{11,9},... | collective-permute-start | bytes 1572872 | tf_op jit(solution)/shard_map/ppermute | solution.py:50
  293.7 9.4 %collective-permute-start.40 = (bf16[144,1536]{1,0:T(8,128)(2,1)S(1)}, bf16[144,1536]{1,0:T(8,128)(2,1)S(1)}, u32[]{:S(2)}, u32[]{:S(2)}) collective-permute-start(bf16[144,1536]{1,0:T(8,128)(2,1)S(1)} %copy-done.21), channel_id=1, source_target_pairs={{0,16},{8,24},{16,0},{24,8},{1,17},{9,25},{17,1},{25,9},{2,18},{10... | collective-permute-start | bytes 1327112 | tf_op jit(solution)/shard_map/ppermute | solution.py:40
  294.3 8.0 %collective-permute-start.41 = (bf16[128,1536]{1,0:T(8,128)(2,1)S(1)}, bf16[128,1536]{1,0:T(8,128)(2,1)S(1)}, u32[]{:S(2)}, u32[]{:S(2)}) collective-permute-start(bf16[128,1536]{1,0:T(8,128)(2,1)S(1)} %copy-done.36), channel_id=1, source_target_pairs={{0,8},{8,0},{16,24},{24,16},{1,9},{9,1},{17,25},{25,17},{2,10},{10... | collective-permute-start | bytes 1179656 | tf_op jit(solution)/shard_map/ppermute | solution.py:40
  308.5 15.8 %collective-permute-start.43 = (bf16[80,1536]{1,0:T(8,128)(2,1)}, bf16[80,1536]{1,0:T(8,128)(2,1)S(1)}, u32[]{:S(2)}, u32[]{:S(2)}) collective-permute-start(bf16[80,1536]{1,0:T(8,128)(2,1)} %get-tuple-element.264), channel_id=1, source_target_pairs={{0,4},{2,6},{4,0},{6,2},{1,5},{3,7},{5,1},{7,3},{8,12},{10,14},{12... | collective-permute-start | bytes 737288 | tf_op jit(solution)/shard_map/ppermute | solution.py:55
  309.5 14.8 %collective-permute-start.44 = (bf16[80,1536]{1,0:T(8,128)(2,1)}, bf16[80,1536]{1,0:T(8,128)(2,1)S(1)}, u32[]{:S(2)}, u32[]{:S(2)}) collective-permute-start(bf16[80,1536]{1,0:T(8,128)(2,1)} %get-tuple-element.265), channel_id=1, source_target_pairs={{0,2},{2,4},{4,6},{6,0},{1,3},{3,5},{5,7},{7,1},{8,10},{10,12},{12... | collective-permute-start | bytes 737288 | tf_op jit(solution)/shard_map/ppermute | solution.py:55
  310.2 14.7 %collective-permute-start.45 = (bf16[80,1536]{1,0:T(8,128)(2,1)}, bf16[80,1536]{1,0:T(8,128)(2,1)S(1)}, u32[]{:S(2)}, u32[]{:S(2)}) collective-permute-start(bf16[80,1536]{1,0:T(8,128)(2,1)} %get-tuple-element.266), channel_id=1, source_target_pairs={{0,6},{2,0},{4,2},{6,4},{1,7},{3,1},{5,3},{7,5},{8,14},{10,8},{12,... | collective-permute-start | bytes 737288 | tf_op jit(solution)/shard_map/ppermute | solution.py:55
  315.6 10.2 %copy-start.15 = (f32[64,1536]{1,0:T(8,128)S(1)}, f32[64,1536]{1,0:T(8,128)}, u32[]{:S(2)}) copy-start(f32[64,1536]{1,0:T(8,128)} %get-tuple-element.267) | copy-start | bytes 1179652
  315.6 12.8 %all-to-all-start.1 = ((bf16[4,64,1920]{2,1,0:T(8,128)(2,1)}), bf16[4,64,1920]{2,1,0:T(8,128)(2,1)S(1)}, u32[]{:S(2)}, u32[]{:S(2)}) async-start(bf16[4,64,1920]{2,1,0:T(8,128)(2,1)} %reduce-scatter.2.cloned.1.call-done), calls=%async_computation.2 | async-start | bytes 1966080 | tf_op jit(solution)/shard_map/all_to_all | solution.py:990
  319.2 16.6 %collective-permute-start.42 = (bf16[2,128,1024]{2,1,0:T(8,128)(2,1)S(1)}, bf16[2,128,1024]{2,1,0:T(8,128)(2,1)S(1)}, u32[]{:S(2)}, u32[]{:S(2)}) collective-permute-start(bf16[2,128,1024]{2,1,0:T(8,128)(2,1)S(1)} %copy-done.30), channel_id=1, source_target_pairs={{2,0},{4,2},{6,4},{3,1},{5,3},{7,5},{10,8},{12,10},{14,12},{11,9},... | collective-permute-start | bytes 1572872 | tf_op jit(solution)/shard_map/ppermute | solution.py:50
  325.7 1.6 collective-permute-start.46
  (27 other events, 75.8 us)
Sparse Core Ops, SparseCore 0:
  71.6 73.8 all-gather.1
  205.2 71.2 reduce-scatter.1

commit v6 on v5

--- a/solution.py
+++ b/solution.py
@@ -48,6 +48,10 @@
 def ctx_down(value, step=1):
     size = lax.axis_size("ctx")
     return lax.ppermute(value, "ctx", [(i + step, i) for i in range(size - step)])
+
+
+def ctx_round(value):
+    return ctx_shift(value, lax.axis_size("ctx") - 1)
 
 
 def ctx_shift(value, step):
@@ -608,29 +612,36 @@
 
 
 def ffn_rest_kernel(
-    xm_ref, xo_ref, gm_ref, go_ref, w_ref, inside_ref, ym_ref, yo_ref, dm_ref, do_ref, gain_ref, grad_ref, inner_ref, sum_ref
+    xm_ref, xo_ref, gm_ref, go_ref, w_ref, first_ref, second_ref,
+    ym_ref, yo_ref, dm_ref, do_ref, gain_ref, grad_ref, own_ref, inner_ref, sum_ref
 ):
     units = w_ref.shape[1] // 3
-    half = xm_ref.shape[0]
+    half = ym_ref.shape[0]
     step = pl.program_id(0)
-    x = jnp.concatenate([xm_ref[...], xo_ref[...]])
-    g = jnp.concatenate([gm_ref[...], go_ref[...]])
+
+    def put(ref, place):
+        inner_ref[place * half : (place + 1) * half] = ref[:half]
+        inner_ref[(place + 2) * half : (place + 3) * half] = ref[half:]
 
     @pl.when(step == 0)
     def _():
-        y, d_x, gain_row = ffn_block(x, g, w_ref, inner_ref)
+        x = jnp.concatenate([xm_ref[:half], xo_ref[:half]])
+        g = jnp.concatenate([gm_ref[:half], go_ref[:half]])
+        y, d_x, gain_row = ffn_block(x, g, w_ref, own_ref)
         ym_ref[...] = y[:half]
         yo_ref[...] = y[half:]
         dm_ref[...] = d_x[:half]
         do_ref[...] = d_x[half:]
         gain_ref[...] = gain_row
+        put(own_ref, 0)
 
     @pl.when(step > 0)
     def _():
-        inner_ref[...] = inside_ref[...]
-
-    left = dot(x, inner_ref[:, : 2 * units], TN)
-    right = dot(g, inner_ref[:, 2 * units :], TN)
+        put(first_ref, 0)
+
+    put(second_ref, 1)
+    left = dot(jnp.concatenate([xm_ref[...], xo_ref[...]]), inner_ref[:, : 2 * units], TN)
+    right = dot(jnp.concatenate([gm_ref[...], go_ref[...]]), inner_ref[:, 2 * units :], TN)
 
     @pl.when(step == 0)
     def _():
@@ -672,22 +683,26 @@
     tokens, width = x_mine.shape
     rows = tokens // parts
     units3 = w.shape[1]
-    block = pl.BlockSpec((rows, width), lambda i: (i, 0))
+    block = pl.BlockSpec((2 * rows, width), lambda i: (i, 0))
     whole = pl.BlockSpec((width, units3), lambda i: (0, 0))
+    first = pl.BlockSpec((2 * rows, units3), lambda i: (jnp.maximum(2 * i - 1, 0), 0))
+    second = pl.BlockSpec((2 * rows, units3), lambda i: (2 * i, 0))
     own = pl.BlockSpec((rows, width), lambda i: (0, 0))
     part = jax.ShapeDtypeStruct((rows, width), BF)
     return pl.pallas_call(
         ffn_rest_kernel,
-        grid=(parts,),
-        in_specs=[block] * 4 + [whole, pl.BlockSpec((2 * rows, units3), lambda i: (jnp.maximum(i - 1, 0), 0))],
+        grid=(parts // 2,),
+        in_specs=[block] * 4 + [whole, first, second],
         out_specs=[own] * 4 + [pl.BlockSpec((1, width), lambda i: (0, 0)), whole],
         out_shape=[part] * 4
         + [jax.ShapeDtypeStruct((1, width), F32), jax.ShapeDtypeStruct((width, units3), BF)],
-        scratch_shapes=[pltpu.VMEM((2 * rows, units3), BF), pltpu.VMEM((width, units3), F32)],
+        scratch_shapes=[
+            pltpu.VMEM((2 * rows, units3), BF), pltpu.VMEM((4 * rows, units3), BF), pltpu.VMEM((width, units3), F32)
+        ],
         compiler_params=pltpu.CompilerParams(vmem_limit_bytes=VMEM_LIMIT),
         cost_estimate=pl.CostEstimate(flops=24 << 30, bytes_accessed=24 << 20, transcendentals=0),
         name="ffn_rest",
-    )(x_mine, x_other, g_mine, g_other, w, inside)
+    )(x_mine, x_other, g_mine, g_other, w, inside, inside)
 
 
 def same_kernel(in_ref, out_ref):
@@ -957,7 +972,7 @@
     mine, other = input_grads(d_q, d_k, d_v, attn_w, 0, n_ctx - 1)
     mine, other, last_other, result, *came = tie(mine, other, last_other, result, *came)
     other = swap_cores(other)
-    total = ctx_down(down_add(last_mine, last_other, 0))
+    total = ctx_round(down_add(last_mine, last_other, 0))
     block = n_ctx - 2
     for step in range(1, len(bits)):
         count = n_fsdp >> step
@@ -978,7 +993,7 @@
         own = sent[0][count // 2 * half :]
         came = [fsdp_xor(sent[0], bits[step]), fsdp_xor(sent[1], bits[-1 - step])]
         if block > 0:
-            total = ctx_down(down_add(mine, other, block, total))
+            total = ctx_round(down_add(mine, other, block, total))
             block -= 1
             total, ffn_reduced, *came = tie(total, ffn_reduced, *came)
     ctx_place = jnp.stack([f, c]).astype(jnp.int32)

time: 353 us -> 352 us (level)
  waiting for transfers between devices: 88.9 us -> 85 us
    ppermute x3 -> x1, waiting for transfers between devices: 14.4 us -> 2.92 us  [ctx_down(): lax.ppermute(value, 'ctx', [(i + step, i) for i in range(size - step)])]
    ppermute x6 -> x8, waiting for transfers between devices: 17.5 us -> 25 us  [ctx_shift(): lax.ppermute(value, 'ctx', [(i, (i + step) % size) for i in range(size)])]
    ppermute x6 -> x8, starting transfers between devices: 8.71 us -> 13.9 us  [ctx_shift(): lax.ppermute(value, 'ctx', [(i, (i + step) % size) for i in range(size)])]
where the time goes in v6:
time: 352 us; the launch traced here: 346 us
  Pallas kernels  135 us (38%)
  waiting for transfers between devices  85 us (24%)
  starting transfers between devices  68.8 us (20%)
  other arithmetic  26.6 us (8%)
  between operations  15 us (4%)
  local copies, waits for them, and re-layouts  12 us (3%)
  matrix products  3.79 us (1%)
    ppermute x20, waiting for transfers between devices, fsdp_xor(): return lax.ppermute(value, 'fsdp', [(i, i ^ mask) for i in range(size)])  32.9 us
    pallas_call x1, Pallas kernels, attend_back(): pl.pallas_call(attend_back_kernel, grid=(slots, pairs), in_specs=[smem, q...  25.3 us
    ppermute x8, waiting for transfers between devices, ctx_shift(): lax.ppermute(value, 'ctx', [(i, (i + step) % size) for i in range(size)])  25 us
    pallas_call x1, Pallas kernels, ffn_rest(): pl.pallas_call(ffn_rest_kernel, grid=(parts // 2,), in_specs=[block] * 4...  23.8 us
    ppermute x20, starting transfers between devices, fsdp_xor(): return lax.ppermute(value, 'fsdp', [(i, i ^ mask) for i in range(size)])  23.5 us
    pallas_call x1, Pallas kernels, attend(): pl.pallas_call(functools.partial(attend_kernel, len(pieces), parts), grid...  21.9 us
    ppermute x3, starting transfers between devices, ctx_up(): lax.ppermute(value, 'ctx', [(i, i + step) for i in range(size - step)])  19.4 us
    pallas_call x1, Pallas kernels, feed_forward(): pl.pallas_call(ffn_kernel, grid=(parts - 1,), in_specs=[block] * 4 + [pl....  19.3 us
  transfers between devices with their start and end apart: 51, of which 22 were waited for; matrix products, arithmetic and copies ran while one was open for 9% of the time, Pallas kernels for 31%

profile of v6, /device:TPU:0, one launch (start us, length us, event | category | flops | bytes accessed | tf_op | source)
XLA Modules:
  0.0 345.6 jit_solution(6081412064087459479)
XLA Ops:
  9.8 5.8 %collective-permute-start = (bf16[2,128,1024]{2,1,0:T(8,128)(2,1)S(1)}, bf16[2,128,1024]{2,1,0:T(8,128)(2,1)}, u32[]{:S(2)}, u32[]{:S(2)}) collective-permute-start(bf16[2,128,1024]{2,1,0:T(8,128)(2,1)S(1)} %fusion.2.refs_0_), channel_id=1, source_target_pairs={{0,2},{2,4},{4,6},{1,3},{3,5},{5,7},{8,10},{10,12},{12,14},{9,11},... | collective-permute-start | bytes 1572872 | tf_op jit(solution)/shard_map/ppermute | solution.py:45
  16.2 1.6 collective-permute-start.2
  17.9 1.6 collective-permute-start.1
  19.4 2.2 pack.1
  21.6 3.7 %all-to-all-start = ((bf16[4,64,1920]{2,1,0:T(8,128)(2,1)}), bf16[4,64,1920]{2,1,0:T(8,128)(2,1)S(1)}, u32[]{:S(2)}, u32[]{:S(2)}) async-start(bf16[4,64,1920]{2,1,0:T(8,128)(2,1)} %pack.1), calls=%async_computation | async-start | bytes 1966080 | tf_op jit(solution)/shard_map/all_to_all | solution.py:872
  25.3 5.9 %collective-permute-done.3 = bf16[64,1536]{1,0:T(8,128)(2,1)S(1)} collective-permute-done((bf16[64,1536]{1,0:T(8,128)(2,1)S(1)}, bf16[64,1536]{1,0:T(8,128)(2,1)S(1)}, u32[]{:S(2)}, u32[]{:S(2)}) %collective-permute-start.3) | collective-permute-done | bytes 196640 | tf_op jit(solution)/shard_map/ppermute | solution.py:59
  31.3 4.2 %collective-permute-done.2 = bf16[64,1536]{1,0:T(8,128)(2,1)S(1)} collective-permute-done((bf16[64,1536]{1,0:T(8,128)(2,1)S(1)}, bf16[64,1536]{1,0:T(8,128)(2,1)S(1)}, u32[]{:S(2)}, u32[]{:S(2)}) %collective-permute-start.2) | collective-permute-done | bytes 196640 | tf_op jit(solution)/shard_map/ppermute | solution.py:59
  35.5 3.1 collective-permute-done.1
  38.8 1.6 collective-permute-start.10
  40.4 1.6 collective-permute-start.12
  42.0 8.5 %collective-permute-start.4 = (bf16[2,128,1024]{2,1,0:T(8,128)(2,1)}, bf16[2,128,1024]{2,1,0:T(8,128)(2,1)}, u32[]{:S(2)}, u32[]{:S(2)}) collective-permute-start(bf16[2,128,1024]{2,1,0:T(8,128)(2,1)} %collective-permute-done.refs_2_), channel_id=1, source_target_pairs={{0,2},{2,4},{4,6},{1,3},{3,5},{5,7},{8,10},{10,12},{12,14},{9,11},... | collective-permute-start | bytes 1572872 | tf_op jit(solution)/shard_map/ppermute | solution.py:45
  53.8 5.9 %collective-permute-done.4.refs_4_ = bf16[2,128,1024]{2,1,0:T(8,128)(2,1)} collective-permute-done((bf16[2,128,1024]{2,1,0:T(8,128)(2,1)}, bf16[2,128,1024]{2,1,0:T(8,128)(2,1)}, u32[]{:S(2)}, u32[]{:S(2)}) %collective-permute-start.4) | collective-permute-done | bytes 524320 | tf_op jit(solution)/shard_map/ppermute | solution.py:45
  59.8 5.2 %collective-permute-start.5 = (bf16[2,128,1024]{2,1,0:T(8,128)(2,1)}, bf16[2,128,1024]{2,1,0:T(8,128)(2,1)}, u32[]{:S(2)}, u32[]{:S(2)}) collective-permute-start(bf16[2,128,1024]{2,1,0:T(8,128)(2,1)} %collective-permute-done.4.refs_4_), channel_id=1, source_target_pairs={{0,2},{2,4},{4,6},{1,3},{3,5},{5,7},{8,10},{10,12},{12,14},{9,11},... | collective-permute-start | bytes 1572872 | tf_op jit(solution)/shard_map/ppermute | solution.py:45
  67.9 3.1 fusion.15
  71.7 1.5 collective-permute-done.5.refs_6_
  75.1 1.9 pad_maximum_fusion.4.refs_11_.refs_12_.refs_13_
  77.6 1.5 collective-permute-start.15
  79.1 1.5 collective-permute-start.14
  81.3 21.9 %attend.1 = (bf16[2,256,512]{2,1,0:T(8,128)(2,1)}, f32[2,2,8,256]{3,2,1,0:T(8,128)}, f32[2,256,512]{2,1,0:T(8,128)}, f32[2,1024,256]{2,1,0:T(8,128)}, bf16[2,102...) custom-call(s32[5]{0:T(128)} %pad_add_fusion.scal_ref, ...), custom_call_target="tpu_custom_call" | custom-call | flops 1048576 | bytes 1048576 | tf_op jit(solution)/shard_map/attend/pallas_call | solution.py:274
  105.4 2.6 collective-permute-done.17
  109.6 2.5 collective-permute-start.20
  112.1 1.6 pad_maximum_fusion.2
  113.9 8.7 %collective-permute-done.19 = bf16[2,128,1024]{2,1,0:T(8,128)(2,1)S(1)} collective-permute-done((bf16[2,128,1024]{2,1,0:T(8,128)(2,1)S(1)}, bf16[2,128,1024]{2,1,0:T(8,128)(2,1)S(1)}, u32[]{:S(2)}, u32[]{:S(2)}) %collective-permute-start.19) | collective-permute-done | bytes 524320 | tf_op jit(solution)/shard_map/ppermute | solution.py:40
  123.9 11.1 %collective-permute-done.20 = bf16[2,128,1024]{2,1,0:T(8,128)(2,1)S(1)} collective-permute-done((bf16[2,128,1024]{2,1,0:T(8,128)(2,1)S(1)}, bf16[2,128,1024]{2,1,0:T(8,128)(2,1)S(1)}, u32[]{:S(2)}, u32[]{:S(2)}) %collective-permute-start.20) | collective-permute-done | bytes 524320 | tf_op jit(solution)/shard_map/ppermute | solution.py:40
  135.0 1.7 pad_maximum_fusion.1
  136.6 8.9 %all-gather.2.cloned.1.call-done = bf16[4,256,1920]{2,1,0:T(8,128)(2,1)} async-done(((bf16[4,64,1920]{2,1,0:T(8,128)(2,1)}), bf16[4,256,1920]{2,1,0:T(8,128)(2,1)}) %all-gather.2.cloned.1.call-update) | async-done | bytes 3932176 | tf_op jit(solution)/shard_map/all_gather | solution.py:884
  145.6 19.3 %feed_forward.1 = (bf16[768,1024]{1,0:T(8,128)(2,1)}, bf16[768,1024]{1,0:T(8,128)(2,1)}, bf16[768,1024]{1,0:T(8,128)(2,1)}, bf16[768,1024]{1,0:T(8,128)(2,1)}, b...) custom-call(bf16[1024,1024]{1,0:T(8,128)(2,1)} %bitcast.25.xm_ref, bf16[1024,1024]{1,0:T(8,128)(2,1)} %bitcast.26.xo_ref, ...), custom_call_target="tpu_custom_call" | custom-call | flops 16106127360 | bytes 25165824 | tf_op jit(solution)/shard_map/feed_forward/pallas_call | solution.py:669
  165.4 1.6 fusion.42
  168.5 1.6 fusion.11
  171.6 1.5 collective-permute-start.26
  174.3 23.8 %ffn_rest.1 = (bf16[256,1024]{1,0:T(8,128)(2,1)}, bf16[256,1024]{1,0:T(8,128)(2,1)}, bf16[256,1024]{1,0:T(8,128)(2,1)}, bf16[256,1024]{1,0:T(8,128)(2,1)}, f32[1...) custom-call(bf16[1024,1024]{1,0:T(8,128)(2,1)} %bitcast.25.xm_ref, bf16[1024,1024]{1,0:T(8,128)(2,1)} %bitcast.26.xo_ref, ...), custom_call_target="tpu_custom_call" | custom-call | flops 25769803776 | bytes 25165824 | tf_op jit(solution)/shard_map/ffn_rest/pallas_call | solution.py:692
  198.2 2.1 collective-permute-done.28
  200.3 1.6 multiply_reduce_fusion
  202.0 1.7 fusion.40
  204.2 1.7 collective-permute-done.29.bo_ref
  205.9 3.0 convolution_convert_fusion.d_ref
  210.4 1.5 collective-permute-start.32
  212.5 25.3 %attend_back.1 = (bf16[2,256,512]{2,1,0:T(8,128)(2,1)}, bf16[2,1024,256]{2,1,0:T(8,128)(2,1)}, bf16[2,1024,256]{2,1,0:T(8,128)(2,1)}, f32[1,128]{1,0:T(1,128)}, f32[1,128]{1,0:T(1,128)}) custom-call(s32[5]{0:T(128)} %pad_add_fusion.scal_ref, f32[2,256,512]{2,1,0:T(8,128)} %get-tuple-element.160.q_ref, f32[2,1024,256]{2,1,0:T(8,128)} %get-tuple-element.161.k_ref, ...), custom_call_target="tpu_custom_call" | custom-call | flops 25769803776 | bytes 12582912 | tf_op jit(solution)/shard_map/attend_back/pallas_call | solution.py:307
  239.2 10.7 %weight_grads.1 = (bf16[272,1536]{1,0:T(8,128)(2,1)}, bf16[256,1536]{1,0:T(8,128)(2,1)}, bf16[256,1536]{1,0:T(8,128)(2,1)}, bf16[256,1536]{1,0:T(8,128)(2,1)}, bf16[16,1536]{1,0:T(8,128)(2,1)}) custom-call(s32[1]{0:T(128)} %bitcast.at_ref, bf16[2,1024,1024]{2,1,0:T(8,128)(2,1)} %get-tuple-element.159.x_ref, bf16[2,256,512]{2,1,0:T(8,128)(2,1)} %get-tuple-element.219.dq_ref, ...), custom_call_target="tpu_custom_call" | custom-call | flops 10737418240 | bytes 8388608 | tf_op jit(solution)/shard_map/weight_grads/pallas_call | solution.py:409
  249.9 1.5 collective-permute-start.36
  251.4 1.5 collective-permute-start.35
  252.9 4.1 %input_grads.3 = (f32[1,2,128,1024]{3,2,1,0:T(8,128)}, bf16[1,2,128,1024]{3,2,1,0:T(8,128)(2,1)}) custom-call(bf16[2,256,512]{2,1,0:T(8,128)(2,1)} %get-tuple-element.219.dq_ref, bf16[2,1024,256]{2,1,0:T(8,128)(2,1)} %get-tuple-element.220.dk_ref, bf16[2,1024,256]{2,1,0:T(8,128)(2,1)} %get-tuple-element.221.dv_ref, bf16[1024,1536]{1,0:T(8,128)(2,1)} %bitcast.118), custom_call_target="tpu_custom_call" | custom-call | flops 6442450944 | bytes 1048576 | tf_op jit(solution)/shard_map/input_grads/pallas_call | solution.py:443
  258.3 7.2 %input_grads.2 = (f32[3,2,128,1024]{3,2,1,0:T(8,128)}, bf16[3,2,128,1024]{3,2,1,0:T(8,128)(2,1)}) custom-call(bf16[2,256,512]{2,1,0:T(8,128)(2,1)} %get-tuple-element.219.dq_ref, bf16[2,1024,256]{2,1,0:T(8,128)(2,1)} %get-tuple-element.220.dk_ref, bf16[2,1024,256]{2,1,0:T(8,128)(2,1)} %get-tuple-element.221.dv_ref, bf16[1024,1536]{1,0:T(8,128)(2,1)} %bitcast.119), custom_call_target="tpu_custom_call" | custom-call | flops 6442450944 | bytes 1048576 | tf_op jit(solution)/shard_map/input_grads/pallas_call | solution.py:443
  265.5 3.4 collective-permute-done.36.came_ref
  268.9 2.2 collective-permute-done.35.came_ref
  271.1 2.4 down_add.3
  274.9 2.4 half_sum.3
  277.3 2.5 half_sum.2
  279.8 6.2 %collective-permute-done.37.refs_2_ = bf16[2,128,1024]{2,1,0:T(8,128)(2,1)S(1)} collective-permute-done((bf16[2,128,1024]{2,1,0:T(8,128)(2,1)}, bf16[2,128,1024]{2,1,0:T(8,128)(2,1)S(1)}, u32[]{:S(2)}, u32[]{:S(2)}) %collective-permute-start.37) | collective-permute-done | bytes 524320 | tf_op jit(solution)/shard_map/ppermute | solution.py:59
  287.3 2.4 down_add.4
  289.6 3.3 collective-permute-start.39
  293.5 1.5 collective-permute-start.41
  296.2 6.0 %collective-permute-done.41.low_came = bf16[128,1536]{1,0:T(8,128)(2,1)S(1)} collective-permute-done((bf16[128,1536]{1,0:T(8,128)(2,1)S(1)}, bf16[128,1536]{1,0:T(8,128)(2,1)S(1)}, u32[]{:S(2)}, u32[]{:S(2)}) %collective-permute-start.41) | collective-permute-done | bytes 393248 | tf_op jit(solution)/shard_map/ppermute | solution.py:40
  303.1 2.8 to_ctx.1
  305.9 1.5 collective-permute-start.43
  307.4 2.3 collective-permute-start.44
  309.8 1.5 collective-permute-start.45
  311.3 2.3 down_add.5
  313.5 4.4 %all-to-all-start.1 = ((bf16[4,64,1920]{2,1,0:T(8,128)(2,1)}), bf16[4,64,1920]{2,1,0:T(8,128)(2,1)S(1)}, u32[]{:S(2)}, u32[]{:S(2)}) async-start(bf16[4,64,1920]{2,1,0:T(8,128)(2,1)} %reduce-scatter.2.cloned.1.call-done), calls=%async_computation.2 | async-start | bytes 1966080 | tf_op jit(solution)/shard_map/all_to_all | solution.py:1005
  319.2 4.1 %collective-permute-done.43 = bf16[80,1536]{1,0:T(8,128)(2,1)S(1)} collective-permute-done((bf16[80,1536]{1,0:T(8,128)(2,1)}, bf16[80,1536]{1,0:T(8,128)(2,1)S(1)}, u32[]{:S(2)}, u32[]{:S(2)}) %collective-permute-start.43) | collective-permute-done | bytes 245792 | tf_op jit(solution)/shard_map/ppermute | solution.py:59
  323.3 1.5 collective-permute-done.45
  329.4 2.4 finish.1
  331.9 2.9 collective-permute-done.42.came_ref
  335.6 3.0 last_step.1
  (205 shorter events, 40.6 us)
Async XLA Ops:
  7.2 8.3 %copy-start.17 = (bf16[512,64]{0,1:T(8,128)(2,1)S(1)}, bf16[512,64]{0,1:T(8,128)(2,1)}, u32[]{:S(2)}) copy-start(bf16[512,64]{0,1:T(8,128)(2,1)} %param.22) | copy-start | bytes 196612
  7.2 8.3 %copy-start.19 = (bf16[64,256]{1,0:T(8,128)(2,1)S(1)}, bf16[64,256]{1,0:T(8,128)(2,1)}, u32[]{:S(2)}) copy-start(bf16[64,256]{1,0:T(8,128)(2,1)} %param.21) | copy-start | bytes 98308
  7.2 8.3 %copy-start.20 = (bf16[64,256]{1,0:T(8,128)(2,1)S(1)}, bf16[64,256]{1,0:T(8,128)(2,1)}, u32[]{:S(2)}) copy-start(bf16[64,256]{1,0:T(8,128)(2,1)} %param.20) | copy-start | bytes 98308
  7.2 8.3 %copy-start.18 = (bf16[64,512]{1,0:T(8,128)(2,1)S(1)}, bf16[64,512]{1,0:T(8,128)(2,1)}, u32[]{:S(2)}) copy-start(bf16[64,512]{1,0:T(8,128)(2,1)} %param.19) | copy-start | bytes 196612
  9.7 61.2 %copy-start.6 = (bf16[2,128,1024]{2,1,0:T(8,128)(2,1)}, bf16[2,128,1024]{2,1,0:T(8,128)(2,1)S(1)}, u32[]{:S(2)}) copy-start(bf16[2,128,1024]{2,1,0:T(8,128)(2,1)S(1)} %fusion.2.refs_0_) | copy-start | bytes 1572868
  9.8 28.8 %collective-permute-start = (bf16[2,128,1024]{2,1,0:T(8,128)(2,1)S(1)}, bf16[2,128,1024]{2,1,0:T(8,128)(2,1)}, u32[]{:S(2)}, u32[]{:S(2)}) collective-permute-start(bf16[2,128,1024]{2,1,0:T(8,128)(2,1)S(1)} %fusion.2.refs_0_), channel_id=1, source_target_pairs={{0,2},{2,4},{4,6},{1,3},{3,5},{5,7},{8,10},{10,12},{12,14},{9,11},... | collective-permute-start | bytes 1572872 | tf_op jit(solution)/shard_map/ppermute | solution.py:45
  15.6 15.7 %collective-permute-start.3 = (bf16[64,1536]{1,0:T(8,128)(2,1)S(1)}, bf16[64,1536]{1,0:T(8,128)(2,1)S(1)}, u32[]{:S(2)}, u32[]{:S(2)}) collective-permute-start(bf16[64,1536]{1,0:T(8,128)(2,1)S(1)} %pad_maximum_fusion.7), channel_id=1, source_target_pairs={{0,6},{2,0},{4,2},{6,4},{1,7},{3,1},{5,3},{7,5},{8,14},{10,8},{12,... | collective-permute-start | bytes 589832 | tf_op jit(solution)/shard_map/ppermute | solution.py:59
  16.2 19.3 %collective-permute-start.2 = (bf16[64,1536]{1,0:T(8,128)(2,1)S(1)}, bf16[64,1536]{1,0:T(8,128)(2,1)S(1)}, u32[]{:S(2)}, u32[]{:S(2)}) collective-permute-start(bf16[64,1536]{1,0:T(8,128)(2,1)S(1)} %pad_maximum_fusion.7), channel_id=1, source_target_pairs={{0,4},{2,6},{4,0},{6,2},{1,5},{3,7},{5,1},{7,3},{8,12},{10,14},{12... | collective-permute-start | bytes 589832 | tf_op jit(solution)/shard_map/ppermute | solution.py:59
  17.9 20.7 %collective-permute-start.1 = (bf16[64,1536]{1,0:T(8,128)(2,1)S(1)}, bf16[64,1536]{1,0:T(8,128)(2,1)S(1)}, u32[]{:S(2)}, u32[]{:S(2)}) collective-permute-start(bf16[64,1536]{1,0:T(8,128)(2,1)S(1)} %pad_maximum_fusion.7), channel_id=1, source_target_pairs={{0,2},{2,4},{4,6},{6,0},{1,3},{3,5},{5,7},{7,1},{8,10},{10,12},{12... | collective-permute-start | bytes 589832 | tf_op jit(solution)/shard_map/ppermute | solution.py:59
  21.6 32.2 %all-to-all-start = ((bf16[4,64,1920]{2,1,0:T(8,128)(2,1)}), bf16[4,64,1920]{2,1,0:T(8,128)(2,1)S(1)}, u32[]{:S(2)}, u32[]{:S(2)}) async-start(bf16[4,64,1920]{2,1,0:T(8,128)(2,1)} %pack.1), calls=%async_computation | async-start | bytes 1966080 | tf_op jit(solution)/shard_map/all_to_all | solution.py:872
  25.3 120.3 %all-gather.2.cloned.1.call-start = ((), (), s32[]{:S(2)}) async-start(), calls=%async_computation.3 | async-start | bytes 4915200 | tf_op jit(solution)/shard_map/all_gather | solution.py:884
  38.8 11.8 %collective-permute-start.10 = (bf16[1,128,1536]{2,1,0:T(8,128)(2,1)S(1)}, bf16[1,128,1536]{2,1,0:T(8,128)(2,1)S(1)}, u32[]{:S(2)}, u32[]{:S(2)}) collective-permute-start(bf16[1,128,1536]{2,1,0:T(8,128)(2,1)S(1)} %bitcast.125), channel_id=1, source_target_pairs={{0,8},{8,0},{16,24},{24,16},{1,9},{9,1},{17,25},{25,17},{2,10},{10... | collective-permute-start | bytes 1179656 | tf_op jit(solution)/shard_map/ppermute | solution.py:40
  40.4 11.7 %collective-permute-start.12 = (bf16[1,128,1536]{2,1,0:T(8,128)(2,1)S(1)}, bf16[1,128,1536]{2,1,0:T(8,128)(2,1)S(1)}, u32[]{:S(2)}, u32[]{:S(2)}) collective-permute-start(bf16[1,128,1536]{2,1,0:T(8,128)(2,1)S(1)} %bitcast.122), channel_id=1, source_target_pairs={{0,16},{8,24},{16,0},{24,8},{1,17},{9,25},{17,1},{25,9},{2,18},{10... | collective-permute-start | bytes 1179656 | tf_op jit(solution)/shard_map/ppermute | solution.py:40
  42.0 24.7 %copy-start.24 = (pred[2,128]{1,0:T(4,128)(4,1)}, pred[2,128]{1,0:T(4,128)(4,1)S(1)}, u32[]{:S(2)}) copy-start(pred[2,128]{1,0:T(4,128)(4,1)S(1)} %broadcast_compare_fusion) | copy-start | bytes 772
  42.0 17.7 %collective-permute-start.4 = (bf16[2,128,1024]{2,1,0:T(8,128)(2,1)}, bf16[2,128,1024]{2,1,0:T(8,128)(2,1)}, u32[]{:S(2)}, u32[]{:S(2)}) collective-permute-start(bf16[2,128,1024]{2,1,0:T(8,128)(2,1)} %collective-permute-done.refs_2_), channel_id=1, source_target_pairs={{0,2},{2,4},{4,6},{1,3},{3,5},{5,7},{8,10},{10,12},{12,14},{9,11},... | collective-permute-start | bytes 1572872 | tf_op jit(solution)/shard_map/ppermute | solution.py:45
  50.5 15.0 %copy-start.38 = (f32[64]{0:T(128)S(1)}, f32[64]{0:T(128)}, u32[]{:S(2)}) copy-start(f32[64]{0:T(128)} %param.17) | copy-start | bytes 772
  50.5 15.6 %copy-start.39 = (f32[64]{0:T(128)S(1)}, f32[64]{0:T(128)}, u32[]{:S(2)}) copy-start(f32[64]{0:T(128)} %param.18) | copy-start | bytes 772
  51.5 21.8 %collective-permute-start.11 = (bf16[2,128,1536]{2,1,0:T(8,128)(2,1)}, bf16[2,128,1536]{2,1,0:T(8,128)(2,1)}, u32[]{:S(2)}, u32[]{:S(2)}) collective-permute-start(bf16[2,128,1536]{2,1,0:T(8,128)(2,1)} %pad_maximum_fusion.5), channel_id=1, source_target_pairs={{0,16},{8,24},{16,0},{24,8},{1,17},{9,25},{17,1},{25,9},{2,18},{10... | collective-permute-start | bytes 2359304 | tf_op jit(solution)/shard_map/ppermute | solution.py:40
  52.0 14.7 %copy-start.9 = (bf16[1,128,1536]{2,1,0:T(8,128)(2,1)}, bf16[1,128,1536]{2,1,0:T(8,128)(2,1)S(1)}, u32[]{:S(2)}) copy-start(bf16[1,128,1536]{2,1,0:T(8,128)(2,1)S(1)} %collective-permute-done.12) | copy-start | bytes 1179652
  53.0 22.1 %collective-permute-start.13 = (bf16[2,128,1536]{2,1,0:T(8,128)(2,1)}, bf16[2,128,1536]{2,1,0:T(8,128)(2,1)}, u32[]{:S(2)}, u32[]{:S(2)}) collective-permute-start(bf16[2,128,1536]{2,1,0:T(8,128)(2,1)} %pad_maximum_fusion.6), channel_id=1, source_target_pairs={{0,8},{8,0},{16,24},{24,16},{1,9},{9,1},{17,25},{25,17},{2,10},{10... | collective-permute-start | bytes 2359304 | tf_op jit(solution)/shard_map/ppermute | solution.py:40
  53.8 17.6 %copy-start.4 = (bf16[4,64,1920]{2,1,0:T(8,128)(2,1)}, bf16[4,64,1920]{2,1,0:T(8,128)(2,1)S(1)}, u32[]{:S(2)}) copy-start(bf16[4,64,1920]{2,1,0:T(8,128)(2,1)S(1)} %all-to-all-done) | copy-start | bytes 2949124
  59.8 13.5 %collective-permute-start.5 = (bf16[2,128,1024]{2,1,0:T(8,128)(2,1)}, bf16[2,128,1024]{2,1,0:T(8,128)(2,1)}, u32[]{:S(2)}, u32[]{:S(2)}) collective-permute-start(bf16[2,128,1024]{2,1,0:T(8,128)(2,1)} %collective-permute-done.4.refs_4_), channel_id=1, source_target_pairs={{0,2},{2,4},{4,6},{1,3},{3,5},{5,7},{8,10},{10,12},{12,14},{9,11},... | collective-permute-start | bytes 1572872 | tf_op jit(solution)/shard_map/ppermute | solution.py:45
  71.0 6.1 %collective-permute-start.7 = (bf16[2,128,1024]{2,1,0:T(8,128)(2,1)}, bf16[2,128,1024]{2,1,0:T(8,128)(2,1)}, u32[]{:S(2)}, u32[]{:S(2)}) collective-permute-start(bf16[2,128,1024]{2,1,0:T(8,128)(2,1)} %collective-permute-done.refs_2_), channel_id=1, source_target_pairs={{0,1},{1,0},{2,3},{3,2},{4,5},{5,4},{6,7},{7,6},{8,9},{9,8},{10,11... | collective-permute-start | bytes 1572872 | tf_op jit(solution)/shard_map/ppermute | solution.py:35
  71.0 6.0 %collective-permute-start.6 = (bf16[2,128,1024]{2,1,0:T(8,128)(2,1)S(1)}, bf16[2,128,1024]{2,1,0:T(8,128)(2,1)}, u32[]{:S(2)}, u32[]{:S(2)}) collective-permute-start(bf16[2,128,1024]{2,1,0:T(8,128)(2,1)S(1)} %fusion.2.refs_0_), channel_id=1, source_target_pairs={{0,1},{1,0},{2,3},{3,2},{4,5},{5,4},{6,7},{7,6},{8,9},{9,8},{10,11... | collective-permute-start | bytes 1572872 | tf_op jit(solution)/shard_map/ppermute | solution.py:35
  71.5 214.5 %reduce-scatter.2.cloned.1.call-start = ((), (), s32[]{:S(2)}) async-start(), calls=%async_computation.4 | async-start | bytes 4915200 | tf_op jit(solution)/shard_map/reduce_scatter | solution.py:935
  73.3 3.8 %collective-permute-start.8 = (bf16[2,128,1024]{2,1,0:T(8,128)(2,1)}, bf16[2,128,1024]{2,1,0:T(8,128)(2,1)S(1)}, u32[]{:S(2)}, u32[]{:S(2)}) collective-permute-start(bf16[2,128,1024]{2,1,0:T(8,128)(2,1)} %collective-permute-done.4.refs_4_), channel_id=1, source_target_pairs={{0,1},{1,0},{2,3},{3,2},{4,5},{5,4},{6,7},{7,6},{8,9},{9,8},{10,11... | collective-permute-start | bytes 1572872 | tf_op jit(solution)/shard_map/ppermute | solution.py:35
  73.3 3.8 %collective-permute-start.9 = (bf16[2,128,1024]{2,1,0:T(8,128)(2,1)}, bf16[2,128,1024]{2,1,0:T(8,128)(2,1)S(1)}, u32[]{:S(2)}, u32[]{:S(2)}) collective-permute-start(bf16[2,128,1024]{2,1,0:T(8,128)(2,1)} %collective-permute-done.5.refs_6_), channel_id=1, source_target_pairs={{0,1},{1,0},{2,3},{3,2},{4,5},{5,4},{6,7},{7,6},{8,9},{9,8},{10,11... | collective-permute-start | bytes 1572872 | tf_op jit(solution)/shard_map/ppermute | solution.py:35
  77.1 26.5 %collective-permute-start.16 = (bf16[2,128,1024]{2,1,0:T(8,128)(2,1)S(1)}, bf16[2,128,1024]{2,1,0:T(8,128)(2,1)S(1)}, u32[]{:S(2)}, u32[]{:S(2)}) collective-permute-start(bf16[2,128,1024]{2,1,0:T(8,128)(2,1)S(1)} %broadcast_select_fusion), channel_id=1, source_target_pairs={{0,24},{8,16},{16,8},{24,0},{1,25},{9,17},{17,9},{25,1},{2,26},{10... | collective-permute-start | bytes 1572872 | tf_op jit(solution)/shard_map/ppermute | solution.py:40
  77.6 26.0 %collective-permute-start.15 = (bf16[2,128,1024]{2,1,0:T(8,128)(2,1)S(1)}, bf16[2,128,1024]{2,1,0:T(8,128)(2,1)S(1)}, u32[]{:S(2)}, u32[]{:S(2)}) collective-permute-start(bf16[2,128,1024]{2,1,0:T(8,128)(2,1)S(1)} %broadcast_select_fusion), channel_id=1, source_target_pairs={{0,16},{8,24},{16,0},{24,8},{1,17},{9,25},{17,1},{25,9},{2,18},{10... | collective-permute-start | bytes 1572872 | tf_op jit(solution)/shard_map/ppermute | solution.py:40
  79.1 24.4 %collective-permute-start.14 = (bf16[2,128,1024]{2,1,0:T(8,128)(2,1)S(1)}, bf16[2,128,1024]{2,1,0:T(8,128)(2,1)S(1)}, u32[]{:S(2)}, u32[]{:S(2)}) collective-permute-start(bf16[2,128,1024]{2,1,0:T(8,128)(2,1)S(1)} %broadcast_select_fusion), channel_id=1, source_target_pairs={{0,8},{8,0},{16,24},{24,16},{1,9},{9,1},{17,25},{25,17},{2,10},{10... | collective-permute-start | bytes 1572872 | tf_op jit(solution)/shard_map/ppermute | solution.py:40
  105.4 2.7 collective-permute-start.17
  108.5 14.0 %collective-permute-start.19 = (bf16[2,128,1024]{2,1,0:T(8,128)(2,1)S(1)}, bf16[2,128,1024]{2,1,0:T(8,128)(2,1)S(1)}, u32[]{:S(2)}, u32[]{:S(2)}) collective-permute-start(bf16[2,128,1024]{2,1,0:T(8,128)(2,1)S(1)} %multiply_convert_fusion), channel_id=1, source_target_pairs={{0,16},{8,24},{16,0},{24,8},{1,17},{9,25},{17,1},{25,9},{2,18},{10... | collective-permute-start | bytes 1572872 | tf_op jit(solution)/shard_map/ppermute | solution.py:40
  109.1 14.8 %collective-permute-start.18 = (bf16[2,128,1024]{2,1,0:T(8,128)(2,1)S(1)}, bf16[2,128,1024]{2,1,0:T(8,128)(2,1)S(1)}, u32[]{:S(2)}, u32[]{:S(2)}) collective-permute-start(bf16[2,128,1024]{2,1,0:T(8,128)(2,1)S(1)} %multiply_convert_fusion), channel_id=1, source_target_pairs={{0,8},{8,0},{16,24},{24,16},{1,9},{9,1},{17,25},{25,17},{2,10},{10... | collective-permute-start | bytes 1572872 | tf_op jit(solution)/shard_map/ppermute | solution.py:40
  109.6 25.4 %collective-permute-start.20 = (bf16[2,128,1024]{2,1,0:T(8,128)(2,1)S(1)}, bf16[2,128,1024]{2,1,0:T(8,128)(2,1)S(1)}, u32[]{:S(2)}, u32[]{:S(2)}) collective-permute-start(bf16[2,128,1024]{2,1,0:T(8,128)(2,1)S(1)} %multiply_convert_fusion), channel_id=1, source_target_pairs={{0,24},{8,16},{16,8},{24,0},{1,25},{9,17},{17,9},{25,1},{2,26},{10... | collective-permute-start | bytes 1572872 | tf_op jit(solution)/shard_map/ppermute | solution.py:40
  113.7 31.9 %collective-permute-start.22 = (bf16[4,2,128,1024]{3,2,1,0:T(8,128)(2,1)}, bf16[4,2,128,1024]{3,2,1,0:T(8,128)(2,1)}, u32[]{:S(2)}, u32[]{:S(2)}) collective-permute-start(bf16[4,2,128,1024]{3,2,1,0:T(8,128)(2,1)} %pad_maximum_fusion.2), channel_id=1, source_target_pairs={{0,1},{1,0},{2,3},{3,2},{4,5},{5,4},{6,7},{7,6},{8,9},{9,8},{10,11... | collective-permute-start | bytes 6291464 | tf_op jit(solution)/shard_map/ppermute | solution.py:35
  136.6 9.0 %collective-permute-start.21 = (bf16[4,2,128,1024]{3,2,1,0:T(8,128)(2,1)}, bf16[4,2,128,1024]{3,2,1,0:T(8,128)(2,1)}, u32[]{:S(2)}, u32[]{:S(2)}) collective-permute-start(bf16[4,2,128,1024]{3,2,1,0:T(8,128)(2,1)} %pad_maximum_fusion.1), channel_id=1, source_target_pairs={{0,1},{1,0},{2,3},{3,2},{4,5},{5,4},{6,7},{7,6},{8,9},{9,8},{10,11... | collective-permute-start | bytes 6291464 | tf_op jit(solution)/shard_map/ppermute | solution.py:35
  164.9 3.7 %collective-permute-start.23 = (bf16[3,2,128,1024]{3,2,1,0:T(8,128)(2,1)}, bf16[3,2,128,1024]{3,2,1,0:T(8,128)(2,1)S(1)}, u32[]{:S(2)}, u32[]{:S(2)}) collective-permute-start(bf16[3,2,128,1024]{3,2,1,0:T(8,128)(2,1)} %bitcast.152), channel_id=1, source_target_pairs={{0,1},{1,0},{2,3},{3,2},{4,5},{5,4},{6,7},{7,6},{8,9},{9,8},{10,11... | collective-permute-start | bytes 4718600 | tf_op jit(solution)/shard_map/ppermute | solution.py:35
  164.9 8.7 %collective-permute-start.24 = (bf16[3,2,128,1024]{3,2,1,0:T(8,128)(2,1)}, bf16[3,2,128,1024]{3,2,1,0:T(8,128)(2,1)S(1)}, u32[]{:S(2)}, u32[]{:S(2)}) collective-permute-start(bf16[3,2,128,1024]{3,2,1,0:T(8,128)(2,1)} %bitcast.151), channel_id=1, source_target_pairs={{0,1},{1,0},{2,3},{3,2},{4,5},{5,4},{6,7},{7,6},{8,9},{9,8},{10,11... | collective-permute-start | bytes 4718600 | tf_op jit(solution)/shard_map/ppermute | solution.py:35
  170.1 28.0 %collective-permute-start.25 = (bf16[2,128,1024]{2,1,0:T(8,128)(2,1)}, bf16[2,128,1024]{2,1,0:T(8,128)(2,1)S(1)}, u32[]{:S(2)}, u32[]{:S(2)}) collective-permute-start(bf16[2,128,1024]{2,1,0:T(8,128)(2,1)} %get-tuple-element.184), channel_id=1, source_target_pairs={{0,8},{8,0},{16,24},{24,16},{1,9},{9,1},{17,25},{25,17},{2,10},{10... | collective-permute-start | bytes 1572872 | tf_op jit(solution)/shard_map/ppermute | solution.py:40
  171.6 26.5 %collective-permute-start.26 = (bf16[2,128,1024]{2,1,0:T(8,128)(2,1)}, bf16[2,128,1024]{2,1,0:T(8,128)(2,1)S(1)}, u32[]{:S(2)}, u32[]{:S(2)}) collective-permute-start(bf16[2,128,1024]{2,1,0:T(8,128)(2,1)} %get-tuple-element.185), channel_id=1, source_target_pairs={{0,16},{8,24},{16,0},{24,8},{1,17},{9,25},{17,1},{25,9},{2,18},{10... | collective-permute-start | bytes 1572872 | tf_op jit(solution)/shard_map/ppermute | solution.py:40
  173.1 25.0 %collective-permute-start.27 = (bf16[2,128,1024]{2,1,0:T(8,128)(2,1)}, bf16[2,128,1024]{2,1,0:T(8,128)(2,1)S(1)}, u32[]{:S(2)}, u32[]{:S(2)}) collective-permute-start(bf16[2,128,1024]{2,1,0:T(8,128)(2,1)} %get-tuple-element.186), channel_id=1, source_target_pairs={{0,24},{8,16},{16,8},{24,0},{1,25},{9,17},{17,9},{25,1},{2,26},{10... | collective-permute-start | bytes 1572872 | tf_op jit(solution)/shard_map/ppermute | solution.py:40
  198.1 2.2 collective-permute-start.28
  203.7 2.3 collective-permute-start.29
  203.8 33.9 %collective-permute-start.30 = (bf16[2,128,1024]{2,1,0:T(8,128)(2,1)}, bf16[2,128,1024]{2,1,0:T(8,128)(2,1)S(1)}, u32[]{:S(2)}, u32[]{:S(2)}) collective-permute-start(bf16[2,128,1024]{2,1,0:T(8,128)(2,1)} %bitcast.52), channel_id=1, source_target_pairs={{0,1},{1,0},{2,3},{3,2},{4,5},{5,4},{6,7},{7,6},{8,9},{9,8},{10,11... | collective-permute-start | bytes 1572872 | tf_op jit(solution)/shard_map/ppermute | solution.py:35
  209.0 28.8 %collective-permute-start.31 = (bf16[2,128,1024]{2,1,0:T(8,128)(2,1)S(1)}, bf16[2,128,1024]{2,1,0:T(8,128)(2,1)S(1)}, u32[]{:S(2)}, u32[]{:S(2)}) collective-permute-start(bf16[2,128,1024]{2,1,0:T(8,128)(2,1)S(1)} %get-tuple-element.205), channel_id=1, source_target_pairs={{0,8},{8,0},{16,24},{24,16},{1,9},{9,1},{17,25},{25,17},{2,10},{10... | collective-permute-start | bytes 1572872 | tf_op jit(solution)/shard_map/ppermute | solution.py:40
  210.4 27.3 %collective-permute-start.32 = (bf16[2,128,1024]{2,1,0:T(8,128)(2,1)S(1)}, bf16[2,128,1024]{2,1,0:T(8,128)(2,1)S(1)}, u32[]{:S(2)}, u32[]{:S(2)}) collective-permute-start(bf16[2,128,1024]{2,1,0:T(8,128)(2,1)S(1)} %get-tuple-element.206), channel_id=1, source_target_pairs={{0,16},{8,24},{16,0},{24,8},{1,17},{9,25},{17,1},{25,9},{2,18},{10... | collective-permute-start | bytes 1572872 | tf_op jit(solution)/shard_map/ppermute | solution.py:40
  211.9 25.9 %collective-permute-start.33 = (bf16[2,128,1024]{2,1,0:T(8,128)(2,1)S(1)}, bf16[2,128,1024]{2,1,0:T(8,128)(2,1)S(1)}, u32[]{:S(2)}, u32[]{:S(2)}) collective-permute-start(bf16[2,128,1024]{2,1,0:T(8,128)(2,1)S(1)} %get-tuple-element.207), channel_id=1, source_target_pairs={{0,24},{8,16},{16,8},{24,0},{1,25},{9,17},{17,9},{25,1},{2,26},{10... | collective-permute-start | bytes 1572872 | tf_op jit(solution)/shard_map/ppermute | solution.py:40
  249.9 7.1 %copy-start.12 = (bf16[256,1024]{1,0:T(8,128)(2,1)S(1)}, bf16[256,1024]{1,0:T(8,128)(2,1)}, u32[]{:S(2)}) copy-start(bf16[256,1024]{1,0:T(8,128)(2,1)} %get-tuple-element.203) | copy-start | bytes 1572868
  249.9 7.1 %copy-start.25 = (pred[2,128]{1,0:T(4,128)(4,1)S(1)}, pred[2,128]{1,0:T(4,128)(4,1)}, u32[]{:S(2)}) copy-start(pred[2,128]{1,0:T(4,128)(4,1)} %copy-done.24) | copy-start | bytes 772
  249.9 19.0 %collective-permute-start.36 = (bf16[256,1536]{1,0:T(8,128)(2,1)}, bf16[256,1536]{1,0:T(8,128)(2,1)S(1)}, u32[]{:S(2)}, u32[]{:S(2)}) collective-permute-start(bf16[256,1536]{1,0:T(8,128)(2,1)} %get-tuple-element.231), channel_id=1, source_target_pairs={{0,16},{8,24},{16,0},{24,8},{1,17},{9,25},{17,1},{25,9},{2,18},{10... | collective-permute-start | bytes 2359304 | tf_op jit(solution)/shard_map/ppermute | solution.py:40
  251.4 19.7 %collective-permute-start.35 = (bf16[272,1536]{1,0:T(8,128)(2,1)}, bf16[272,1536]{1,0:T(8,128)(2,1)S(1)}, u32[]{:S(2)}, u32[]{:S(2)}) collective-permute-start(bf16[272,1536]{1,0:T(8,128)(2,1)} %get-tuple-element.230), channel_id=1, source_target_pairs={{0,8},{8,0},{16,24},{24,16},{1,9},{9,1},{17,25},{25,17},{2,10},{10... | collective-permute-start | bytes 2506760 | tf_op jit(solution)/shard_map/ppermute | solution.py:40
  256.9 8.5 %collective-permute-start.34 = (bf16[1,2,128,1024]{3,2,1,0:T(8,128)(2,1)}, bf16[1,2,128,1024]{3,2,1,0:T(8,128)(2,1)S(1)}, u32[]{:S(2)}, u32[]{:S(2)}) collective-permute-start(bf16[1,2,128,1024]{3,2,1,0:T(8,128)(2,1)} %get-tuple-element.224), channel_id=1, source_target_pairs={{0,1},{1,0},{2,3},{3,2},{4,5},{5,4},{6,7},{7,6},{8,9},{9,8},{10,11... | collective-permute-start | bytes 1572872 | tf_op jit(solution)/shard_map/ppermute | solution.py:35
  273.6 12.4 %collective-permute-start.37 = (bf16[2,128,1024]{2,1,0:T(8,128)(2,1)}, bf16[2,128,1024]{2,1,0:T(8,128)(2,1)S(1)}, u32[]{:S(2)}, u32[]{:S(2)}) collective-permute-start(bf16[2,128,1024]{2,1,0:T(8,128)(2,1)} %down_add.3), channel_id=1, source_target_pairs={{0,6},{2,0},{4,2},{6,4},{1,7},{3,1},{5,3},{7,5},{8,14},{10,8},{12,... | collective-permute-start | bytes 1572872 | tf_op jit(solution)/shard_map/ppermute | solution.py:59
  274.9 11.0 %collective-permute-start.38 = (bf16[3,2,128,1024]{3,2,1,0:T(8,128)(2,1)}, bf16[3,2,128,1024]{3,2,1,0:T(8,128)(2,1)S(1)}, u32[]{:S(2)}, u32[]{:S(2)}) collective-permute-start(bf16[3,2,128,1024]{3,2,1,0:T(8,128)(2,1)} %get-tuple-element.235), channel_id=1, source_target_pairs={{0,1},{1,0},{2,3},{3,2},{4,5},{5,4},{6,7},{7,6},{8,9},{9,8},{10,11... | collective-permute-start | bytes 4718600 | tf_op jit(solution)/shard_map/ppermute | solution.py:35
  289.6 12.7 %collective-permute-start.39 = (bf16[2,128,1024]{2,1,0:T(8,128)(2,1)}, bf16[2,128,1024]{2,1,0:T(8,128)(2,1)S(1)}, u32[]{:S(2)}, u32[]{:S(2)}) collective-permute-start(bf16[2,128,1024]{2,1,0:T(8,128)(2,1)} %down_add.4), channel_id=1, source_target_pairs={{0,6},{2,0},{4,2},{6,4},{1,7},{3,1},{5,3},{7,5},{8,14},{10,8},{12,... | collective-permute-start | bytes 1572872 | tf_op jit(solution)/shard_map/ppermute | solution.py:59
  292.9 9.4 %collective-permute-start.40 = (bf16[144,1536]{1,0:T(8,128)(2,1)S(1)}, bf16[144,1536]{1,0:T(8,128)(2,1)S(1)}, u32[]{:S(2)}, u32[]{:S(2)}) collective-permute-start(bf16[144,1536]{1,0:T(8,128)(2,1)S(1)} %copy-done.21), channel_id=1, source_target_pairs={{0,16},{8,24},{16,0},{24,8},{1,17},{9,25},{17,1},{25,9},{2,18},{10... | collective-permute-start | bytes 1327112 | tf_op jit(solution)/shard_map/ppermute | solution.py:40
  293.5 8.7 %collective-permute-start.41 = (bf16[128,1536]{1,0:T(8,128)(2,1)S(1)}, bf16[128,1536]{1,0:T(8,128)(2,1)S(1)}, u32[]{:S(2)}, u32[]{:S(2)}) collective-permute-start(bf16[128,1536]{1,0:T(8,128)(2,1)S(1)} %copy-done.36), channel_id=1, source_target_pairs={{0,8},{8,0},{16,24},{24,16},{1,9},{9,1},{17,25},{25,17},{2,10},{10... | collective-permute-start | bytes 1179656 | tf_op jit(solution)/shard_map/ppermute | solution.py:40
  305.9 17.4 %collective-permute-start.43 = (bf16[80,1536]{1,0:T(8,128)(2,1)}, bf16[80,1536]{1,0:T(8,128)(2,1)S(1)}, u32[]{:S(2)}, u32[]{:S(2)}) collective-permute-start(bf16[80,1536]{1,0:T(8,128)(2,1)} %get-tuple-element.264), channel_id=1, source_target_pairs={{0,4},{2,6},{4,0},{6,2},{1,5},{3,7},{5,1},{7,3},{8,12},{10,14},{12... | collective-permute-start | bytes 737288 | tf_op jit(solution)/shard_map/ppermute | solution.py:59
  307.4 15.9 %collective-permute-start.44 = (bf16[80,1536]{1,0:T(8,128)(2,1)}, bf16[80,1536]{1,0:T(8,128)(2,1)S(1)}, u32[]{:S(2)}, u32[]{:S(2)}) collective-permute-start(bf16[80,1536]{1,0:T(8,128)(2,1)} %get-tuple-element.265), channel_id=1, source_target_pairs={{0,2},{2,4},{4,6},{6,0},{1,3},{3,5},{5,7},{7,1},{8,10},{10,12},{12... | collective-permute-start | bytes 737288 | tf_op jit(solution)/shard_map/ppermute | solution.py:59
  309.8 15.1 %collective-permute-start.45 = (bf16[80,1536]{1,0:T(8,128)(2,1)}, bf16[80,1536]{1,0:T(8,128)(2,1)S(1)}, u32[]{:S(2)}, u32[]{:S(2)}) collective-permute-start(bf16[80,1536]{1,0:T(8,128)(2,1)} %get-tuple-element.266), channel_id=1, source_target_pairs={{0,6},{2,0},{4,2},{6,4},{1,7},{3,1},{5,3},{7,5},{8,14},{10,8},{12,... | collective-permute-start | bytes 737288 | tf_op jit(solution)/shard_map/ppermute | solution.py:59
  313.5 12.2 %copy-start.15 = (f32[64,1536]{1,0:T(8,128)S(1)}, f32[64,1536]{1,0:T(8,128)}, u32[]{:S(2)}) copy-start(f32[64,1536]{1,0:T(8,128)} %get-tuple-element.267) | copy-start | bytes 1179652
  313.5 15.0 %all-to-all-start.1 = ((bf16[4,64,1920]{2,1,0:T(8,128)(2,1)}), bf16[4,64,1920]{2,1,0:T(8,128)(2,1)S(1)}, u32[]{:S(2)}, u32[]{:S(2)}) async-start(bf16[4,64,1920]{2,1,0:T(8,128)(2,1)} %reduce-scatter.2.cloned.1.call-done), calls=%async_computation.2 | async-start | bytes 1966080 | tf_op jit(solution)/shard_map/all_to_all | solution.py:1005
  317.9 16.9 %collective-permute-start.42 = (bf16[2,128,1024]{2,1,0:T(8,128)(2,1)S(1)}, bf16[2,128,1024]{2,1,0:T(8,128)(2,1)S(1)}, u32[]{:S(2)}, u32[]{:S(2)}) collective-permute-start(bf16[2,128,1024]{2,1,0:T(8,128)(2,1)S(1)} %copy-done.30), channel_id=1, source_target_pairs={{2,0},{4,2},{6,4},{3,1},{5,3},{7,5},{10,8},{12,10},{14,12},{11,9},... | collective-permute-start | bytes 1572872 | tf_op jit(solution)/shard_map/ppermute | solution.py:50
  325.7 1.6 collective-permute-start.46
  (27 other events, 76.2 us)
Sparse Core Ops, SparseCore 0:
  71.6 73.8 all-gather.1
  204.3 71.2 reduce-scatter.1

commit v7 on v6

--- a/solution.py
+++ b/solution.py
@@ -348,11 +348,9 @@
         out = out + dot(jnp.concatenate([bm_ref[s], bo_ref[s]]), o_ref[s], TN)
     total = jnp.concatenate([query, key, value, out], axis=1)
     product = total[:, : q_cols + 2 * k_cols] * w_ref[:, : q_cols + 2 * k_cols].astype(F32)
-    ones = jnp.ones((8, q_cols + 2 * k_cols), BF)
-    high = product.astype(BF)
-    low = (product - high.astype(F32)).astype(BF)
+    column = jnp.sum(product, axis=1, keepdims=True)
     place = pl.ds(pl.multiple_of((at_ref[0] ^ m) * depth, TILE), depth)
-    sum_ref[:, place] = dot(ones, high, NT) + dot(ones, low, NT)
+    sum_ref[:, place] = jnp.broadcast_to(column, (depth, TILE)).T[:8]
     total = total.astype(BF)
     bits = bits_of(parts)
     for bit, rows_of, send, keep in (

time: 352 us -> 353 us (level)
  transfers between devices with their start and end apart: 51 -> 51, of which waited for: 22 -> 19; matrix products, arithmetic and copies ran while one was open for 9% -> 9% of each run, Pallas kernels for 31% -> 30%
where the time goes in v7:
time: 353 us; the launch traced here: 347 us
  Pallas kernels  133 us (38%)
  waiting for transfers between devices  87.2 us (25%)
  starting transfers between devices  68.8 us (19%)
  other arithmetic  26.6 us (8%)
  between operations  15 us (4%)
  local copies, waits for them, and re-layouts  12.1 us (3%)
  matrix products  3.79 us (1%)
    ppermute x20, waiting for transfers between devices, fsdp_xor(): return lax.ppermute(value, 'fsdp', [(i, i ^ mask) for i in range(size)])  33.4 us
    ppermute x8, waiting for transfers between devices, ctx_shift(): lax.ppermute(value, 'ctx', [(i, (i + step) % size) for i in range(size)])  26.2 us
    pallas_call x1, Pallas kernels, attend_back(): pl.pallas_call(attend_back_kernel, grid=(slots, pairs), in_specs=[smem, q...  25.3 us
    ppermute x20, starting transfers between devices, fsdp_xor(): return lax.ppermute(value, 'fsdp', [(i, i ^ mask) for i in range(size)])  24.7 us
    pallas_call x1, Pallas kernels, ffn_rest(): pl.pallas_call(ffn_rest_kernel, grid=(parts // 2,), in_specs=[block] * 4...  23.8 us
    pallas_call x1, Pallas kernels, attend(): pl.pallas_call(functools.partial(attend_kernel, len(pieces), parts), grid...  21.9 us
    ppermute x3, starting transfers between devices, ctx_up(): lax.ppermute(value, 'ctx', [(i, i + step) for i in range(size - step)])  19.4 us
    pallas_call x1, Pallas kernels, feed_forward(): pl.pallas_call(ffn_kernel, grid=(parts - 1,), in_specs=[block] * 4 + [pl....  19.3 us
  transfers between devices with their start and end apart: 51, of which 19 were waited for; matrix products, arithmetic and copies ran while one was open for 9% of the time, Pallas kernels for 30%

profile of v7, /device:TPU:0, one launch (start us, length us, event | category | flops | bytes accessed | tf_op | source)
XLA Modules:
  0.0 346.5 jit_solution(10089081151791183137)
XLA Ops:
  9.8 5.8 %collective-permute-start = (bf16[2,128,1024]{2,1,0:T(8,128)(2,1)S(1)}, bf16[2,128,1024]{2,1,0:T(8,128)(2,1)}, u32[]{:S(2)}, u32[]{:S(2)}) collective-permute-start(bf16[2,128,1024]{2,1,0:T(8,128)(2,1)S(1)} %fusion.2.refs_0_), channel_id=1, source_target_pairs={{0,2},{2,4},{4,6},{1,3},{3,5},{5,7},{8,10},{10,12},{12,14},{9,11},... | collective-permute-start | bytes 1572872 | tf_op jit(solution)/shard_map/ppermute | solution.py:45
  16.2 1.6 collective-permute-start.2
  17.9 1.6 collective-permute-start.1
  19.4 2.2 pack.1
  21.6 3.7 %all-to-all-start = ((bf16[4,64,1920]{2,1,0:T(8,128)(2,1)}), bf16[4,64,1920]{2,1,0:T(8,128)(2,1)S(1)}, u32[]{:S(2)}, u32[]{:S(2)}) async-start(bf16[4,64,1920]{2,1,0:T(8,128)(2,1)} %pack.1), calls=%async_computation | async-start | bytes 1966080 | tf_op jit(solution)/shard_map/all_to_all | solution.py:870
  25.3 5.9 %collective-permute-done.3 = bf16[64,1536]{1,0:T(8,128)(2,1)S(1)} collective-permute-done((bf16[64,1536]{1,0:T(8,128)(2,1)S(1)}, bf16[64,1536]{1,0:T(8,128)(2,1)S(1)}, u32[]{:S(2)}, u32[]{:S(2)}) %collective-permute-start.3) | collective-permute-done | bytes 196640 | tf_op jit(solution)/shard_map/ppermute | solution.py:59
  31.3 4.2 %collective-permute-done.2 = bf16[64,1536]{1,0:T(8,128)(2,1)S(1)} collective-permute-done((bf16[64,1536]{1,0:T(8,128)(2,1)S(1)}, bf16[64,1536]{1,0:T(8,128)(2,1)S(1)}, u32[]{:S(2)}, u32[]{:S(2)}) %collective-permute-start.2) | collective-permute-done | bytes 196640 | tf_op jit(solution)/shard_map/ppermute | solution.py:59
  35.5 3.1 collective-permute-done.1
  38.8 1.6 collective-permute-start.10
  40.4 1.6 collective-permute-start.12
  42.0 8.5 %collective-permute-start.4 = (bf16[2,128,1024]{2,1,0:T(8,128)(2,1)}, bf16[2,128,1024]{2,1,0:T(8,128)(2,1)}, u32[]{:S(2)}, u32[]{:S(2)}) collective-permute-start(bf16[2,128,1024]{2,1,0:T(8,128)(2,1)} %collective-permute-done.refs_2_), channel_id=1, source_target_pairs={{0,2},{2,4},{4,6},{1,3},{3,5},{5,7},{8,10},{10,12},{12,14},{9,11},... | collective-permute-start | bytes 1572872 | tf_op jit(solution)/shard_map/ppermute | solution.py:45
  53.8 5.9 %collective-permute-done.4.refs_4_ = bf16[2,128,1024]{2,1,0:T(8,128)(2,1)} collective-permute-done((bf16[2,128,1024]{2,1,0:T(8,128)(2,1)}, bf16[2,128,1024]{2,1,0:T(8,128)(2,1)}, u32[]{:S(2)}, u32[]{:S(2)}) %collective-permute-start.4) | collective-permute-done | bytes 524320 | tf_op jit(solution)/shard_map/ppermute | solution.py:45
  59.8 5.2 %collective-permute-start.5 = (bf16[2,128,1024]{2,1,0:T(8,128)(2,1)}, bf16[2,128,1024]{2,1,0:T(8,128)(2,1)}, u32[]{:S(2)}, u32[]{:S(2)}) collective-permute-start(bf16[2,128,1024]{2,1,0:T(8,128)(2,1)} %collective-permute-done.4.refs_4_), channel_id=1, source_target_pairs={{0,2},{2,4},{4,6},{1,3},{3,5},{5,7},{8,10},{10,12},{12,14},{9,11},... | collective-permute-start | bytes 1572872 | tf_op jit(solution)/shard_map/ppermute | solution.py:45
  67.9 3.1 fusion.15
  71.7 1.5 collective-permute-done.5.refs_6_
  75.1 1.9 pad_maximum_fusion.4.refs_11_.refs_12_.refs_13_
  77.6 1.5 collective-permute-start.15
  79.1 1.5 collective-permute-start.14
  81.3 21.9 %attend.1 = (bf16[2,256,512]{2,1,0:T(8,128)(2,1)}, f32[2,2,8,256]{3,2,1,0:T(8,128)}, f32[2,256,512]{2,1,0:T(8,128)}, f32[2,1024,256]{2,1,0:T(8,128)}, bf16[2,102...) custom-call(s32[5]{0:T(128)} %pad_add_fusion.scal_ref, ...), custom_call_target="tpu_custom_call" | custom-call | flops 1048576 | bytes 1048576 | tf_op jit(solution)/shard_map/attend/pallas_call | solution.py:274
  105.4 2.6 collective-permute-done.17
  109.6 2.5 collective-permute-start.20
  112.1 1.6 pad_maximum_fusion.2
  113.9 8.7 %collective-permute-done.19 = bf16[2,128,1024]{2,1,0:T(8,128)(2,1)S(1)} collective-permute-done((bf16[2,128,1024]{2,1,0:T(8,128)(2,1)S(1)}, bf16[2,128,1024]{2,1,0:T(8,128)(2,1)S(1)}, u32[]{:S(2)}, u32[]{:S(2)}) %collective-permute-start.19) | collective-permute-done | bytes 524320 | tf_op jit(solution)/shard_map/ppermute | solution.py:40
  123.9 11.1 %collective-permute-done.20 = bf16[2,128,1024]{2,1,0:T(8,128)(2,1)S(1)} collective-permute-done((bf16[2,128,1024]{2,1,0:T(8,128)(2,1)S(1)}, bf16[2,128,1024]{2,1,0:T(8,128)(2,1)S(1)}, u32[]{:S(2)}, u32[]{:S(2)}) %collective-permute-start.20) | collective-permute-done | bytes 524320 | tf_op jit(solution)/shard_map/ppermute | solution.py:40
  135.0 1.7 pad_maximum_fusion.1
  136.6 8.9 %all-gather.2.cloned.1.call-done = bf16[4,256,1920]{2,1,0:T(8,128)(2,1)} async-done(((bf16[4,64,1920]{2,1,0:T(8,128)(2,1)}), bf16[4,256,1920]{2,1,0:T(8,128)(2,1)}) %all-gather.2.cloned.1.call-update) | async-done | bytes 3932176 | tf_op jit(solution)/shard_map/all_gather | solution.py:882
  145.6 19.3 %feed_forward.1 = (bf16[768,1024]{1,0:T(8,128)(2,1)}, bf16[768,1024]{1,0:T(8,128)(2,1)}, bf16[768,1024]{1,0:T(8,128)(2,1)}, bf16[768,1024]{1,0:T(8,128)(2,1)}, b...) custom-call(bf16[1024,1024]{1,0:T(8,128)(2,1)} %bitcast.25.xm_ref, bf16[1024,1024]{1,0:T(8,128)(2,1)} %bitcast.26.xo_ref, ...), custom_call_target="tpu_custom_call" | custom-call | flops 16106127360 | bytes 25165824 | tf_op jit(solution)/shard_map/feed_forward/pallas_call | solution.py:667
  165.4 1.6 fusion.42
  168.5 1.6 fusion.11
  170.1 1.5 collective-permute-start.25
  171.6 1.5 collective-permute-start.26
  174.3 23.8 %ffn_rest.1 = (bf16[256,1024]{1,0:T(8,128)(2,1)}, bf16[256,1024]{1,0:T(8,128)(2,1)}, bf16[256,1024]{1,0:T(8,128)(2,1)}, bf16[256,1024]{1,0:T(8,128)(2,1)}, f32[1...) custom-call(bf16[1024,1024]{1,0:T(8,128)(2,1)} %bitcast.25.xm_ref, bf16[1024,1024]{1,0:T(8,128)(2,1)} %bitcast.26.xo_ref, ...), custom_call_target="tpu_custom_call" | custom-call | flops 25769803776 | bytes 25165824 | tf_op jit(solution)/shard_map/ffn_rest/pallas_call | solution.py:690
  198.2 2.1 collective-permute-done.28
  200.3 1.6 multiply_reduce_fusion
  202.0 1.7 fusion.40
  204.2 1.7 collective-permute-done.29.bo_ref
  205.9 3.0 convolution_convert_fusion.d_ref
  210.4 1.5 collective-permute-start.32
  212.5 25.3 %attend_back.1 = (bf16[2,256,512]{2,1,0:T(8,128)(2,1)}, bf16[2,1024,256]{2,1,0:T(8,128)(2,1)}, bf16[2,1024,256]{2,1,0:T(8,128)(2,1)}, f32[1,128]{1,0:T(1,128)}, f32[1,128]{1,0:T(1,128)}) custom-call(s32[5]{0:T(128)} %pad_add_fusion.scal_ref, f32[2,256,512]{2,1,0:T(8,128)} %get-tuple-element.160.q_ref, f32[2,1024,256]{2,1,0:T(8,128)} %get-tuple-element.161.k_ref, ...), custom_call_target="tpu_custom_call" | custom-call | flops 25769803776 | bytes 12582912 | tf_op jit(solution)/shard_map/attend_back/pallas_call | solution.py:307
  239.2 9.4 %weight_grads.1 = (bf16[272,1536]{1,0:T(8,128)(2,1)}, bf16[256,1536]{1,0:T(8,128)(2,1)}, bf16[256,1536]{1,0:T(8,128)(2,1)}, bf16[256,1536]{1,0:T(8,128)(2,1)}, bf16[16,1536]{1,0:T(8,128)(2,1)}) custom-call(s32[1]{0:T(128)} %bitcast.at_ref, bf16[2,1024,1024]{2,1,0:T(8,128)(2,1)} %get-tuple-element.159.x_ref, bf16[2,256,512]{2,1,0:T(8,128)(2,1)} %get-tuple-element.219.dq_ref, ...), custom_call_target="tpu_custom_call" | custom-call | flops 10737418240 | bytes 8388608 | tf_op jit(solution)/shard_map/weight_grads/pallas_call | solution.py:407
  248.5 1.5 collective-permute-start.36
  250.1 1.5 collective-permute-start.35
  251.5 4.1 %input_grads.3 = (f32[1,2,128,1024]{3,2,1,0:T(8,128)}, bf16[1,2,128,1024]{3,2,1,0:T(8,128)(2,1)}) custom-call(bf16[2,256,512]{2,1,0:T(8,128)(2,1)} %get-tuple-element.219.dq_ref, bf16[2,1024,256]{2,1,0:T(8,128)(2,1)} %get-tuple-element.220.dk_ref, bf16[2,1024,256]{2,1,0:T(8,128)(2,1)} %get-tuple-element.221.dv_ref, bf16[1024,1536]{1,0:T(8,128)(2,1)} %bitcast.118), custom_call_target="tpu_custom_call" | custom-call | flops 6442450944 | bytes 1048576 | tf_op jit(solution)/shard_map/input_grads/pallas_call | solution.py:441
  257.1 7.1 %input_grads.2 = (f32[3,2,128,1024]{3,2,1,0:T(8,128)}, bf16[3,2,128,1024]{3,2,1,0:T(8,128)(2,1)}) custom-call(bf16[2,256,512]{2,1,0:T(8,128)(2,1)} %get-tuple-element.219.dq_ref, bf16[2,1024,256]{2,1,0:T(8,128)(2,1)} %get-tuple-element.220.dk_ref, bf16[2,1024,256]{2,1,0:T(8,128)(2,1)} %get-tuple-element.221.dv_ref, bf16[1024,1536]{1,0:T(8,128)(2,1)} %bitcast.119), custom_call_target="tpu_custom_call" | custom-call | flops 6442450944 | bytes 1048576 | tf_op jit(solution)/shard_map/input_grads/pallas_call | solution.py:441
  264.1 3.4 collective-permute-done.36.came_ref
  267.6 2.2 collective-permute-done.35.came_ref
  269.8 2.4 down_add.3
  273.6 2.3 half_sum.3
  275.9 2.5 half_sum.2
  278.4 7.0 %collective-permute-done.37.refs_2_ = bf16[2,128,1024]{2,1,0:T(8,128)(2,1)S(1)} collective-permute-done((bf16[2,128,1024]{2,1,0:T(8,128)(2,1)}, bf16[2,128,1024]{2,1,0:T(8,128)(2,1)S(1)}, u32[]{:S(2)}, u32[]{:S(2)}) %collective-permute-start.37) | collective-permute-done | bytes 524320 | tf_op jit(solution)/shard_map/ppermute | solution.py:59
  286.7 2.4 down_add.4
  289.0 2.6 collective-permute-start.39
  291.6 1.7 collective-permute-start.40
  293.3 1.5 collective-permute-start.41
  296.0 6.6 %collective-permute-done.41.low_came = bf16[128,1536]{1,0:T(8,128)(2,1)S(1)} collective-permute-done((bf16[128,1536]{1,0:T(8,128)(2,1)S(1)}, bf16[128,1536]{1,0:T(8,128)(2,1)S(1)}, u32[]{:S(2)}, u32[]{:S(2)}) %collective-permute-start.41) | collective-permute-done | bytes 393248 | tf_op jit(solution)/shard_map/ppermute | solution.py:40
  303.5 2.8 to_ctx.1
  306.4 1.7 collective-permute-start.43
  309.5 2.4 collective-permute-start.45
  311.9 2.3 down_add.5
  314.2 3.8 %all-to-all-start.1 = ((bf16[4,64,1920]{2,1,0:T(8,128)(2,1)}), bf16[4,64,1920]{2,1,0:T(8,128)(2,1)S(1)}, u32[]{:S(2)}, u32[]{:S(2)}) async-start(bf16[4,64,1920]{2,1,0:T(8,128)(2,1)} %reduce-scatter.2.cloned.1.call-done), calls=%async_computation.2 | async-start | bytes 1966080 | tf_op jit(solution)/shard_map/all_to_all | solution.py:1003
  319.2 6.0 %collective-permute-done.43 = bf16[80,1536]{1,0:T(8,128)(2,1)S(1)} collective-permute-done((bf16[80,1536]{1,0:T(8,128)(2,1)}, bf16[80,1536]{1,0:T(8,128)(2,1)S(1)}, u32[]{:S(2)}, u32[]{:S(2)}) %collective-permute-start.43) | collective-permute-done | bytes 245792 | tf_op jit(solution)/shard_map/ppermute | solution.py:59
  329.7 2.4 finish.1
  332.2 3.5 %collective-permute-done.42.came_ref = bf16[2,128,1024]{2,1,0:T(8,128)(2,1)S(1)} collective-permute-done((bf16[2,128,1024]{2,1,0:T(8,128)(2,1)S(1)}, bf16[2,128,1024]{2,1,0:T(8,128)(2,1)S(1)}, u32[]{:S(2)}, u32[]{:S(2)}) %collective-permute-start.42) | collective-permute-done | bytes 524320 | tf_op jit(solution)/shard_map/ppermute | solution.py:50
  336.5 3.0 last_step.1
  (205 shorter events, 39.9 us)
Async XLA Ops:
  7.2 8.3 %copy-start.17 = (bf16[512,64]{0,1:T(8,128)(2,1)S(1)}, bf16[512,64]{0,1:T(8,128)(2,1)}, u32[]{:S(2)}) copy-start(bf16[512,64]{0,1:T(8,128)(2,1)} %param.22) | copy-start | bytes 196612
  7.2 8.3 %copy-start.19 = (bf16[64,256]{1,0:T(8,128)(2,1)S(1)}, bf16[64,256]{1,0:T(8,128)(2,1)}, u32[]{:S(2)}) copy-start(bf16[64,256]{1,0:T(8,128)(2,1)} %param.21) | copy-start | bytes 98308
  7.2 8.3 %copy-start.20 = (bf16[64,256]{1,0:T(8,128)(2,1)S(1)}, bf16[64,256]{1,0:T(8,128)(2,1)}, u32[]{:S(2)}) copy-start(bf16[64,256]{1,0:T(8,128)(2,1)} %param.20) | copy-start | bytes 98308
  7.2 8.3 %copy-start.18 = (bf16[64,512]{1,0:T(8,128)(2,1)S(1)}, bf16[64,512]{1,0:T(8,128)(2,1)}, u32[]{:S(2)}) copy-start(bf16[64,512]{1,0:T(8,128)(2,1)} %param.19) | copy-start | bytes 196612
  9.7 61.2 %copy-start.6 = (bf16[2,128,1024]{2,1,0:T(8,128)(2,1)}, bf16[2,128,1024]{2,1,0:T(8,128)(2,1)S(1)}, u32[]{:S(2)}) copy-start(bf16[2,128,1024]{2,1,0:T(8,128)(2,1)S(1)} %fusion.2.refs_0_) | copy-start | bytes 1572868
  9.8 28.8 %collective-permute-start = (bf16[2,128,1024]{2,1,0:T(8,128)(2,1)S(1)}, bf16[2,128,1024]{2,1,0:T(8,128)(2,1)}, u32[]{:S(2)}, u32[]{:S(2)}) collective-permute-start(bf16[2,128,1024]{2,1,0:T(8,128)(2,1)S(1)} %fusion.2.refs_0_), channel_id=1, source_target_pairs={{0,2},{2,4},{4,6},{1,3},{3,5},{5,7},{8,10},{10,12},{12,14},{9,11},... | collective-permute-start | bytes 1572872 | tf_op jit(solution)/shard_map/ppermute | solution.py:45
  15.6 15.7 %collective-permute-start.3 = (bf16[64,1536]{1,0:T(8,128)(2,1)S(1)}, bf16[64,1536]{1,0:T(8,128)(2,1)S(1)}, u32[]{:S(2)}, u32[]{:S(2)}) collective-permute-start(bf16[64,1536]{1,0:T(8,128)(2,1)S(1)} %pad_maximum_fusion.7), channel_id=1, source_target_pairs={{0,6},{2,0},{4,2},{6,4},{1,7},{3,1},{5,3},{7,5},{8,14},{10,8},{12,... | collective-permute-start | bytes 589832 | tf_op jit(solution)/shard_map/ppermute | solution.py:59
  16.2 19.3 %collective-permute-start.2 = (bf16[64,1536]{1,0:T(8,128)(2,1)S(1)}, bf16[64,1536]{1,0:T(8,128)(2,1)S(1)}, u32[]{:S(2)}, u32[]{:S(2)}) collective-permute-start(bf16[64,1536]{1,0:T(8,128)(2,1)S(1)} %pad_maximum_fusion.7), channel_id=1, source_target_pairs={{0,4},{2,6},{4,0},{6,2},{1,5},{3,7},{5,1},{7,3},{8,12},{10,14},{12... | collective-permute-start | bytes 589832 | tf_op jit(solution)/shard_map/ppermute | solution.py:59
  17.9 20.7 %collective-permute-start.1 = (bf16[64,1536]{1,0:T(8,128)(2,1)S(1)}, bf16[64,1536]{1,0:T(8,128)(2,1)S(1)}, u32[]{:S(2)}, u32[]{:S(2)}) collective-permute-start(bf16[64,1536]{1,0:T(8,128)(2,1)S(1)} %pad_maximum_fusion.7), channel_id=1, source_target_pairs={{0,2},{2,4},{4,6},{6,0},{1,3},{3,5},{5,7},{7,1},{8,10},{10,12},{12... | collective-permute-start | bytes 589832 | tf_op jit(solution)/shard_map/ppermute | solution.py:59
  21.6 32.2 %all-to-all-start = ((bf16[4,64,1920]{2,1,0:T(8,128)(2,1)}), bf16[4,64,1920]{2,1,0:T(8,128)(2,1)S(1)}, u32[]{:S(2)}, u32[]{:S(2)}) async-start(bf16[4,64,1920]{2,1,0:T(8,128)(2,1)} %pack.1), calls=%async_computation | async-start | bytes 1966080 | tf_op jit(solution)/shard_map/all_to_all | solution.py:870
  25.3 120.3 %all-gather.2.cloned.1.call-start = ((), (), s32[]{:S(2)}) async-start(), calls=%async_computation.3 | async-start | bytes 4915200 | tf_op jit(solution)/shard_map/all_gather | solution.py:882
  38.8 11.8 %collective-permute-start.10 = (bf16[1,128,1536]{2,1,0:T(8,128)(2,1)S(1)}, bf16[1,128,1536]{2,1,0:T(8,128)(2,1)S(1)}, u32[]{:S(2)}, u32[]{:S(2)}) collective-permute-start(bf16[1,128,1536]{2,1,0:T(8,128)(2,1)S(1)} %bitcast.125), channel_id=1, source_target_pairs={{0,8},{8,0},{16,24},{24,16},{1,9},{9,1},{17,25},{25,17},{2,10},{10... | collective-permute-start | bytes 1179656 | tf_op jit(solution)/shard_map/ppermute | solution.py:40
  40.4 11.7 %collective-permute-start.12 = (bf16[1,128,1536]{2,1,0:T(8,128)(2,1)S(1)}, bf16[1,128,1536]{2,1,0:T(8,128)(2,1)S(1)}, u32[]{:S(2)}, u32[]{:S(2)}) collective-permute-start(bf16[1,128,1536]{2,1,0:T(8,128)(2,1)S(1)} %bitcast.122), channel_id=1, source_target_pairs={{0,16},{8,24},{16,0},{24,8},{1,17},{9,25},{17,1},{25,9},{2,18},{10... | collective-permute-start | bytes 1179656 | tf_op jit(solution)/shard_map/ppermute | solution.py:40
  42.0 24.7 %copy-start.24 = (pred[2,128]{1,0:T(4,128)(4,1)}, pred[2,128]{1,0:T(4,128)(4,1)S(1)}, u32[]{:S(2)}) copy-start(pred[2,128]{1,0:T(4,128)(4,1)S(1)} %broadcast_compare_fusion) | copy-start | bytes 772
  42.0 17.7 %collective-permute-start.4 = (bf16[2,128,1024]{2,1,0:T(8,128)(2,1)}, bf16[2,128,1024]{2,1,0:T(8,128)(2,1)}, u32[]{:S(2)}, u32[]{:S(2)}) collective-permute-start(bf16[2,128,1024]{2,1,0:T(8,128)(2,1)} %collective-permute-done.refs_2_), channel_id=1, source_target_pairs={{0,2},{2,4},{4,6},{1,3},{3,5},{5,7},{8,10},{10,12},{12,14},{9,11},... | collective-permute-start | bytes 1572872 | tf_op jit(solution)/shard_map/ppermute | solution.py:45
  50.5 15.0 %copy-start.38 = (f32[64]{0:T(128)S(1)}, f32[64]{0:T(128)}, u32[]{:S(2)}) copy-start(f32[64]{0:T(128)} %param.17) | copy-start | bytes 772
  50.5 15.6 %copy-start.39 = (f32[64]{0:T(128)S(1)}, f32[64]{0:T(128)}, u32[]{:S(2)}) copy-start(f32[64]{0:T(128)} %param.18) | copy-start | bytes 772
  51.5 21.8 %collective-permute-start.11 = (bf16[2,128,1536]{2,1,0:T(8,128)(2,1)}, bf16[2,128,1536]{2,1,0:T(8,128)(2,1)}, u32[]{:S(2)}, u32[]{:S(2)}) collective-permute-start(bf16[2,128,1536]{2,1,0:T(8,128)(2,1)} %pad_maximum_fusion.5), channel_id=1, source_target_pairs={{0,16},{8,24},{16,0},{24,8},{1,17},{9,25},{17,1},{25,9},{2,18},{10... | collective-permute-start | bytes 2359304 | tf_op jit(solution)/shard_map/ppermute | solution.py:40
  52.0 14.7 %copy-start.9 = (bf16[1,128,1536]{2,1,0:T(8,128)(2,1)}, bf16[1,128,1536]{2,1,0:T(8,128)(2,1)S(1)}, u32[]{:S(2)}) copy-start(bf16[1,128,1536]{2,1,0:T(8,128)(2,1)S(1)} %collective-permute-done.12) | copy-start | bytes 1179652
  53.0 22.1 %collective-permute-start.13 = (bf16[2,128,1536]{2,1,0:T(8,128)(2,1)}, bf16[2,128,1536]{2,1,0:T(8,128)(2,1)}, u32[]{:S(2)}, u32[]{:S(2)}) collective-permute-start(bf16[2,128,1536]{2,1,0:T(8,128)(2,1)} %pad_maximum_fusion.6), channel_id=1, source_target_pairs={{0,8},{8,0},{16,24},{24,16},{1,9},{9,1},{17,25},{25,17},{2,10},{10... | collective-permute-start | bytes 2359304 | tf_op jit(solution)/shard_map/ppermute | solution.py:40
  53.8 17.6 %copy-start.4 = (bf16[4,64,1920]{2,1,0:T(8,128)(2,1)}, bf16[4,64,1920]{2,1,0:T(8,128)(2,1)S(1)}, u32[]{:S(2)}) copy-start(bf16[4,64,1920]{2,1,0:T(8,128)(2,1)S(1)} %all-to-all-done) | copy-start | bytes 2949124
  59.8 13.5 %collective-permute-start.5 = (bf16[2,128,1024]{2,1,0:T(8,128)(2,1)}, bf16[2,128,1024]{2,1,0:T(8,128)(2,1)}, u32[]{:S(2)}, u32[]{:S(2)}) collective-permute-start(bf16[2,128,1024]{2,1,0:T(8,128)(2,1)} %collective-permute-done.4.refs_4_), channel_id=1, source_target_pairs={{0,2},{2,4},{4,6},{1,3},{3,5},{5,7},{8,10},{10,12},{12,14},{9,11},... | collective-permute-start | bytes 1572872 | tf_op jit(solution)/shard_map/ppermute | solution.py:45
  71.0 6.1 %collective-permute-start.7 = (bf16[2,128,1024]{2,1,0:T(8,128)(2,1)}, bf16[2,128,1024]{2,1,0:T(8,128)(2,1)}, u32[]{:S(2)}, u32[]{:S(2)}) collective-permute-start(bf16[2,128,1024]{2,1,0:T(8,128)(2,1)} %collective-permute-done.refs_2_), channel_id=1, source_target_pairs={{0,1},{1,0},{2,3},{3,2},{4,5},{5,4},{6,7},{7,6},{8,9},{9,8},{10,11... | collective-permute-start | bytes 1572872 | tf_op jit(solution)/shard_map/ppermute | solution.py:35
  71.0 6.0 %collective-permute-start.6 = (bf16[2,128,1024]{2,1,0:T(8,128)(2,1)S(1)}, bf16[2,128,1024]{2,1,0:T(8,128)(2,1)}, u32[]{:S(2)}, u32[]{:S(2)}) collective-permute-start(bf16[2,128,1024]{2,1,0:T(8,128)(2,1)S(1)} %fusion.2.refs_0_), channel_id=1, source_target_pairs={{0,1},{1,0},{2,3},{3,2},{4,5},{5,4},{6,7},{7,6},{8,9},{9,8},{10,11... | collective-permute-start | bytes 1572872 | tf_op jit(solution)/shard_map/ppermute | solution.py:35
  71.5 213.9 %reduce-scatter.2.cloned.1.call-start = ((), (), s32[]{:S(2)}) async-start(), calls=%async_computation.4 | async-start | bytes 4915200 | tf_op jit(solution)/shard_map/reduce_scatter | solution.py:933
  73.3 3.8 %collective-permute-start.8 = (bf16[2,128,1024]{2,1,0:T(8,128)(2,1)}, bf16[2,128,1024]{2,1,0:T(8,128)(2,1)S(1)}, u32[]{:S(2)}, u32[]{:S(2)}) collective-permute-start(bf16[2,128,1024]{2,1,0:T(8,128)(2,1)} %collective-permute-done.4.refs_4_), channel_id=1, source_target_pairs={{0,1},{1,0},{2,3},{3,2},{4,5},{5,4},{6,7},{7,6},{8,9},{9,8},{10,11... | collective-permute-start | bytes 1572872 | tf_op jit(solution)/shard_map/ppermute | solution.py:35
  73.3 3.8 %collective-permute-start.9 = (bf16[2,128,1024]{2,1,0:T(8,128)(2,1)}, bf16[2,128,1024]{2,1,0:T(8,128)(2,1)S(1)}, u32[]{:S(2)}, u32[]{:S(2)}) collective-permute-start(bf16[2,128,1024]{2,1,0:T(8,128)(2,1)} %collective-permute-done.5.refs_6_), channel_id=1, source_target_pairs={{0,1},{1,0},{2,3},{3,2},{4,5},{5,4},{6,7},{7,6},{8,9},{9,8},{10,11... | collective-permute-start | bytes 1572872 | tf_op jit(solution)/shard_map/ppermute | solution.py:35
  77.1 26.5 %collective-permute-start.16 = (bf16[2,128,1024]{2,1,0:T(8,128)(2,1)S(1)}, bf16[2,128,1024]{2,1,0:T(8,128)(2,1)S(1)}, u32[]{:S(2)}, u32[]{:S(2)}) collective-permute-start(bf16[2,128,1024]{2,1,0:T(8,128)(2,1)S(1)} %broadcast_select_fusion), channel_id=1, source_target_pairs={{0,24},{8,16},{16,8},{24,0},{1,25},{9,17},{17,9},{25,1},{2,26},{10... | collective-permute-start | bytes 1572872 | tf_op jit(solution)/shard_map/ppermute | solution.py:40
  77.6 26.0 %collective-permute-start.15 = (bf16[2,128,1024]{2,1,0:T(8,128)(2,1)S(1)}, bf16[2,128,1024]{2,1,0:T(8,128)(2,1)S(1)}, u32[]{:S(2)}, u32[]{:S(2)}) collective-permute-start(bf16[2,128,1024]{2,1,0:T(8,128)(2,1)S(1)} %broadcast_select_fusion), channel_id=1, source_target_pairs={{0,16},{8,24},{16,0},{24,8},{1,17},{9,25},{17,1},{25,9},{2,18},{10... | collective-permute-start | bytes 1572872 | tf_op jit(solution)/shard_map/ppermute | solution.py:40
  79.1 24.4 %collective-permute-start.14 = (bf16[2,128,1024]{2,1,0:T(8,128)(2,1)S(1)}, bf16[2,128,1024]{2,1,0:T(8,128)(2,1)S(1)}, u32[]{:S(2)}, u32[]{:S(2)}) collective-permute-start(bf16[2,128,1024]{2,1,0:T(8,128)(2,1)S(1)} %broadcast_select_fusion), channel_id=1, source_target_pairs={{0,8},{8,0},{16,24},{24,16},{1,9},{9,1},{17,25},{25,17},{2,10},{10... | collective-permute-start | bytes 1572872 | tf_op jit(solution)/shard_map/ppermute | solution.py:40
  105.4 2.7 collective-permute-start.17
  108.5 14.0 %collective-permute-start.19 = (bf16[2,128,1024]{2,1,0:T(8,128)(2,1)S(1)}, bf16[2,128,1024]{2,1,0:T(8,128)(2,1)S(1)}, u32[]{:S(2)}, u32[]{:S(2)}) collective-permute-start(bf16[2,128,1024]{2,1,0:T(8,128)(2,1)S(1)} %multiply_convert_fusion), channel_id=1, source_target_pairs={{0,16},{8,24},{16,0},{24,8},{1,17},{9,25},{17,1},{25,9},{2,18},{10... | collective-permute-start | bytes 1572872 | tf_op jit(solution)/shard_map/ppermute | solution.py:40
  109.1 14.8 %collective-permute-start.18 = (bf16[2,128,1024]{2,1,0:T(8,128)(2,1)S(1)}, bf16[2,128,1024]{2,1,0:T(8,128)(2,1)S(1)}, u32[]{:S(2)}, u32[]{:S(2)}) collective-permute-start(bf16[2,128,1024]{2,1,0:T(8,128)(2,1)S(1)} %multiply_convert_fusion), channel_id=1, source_target_pairs={{0,8},{8,0},{16,24},{24,16},{1,9},{9,1},{17,25},{25,17},{2,10},{10... | collective-permute-start | bytes 1572872 | tf_op jit(solution)/shard_map/ppermute | solution.py:40
  109.6 25.4 %collective-permute-start.20 = (bf16[2,128,1024]{2,1,0:T(8,128)(2,1)S(1)}, bf16[2,128,1024]{2,1,0:T(8,128)(2,1)S(1)}, u32[]{:S(2)}, u32[]{:S(2)}) collective-permute-start(bf16[2,128,1024]{2,1,0:T(8,128)(2,1)S(1)} %multiply_convert_fusion), channel_id=1, source_target_pairs={{0,24},{8,16},{16,8},{24,0},{1,25},{9,17},{17,9},{25,1},{2,26},{10... | collective-permute-start | bytes 1572872 | tf_op jit(solution)/shard_map/ppermute | solution.py:40
  113.7 31.9 %collective-permute-start.22 = (bf16[4,2,128,1024]{3,2,1,0:T(8,128)(2,1)}, bf16[4,2,128,1024]{3,2,1,0:T(8,128)(2,1)}, u32[]{:S(2)}, u32[]{:S(2)}) collective-permute-start(bf16[4,2,128,1024]{3,2,1,0:T(8,128)(2,1)} %pad_maximum_fusion.2), channel_id=1, source_target_pairs={{0,1},{1,0},{2,3},{3,2},{4,5},{5,4},{6,7},{7,6},{8,9},{9,8},{10,11... | collective-permute-start | bytes 6291464 | tf_op jit(solution)/shard_map/ppermute | solution.py:35
  136.6 9.0 %collective-permute-start.21 = (bf16[4,2,128,1024]{3,2,1,0:T(8,128)(2,1)}, bf16[4,2,128,1024]{3,2,1,0:T(8,128)(2,1)}, u32[]{:S(2)}, u32[]{:S(2)}) collective-permute-start(bf16[4,2,128,1024]{3,2,1,0:T(8,128)(2,1)} %pad_maximum_fusion.1), channel_id=1, source_target_pairs={{0,1},{1,0},{2,3},{3,2},{4,5},{5,4},{6,7},{7,6},{8,9},{9,8},{10,11... | collective-permute-start | bytes 6291464 | tf_op jit(solution)/shard_map/ppermute | solution.py:35
  164.9 3.7 %collective-permute-start.23 = (bf16[3,2,128,1024]{3,2,1,0:T(8,128)(2,1)}, bf16[3,2,128,1024]{3,2,1,0:T(8,128)(2,1)S(1)}, u32[]{:S(2)}, u32[]{:S(2)}) collective-permute-start(bf16[3,2,128,1024]{3,2,1,0:T(8,128)(2,1)} %bitcast.152), channel_id=1, source_target_pairs={{0,1},{1,0},{2,3},{3,2},{4,5},{5,4},{6,7},{7,6},{8,9},{9,8},{10,11... | collective-permute-start | bytes 4718600 | tf_op jit(solution)/shard_map/ppermute | solution.py:35
  164.9 8.7 %collective-permute-start.24 = (bf16[3,2,128,1024]{3,2,1,0:T(8,128)(2,1)}, bf16[3,2,128,1024]{3,2,1,0:T(8,128)(2,1)S(1)}, u32[]{:S(2)}, u32[]{:S(2)}) collective-permute-start(bf16[3,2,128,1024]{3,2,1,0:T(8,128)(2,1)} %bitcast.151), channel_id=1, source_target_pairs={{0,1},{1,0},{2,3},{3,2},{4,5},{5,4},{6,7},{7,6},{8,9},{9,8},{10,11... | collective-permute-start | bytes 4718600 | tf_op jit(solution)/shard_map/ppermute | solution.py:35
  170.1 28.0 %collective-permute-start.25 = (bf16[2,128,1024]{2,1,0:T(8,128)(2,1)}, bf16[2,128,1024]{2,1,0:T(8,128)(2,1)S(1)}, u32[]{:S(2)}, u32[]{:S(2)}) collective-permute-start(bf16[2,128,1024]{2,1,0:T(8,128)(2,1)} %get-tuple-element.184), channel_id=1, source_target_pairs={{0,8},{8,0},{16,24},{24,16},{1,9},{9,1},{17,25},{25,17},{2,10},{10... | collective-permute-start | bytes 1572872 | tf_op jit(solution)/shard_map/ppermute | solution.py:40
  171.6 26.5 %collective-permute-start.26 = (bf16[2,128,1024]{2,1,0:T(8,128)(2,1)}, bf16[2,128,1024]{2,1,0:T(8,128)(2,1)S(1)}, u32[]{:S(2)}, u32[]{:S(2)}) collective-permute-start(bf16[2,128,1024]{2,1,0:T(8,128)(2,1)} %get-tuple-element.185), channel_id=1, source_target_pairs={{0,16},{8,24},{16,0},{24,8},{1,17},{9,25},{17,1},{25,9},{2,18},{10... | collective-permute-start | bytes 1572872 | tf_op jit(solution)/shard_map/ppermute | solution.py:40
  173.1 25.0 %collective-permute-start.27 = (bf16[2,128,1024]{2,1,0:T(8,128)(2,1)}, bf16[2,128,1024]{2,1,0:T(8,128)(2,1)S(1)}, u32[]{:S(2)}, u32[]{:S(2)}) collective-permute-start(bf16[2,128,1024]{2,1,0:T(8,128)(2,1)} %get-tuple-element.186), channel_id=1, source_target_pairs={{0,24},{8,16},{16,8},{24,0},{1,25},{9,17},{17,9},{25,1},{2,26},{10... | collective-permute-start | bytes 1572872 | tf_op jit(solution)/shard_map/ppermute | solution.py:40
  198.1 2.2 collective-permute-start.28
  203.7 2.3 collective-permute-start.29
  203.8 33.9 %collective-permute-start.30 = (bf16[2,128,1024]{2,1,0:T(8,128)(2,1)}, bf16[2,128,1024]{2,1,0:T(8,128)(2,1)S(1)}, u32[]{:S(2)}, u32[]{:S(2)}) collective-permute-start(bf16[2,128,1024]{2,1,0:T(8,128)(2,1)} %bitcast.52), channel_id=1, source_target_pairs={{0,1},{1,0},{2,3},{3,2},{4,5},{5,4},{6,7},{7,6},{8,9},{9,8},{10,11... | collective-permute-start | bytes 1572872 | tf_op jit(solution)/shard_map/ppermute | solution.py:35
  209.0 28.8 %collective-permute-start.31 = (bf16[2,128,1024]{2,1,0:T(8,128)(2,1)S(1)}, bf16[2,128,1024]{2,1,0:T(8,128)(2,1)S(1)}, u32[]{:S(2)}, u32[]{:S(2)}) collective-permute-start(bf16[2,128,1024]{2,1,0:T(8,128)(2,1)S(1)} %get-tuple-element.205), channel_id=1, source_target_pairs={{0,8},{8,0},{16,24},{24,16},{1,9},{9,1},{17,25},{25,17},{2,10},{10... | collective-permute-start | bytes 1572872 | tf_op jit(solution)/shard_map/ppermute | solution.py:40
  210.4 27.3 %collective-permute-start.32 = (bf16[2,128,1024]{2,1,0:T(8,128)(2,1)S(1)}, bf16[2,128,1024]{2,1,0:T(8,128)(2,1)S(1)}, u32[]{:S(2)}, u32[]{:S(2)}) collective-permute-start(bf16[2,128,1024]{2,1,0:T(8,128)(2,1)S(1)} %get-tuple-element.206), channel_id=1, source_target_pairs={{0,16},{8,24},{16,0},{24,8},{1,17},{9,25},{17,1},{25,9},{2,18},{10... | collective-permute-start | bytes 1572872 | tf_op jit(solution)/shard_map/ppermute | solution.py:40
  211.9 25.9 %collective-permute-start.33 = (bf16[2,128,1024]{2,1,0:T(8,128)(2,1)S(1)}, bf16[2,128,1024]{2,1,0:T(8,128)(2,1)S(1)}, u32[]{:S(2)}, u32[]{:S(2)}) collective-permute-start(bf16[2,128,1024]{2,1,0:T(8,128)(2,1)S(1)} %get-tuple-element.207), channel_id=1, source_target_pairs={{0,24},{8,16},{16,8},{24,0},{1,25},{9,17},{17,9},{25,1},{2,26},{10... | collective-permute-start | bytes 1572872 | tf_op jit(solution)/shard_map/ppermute | solution.py:40
  248.5 7.2 %copy-start.12 = (bf16[256,1024]{1,0:T(8,128)(2,1)S(1)}, bf16[256,1024]{1,0:T(8,128)(2,1)}, u32[]{:S(2)}) copy-start(bf16[256,1024]{1,0:T(8,128)(2,1)} %get-tuple-element.203) | copy-start | bytes 1572868
  248.5 7.1 %copy-start.25 = (pred[2,128]{1,0:T(4,128)(4,1)S(1)}, pred[2,128]{1,0:T(4,128)(4,1)}, u32[]{:S(2)}) copy-start(pred[2,128]{1,0:T(4,128)(4,1)} %copy-done.24) | copy-start | bytes 772
  248.5 19.0 %collective-permute-start.36 = (bf16[256,1536]{1,0:T(8,128)(2,1)}, bf16[256,1536]{1,0:T(8,128)(2,1)S(1)}, u32[]{:S(2)}, u32[]{:S(2)}) collective-permute-start(bf16[256,1536]{1,0:T(8,128)(2,1)} %get-tuple-element.231), channel_id=1, source_target_pairs={{0,16},{8,24},{16,0},{24,8},{1,17},{9,25},{17,1},{25,9},{2,18},{10... | collective-permute-start | bytes 2359304 | tf_op jit(solution)/shard_map/ppermute | solution.py:40
  250.1 19.7 %collective-permute-start.35 = (bf16[272,1536]{1,0:T(8,128)(2,1)}, bf16[272,1536]{1,0:T(8,128)(2,1)S(1)}, u32[]{:S(2)}, u32[]{:S(2)}) collective-permute-start(bf16[272,1536]{1,0:T(8,128)(2,1)} %get-tuple-element.230), channel_id=1, source_target_pairs={{0,8},{8,0},{16,24},{24,16},{1,9},{9,1},{17,25},{25,17},{2,10},{10... | collective-permute-start | bytes 2506760 | tf_op jit(solution)/shard_map/ppermute | solution.py:40
  255.7 8.5 %collective-permute-start.34 = (bf16[1,2,128,1024]{3,2,1,0:T(8,128)(2,1)}, bf16[1,2,128,1024]{3,2,1,0:T(8,128)(2,1)S(1)}, u32[]{:S(2)}, u32[]{:S(2)}) collective-permute-start(bf16[1,2,128,1024]{3,2,1,0:T(8,128)(2,1)} %get-tuple-element.224), channel_id=1, source_target_pairs={{0,1},{1,0},{2,3},{3,2},{4,5},{5,4},{6,7},{7,6},{8,9},{9,8},{10,11... | collective-permute-start | bytes 1572872 | tf_op jit(solution)/shard_map/ppermute | solution.py:35
  272.2 13.1 %collective-permute-start.37 = (bf16[2,128,1024]{2,1,0:T(8,128)(2,1)}, bf16[2,128,1024]{2,1,0:T(8,128)(2,1)S(1)}, u32[]{:S(2)}, u32[]{:S(2)}) collective-permute-start(bf16[2,128,1024]{2,1,0:T(8,128)(2,1)} %down_add.3), channel_id=1, source_target_pairs={{0,6},{2,0},{4,2},{6,4},{1,7},{3,1},{5,3},{7,5},{8,14},{10,8},{12,... | collective-permute-start | bytes 1572872 | tf_op jit(solution)/shard_map/ppermute | solution.py:59
  273.6 11.8 %collective-permute-start.38 = (bf16[3,2,128,1024]{3,2,1,0:T(8,128)(2,1)}, bf16[3,2,128,1024]{3,2,1,0:T(8,128)(2,1)S(1)}, u32[]{:S(2)}, u32[]{:S(2)}) collective-permute-start(bf16[3,2,128,1024]{3,2,1,0:T(8,128)(2,1)} %get-tuple-element.235), channel_id=1, source_target_pairs={{0,1},{1,0},{2,3},{3,2},{4,5},{5,4},{6,7},{7,6},{8,9},{9,8},{10,11... | collective-permute-start | bytes 4718600 | tf_op jit(solution)/shard_map/ppermute | solution.py:35
  289.0 13.6 %collective-permute-start.39 = (bf16[2,128,1024]{2,1,0:T(8,128)(2,1)}, bf16[2,128,1024]{2,1,0:T(8,128)(2,1)S(1)}, u32[]{:S(2)}, u32[]{:S(2)}) collective-permute-start(bf16[2,128,1024]{2,1,0:T(8,128)(2,1)} %down_add.4), channel_id=1, source_target_pairs={{0,6},{2,0},{4,2},{6,4},{1,7},{3,1},{5,3},{7,5},{8,14},{10,8},{12,... | collective-permute-start | bytes 1572872 | tf_op jit(solution)/shard_map/ppermute | solution.py:59
  291.6 11.0 %collective-permute-start.40 = (bf16[144,1536]{1,0:T(8,128)(2,1)S(1)}, bf16[144,1536]{1,0:T(8,128)(2,1)S(1)}, u32[]{:S(2)}, u32[]{:S(2)}) collective-permute-start(bf16[144,1536]{1,0:T(8,128)(2,1)S(1)} %copy-done.21), channel_id=1, source_target_pairs={{0,16},{8,24},{16,0},{24,8},{1,17},{9,25},{17,1},{25,9},{2,18},{10... | collective-permute-start | bytes 1327112 | tf_op jit(solution)/shard_map/ppermute | solution.py:40
  293.3 9.3 %collective-permute-start.41 = (bf16[128,1536]{1,0:T(8,128)(2,1)S(1)}, bf16[128,1536]{1,0:T(8,128)(2,1)S(1)}, u32[]{:S(2)}, u32[]{:S(2)}) collective-permute-start(bf16[128,1536]{1,0:T(8,128)(2,1)S(1)} %copy-done.36), channel_id=1, source_target_pairs={{0,8},{8,0},{16,24},{24,16},{1,9},{9,1},{17,25},{25,17},{2,10},{10... | collective-permute-start | bytes 1179656 | tf_op jit(solution)/shard_map/ppermute | solution.py:40
  306.4 18.8 %collective-permute-start.43 = (bf16[80,1536]{1,0:T(8,128)(2,1)}, bf16[80,1536]{1,0:T(8,128)(2,1)S(1)}, u32[]{:S(2)}, u32[]{:S(2)}) collective-permute-start(bf16[80,1536]{1,0:T(8,128)(2,1)} %get-tuple-element.264), channel_id=1, source_target_pairs={{0,4},{2,6},{4,0},{6,2},{1,5},{3,7},{5,1},{7,3},{8,12},{10,14},{12... | collective-permute-start | bytes 737288 | tf_op jit(solution)/shard_map/ppermute | solution.py:59
  308.0 17.2 %collective-permute-start.44 = (bf16[80,1536]{1,0:T(8,128)(2,1)}, bf16[80,1536]{1,0:T(8,128)(2,1)S(1)}, u32[]{:S(2)}, u32[]{:S(2)}) collective-permute-start(bf16[80,1536]{1,0:T(8,128)(2,1)} %get-tuple-element.265), channel_id=1, source_target_pairs={{0,2},{2,4},{4,6},{6,0},{1,3},{3,5},{5,7},{7,1},{8,10},{10,12},{12... | collective-permute-start | bytes 737288 | tf_op jit(solution)/shard_map/ppermute | solution.py:59
  309.5 15.7 %collective-permute-start.45 = (bf16[80,1536]{1,0:T(8,128)(2,1)}, bf16[80,1536]{1,0:T(8,128)(2,1)S(1)}, u32[]{:S(2)}, u32[]{:S(2)}) collective-permute-start(bf16[80,1536]{1,0:T(8,128)(2,1)} %get-tuple-element.266), channel_id=1, source_target_pairs={{0,6},{2,0},{4,2},{6,4},{1,7},{3,1},{5,3},{7,5},{8,14},{10,8},{12,... | collective-permute-start | bytes 737288 | tf_op jit(solution)/shard_map/ppermute | solution.py:59
  314.2 12.0 %copy-start.15 = (f32[64,1536]{1,0:T(8,128)S(1)}, f32[64,1536]{1,0:T(8,128)}, u32[]{:S(2)}) copy-start(f32[64,1536]{1,0:T(8,128)} %get-tuple-element.267) | copy-start | bytes 1179652
  314.2 14.6 %all-to-all-start.1 = ((bf16[4,64,1920]{2,1,0:T(8,128)(2,1)}), bf16[4,64,1920]{2,1,0:T(8,128)(2,1)S(1)}, u32[]{:S(2)}, u32[]{:S(2)}) async-start(bf16[4,64,1920]{2,1,0:T(8,128)(2,1)} %reduce-scatter.2.cloned.1.call-done), calls=%async_computation.2 | async-start | bytes 1966080 | tf_op jit(solution)/shard_map/all_to_all | solution.py:1003
  317.9 17.8 %collective-permute-start.42 = (bf16[2,128,1024]{2,1,0:T(8,128)(2,1)S(1)}, bf16[2,128,1024]{2,1,0:T(8,128)(2,1)S(1)}, u32[]{:S(2)}, u32[]{:S(2)}) collective-permute-start(bf16[2,128,1024]{2,1,0:T(8,128)(2,1)S(1)} %copy-done.30), channel_id=1, source_target_pairs={{2,0},{4,2},{6,4},{3,1},{5,3},{7,5},{10,8},{12,10},{14,12},{11,9},... | collective-permute-start | bytes 1572872 | tf_op jit(solution)/shard_map/ppermute | solution.py:50
  326.1 1.6 collective-permute-start.46
  (27 other events, 75.5 us)
Sparse Core Ops, SparseCore 0:
  71.6 73.8 all-gather.1
  204.3 71.2 reduce-scatter.1
